TPU v7x, 32 devices: a whole 2x2x4 slice. The times are simulated.
32 devices in a mesh: dp: 4 (over y, x), vocab: 8 (over z, core).
Axes of the slice: x: 2, y: 2, z: 4, core: 2. Of those that a mesh axis runs over, the one named last changes fastest.
Arguments:
- hidden_t: bfloat16 [8192, 768], P(('dp', 'vocab')), may hold values from -6 to 6
- head: bfloat16 [8192, 10240], P('dp', 'vocab'), may hold values from -0.2 to 0.2
- teacher: bfloat16 [768, 10240], P('dp', 'vocab'), may hold values from -16 to 960
- labels: int32 [768], P('dp'), may hold values from 0 to 10239
- temps: float32 [4], replicated, may hold values from 1 to 4
- mix: float32 [2], replicated, may hold values from 0.3 to 1
Outputs:
- hidden_grad: float32 [8192, 768], P(('dp', 'vocab'))
- head_grad: bfloat16 [8192, 10240], P('dp', 'vocab')
All inputs are finite; a program needn't handle non-finite values.
Results may differ from a plain program's by a relative error of at most 0.012.
Values may be sent and summed in bfloat16 or wider, within the bound.
No kernel may reach another device: no remote copies, remote signals or barrier semaphores. Data moves between devices by JAX's collectives and lax.ppermute only.
A program may use at most 128 MiB of HBM per device.

v0:
```python
import jax
import jax.numpy as jnp
from jax import lax
from jax.sharding import PartitionSpec as P


def merged(value, axis, join):
    pieces = jax.tree.map(lambda part: lax.all_gather(part, axis), value)
    head = jax.tree.map(lambda part: part[0], pieces)
    tail = jax.tree.map(lambda part: part[1:], pieces)
    subtotal, _ = lax.scan(lambda subtotal, slab: (join(subtotal, slab), None), head, tail)
    return subtotal


def combine_stats(earlier, later):
    highest = jnp.maximum(earlier[0], later[0])
    summed = earlier[1] * jnp.exp(earlier[0] - highest) + later[1] * jnp.exp(later[0] - highest)
    return (highest, summed)


def shards(hidden_t, head, teacher, labels, temps, mix):
    h_block = lax.all_gather(hidden_t, "vocab", axis=0, tiled=True)
    block_width = head.shape[1]
    logits = lax.psum_scatter(
        lax.dot_general(
            h_block, head, (((0,), (0,)), ((), ())), preferred_element_type=jnp.float32
        ),
        "dp",
        scatter_dimension=0,
        tiled=True,
    )
    target = teacher.astype(jnp.float32)
    inverse = 1.0 / temps
    student = jnp.concatenate([logits[None], logits[None] * inverse[:, None, None]], axis=0)
    teacher_scaled = target[None] * inverse[:, None, None]
    stacked = jnp.concatenate([student, teacher_scaled], axis=0)
    local_peak = jnp.max(stacked, axis=2)
    local_total = jnp.sum(jnp.exp(stacked - local_peak[:, :, None]), axis=2)
    highest, summed = merged((local_peak, local_total), "vocab", combine_stats)
    softmaxes = jnp.exp(stacked - highest[:, :, None]) / summed[:, :, None]
    offset = lax.axis_index("vocab") * block_width
    columns = jnp.arange(block_width, dtype=jnp.int32)[None, :] + offset
    onehot = (columns == labels[:, None]).astype(jnp.float32)
    heat_count = temps.shape[0]
    logit_grad = mix[0] * (softmaxes[0] - onehot)
    weights = mix[1] * temps
    logit_grad = logit_grad + jnp.einsum(
        "k,kab->ab", weights, softmaxes[1 : 1 + heat_count] - softmaxes[1 + heat_count :]
    )
    logit_grad = logit_grad.astype(jnp.bfloat16)
    grad_all = lax.all_gather(logit_grad, "dp", axis=0, tiled=True)
    head_grad = jnp.dot(h_block, grad_all, preferred_element_type=jnp.float32).astype(jnp.bfloat16)
    hidden_grad = lax.psum_scatter(
        lax.dot_general(
            head, grad_all, (((1,), (1,)), ((), ())), preferred_element_type=jnp.float32
        ),
        "vocab",
        scatter_dimension=0,
        tiled=True,
    )
    return (hidden_grad, head_grad)


def solution(mesh):
    placed = (P(("dp", "vocab"), None), P("dp", "vocab"), P("dp", "vocab"), P("dp"), P(), P())
    return jax.shard_map(
        shards,
        mesh=mesh,
        in_specs=placed,
        out_specs=(P(("dp", "vocab"), None), P("dp", "vocab")),
        check_vma=False,
    )
```

profile of v0, /device:TPU:0, one launch (start us, length us, event | category | flops | bytes accessed | tf_op | source)
XLA Modules:
  0.0 275.8 jit_solution(13614077735387655445)
XLA Ops:
  7.2 0.0 all-gather.7.cloned.1.call-start
  7.2 0.7 all-gather.7.cloned.1.call-update
  7.9 0.0 copy-start.3
  7.9 0.0 reduce-scatter.3.cloned.1.call-start
  8.0 42.7 %all-gather.7.cloned.1.call-done = bf16[2048,768]{1,0:T(8,128)(2,1)} async-done(((bf16[256,768]{1,0:T(8,128)(2,1)}), bf16[2048,768]{1,0:T(8,128)(2,1)}) %all-gather.7.cloned.1.call-update) | async-done | bytes 3145744 | tf_op jit(solution)/shard_map/all_gather | solution.py:22
  50.7 9.7 %fusion.14 = f32[768,1280]{1,0:T(8,128)} fusion(bf16[2048,768]{1,0:T(8,128)(2,1)} %all-gather.7.cloned.1.call-done, bf16[2048,1280]{1,0:T(8,128)(2,1)} %param.9), kind=kOutput, calls=%fused_computation.30 | convolution fusion | flops 4026531840 | bytes 12320768 | tf_op jit(solution)/shard_map/dot_general | solution.py:25
  60.3 0.0 copy-start.4
  60.3 0.0 copy-start.7
  60.3 0.0 reduce-scatter.3.cloned.1.call-update
  60.4 0.0 all-gather.9.cloned.1.call-start
  60.4 0.0 copy-done.3
  60.4 0.1 convert_element_type.15
  60.5 0.5 copy-done.4
  61.0 0.6 fusion.13
  61.6 0.0 copy-done.7
  61.6 48.2 %reduce-scatter.3.cloned.1.call-done = f32[192,1280]{1,0:T(8,128)} async-done(((f32[768,1280]{1,0:T(8,128)}), f32[192,1280]{1,0:T(8,128)}) %reduce-scatter.3.cloned.1.call-update) | async-done | bytes 983056 | tf_op jit(solution)/shard_map/reduce_scatter | solution.py:24
  109.9 0.0 copy-start.2
  109.9 2.0 broadcast_multiply_fusion.1
  111.9 0.0 copy-start
  111.9 0.0 copy-start.1
  111.9 0.0 copy-done.2
  111.9 0.8 fusion.5
  112.8 2.1 exponential_reduce_fusion
  114.8 0.0 copy-done
  114.8 0.3 copy-done.1
  115.1 14.1 %all-gather.3 = f32[8,9,192]{2,1,0:T(8,128)S(1)} all-gather(f32[1,9,192]{2,1,0:T(8,128)S(1)} %bitcast.52), channel_id=3, replica_groups=mesh['dp'=4,'vocab'=8] {'vocab'}, dimensions={0}, use_global_device_ids=true | all-gather | bytes 62208 | tf_op jit(solution)/shard_map/all_gather | solution.py:8
  129.2 14.0 %all-gather.2 = f32[8,9,192]{2,1,0:T(8,128)S(1)} all-gather(f32[1,9,192]{2,1,0:T(8,128)S(1)} %bitcast.51), channel_id=2, replica_groups=mesh['dp'=4,'vocab'=8] {'vocab'}, dimensions={0}, use_global_device_ids=true | all-gather | bytes 62208 | tf_op jit(solution)/shard_map/all_gather | solution.py:8
  143.3 0.3 while.12
  143.6 4.6 %exponential_divide_fusion = f32[9,192,1280]{2,1,0:T(8,128)S(1)} fusion(f32[9,192]{1,0:T(8,128)S(1)} %get-tuple-element.31, f32[9,192]{1,0:T(8,128)S(1)} %get-tuple-element.30, f32[4,192,1280]{2,1,0:T(8,128)} %copy-done.1, f32[4,192,1280]{2,1,0:T(8,128)} %copy-done, f32[1,192,1280]{2,1,0:T(8,128)S(1)} %bitcast.50), kind=kLoop, calls=%fused_computation.6 | loop fusion | flops 8847360 | bytes 17708544 | tf_op jit(solution)/shard_map/div | solution.py:40
  148.2 0.0 copy-start.5
  148.2 0.5 slice_subtract_fusion
  148.7 2.3 fusion.3
  151.0 0.0 copy-done.5
  151.0 1.7 fusion.9
  152.7 0.0 all-gather.9.cloned.1.call-update
  152.7 0.2 reduce-scatter.5.cloned.1.call-start
  152.9 34.1 %all-gather.9.cloned.1.call-done = bf16[768,1280]{1,0:T(8,128)(2,1)} async-done(((bf16[192,1280]{1,0:T(8,128)(2,1)}), bf16[768,1280]{1,0:T(8,128)(2,1)}) %all-gather.9.cloned.1.call-update) | async-done | bytes 1966096 | tf_op jit(solution)/shard_map/all_gather | solution.py:51
  187.0 10.0 %convolution_bitcast_fusion = f32[2048,768]{0,1:T(8,128)} fusion(bf16[768,1280]{1,0:T(8,128)(2,1)} %all-gather.9.cloned.1.call-done, bf16[2048,1280]{1,0:T(8,128)(2,1)} %param.9), kind=kOutput, calls=%fused_computation.13 | convolution fusion | flops 4026531840 | bytes 13500416 | tf_op jit(solution)/shard_map/dot_general | solution.py:54
  197.0 0.0 copy-start.6
  197.0 0.0 reduce-scatter.5.cloned.1.call-update
  197.0 1.9 copy-done.6
  198.9 7.6 %fusion.2 = bf16[2048,1280]{0,1:T(8,128)(2,1)} fusion(bf16[768,1280]{1,0:T(8,128)(2,1)} %all-gather.9.cloned.1.call-done, bf16[2048,768]{1,0:T(8,128)(2,1)S(1)} %copy-done.6), kind=kOutput, calls=%fused_computation.9 | convolution fusion | flops 4029153280 | bytes 10354688 | tf_op jit(solution)/shard_map/dot_general | solution.py:52
  206.5 7.9 %copy.13 = bf16[2048,1280]{1,0:T(8,128)(2,1)} copy(bf16[2048,1280]{0,1:T(8,128)(2,1)} %fusion.2) | data formatting | bytes 10485760
  214.4 52.6 %reduce-scatter.5.cloned.1.call-done = f32[256,768]{0,1:T(8,128)} async-done(((f32[2048,768]{0,1:T(8,128)}), f32[256,768]{0,1:T(8,128)}) %reduce-scatter.5.cloned.1.call-update) | async-done | bytes 786448 | tf_op jit(solution)/shard_map/reduce_scatter | solution.py:53
  267.0 2.3 copy.12
  (13 shorter events, 0.2 us)
Async XLA Ops:
  7.2 43.5 %all-gather.7.cloned.1.call-start = ((), (), s32[]{:S(2)}) async-start(), calls=%async_computation.2 | async-start | bytes 3538944 | tf_op jit(solution)/shard_map/all_gather | solution.py:22
  7.9 52.5 %copy-start.3 = (bf16[192,1280]{1,0:T(8,128)(2,1)S(1)}, bf16[192,1280]{1,0:T(8,128)(2,1)}, u32[]{:S(2)}) copy-start(bf16[192,1280]{1,0:T(8,128)(2,1)} %param.10) | copy-start | bytes 1474564
  7.9 102.0 %reduce-scatter.3.cloned.1.call-start = ((), (), s32[]{:S(2)}) async-start(), calls=%async_computation.3 | async-start | bytes 4915200 | tf_op jit(solution)/shard_map/reduce_scatter | solution.py:24
  60.3 0.7 copy-start.4
  60.3 1.3 copy-start.7
  60.4 126.6 %all-gather.9.cloned.1.call-start = ((), (), s32[]{:S(2)}) async-start(), calls=%async_computation.4 | async-start | bytes 2457600 | tf_op jit(solution)/shard_map/all_gather | solution.py:51
  109.9 2.1 copy-start.2
  111.9 2.9 %copy-start = (f32[4,192,1280]{2,1,0:T(8,128)}, f32[4,192,1280]{2,1,0:T(8,128)S(1)}, u32[]{:S(2)}) copy-start(f32[4,192,1280]{2,1,0:T(8,128)S(1)} %get-tuple-element.52) | copy-start | bytes 11796484
  111.9 3.2 %copy-start.1 = (f32[4,192,1280]{2,1,0:T(8,128)}, f32[4,192,1280]{2,1,0:T(8,128)S(1)}, u32[]{:S(2)}) copy-start(f32[4,192,1280]{2,1,0:T(8,128)S(1)} %get-tuple-element.53) | copy-start | bytes 11796484
  148.2 2.8 %copy-start.5 = (s32[192]{0:T(256)S(1)}, s32[192]{0:T(256)}, u32[]{:S(2)}) copy-start(s32[192]{0:T(256)} %param.11) | copy-start | bytes 2308
  152.7 114.3 %reduce-scatter.5.cloned.1.call-start = ((), (), s32[]{:S(2)}) async-start(), calls=%async_computation.5 | async-start | bytes 7077888 | tf_op jit(solution)/shard_map/reduce_scatter | solution.py:53
  197.0 1.9 copy-start.6
Sparse Core Ops, SparseCore 0:
  9.6 40.9 all-gather.6
  60.5 49.3 reduce-scatter.2
  152.8 34.1 all-gather.8
  197.1 69.7 reduce-scatter.4
where the time goes:
time: 276 us
  waiting for transfers between devices  178 us (64%)
  matrix products  29.5 us (11%)
  blocking collectives  28.1 us (10%)
  between operations  13.9 us (5%)
  local copies, waits for them, and re-layouts  13.5 us (5%)
  other arithmetic  11.9 us (4%)
    reduce_scatter x1, waiting for transfers between devices, shards(): lax.psum_scatter(lax.dot_general(head, grad_all, (((1,), (1,)), ((), ()))...  52.6 us
    reduce_scatter x1, waiting for transfers between devices, shards(): lax.psum_scatter(lax.dot_general(h_block, head, (((0,), (0,)), ((), ())),...  48.2 us
    all_gather x1, waiting for transfers between devices, shards(): h_block = lax.all_gather(hidden_t, 'vocab', axis=0, tiled=True)  42.7 us
    all_gather x1, waiting for transfers between devices, shards(): grad_all = lax.all_gather(logit_grad, 'dp', axis=0, tiled=True)  34.1 us
    all_gather x2, blocking collectives, merged(): pieces = jax.tree.map(lambda part: lax.all_gather(part, axis), value)  28.1 us
    unnamed x18, local copies, waits for them, and re-layouts  12.9 us
    dot_general x1, matrix products, shards(): lax.dot_general(head, grad_all, (((1,), (1,)), ((), ())), preferred_eleme...  9.99 us
    dot_general x1, matrix products, shards(): lax.dot_general(h_block, head, (((0,), (0,)), ((), ())), preferred_elemen...  9.67 us
  transfers between devices with their start and end apart: 4, of which 4 were waited for; matrix products, arithmetic and copies ran while one was open for 6% of the time, Pallas kernels for 0%

commit v1 on v0

v1 whole, which is shorter than its diff:
```python
import jax
import jax.numpy as jnp
from jax import lax
from jax.sharding import PartitionSpec as P

CHUNKS = 1


def swap(value, axis, mask):
    count = lax.axis_size(axis)
    return lax.ppermute(value, axis, [(k, k ^ mask) for k in range(count)])


def masks_far_first(count):
    mask = count // 2
    while mask:
        yield mask
        mask //= 2


def doubling(block, axis, order):
    have = {0: block}
    for mask in order:
        keys = sorted(have)
        other = swap(jnp.concatenate([have[k] for k in keys], axis=0), axis, mask)
        for place, k in enumerate(keys):
            have[k ^ mask] = other[place : place + 1]
    return jnp.concatenate([have[k] for k in sorted(have)], axis=0)


def halving(parts, axis, order, wire):
    keep = {k: parts[k] for k in range(parts.shape[0])}
    for mask in order:
        sent = [k for k in sorted(keep) if k & mask]
        other = swap(jnp.stack([keep[k].astype(wire) for k in sent]), axis, mask)
        keep = {
            k ^ mask: keep[k ^ mask].astype(jnp.float32) + other[place].astype(jnp.float32)
            for place, k in enumerate(sent)
        }
    return keep[0].astype(jnp.float32)


def merge_stats(peak, total, inverse, axis):
    for mask in reversed(list(masks_far_first(lax.axis_size(axis)))):
        other = swap(jnp.concatenate([peak[None], total], axis=0), axis, mask)
        highest = jnp.maximum(peak, other[0])
        total = total * jnp.exp((peak - highest)[None] * inverse[:, None]) + other[1:] * jnp.exp(
            (other[0] - highest)[None] * inverse[:, None]
        )
        peak = highest
    return peak, total


def local_stats(values, inverse):
    peak = jnp.max(values, axis=1)
    total = jnp.stack(
        [jnp.sum(jnp.exp((values - peak[:, None]) * inverse[k]), axis=1) for k in range(inverse.shape[0])]
    )
    return peak, total


def mixture(values, peak, total, inverse, weights):
    result = 0.0
    for k in range(inverse.shape[0]):
        result = result + jnp.exp((values - peak[:, None]) * inverse[k]) * (weights[k] / total[k])[:, None]
    return result


def shards(hidden_t, head, teacher, labels, temps, mix):
    count_dp, count_vocab = lax.axis_size("dp"), lax.axis_size("vocab")
    me_dp, me_vocab = lax.axis_index("dp"), lax.axis_index("vocab")
    rows = hidden_t.shape[0]
    tokens, width = teacher.shape
    part = tokens // CHUNKS

    by_owner = hidden_t.T.reshape(count_dp, CHUNKS, part, rows)
    own = jnp.stack([lax.dynamic_index_in_dim(by_owner, me_dp ^ r, 0, False) for r in range(count_dp)])
    head_by_owner = head.reshape(count_vocab, rows, width)
    head_rel = jnp.stack(
        [lax.dynamic_index_in_dim(head_by_owner, me_vocab ^ r, 0, False) for r in range(count_vocab)]
    )

    inverse = 1.0 / temps
    weights = mix[1] * temps
    target = teacher.astype(jnp.float32)
    peak, total = merge_stats(*local_stats(target, inverse), inverse, "vocab")
    columns = jnp.arange(width, dtype=jnp.int32)[None, :] + me_vocab * width
    fixed = mixture(target, peak, total, inverse, weights) + jnp.where(columns == labels[:, None], mix[0], 0.0)

    student_inverse = jnp.concatenate([jnp.ones((1,), jnp.float32), inverse])
    student_weights = jnp.concatenate([mix[:1], weights])
    vocab_far = list(masks_far_first(count_vocab))
    dp_far = list(masks_far_first(count_dp))

    hidden_parts, head_grad = [], 0.0
    for c in range(CHUNKS):
        dp_order = dp_far if c % 2 == 0 else dp_far[::-1]
        mine = own[:, c].reshape(1, count_dp * part, rows)
        gathered = doubling(mine, "vocab", vocab_far)
        logits = lax.dot_general(
            gathered, head_rel, (((0, 2), (0, 1)), ((), ())), preferred_element_type=jnp.float32
        )
        logits = halving(logits.reshape(count_dp, part, width), "dp", dp_order, jnp.float16)
        peak, total = merge_stats(*local_stats(logits, student_inverse), student_inverse, "vocab")
        grad = mixture(logits, peak, total, student_inverse, student_weights) - fixed[c * part : (c + 1) * part]
        grad_rel = doubling(grad.astype(jnp.bfloat16)[None], "dp", dp_order)
        grad_nat = jnp.concatenate(
            [lax.dynamic_index_in_dim(grad_rel, me_dp ^ r, 0, False) for r in range(count_dp)]
        )
        partial = lax.dot_general(
            head_rel, grad_nat, (((2,), (1,)), ((), ())), preferred_element_type=jnp.float32
        )
        hidden_parts.append(halving(partial, "vocab", vocab_far[::-1], jnp.bfloat16))
        gathered_nat = jnp.concatenate(
            [lax.dynamic_index_in_dim(gathered, me_vocab ^ r, 0, False) for r in range(count_vocab)], axis=1
        )
        head_grad = head_grad + lax.dot_general(
            gathered_nat,
            grad_rel.reshape(count_dp * part, width),
            (((0,), (0,)), ((), ())),
            preferred_element_type=jnp.float32,
        )
    hidden_grad = jnp.stack([p.reshape(rows, count_dp, part) for p in hidden_parts], axis=2)
    return (hidden_grad.reshape(rows, count_dp * tokens), head_grad.astype(jnp.bfloat16))


def solution(mesh):
    placed = (P(("dp", "vocab"), None), P("dp", "vocab"), P("dp", "vocab"), P("dp"), P(), P())
    return jax.shard_map(
        shards,
        mesh=mesh,
        in_specs=placed,
        out_specs=(P(("dp", "vocab"), None), P("dp", "vocab")),
        check_vma=False,
    )
```

time: 276 us -> 209 us (0.76)
  waiting for transfers between devices: 178 us -> 132 us
  blocking collectives: 28.1 us -> 0 us
  starting transfers between devices: 0.34 us -> 20.8 us
  other arithmetic: 11.9 us -> 27 us
  matrix products: 29.5 us -> 16.6 us
  between operations: 13.9 us -> 1.14 us
  local copies, waits for them, and re-layouts: 13.5 us -> 10.7 us
    ppermute x0 -> x16, waiting for transfers between devices: none -> 132 us  [swap(): return lax.ppermute(value, axis, [(k, k ^ mask) for k in range(count)])]
    reduce_scatter x2 -> x0, waiting for transfers between devices: 101 us -> none  [the longest x1 52.6 us: shards(): lax.psum_scatter(lax.dot_general(head, grad_all, (((1,), (1,)), ((), ()))...]
    all_gather x2 -> x0, waiting for transfers between devices: 76.8 us -> none  [the longest x1 42.7 us: shards(): h_block = lax.all_gather(hidden_t, 'vocab', axis=0, tiled=True)]
    all_gather x2 -> x0, blocking collectives: 28.1 us -> none  [merged(): pieces = jax.tree.map(lambda part: lax.all_gather(part, axis), value)]
    ppermute x0 -> x16, starting transfers between devices: none -> 20.8 us  [swap(): return lax.ppermute(value, axis, [(k, k ^ mask) for k in range(count)])]
    dot_general x4 -> x3, matrix products: 29.5 us -> 16.6 us  [the longest x1 6.17 us: shards(): lax.dot_general(gathered_nat, grad_rel.reshape(count_dp * part, width), (...]
    broadcast_in_dim x0 -> x1, other arithmetic: none -> 6.26 us  [shards(): grad_rel = doubling(grad.astype(jnp.bfloat16)[None], 'dp', dp_order)]
    unnamed x18 -> x46, local copies, waits for them, and re-layouts: 12.9 us -> 7.98 us
  transfers between devices with their start and end apart: 4 -> 16, of which waited for: 4 -> 13; matrix products, arithmetic and copies ran while one was open for 6% -> 8% of each run, Pallas kernels for 0% -> 0%
where the time goes in v1:
time: 209 us; the launch traced here: 208 us
  waiting for transfers between devices  132 us (63%)
  other arithmetic  27 us (13%)
  starting transfers between devices  20.8 us (10%)
  matrix products  16.6 us (8%)
  local copies, waits for them, and re-layouts  10.7 us (5%)
    ppermute x16, waiting for transfers between devices, swap(): return lax.ppermute(value, axis, [(k, k ^ mask) for k in range(count)])  132 us
    ppermute x16, starting transfers between devices, swap(): return lax.ppermute(value, axis, [(k, k ^ mask) for k in range(count)])  20.8 us
    unnamed x46, local copies, waits for them, and re-layouts  7.98 us
    broadcast_in_dim x1, other arithmetic, shards(): grad_rel = doubling(grad.astype(jnp.bfloat16)[None], 'dp', dp_order)  6.26 us
    dot_general x1, matrix products, shards(): lax.dot_general(gathered_nat, grad_rel.reshape(count_dp * part, width), (...  6.17 us
    dot_general x1, matrix products, shards(): lax.dot_general(gathered, head_rel, (((0, 2), (0, 1)), ((), ())), preferr...  6.08 us
    div x2, other arithmetic, mixture(): weights[k] / total[k]  5.68 us
    reduce_sum x1, other arithmetic, local_stats(): jnp.sum(jnp.exp((values - peak[:, None]) * inverse[k]), axis=1)  4.92 us
  transfers between devices with their start and end apart: 16, of which 13 were waited for; matrix products, arithmetic and copies ran while one was open for 8% of the time, Pallas kernels for 0%

profile of v1, /device:TPU:0, one launch (start us, length us, event | category | flops | bytes accessed | tf_op | source)
XLA Modules:
  0.0 208.0 jit_solution(17997910457656866120)
XLA Ops:
  0.6 1.2 copy.12
  1.9 4.1 %collective-permute-start = (bf16[1,768,256]{2,1,0:T(8,128)(2,1)S(1)}, bf16[1,768,256]{2,1,0:T(8,128)(2,1)S(1)}, u32[]{:S(2)}, u32[]{:S(2)}) collective-permute-start(bf16[1,768,256]{2,1,0:T(8,128)(2,1)S(1)} %bitcast.115), channel_id=1, source_target_pairs={{0,4},{1,5},{2,6},{3,7},{4,0},{5,1},{6,2},{7,3},{8,12},{9,13},{10,... | collective-permute-start | bytes 1179656 | tf_op jit(solution)/shard_map/ppermute | solution.py:11
  6.0 17.5 %collective-permute-done = bf16[1,768,256]{2,1,0:T(8,128)(2,1)S(1)} collective-permute-done((bf16[1,768,256]{2,1,0:T(8,128)(2,1)S(1)}, bf16[1,768,256]{2,1,0:T(8,128)(2,1)S(1)}, u32[]{:S(2)}, u32[]{:S(2)}) %collective-permute-start) | collective-permute-done | bytes 393248 | tf_op jit(solution)/shard_map/ppermute | solution.py:11
  23.7 0.8 collective-permute-start.1
  24.4 1.1 dynamic-slice_dynamic-update-slice_fusion.7
  25.6 1.3 dynamic-slice_dynamic-update-slice_fusion.6
  26.9 15.6 %collective-permute-done.1 = bf16[2,768,256]{2,1,0:T(8,128)(2,1)S(1)} collective-permute-done((bf16[2,768,256]{2,1,0:T(8,128)(2,1)S(1)}, bf16[2,768,256]{2,1,0:T(8,128)(2,1)S(1)}, u32[]{:S(2)}, u32[]{:S(2)}) %collective-permute-start.1) | collective-permute-done | bytes 786464 | tf_op jit(solution)/shard_map/ppermute | solution.py:11
  42.5 0.2 pad_maximum_fusion.1
  42.7 0.6 copy-done.3
  43.8 3.0 %collective-permute-done.2 = bf16[4,768,256]{2,1,0:T(8,128)(2,1)S(1)} collective-permute-done((bf16[4,768,256]{2,1,0:T(8,128)(2,1)S(1)}, bf16[4,768,256]{2,1,0:T(8,128)(2,1)S(1)}, u32[]{:S(2)}, u32[]{:S(2)}) %collective-permute-start.2) | collective-permute-done | bytes 1572896 | tf_op jit(solution)/shard_map/ppermute | solution.py:11
  47.0 6.1 %fusion.67 = (f16[768,1280]{1,0:T(8,128)(2,1)S(1)}, f32[768,1280]{1,0:T(8,128)}) fusion(bf16[8,768,256]{2,1,0:T(8,128)(2,1)S(1)} %slice_dynamic-update-slice_fusion, bf16[8,256,1280]{2,1,0:T(8,128)(2,1)S(1)} %dynamic-slice_dynamic-update-slice_fusion), kind=kOutput, calls=%fused_computation.163 | convolution fusion | flops 4027514880 | bytes 14286848 | tf_op jit(solution)/shard_map/dot_general | solution.py:100
  53.1 0.2 slice_bitcast_fusion.3
  53.3 1.2 pad_maximum_fusion.3
  54.5 1.3 collective-permute-start.3
  55.8 22.8 %collective-permute-done.3 = f16[2,192,1280]{2,1,0:T(8,128)(2,1)} collective-permute-done((f16[2,192,1280]{2,1,0:T(8,128)(2,1)}, f16[2,192,1280]{2,1,0:T(8,128)(2,1)}, u32[]{:S(2)}, u32[]{:S(2)}) %collective-permute-start.3) | collective-permute-done | bytes 983072 | tf_op jit(solution)/shard_map/ppermute | solution.py:11
  78.6 2.2 %fusion.38 = f16[1,192,1280]{2,1,0:T(8,128)(2,1)} fusion(f32[768,1280]{1,0:T(8,128)} %get-tuple-element.73, f16[2,192,1280]{2,1,0:T(8,128)(2,1)} %collective-permute-done.3), kind=kLoop, calls=%fused_computation.47 | loop fusion | flops 737280 | bytes 1966080 | tf_op jit(solution)/shard_map/convert_element_type | solution.py:35
  80.8 1.2 collective-permute-start.4
  82.1 0.7 fusion.65
  82.7 1.2 reduce_max.28
  83.9 0.7 broadcast_multiply_fusion
  84.6 0.6 fusion.66
  85.3 0.7 fusion.64
  85.9 7.6 %collective-permute-done.4 = f16[1,192,1280]{2,1,0:T(8,128)(2,1)} collective-permute-done((f16[1,192,1280]{2,1,0:T(8,128)(2,1)}, f16[1,192,1280]{2,1,0:T(8,128)(2,1)}, u32[]{:S(2)}, u32[]{:S(2)}) %collective-permute-start.4) | collective-permute-done | bytes 491552 | tf_op jit(solution)/shard_map/ppermute | solution.py:11
  93.6 1.7 fusion.57
  95.3 1.0 copy-done.5
  96.3 4.9 %fusion.36 = (f32[192]{0:T(256)S(1)}, f32[192]{0:T(256)S(1)}, f32[192]{0:T(256)S(1)}, f32[192]{0:T(256)S(1)}, f32[192]{0:T(256)S(1)}, /*index=5*/f32[192]{0:T(25...) fusion(bf16[192,1280]{1,0:T(8,128)(2,1)} %param.8, f32[192]{0:T(256)S(1)} %reduce_max.29, f32[]{:T(128)} %bitcast.19, ...), kind=kLoop, calls=%fused_computation.44 | loop fusion | flops 4913472 | bytes 1483024 | tf_op jit(solution)/shard_map/reduce_sum | solution.py:57
  101.4 0.6 collective-permute-start.5
  102.0 0.5 collective-permute-done.8
  102.5 0.1 fusion.53
  102.6 1.5 collective-permute-start.9
  104.1 0.1 fusion.50
  104.2 0.6 collective-permute-start.6
  104.8 1.4 collective-permute-done.9
  106.3 0.1 fusion.52
  106.4 3.2 %collective-permute-start.10 = (f32[5,192]{1,0:T(8,128)S(1)}, f32[5,192]{1,0:T(8,128)S(1)}, u32[]{:S(2)}, u32[]{:S(2)}) collective-permute-start(f32[5,192]{1,0:T(8,128)S(1)} %pad_maximum_fusion.11), channel_id=1, source_target_pairs={{0,4},{1,5},{2,6},{3,7},{4,0},{5,1},{6,2},{7,3},{8,12},{9,13},{10,... | collective-permute-start | bytes 11528 | tf_op jit(solution)/shard_map/ppermute | solution.py:11
  109.6 0.1 fusion.49
  109.7 1.8 collective-permute-start.7
  111.5 0.1 fusion.51
  111.6 2.5 %slice_divide_fusion.3 = (f32[1,192]{1,0:T(1,128)S(1)}, f32[1,192]{1,0:T(1,128)S(1)}, f32[1,192]{1,0:T(1,128)S(1)}, f32[1,192]{1,0:T(1,128)S(1)}) fusion(f32[4,192]{1,0:T(4,128)S(1)} %fusion.51, f32[]{:T(128)} %bitcast.33, f32[]{:T(128)} %bitcast.39, f32[]{:T(128)} %bitcast.37, f32[]{:T(128)} %bitcast.35), kind=kLoop, calls=%fused_computation.132 | loop fusion | flops 768 | bytes 6160 | tf_op jit(solution)/shard_map/div | solution.py:65
  114.2 0.1 collective-permute-done.7
  114.3 0.1 fusion.48
  114.4 3.1 %slice_divide_fusion.8 = (f32[1,192]{1,0:T(1,128)S(1)}, f32[1,192]{1,0:T(1,128)S(1)}, f32[1,192]{1,0:T(1,128)S(1)}, f32[1,192]{1,0:T(1,128)S(1)}, f32[1,192]{1,0:T(1,128)S(1)}) fusion(f32[5,192]{1,0:T(8,128)S(1)} %fusion.48, f32[]{:T(128)} %bitcast.28, f32[]{:T(128)} %bitcast.39, f32[]{:T(128)} %bitcast.37, f32[]{:T(128)} %bitcast.35, f32[]{:T(128)} %bitcast.33), kind=kLoop, calls=%fused_computation.137 | loop fusion | flops 960 | bytes 7700 | tf_op jit(solution)/shard_map/div | solution.py:65
  117.5 6.3 %fusion.47 = bf16[1,192,1280]{2,1,0:T(8,128)(2,1)S(1)} fusion(f32[]{:T(128)} %bitcast.28, s32[192]{0:T(256)S(1)} %copy-done.9, s32[1280]{0:T(1024)S(1)} %iota_add_fusion, f32[192]{0:T(256)S(1)} %bitcast.177, f32[192]{0:T(256)S(1)} %bitcast.178, f32[192]{0:T(256)S(1)} %bitcast.179, f32[192]{0:T(256)S(1)} %bitcast.176, f32[192]{0:T(256)S(1)} %maximum_maximum_fusion, ...), kind=kLoop, calls=%fused_computation.85 | loop fusion | flops 7864320 | bytes 1980436 | tf_op jit(solution)/shard_map/broadcast_in_dim | solution.py:106
  123.8 1.6 collective-permute-start.11
  125.4 9.9 %collective-permute-done.11 = bf16[1,192,1280]{2,1,0:T(8,128)(2,1)S(1)} collective-permute-done((bf16[1,192,1280]{2,1,0:T(8,128)(2,1)S(1)}, bf16[1,192,1280]{2,1,0:T(8,128)(2,1)S(1)}, u32[]{:S(2)}, u32[]{:S(2)}) %collective-permute-start.11) | collective-permute-done | bytes 491552 | tf_op jit(solution)/shard_map/ppermute | solution.py:11
  135.3 0.1 pad_maximum_fusion.4
  135.4 1.6 collective-permute-start.12
  136.9 19.6 %collective-permute-done.12 = bf16[2,192,1280]{2,1,0:T(8,128)(2,1)S(1)} collective-permute-done((bf16[2,192,1280]{2,1,0:T(8,128)(2,1)S(1)}, bf16[2,192,1280]{2,1,0:T(8,128)(2,1)S(1)}, u32[]{:S(2)}, u32[]{:S(2)}) %collective-permute-start.12) | collective-permute-done | bytes 983072 | tf_op jit(solution)/shard_map/ppermute | solution.py:11
  156.6 0.2 pad_maximum_fusion
  156.8 0.1 dynamic-slice_bitcast_fusion.3
  157.0 1.7 slice-done
  158.7 0.3 slice-done.1
  159.0 4.3 %fusion.68 = (bf16[8,256,768]{2,1,0:T(8,128)(2,1)S(1)}, f32[8,256,768]{2,1,0:T(8,128)S(1)}) fusion(bf16[8,256,1280]{2,1,0:T(8,128)(2,1)S(1)} %bitcast.129, bf16[192,1280]{1,0:T(8,128)(2,1)S(1)} %get-tuple-element.28, bf16[192,1280]{1,0:T(8,128)(2,1)S(1)} %get-tuple-element.29, bf16[192,1280]{1,0:T(8,128)(2,1)S(1)} %get-tuple-element.30, ...), kind=kOutput, calls=%fused_computation.164 | convolution fusion | flops 4035969024 | bytes 16646144 | tf_op jit(solution)/shard_map/dot_general | solution.py:110
  163.3 0.1 fusion.61
  163.4 0.2 pad_maximum_fusion.2
  163.8 3.3 %collective-permute-done.13 = bf16[4,256,768]{2,1,0:T(8,128)(2,1)S(1)} collective-permute-done((bf16[4,256,768]{2,1,0:T(8,128)(2,1)S(1)}, bf16[4,256,768]{2,1,0:T(8,128)(2,1)S(1)}, u32[]{:S(2)}, u32[]{:S(2)}) %collective-permute-start.13) | collective-permute-done | bytes 1572896 | tf_op jit(solution)/shard_map/ppermute | solution.py:11
  167.1 0.2 fusion.43
  167.4 0.7 collective-permute-start.14
  168.5 18.6 %collective-permute-done.14 = bf16[2,256,768]{2,1,0:T(8,128)(2,1)S(1)} collective-permute-done((bf16[2,256,768]{2,1,0:T(8,128)(2,1)S(1)}, bf16[2,256,768]{2,1,0:T(8,128)(2,1)S(1)}, u32[]{:S(2)}, u32[]{:S(2)}) %collective-permute-start.14) | collective-permute-done | bytes 786464 | tf_op jit(solution)/shard_map/ppermute | solution.py:11
  187.1 0.1 fusion.41
  187.2 1.7 collective-permute-start.15
  188.9 6.2 %convolution_convert_fusion = bf16[2048,1280]{1,0:T(8,128)(2,1)} fusion(bf16[768,2048]{1,0:T(8,128)(2,1)S(1)} %bitcast_dynamic-update-slice_fusion, bf16[768,1280]{1,0:T(8,128)(2,1)S(1)} %bitcast.114), kind=kOutput, calls=%fused_computation | convolution fusion | flops 4029153280 | bytes 10354688 | tf_op jit(solution)/shard_map/dot_general | solution.py:117
  195.1 11.9 %collective-permute-done.15 = bf16[1,256,768]{2,1,0:T(8,128)(2,1)S(1)} collective-permute-done((bf16[1,256,768]{2,1,0:T(8,128)(2,1)S(1)}, bf16[1,256,768]{2,1,0:T(8,128)(2,1)S(1)}, u32[]{:S(2)}, u32[]{:S(2)}) %collective-permute-start.15) | collective-permute-done | bytes 393248 | tf_op jit(solution)/shard_map/ppermute | solution.py:11
  206.9 1.1 fusion.46
  (77 shorter events, 1.7 us)
Async XLA Ops:
  1.9 21.6 %collective-permute-start = (bf16[1,768,256]{2,1,0:T(8,128)(2,1)S(1)}, bf16[1,768,256]{2,1,0:T(8,128)(2,1)S(1)}, u32[]{:S(2)}, u32[]{:S(2)}) collective-permute-start(bf16[1,768,256]{2,1,0:T(8,128)(2,1)S(1)} %bitcast.115), channel_id=1, source_target_pairs={{0,4},{1,5},{2,6},{3,7},{4,0},{5,1},{6,2},{7,3},{8,12},{9,13},{10,... | collective-permute-start | bytes 1179656 | tf_op jit(solution)/shard_map/ppermute | solution.py:11
  23.6 19.1 %copy-start.1 = (bf16[1,768,256]{2,1,0:T(8,128)(2,1)}, bf16[1,768,256]{2,1,0:T(8,128)(2,1)S(1)}, u32[]{:S(2)}) copy-start(bf16[1,768,256]{2,1,0:T(8,128)(2,1)S(1)} %collective-permute-done) | copy-start | bytes 1179652
  23.7 18.8 %collective-permute-start.1 = (bf16[2,768,256]{2,1,0:T(8,128)(2,1)S(1)}, bf16[2,768,256]{2,1,0:T(8,128)(2,1)S(1)}, u32[]{:S(2)}, u32[]{:S(2)}) collective-permute-start(bf16[2,768,256]{2,1,0:T(8,128)(2,1)S(1)} %pad_maximum_fusion.5), channel_id=1, source_target_pairs={{0,2},{1,3},{2,0},{3,1},{4,6},{5,7},{6,4},{7,5},{8,10},{9,11},{10,... | collective-permute-start | bytes 2359304 | tf_op jit(solution)/shard_map/ppermute | solution.py:11
  25.6 17.8 %copy-start = (bf16[2048,1280]{1,0:T(8,128)(2,1)S(1)}, bf16[2048,1280]{1,0:T(8,128)(2,1)}, u32[]{:S(2)}) copy-start(bf16[2048,1280]{1,0:T(8,128)(2,1)} %param.7) | copy-start | bytes 15728644
  42.5 0.9 copy-start.3
  43.3 3.4 %collective-permute-start.2 = (bf16[4,768,256]{2,1,0:T(8,128)(2,1)S(1)}, bf16[4,768,256]{2,1,0:T(8,128)(2,1)S(1)}, u32[]{:S(2)}, u32[]{:S(2)}) collective-permute-start(bf16[4,768,256]{2,1,0:T(8,128)(2,1)S(1)} %pad_maximum_fusion.1), channel_id=1, source_target_pairs={{0,1},{1,0},{2,3},{3,2},{4,5},{5,4},{6,7},{7,6},{8,9},{9,8},{10,11... | collective-permute-start | bytes 4718600 | tf_op jit(solution)/shard_map/ppermute | solution.py:11
  43.5 3.3 %copy-start.4 = (bf16[2,768,256]{2,1,0:T(8,128)(2,1)S(1)}, bf16[2,768,256]{2,1,0:T(8,128)(2,1)}, u32[]{:S(2)}) copy-start(bf16[2,768,256]{2,1,0:T(8,128)(2,1)} %copy-done.3) | copy-start | bytes 2359300
  43.6 3.3 %copy-start.2 = (bf16[1,768,256]{2,1,0:T(8,128)(2,1)S(1)}, bf16[1,768,256]{2,1,0:T(8,128)(2,1)}, u32[]{:S(2)}) copy-start(bf16[1,768,256]{2,1,0:T(8,128)(2,1)} %copy-done.1) | copy-start | bytes 1179652
  43.8 9.3 %copy-start.6 = (bf16[8,256,1280]{2,1,0:T(8,128)(2,1)}, bf16[8,256,1280]{2,1,0:T(8,128)(2,1)S(1)}, u32[]{:S(2)}) copy-start(bf16[8,256,1280]{2,1,0:T(8,128)(2,1)S(1)} %dynamic-slice_dynamic-update-slice_fusion) | copy-start | bytes 15728644
  53.1 29.0 %copy-start.7 = (f32[2]{0:T(128)S(1)}, f32[2]{0:T(128)}, u32[]{:S(2)}) copy-start(f32[2]{0:T(128)} %param.11) | copy-start | bytes 28
  53.1 30.8 %copy-start.8 = (f32[4]{0:T(128)S(1)}, f32[4]{0:T(128)}, u32[]{:S(2)}) copy-start(f32[4]{0:T(128)} %param.10) | copy-start | bytes 52
  54.5 24.1 %collective-permute-start.3 = (f16[2,192,1280]{2,1,0:T(8,128)(2,1)}, f16[2,192,1280]{2,1,0:T(8,128)(2,1)}, u32[]{:S(2)}, u32[]{:S(2)}) collective-permute-start(f16[2,192,1280]{2,1,0:T(8,128)(2,1)} %pad_maximum_fusion.3), channel_id=1, source_target_pairs={{0,16},{8,24},{16,0},{24,8},{1,17},{9,25},{17,1},{25,9},{2,18},{10... | collective-permute-start | bytes 2949128 | tf_op jit(solution)/shard_map/ppermute | solution.py:11
  80.8 12.8 %collective-permute-start.4 = (f16[1,192,1280]{2,1,0:T(8,128)(2,1)}, f16[1,192,1280]{2,1,0:T(8,128)(2,1)}, u32[]{:S(2)}, u32[]{:S(2)}) collective-permute-start(f16[1,192,1280]{2,1,0:T(8,128)(2,1)} %fusion.38), channel_id=1, source_target_pairs={{0,8},{8,0},{16,24},{24,16},{1,9},{9,1},{17,25},{25,17},{2,10},{10... | collective-permute-start | bytes 1474568 | tf_op jit(solution)/shard_map/ppermute | solution.py:11
  85.9 31.6 %copy-start.9 = (s32[192]{0:T(256)S(1)}, s32[192]{0:T(256)}, u32[]{:S(2)}) copy-start(s32[192]{0:T(256)} %param.9) | copy-start | bytes 2308
  95.3 1.0 copy-start.5
  101.2 1.2 collective-permute-start.8
  101.4 2.7 %collective-permute-start.5 = (f32[6,192]{1,0:T(8,128)S(1)}, f32[6,192]{1,0:T(8,128)S(1)}, u32[]{:S(2)}, u32[]{:S(2)}) collective-permute-start(f32[6,192]{1,0:T(8,128)S(1)} %concatenate.47), channel_id=1, source_target_pairs={{0,1},{1,0},{2,3},{3,2},{4,5},{5,4},{6,7},{7,6},{8,9},{9,8},{10,11... | collective-permute-start | bytes 13832 | tf_op jit(solution)/shard_map/ppermute | solution.py:11
  102.6 3.7 %collective-permute-start.9 = (f32[5,192]{1,0:T(8,128)S(1)}, f32[5,192]{1,0:T(8,128)S(1)}, u32[]{:S(2)}, u32[]{:S(2)}) collective-permute-start(f32[5,192]{1,0:T(8,128)S(1)} %pad_maximum_fusion.10), channel_id=1, source_target_pairs={{0,2},{1,3},{2,0},{3,1},{4,6},{5,7},{6,4},{7,5},{8,10},{9,11},{10,... | collective-permute-start | bytes 11528 | tf_op jit(solution)/shard_map/ppermute | solution.py:11
  104.2 5.4 %collective-permute-start.6 = (f32[6,192]{1,0:T(8,128)S(1)}, f32[6,192]{1,0:T(8,128)S(1)}, u32[]{:S(2)}, u32[]{:S(2)}) collective-permute-start(f32[6,192]{1,0:T(8,128)S(1)} %pad_maximum_fusion.8), channel_id=1, source_target_pairs={{0,2},{1,3},{2,0},{3,1},{4,6},{5,7},{6,4},{7,5},{8,10},{9,11},{10,... | collective-permute-start | bytes 13832 | tf_op jit(solution)/shard_map/ppermute | solution.py:11
  106.4 5.1 %collective-permute-start.10 = (f32[5,192]{1,0:T(8,128)S(1)}, f32[5,192]{1,0:T(8,128)S(1)}, u32[]{:S(2)}, u32[]{:S(2)}) collective-permute-start(f32[5,192]{1,0:T(8,128)S(1)} %pad_maximum_fusion.11), channel_id=1, source_target_pairs={{0,4},{1,5},{2,6},{3,7},{4,0},{5,1},{6,2},{7,3},{8,12},{9,13},{10,... | collective-permute-start | bytes 11528 | tf_op jit(solution)/shard_map/ppermute | solution.py:11
  109.7 4.6 %collective-permute-start.7 = (f32[6,192]{1,0:T(8,128)S(1)}, f32[6,192]{1,0:T(8,128)S(1)}, u32[]{:S(2)}, u32[]{:S(2)}) collective-permute-start(f32[6,192]{1,0:T(8,128)S(1)} %pad_maximum_fusion.9), channel_id=1, source_target_pairs={{0,4},{1,5},{2,6},{3,7},{4,0},{5,1},{6,2},{7,3},{8,12},{9,13},{10,... | collective-permute-start | bytes 13832 | tf_op jit(solution)/shard_map/ppermute | solution.py:11
  123.8 11.5 %collective-permute-start.11 = (bf16[1,192,1280]{2,1,0:T(8,128)(2,1)S(1)}, bf16[1,192,1280]{2,1,0:T(8,128)(2,1)S(1)}, u32[]{:S(2)}, u32[]{:S(2)}) collective-permute-start(bf16[1,192,1280]{2,1,0:T(8,128)(2,1)S(1)} %fusion.47), channel_id=1, source_target_pairs={{0,16},{8,24},{16,0},{24,8},{1,17},{9,25},{17,1},{25,9},{2,18},{10... | collective-permute-start | bytes 1474568 | tf_op jit(solution)/shard_map/ppermute | solution.py:11
  135.4 21.1 %collective-permute-start.12 = (bf16[2,192,1280]{2,1,0:T(8,128)(2,1)S(1)}, bf16[2,192,1280]{2,1,0:T(8,128)(2,1)S(1)}, u32[]{:S(2)}, u32[]{:S(2)}) collective-permute-start(bf16[2,192,1280]{2,1,0:T(8,128)(2,1)S(1)} %pad_maximum_fusion.4), channel_id=1, source_target_pairs={{0,8},{8,0},{16,24},{24,16},{1,9},{9,1},{17,25},{25,17},{2,10},{10... | collective-permute-start | bytes 2949128 | tf_op jit(solution)/shard_map/ppermute | solution.py:11
  156.5 2.2 %slice-start = ((s8[5242880]{0:T(1024)(128)(4,1)}), s8[4194304]{0:T(1024)(128)(4,1)S(1)}, s32[]{:S(2)}) async-start(s8[5242880]{0:T(1024)(128)(4,1)} %bitcast.128), calls=%async_computation | async-start | bytes 8388608
  156.6 2.4 %slice-start.1 = ((s8[5242880]{0:T(1024)(128)(4,1)}), s8[1048576]{0:T(1024)(128)(4,1)S(1)}, s32[]{:S(2)}) async-start(s8[5242880]{0:T(1024)(128)(4,1)} %bitcast.128), calls=%async_computation.1 | async-start | bytes 2097152
  163.6 3.5 %collective-permute-start.13 = (bf16[4,256,768]{2,1,0:T(8,128)(2,1)S(1)}, bf16[4,256,768]{2,1,0:T(8,128)(2,1)S(1)}, u32[]{:S(2)}, u32[]{:S(2)}) collective-permute-start(bf16[4,256,768]{2,1,0:T(8,128)(2,1)S(1)} %pad_maximum_fusion.2), channel_id=1, source_target_pairs={{0,1},{1,0},{2,3},{3,2},{4,5},{5,4},{6,7},{7,6},{8,9},{9,8},{10,11... | collective-permute-start | bytes 4718600 | tf_op jit(solution)/shard_map/ppermute | solution.py:11
  167.4 19.6 %collective-permute-start.14 = (bf16[2,256,768]{2,1,0:T(8,128)(2,1)S(1)}, bf16[2,256,768]{2,1,0:T(8,128)(2,1)S(1)}, u32[]{:S(2)}, u32[]{:S(2)}) collective-permute-start(bf16[2,256,768]{2,1,0:T(8,128)(2,1)S(1)} %pad_maximum_fusion.6), channel_id=1, source_target_pairs={{0,2},{1,3},{2,0},{3,1},{4,6},{5,7},{6,4},{7,5},{8,10},{9,11},{10,... | collective-permute-start | bytes 2359304 | tf_op jit(solution)/shard_map/ppermute | solution.py:11
  187.2 19.7 %collective-permute-start.15 = (bf16[1,256,768]{2,1,0:T(8,128)(2,1)S(1)}, bf16[1,256,768]{2,1,0:T(8,128)(2,1)S(1)}, u32[]{:S(2)}, u32[]{:S(2)}) collective-permute-start(bf16[1,256,768]{2,1,0:T(8,128)(2,1)S(1)} %fusion.41), channel_id=1, source_target_pairs={{0,4},{1,5},{2,6},{3,7},{4,0},{5,1},{6,2},{7,3},{8,12},{9,13},{10,... | collective-permute-start | bytes 1179656 | tf_op jit(solution)/shard_map/ppermute | solution.py:11

commit v2 on v0

v2 whole, which is shorter than its diff:
```python
import functools

import jax
import jax.numpy as jnp
from jax import lax
from jax.experimental import pallas as pl
from jax.experimental.pallas import tpu as pltpu
from jax.sharding import PartitionSpec as P

CHUNKS = 2
STRIP = 16
LANES = 128


def swap(value, axis, mask):
    count = lax.axis_size(axis)
    return lax.ppermute(value, axis, [(k, k ^ mask) for k in range(count)])


def masks_far_first(count):
    mask = count // 2
    while mask:
        yield mask
        mask //= 2


def pick(parts, place, axis=0):
    return lax.dynamic_index_in_dim(parts, place, axis, keepdims=False)


def padded(count):
    return -(-count // LANES) * LANES


VMEM = pl.BlockSpec(memory_space=pltpu.VMEM)
SMEM = pl.BlockSpec(memory_space=pltpu.SMEM)


def stats_kernel(heats, x_ref, inverse_ref, out_ref, column):
    tokens = x_ref.shape[0]
    column[...] = jnp.zeros_like(column)
    lane = lax.broadcasted_iota(jnp.int32, (STRIP, LANES), 1)

    @pl.loop(0, tokens // STRIP)
    def _(strip):
        rows = pl.ds(pl.multiple_of(strip * STRIP, STRIP), STRIP)
        x = x_ref[rows, :].astype(jnp.float32)
        peak = jnp.max(x, axis=1, keepdims=True)
        x = x - peak
        record = jnp.where(lane == 0, peak, 0.0)
        for k in range(heats):
            total = jnp.sum(jnp.exp(x * inverse_ref[k]), axis=1, keepdims=True)
            record = jnp.where(lane == k + 1, total, record)
        column[rows, :] = record

    out_ref[...] = column[...].T[: out_ref.shape[0], :]


def local_stats(values, inverse):
    tokens, heats = values.shape[0], inverse.shape[0]
    return pl.pallas_call(
        functools.partial(stats_kernel, heats),
        out_shape=jax.ShapeDtypeStruct((8, padded(tokens)), jnp.float32),
        in_specs=[VMEM, SMEM],
        out_specs=VMEM,
        scratch_shapes=[pltpu.VMEM((padded(tokens), LANES), jnp.float32)],
        compiler_params=pltpu.CompilerParams(vmem_limit_bytes=16 << 20),
        name="stats",
    )(values, inverse)


def fixed_kernel(heats, x_ref, stats_ref, scalars_ref, out_ref, column):
    tokens, width = x_ref.shape
    column[...] = stats_ref[...].T
    lane = lax.broadcasted_iota(jnp.int32, (STRIP, width), 1).astype(jnp.float32)

    @pl.loop(0, tokens // STRIP)
    def _(strip):
        rows = pl.ds(pl.multiple_of(strip * STRIP, STRIP), STRIP)
        record = column[rows, :]
        x = x_ref[rows, :].astype(jnp.float32) - record[:, 0:1]
        result = jnp.where(lane == record[:, heats + 1 : heats + 2], scalars_ref[2 * heats], 0.0)
        for k in range(heats):
            factor = scalars_ref[heats + k] / record[:, k + 1 : k + 2]
            result = result + jnp.exp(x * scalars_ref[k]) * factor
        out_ref[rows, :] = result


def grad_kernel(heats, x_ref, stats_ref, scalars_ref, fixed_ref, out_ref, column):
    tokens = x_ref.shape[0]
    column[...] = stats_ref[...].T

    @pl.loop(0, tokens // STRIP)
    def _(strip):
        rows = pl.ds(pl.multiple_of(strip * STRIP, STRIP), STRIP)
        record = column[rows, :]
        x = x_ref[rows, :] - record[:, 0:1]
        result = -fixed_ref[rows, :]
        for k in range(heats):
            factor = scalars_ref[heats + k] / record[:, k + 1 : k + 2]
            result = result + jnp.exp(x * scalars_ref[k]) * factor
        out_ref[rows, :] = result.astype(out_ref.dtype)


def mixture(kernel, heats, values, stats, scalars, *more, dtype, name):
    return pl.pallas_call(
        functools.partial(kernel, heats),
        out_shape=jax.ShapeDtypeStruct(values.shape, dtype),
        in_specs=[VMEM, VMEM, SMEM] + [VMEM] * len(more),
        out_specs=VMEM,
        scratch_shapes=[pltpu.VMEM((padded(values.shape[0]), 8), jnp.float32)],
        compiler_params=pltpu.CompilerParams(vmem_limit_bytes=16 << 20),
        name=name,
    )(values, stats, scalars, *more)


def merge(mine, other, inverse):
    heats = inverse.shape[0]
    highest = jnp.maximum(mine[0:1], other[0:1])
    total = mine[1 : heats + 1] * jnp.exp((mine[0:1] - highest) * inverse[:, None]) + other[
        1 : heats + 1
    ] * jnp.exp((other[0:1] - highest) * inverse[:, None])
    return jnp.concatenate([highest, total, mine[heats + 1 :]], axis=0)


def send_kernel(order_ref, place_ref, head_ref, found_ref, out_ref, grad_ref):
    part = found_ref.shape[1]

    @pl.when(pl.program_id(0) == 0)
    def _():
        for n in range(found_ref.shape[0]):
            grad_ref[n * part : (n + 1) * part, :] = found_ref[place_ref[n]]

    out_ref[0] = lax.dot_general(
        head_ref[...], grad_ref[...], (((1,), (1,)), ((), ())), preferred_element_type=jnp.float32
    ).astype(out_ref.dtype)


def keep_kernel(order_ref, head_ref, grad_ref, out_ref):
    out_ref[0] = lax.dot_general(
        head_ref[...], grad_ref[...], (((1,), (1,)), ((), ())), preferred_element_type=jnp.float32
    )


def products_to_send(order, place, head, found, rows):
    blocks, width = order.shape[0], head.shape[1]
    tokens = found.shape[0] * found.shape[1]
    return pl.pallas_call(
        send_kernel,
        grid_spec=pltpu.PrefetchScalarGridSpec(
            num_scalar_prefetch=2,
            grid=(blocks,),
            in_specs=[
                pl.BlockSpec((rows, width), lambda s, order, place: (order[s], 0)),
                pl.BlockSpec(found.shape, lambda s, order, place: (0, 0, 0)),
            ],
            out_specs=[
                pl.BlockSpec((1, rows, tokens), lambda s, order, place: (s, 0, 0)),
                pl.BlockSpec((tokens, width), lambda s, order, place: (0, 0)),
            ],
        ),
        out_shape=[
            jax.ShapeDtypeStruct((blocks, rows, tokens), jnp.bfloat16),
            jax.ShapeDtypeStruct((tokens, width), jnp.bfloat16),
        ],
        compiler_params=pltpu.CompilerParams(vmem_limit_bytes=24 << 20),
        name="products_to_send",
    )(order, place, head, found)


def products_to_keep(order, head, grad, rows):
    blocks, width, tokens = order.shape[0], head.shape[1], grad.shape[0]
    return pl.pallas_call(
        keep_kernel,
        grid_spec=pltpu.PrefetchScalarGridSpec(
            num_scalar_prefetch=1,
            grid=(blocks,),
            in_specs=[
                pl.BlockSpec((rows, width), lambda s, order: (order[s], 0)),
                pl.BlockSpec((tokens, width), lambda s, order: (0, 0)),
            ],
            out_specs=pl.BlockSpec((1, rows, tokens), lambda s, order: (s, 0, 0)),
        ),
        out_shape=jax.ShapeDtypeStruct((blocks, rows, tokens), jnp.float32),
        compiler_params=pltpu.CompilerParams(vmem_limit_bytes=24 << 20),
        name="products_to_keep",
    )(order, head, grad)


def shards(hidden_t, head, teacher, labels, temps, mix):
    count_dp, count_vocab = lax.axis_size("dp"), lax.axis_size("vocab")
    me_dp, me_vocab = lax.axis_index("dp"), lax.axis_index("vocab")
    rows = hidden_t.shape[0]
    tokens, width = teacher.shape
    part = tokens // CHUNKS
    heats = temps.shape[0]
    far = list(masks_far_first(count_vocab))
    near = far[::-1]

    own = hidden_t.T.reshape(count_dp, CHUNKS, part, rows)

    inverse = 1.0 / temps
    weights = mix[1] * temps
    student_inverse = jnp.concatenate([jnp.ones((1,), jnp.float32), inverse])
    teacher_scalars = jnp.concatenate([inverse, weights, mix[:1]])
    student_scalars = jnp.concatenate([student_inverse, mix[:1], weights])
    relative = jnp.arange(0, count_vocab, 2, dtype=jnp.int32)
    keep_order = me_vocab ^ relative
    send_order = me_vocab ^ (relative + 1)
    dp_order = me_dp ^ jnp.arange(count_dp, dtype=jnp.int32)

    def gather_hidden(block):
        have = {0: block[None]}
        for mask in far:
            keys = sorted(have)
            other = swap(jnp.concatenate([have[k] for k in keys], axis=0), "vocab", mask)
            for place, k in enumerate(keys):
                have[k ^ mask] = other[place : place + 1]
        found = jnp.concatenate([have[k] for k in range(count_vocab)], axis=0)
        return jnp.concatenate([pick(found, me_vocab ^ n) for n in range(count_vocab)], axis=1)

    def partial_logits(gathered):
        partial = jnp.dot(gathered, head, preferred_element_type=jnp.float32).reshape(count_dp, part, width)
        coded = partial.astype(jnp.float16)
        return pick(partial, me_dp), [pick(coded, me_dp ^ r) for r in range(1, count_dp)]

    def merged(stats, inverse):
        for mask in near:
            stats = merge(stats, swap(stats, "vocab", mask), inverse)
        return stats

    def reduced(keep, send):
        for mask in near:
            if mask > 1:
                send = jnp.concatenate([keep[k][None] for k in range(1, keep.shape[0], 2)]).astype(jnp.bfloat16)
                keep = jnp.concatenate([keep[k][None] for k in range(0, keep.shape[0], 2)])
            keep = keep + swap(send, "vocab", mask).astype(jnp.float32)
        return keep[0]

    gathered = [gather_hidden(own[:, c].reshape(count_dp * part, rows)) for c in range(CHUNKS)]

    teacher_stats = merged(local_stats(teacher, inverse), inverse)
    place = (labels - me_vocab * width).astype(jnp.float32)
    place = jnp.pad(place, (0, teacher_stats.shape[1] - tokens))[None]
    teacher_stats = jnp.concatenate([teacher_stats[: heats + 1], place, teacher_stats[heats + 2 :]], axis=0)
    fixed = mixture(
        fixed_kernel, heats, teacher, teacher_stats, teacher_scalars, dtype=jnp.float32, name="fixed"
    )

    kept, sent, received = [], [], []
    for c in range(CHUNKS):
        if c:
            sent[c - 1][0], gathered[c] = lax.optimization_barrier((sent[c - 1][0], gathered[c]))
        mine, parts = partial_logits(gathered[c])
        kept.append(mine)
        sent.append(parts)
        received.append([swap(parts[r - 1], "dp", r) for r in range(1, count_dp)])

    grads, found = [], []
    for c in range(CHUNKS):
        if c:
            grads[c - 1], received[c] = lax.optimization_barrier((grads[c - 1], received[c]))
            found[c - 1] = [grads[c - 1]] + [swap(grads[c - 1], "dp", r) for r in range(1, count_dp)]
        logits = kept[c]
        for other in received[c]:
            logits = logits + other.astype(jnp.float32)
        stats = merged(local_stats(logits, student_inverse), student_inverse)
        grads.append(
            mixture(
                grad_kernel,
                heats + 1,
                logits,
                stats,
                student_scalars,
                fixed[c * part : (c + 1) * part],
                dtype=jnp.bfloat16,
                name="grad",
            )
        )
        found.append([grads[c]] + [swap(grads[c], "dp", r) for r in range(1, count_dp)])

    all_grads, hidden_parts = [], []
    for c in range(CHUNKS):
        if c < CHUNKS - 1:
            grads[c + 1], found[c] = lax.optimization_barrier((grads[c + 1], found[c]))
            found[c + 1] = [grads[c + 1]] + [swap(grads[c + 1], "dp", r) for r in range(1, count_dp)]
        send, grad_all = products_to_send(send_order, dp_order, head, jnp.stack(found[c]), rows)
        keep = products_to_keep(keep_order, head, grad_all, rows)
        all_grads.append(grad_all)
        hidden_parts.append(reduced(keep, send))

    head_grad = lax.dot_general(
        jnp.concatenate(gathered, axis=0),
        jnp.concatenate(all_grads, axis=0),
        (((0,), (0,)), ((), ())),
        preferred_element_type=jnp.float32,
    ).astype(jnp.bfloat16)
    hidden_grad = jnp.stack([p.reshape(rows, count_dp, part) for p in hidden_parts], axis=2)
    return (hidden_grad.reshape(rows, count_dp * tokens), head_grad)


def solution(mesh):
    placed = (P(("dp", "vocab"), None), P("dp", "vocab"), P("dp", "vocab"), P("dp"), P(), P())
    return jax.shard_map(
        shards,
        mesh=mesh,
        in_specs=placed,
        out_specs=(P(("dp", "vocab"), None), P("dp", "vocab")),
        check_vma=False,
    )
```

time: 276 us -> 168 us (0.61)
  waiting for transfers between devices: 178 us -> 85.7 us
  starting transfers between devices: 0.34 us -> 36.8 us
  blocking collectives: 28.1 us -> 0 us
  Pallas kernels: 0 us -> 23.1 us
  matrix products: 29.5 us -> 10.8 us
  between operations: 13.9 us -> 1.49 us
  local copies, waits for them, and re-layouts: 13.5 us -> 5.29 us
  other arithmetic: 11.9 us -> 4.85 us
    reduce_scatter x2 -> x0, waiting for transfers between devices: 101 us -> none  [the longest x1 52.6 us: shards(): lax.psum_scatter(lax.dot_general(head, grad_all, (((1,), (1,)), ((), ()))...]
    ppermute x0 -> x33, waiting for transfers between devices: none -> 85.7 us  [swap(): return lax.ppermute(value, axis, [(k, k ^ mask) for k in range(count)])]
    all_gather x2 -> x0, waiting for transfers between devices: 76.8 us -> none  [the longest x1 42.7 us: shards(): h_block = lax.all_gather(hidden_t, 'vocab', axis=0, tiled=True)]
    ppermute x0 -> x33, starting transfers between devices: none -> 36.8 us  [swap(): return lax.ppermute(value, axis, [(k, k ^ mask) for k in range(count)])]
    all_gather x2 -> x0, blocking collectives: 28.1 us -> none  [merged(): pieces = jax.tree.map(lambda part: lax.all_gather(part, axis), value)]
    pallas_call x0 -> x10, Pallas kernels: none -> 23.1 us  [the longest x3 6.99 us: local_stats(): pl.pallas_call(functools.partial(stats_kernel, heats), out_shape=jax.Shap...]
    dot_general x4 -> x3, matrix products: 29.5 us -> 10.8 us  [the longest x1 6.37 us: shards(): lax.dot_general(jnp.concatenate(gathered, axis=0), jnp.concatenate(all_gr...]
    unnamed x18 -> x43, local copies, waits for them, and re-layouts: 12.9 us -> 3.6 us
  transfers between devices with their start and end apart: 4 -> 33, of which waited for: 4 -> 22; matrix products, arithmetic and copies ran while one was open for 6% -> 9% of each run, Pallas kernels for 0% -> 11%
where the time goes in v2:
time: 168 us
  waiting for transfers between devices  85.7 us (51%)
  starting transfers between devices  36.8 us (22%)
  Pallas kernels  23.1 us (14%)
  matrix products  10.8 us (6%)
  local copies, waits for them, and re-layouts  5.29 us (3%)
  other arithmetic  4.85 us (3%)
    ppermute x33, waiting for transfers between devices, swap(): return lax.ppermute(value, axis, [(k, k ^ mask) for k in range(count)])  85.7 us
    ppermute x33, starting transfers between devices, swap(): return lax.ppermute(value, axis, [(k, k ^ mask) for k in range(count)])  36.8 us
    pallas_call x3, Pallas kernels, local_stats(): pl.pallas_call(functools.partial(stats_kernel, heats), out_shape=jax.Shap...  6.99 us
    dot_general x1, matrix products, shards(): lax.dot_general(jnp.concatenate(gathered, axis=0), jnp.concatenate(all_gr...  6.37 us
    pallas_call x2, Pallas kernels, products_to_send(): pl.pallas_call(send_kernel, grid_spec=pltpu.PrefetchScalarGridSpec(num_sc...  5.51 us
    pallas_call x3, Pallas kernels, mixture(): pl.pallas_call(functools.partial(kernel, heats), out_shape=jax.ShapeDtype...  5.33 us
    pallas_call x2, Pallas kernels, products_to_keep(): pl.pallas_call(keep_kernel, grid_spec=pltpu.PrefetchScalarGridSpec(num_sc...  5.3 us
    dot_general x2, matrix products, partial_logits(): jnp.dot(gathered, head, preferred_element_type=jnp.float32)  4.45 us
  transfers between devices with their start and end apart: 33, of which 22 were waited for; matrix products, arithmetic and copies ran while one was open for 9% of the time, Pallas kernels for 11%

profile of v2, /device:TPU:0, one launch (start us, length us, event | category | flops | bytes accessed | tf_op | source)
XLA Modules:
  0.0 168.1 jit_solution(5408157313870423872)
XLA Ops:
  0.7 1.2 copy.9
  1.9 4.1 %collective-permute-start.3 = (bf16[1,384,256]{2,1,0:T(8,128)(2,1)S(1)}, bf16[1,384,256]{2,1,0:T(8,128)(2,1)S(1)}, u32[]{:S(2)}, u32[]{:S(2)}) collective-permute-start(bf16[1,384,256]{2,1,0:T(8,128)(2,1)S(1)} %bitcast.119), channel_id=1, source_target_pairs={{0,4},{1,5},{2,6},{3,7},{4,0},{5,1},{6,2},{7,3},{8,12},{9,13},{10,... | collective-permute-start | bytes 589832 | tf_op jit(solution)/shard_map/ppermute | solution.py:17
  6.1 0.6 fusion.27
  6.7 0.6 broadcast_multiply_fusion
  7.4 3.2 %stats.4 = f32[8,256]{1,0:T(8,128)S(1)} custom-call(bf16[192,1280]{1,0:T(8,128)(2,1)S(1)} %copy-done, f32[4]{0:T(128)S(1)} %get-tuple-element.79.inverse_ref), custom_call_target="tpu_custom_call" | custom-call | tf_op jit(solution)/shard_map/stats/pallas_call | solution.py:61
  10.6 0.7 constant_dynamic-update-slice_fusion.7
  11.8 1.9 %collective-permute-start.13 = (f32[8,256]{1,0:T(8,128)S(1)}, f32[8,256]{1,0:T(8,128)S(1)}, u32[]{:S(2)}, u32[]{:S(2)}) collective-permute-start(f32[8,256]{1,0:T(8,128)S(1)} %pad_maximum_fusion.10), channel_id=1, source_target_pairs={{0,2},{1,3},{2,0},{3,1},{4,6},{5,7},{6,4},{7,5},{8,10},{9,11},{10,... | collective-permute-start | bytes 24584 | tf_op jit(solution)/shard_map/ppermute | solution.py:17
  13.7 0.7 pad_maximum_fusion.19.scalars_ref
  14.5 1.1 collective-permute-done.13
  15.7 2.9 %collective-permute-start.14 = (f32[8,256]{1,0:T(8,128)S(1)}, f32[8,256]{1,0:T(8,128)S(1)}, u32[]{:S(2)}, u32[]{:S(2)}) collective-permute-start(f32[8,256]{1,0:T(8,128)S(1)} %pad_maximum_fusion.9), channel_id=1, source_target_pairs={{0,4},{1,5},{2,6},{3,7},{4,0},{5,1},{6,2},{7,3},{8,12},{9,13},{10,... | collective-permute-start | bytes 24584 | tf_op jit(solution)/shard_map/ppermute | solution.py:17
  18.6 0.7 pad_maximum_fusion.20.scalars_ref
  19.4 4.6 %collective-permute-done.14 = f32[8,256]{1,0:T(8,128)S(1)} collective-permute-done((f32[8,256]{1,0:T(8,128)S(1)}, f32[8,256]{1,0:T(8,128)S(1)}, u32[]{:S(2)}, u32[]{:S(2)}) %collective-permute-start.14) | collective-permute-done | bytes 8224 | tf_op jit(solution)/shard_map/ppermute | solution.py:17
  24.0 0.8 collective-permute-start.4
  24.9 2.3 %fixed.1 = f32[192,1280]{1,0:T(8,128)S(1)} custom-call(bf16[192,1280]{1,0:T(8,128)(2,1)S(1)} %copy-done, f32[8,256]{1,0:T(8,128)S(1)} %pad_maximum_fusion.11.stats_ref, f32[9]{0:T(128)S(1)} %pad_maximum_fusion.20.scalars_ref), custom_call_target="tpu_custom_call" | custom-call | tf_op jit(solution)/shard_map/fixed/pallas_call | solution.py:106
  27.3 1.3 collective-permute-start.1
  28.6 7.5 %collective-permute-done.4 = bf16[2,384,256]{2,1,0:T(8,128)(2,1)S(1)} collective-permute-done((bf16[2,384,256]{2,1,0:T(8,128)(2,1)S(1)}, bf16[2,384,256]{2,1,0:T(8,128)(2,1)S(1)}, u32[]{:S(2)}, u32[]{:S(2)}) %collective-permute-start.4) | collective-permute-done | bytes 393248 | tf_op jit(solution)/shard_map/ppermute | solution.py:17
  36.4 6.4 %collective-permute-done.1 = bf16[2,384,256]{2,1,0:T(8,128)(2,1)S(1)} collective-permute-done((bf16[2,384,256]{2,1,0:T(8,128)(2,1)S(1)}, bf16[2,384,256]{2,1,0:T(8,128)(2,1)S(1)}, u32[]{:S(2)}, u32[]{:S(2)}) %collective-permute-start.1) | collective-permute-done | bytes 393248 | tf_op jit(solution)/shard_map/ppermute | solution.py:17
  43.2 2.1 %collective-permute-done.2 = bf16[4,384,256]{2,1,0:T(8,128)(2,1)S(1)} collective-permute-done((bf16[4,384,256]{2,1,0:T(8,128)(2,1)S(1)}, bf16[4,384,256]{2,1,0:T(8,128)(2,1)S(1)}, u32[]{:S(2)}, u32[]{:S(2)}) %collective-permute-start.2) | collective-permute-done | bytes 786464 | tf_op jit(solution)/shard_map/ppermute | solution.py:17
  45.7 2.2 %fusion.28 = f32[384,1280]{1,0:T(8,128)S(1)} fusion(bf16[384,2048]{1,0:T(8,128)(2,1)S(1)} %bitcast_dynamic-update-slice_fusion.8, bf16[2048,1280]{1,0:T(8,128)(2,1)S(1)} %bitcast.111), kind=kOutput, calls=%fused_computation.139 | convolution fusion | flops 2013265920 | bytes 8781824 | tf_op jit(solution)/shard_map/dot_general | solution.py:223
  48.2 2.3 %collective-permute-start.8 = (f16[96,1280]{1,0:T(8,128)(2,1)S(1)}, f16[96,1280]{1,0:T(8,128)(2,1)S(1)}, u32[]{:S(2)}, u32[]{:S(2)}) collective-permute-start(f16[96,1280]{1,0:T(8,128)(2,1)S(1)} %get-tuple-element.64), channel_id=1, source_target_pairs={{0,24},{8,16},{16,8},{24,0},{1,25},{9,17},{17,9},{25,1},{2,26},{10... | collective-permute-start | bytes 737288 | tf_op jit(solution)/shard_map/ppermute | solution.py:17
  50.5 0.5 collective-permute-start.7
  51.0 0.8 collective-permute-start.6
  51.9 6.1 %collective-permute-done.8 = f16[96,1280]{1,0:T(8,128)(2,1)S(1)} collective-permute-done((f16[96,1280]{1,0:T(8,128)(2,1)S(1)}, f16[96,1280]{1,0:T(8,128)(2,1)S(1)}, u32[]{:S(2)}, u32[]{:S(2)}) %collective-permute-start.8) | collective-permute-done | bytes 245792 | tf_op jit(solution)/shard_map/ppermute | solution.py:17
  58.0 4.4 %collective-permute-done.7 = f16[96,1280]{1,0:T(8,128)(2,1)S(1)} collective-permute-done((f16[96,1280]{1,0:T(8,128)(2,1)S(1)}, f16[96,1280]{1,0:T(8,128)(2,1)S(1)}, u32[]{:S(2)}, u32[]{:S(2)}) %collective-permute-start.7) | collective-permute-done | bytes 245792 | tf_op jit(solution)/shard_map/ppermute | solution.py:17
  62.6 1.9 %stats.3 = f32[8,128]{1,0:T(8,128)S(1)} custom-call(f32[96,1280]{1,0:T(8,128)S(1)} %fusion.7.x_ref, f32[5]{0:T(128)S(1)} %pad_maximum_fusion.18.inverse_ref), custom_call_target="tpu_custom_call" | custom-call | tf_op jit(solution)/shard_map/stats/pallas_call | solution.py:61
  64.6 1.1 collective-permute-done.9
  65.8 1.6 collective-permute-start.10
  67.5 2.2 %fusion.29 = f32[384,1280]{1,0:T(8,128)S(1)} fusion(bf16[384,2048]{1,0:T(8,128)(2,1)S(1)} %bitcast_dynamic-update-slice_fusion, bf16[2048,1280]{1,0:T(8,128)(2,1)S(1)} %bitcast.111), kind=kOutput, calls=%fused_computation.140 | convolution fusion | flops 2013265920 | bytes 8781824 | tf_op jit(solution)/shard_map/dot_general | solution.py:223
  70.0 3.4 %collective-permute-start.11 = (f32[8,128]{1,0:T(8,128)S(1)}, f32[8,128]{1,0:T(8,128)S(1)}, u32[]{:S(2)}, u32[]{:S(2)}) collective-permute-start(f32[8,128]{1,0:T(8,128)S(1)} %pad_maximum_fusion.13), channel_id=1, source_target_pairs={{0,4},{1,5},{2,6},{3,7},{4,0},{5,1},{6,2},{7,3},{8,12},{9,13},{10,... | collective-permute-start | bytes 12296 | tf_op jit(solution)/shard_map/ppermute | solution.py:17
  73.5 1.6 collective-permute-start.15
  75.1 0.7 collective-permute-start.16
  75.8 1.3 collective-permute-start.17
  77.2 1.5 grad.2
  78.7 3.8 %collective-permute-done.15 = f16[96,1280]{1,0:T(8,128)(2,1)S(1)} collective-permute-done((f16[96,1280]{1,0:T(8,128)(2,1)S(1)}, f16[96,1280]{1,0:T(8,128)(2,1)S(1)}, u32[]{:S(2)}, u32[]{:S(2)}) %collective-permute-start.15) | collective-permute-done | bytes 245792 | tf_op jit(solution)/shard_map/ppermute | solution.py:17
  82.5 5.1 %collective-permute-done.16 = f16[96,1280]{1,0:T(8,128)(2,1)S(1)} collective-permute-done((f16[96,1280]{1,0:T(8,128)(2,1)S(1)}, f16[96,1280]{1,0:T(8,128)(2,1)S(1)}, u32[]{:S(2)}, u32[]{:S(2)}) %collective-permute-start.16) | collective-permute-done | bytes 245792 | tf_op jit(solution)/shard_map/ppermute | solution.py:17
  87.7 1.9 %stats.5 = f32[8,128]{1,0:T(8,128)S(1)} custom-call(f32[96,1280]{1,0:T(8,128)S(1)} %fusion.9.x_ref, f32[5]{0:T(128)S(1)} %pad_maximum_fusion.18.inverse_ref), custom_call_target="tpu_custom_call" | custom-call | tf_op jit(solution)/shard_map/stats/pallas_call | solution.py:61
  89.6 1.1 collective-permute-done.18
  90.9 0.4 collective-permute-start.19
  91.3 3.2 %collective-permute-done.19 = f32[8,128]{1,0:T(8,128)S(1)} collective-permute-done((f32[8,128]{1,0:T(8,128)S(1)}, f32[8,128]{1,0:T(8,128)S(1)}, u32[]{:S(2)}, u32[]{:S(2)}) %collective-permute-start.19) | collective-permute-done | bytes 4128 | tf_op jit(solution)/shard_map/ppermute | solution.py:17
  94.7 0.4 collective-permute-start.20
  95.0 0.5 collective-permute-start.21
  95.6 1.4 collective-permute-start.22
  97.0 1.5 collective-permute-start.23
  98.5 0.7 collective-permute-done.20
  99.3 1.5 grad.3
  100.8 3.1 %collective-permute-done.21 = bf16[96,1280]{1,0:T(8,128)(2,1)S(1)} collective-permute-done((bf16[96,1280]{1,0:T(8,128)(2,1)S(1)}, bf16[96,1280]{1,0:T(8,128)(2,1)S(1)}, u32[]{:S(2)}, u32[]{:S(2)}) %collective-permute-start.21) | collective-permute-done | bytes 245792 | tf_op jit(solution)/shard_map/ppermute | solution.py:17
  104.2 3.0 %collective-permute-done.23 = bf16[96,1280]{1,0:T(8,128)(2,1)S(1)} collective-permute-done((bf16[96,1280]{1,0:T(8,128)(2,1)S(1)}, bf16[96,1280]{1,0:T(8,128)(2,1)S(1)}, u32[]{:S(2)}, u32[]{:S(2)}) %collective-permute-start.23) | collective-permute-done | bytes 245792 | tf_op jit(solution)/shard_map/ppermute | solution.py:17
  107.2 1.7 collective-permute-start.29
  108.9 1.3 collective-permute-start.28
  110.2 0.5 collective-permute-start.27
  110.8 2.8 %products_to_send.2 = (bf16[4,256,384]{2,1,0:T(8,128)(2,1)S(1)}, bf16[384,1280]{1,0:T(8,128)(2,1)S(1)}) custom-call(s32[4]{0:T(128)S(1)} %get-tuple-element.83.order_ref, s32[4]{0:T(128)S(1)} %get-tuple-element.82.place_ref, bf16[2048,1280]{1,0:T(8,128)(2,1)S(1)} %bitcast.111, bf16[4,96,1280]{2,1,0:T(8,128)(2,1)S(1)} %pad_maximum_fusion.found_ref), custom_call_target="tpu_custom_call" | custom-call | tf_op jit(solution)/shard_map/products_to_send/pallas_call | solution.py:148
  113.7 2.7 %products_to_keep.2 = f32[4,256,384]{2,1,0:T(8,128)S(1)} custom-call(s32[4]{0:T(128)S(1)} %fusion.13.order_ref, bf16[2048,1280]{1,0:T(8,128)(2,1)S(1)} %bitcast.111, bf16[384,1280]{1,0:T(8,128)(2,1)S(1)} %get-tuple-element.25.grad_ref), custom_call_target="tpu_custom_call" | custom-call | tf_op jit(solution)/shard_map/products_to_keep/pallas_call | solution.py:173
  116.5 2.5 %collective-permute-done.28 = bf16[96,1280]{1,0:T(8,128)(2,1)S(1)} collective-permute-done((bf16[96,1280]{1,0:T(8,128)(2,1)S(1)}, bf16[96,1280]{1,0:T(8,128)(2,1)S(1)}, u32[]{:S(2)}, u32[]{:S(2)}) %collective-permute-start.28) | collective-permute-done | bytes 245792 | tf_op jit(solution)/shard_map/ppermute | solution.py:17
  119.1 2.8 %products_to_send.3 = (bf16[4,256,384]{2,1,0:T(8,128)(2,1)S(1)}, bf16[384,1280]{1,0:T(8,128)(2,1)S(1)}) custom-call(s32[4]{0:T(128)S(1)} %get-tuple-element.83.order_ref, s32[4]{0:T(128)S(1)} %get-tuple-element.82.place_ref, bf16[2048,1280]{1,0:T(8,128)(2,1)S(1)} %bitcast.111, bf16[4,96,1280]{2,1,0:T(8,128)(2,1)S(1)} %pad_maximum_fusion.1.found_ref), custom_call_target="tpu_custom_call" | custom-call | tf_op jit(solution)/shard_map/products_to_send/pallas_call | solution.py:148
  121.9 2.6 %products_to_keep.3 = f32[4,256,384]{2,1,0:T(8,128)S(1)} custom-call(s32[4]{0:T(128)S(1)} %fusion.13.order_ref, bf16[2048,1280]{1,0:T(8,128)(2,1)S(1)} %bitcast.111, bf16[384,1280]{1,0:T(8,128)(2,1)S(1)} %get-tuple-element.28.grad_ref), custom_call_target="tpu_custom_call" | custom-call | tf_op jit(solution)/shard_map/products_to_keep/pallas_call | solution.py:173
  124.6 6.4 %convolution_convert_fusion = bf16[2048,1280]{1,0:T(8,128)(2,1)} fusion(bf16[384,2048]{1,0:T(8,128)(2,1)S(1)} %bitcast_dynamic-update-slice_fusion, bf16[384,2048]{1,0:T(8,128)(2,1)S(1)} %bitcast_dynamic-update-slice_fusion.8, bf16[384,1280]{1,0:T(8,128)(2,1)S(1)} %get-tuple-element.28.grad_ref, bf16[384,1280]{1,0:T(8,128)(2,1)S(1)} %get-tuple-element.25.grad_ref), kind=kOutput, calls=%fused_computation | convolution fusion | flops 4039376896 | bytes 10354688 | tf_op jit(solution)/shard_map/dot_general | solution.py:292
  131.3 0.4 collective-permute-start.25
  132.2 1.7 %collective-permute-start.31 = (bf16[2,256,384]{2,1,0:T(8,128)(2,1)S(1)}, bf16[2,256,384]{2,1,0:T(8,128)(2,1)S(1)}, u32[]{:S(2)}, u32[]{:S(2)}) collective-permute-start(bf16[2,256,384]{2,1,0:T(8,128)(2,1)S(1)} %pad_maximum_fusion.8), channel_id=1, source_target_pairs={{0,2},{1,3},{2,0},{3,1},{4,6},{5,7},{6,4},{7,5},{8,10},{9,11},{10,... | collective-permute-start | bytes 1179656 | tf_op jit(solution)/shard_map/ppermute | solution.py:17
  133.9 9.4 %collective-permute-done.25 = bf16[2,256,384]{2,1,0:T(8,128)(2,1)S(1)} collective-permute-done((bf16[2,256,384]{2,1,0:T(8,128)(2,1)S(1)}, bf16[2,256,384]{2,1,0:T(8,128)(2,1)S(1)}, u32[]{:S(2)}, u32[]{:S(2)}) %collective-permute-start.25) | collective-permute-done | bytes 393248 | tf_op jit(solution)/shard_map/ppermute | solution.py:17
  143.4 2.6 %collective-permute-start.26 = (bf16[1,256,384]{2,1,0:T(8,128)(2,1)S(1)}, bf16[1,256,384]{2,1,0:T(8,128)(2,1)S(1)}, u32[]{:S(2)}, u32[]{:S(2)}) collective-permute-start(bf16[1,256,384]{2,1,0:T(8,128)(2,1)S(1)} %slice.351), channel_id=1, source_target_pairs={{0,4},{1,5},{2,6},{3,7},{4,0},{5,1},{6,2},{7,3},{8,12},{9,13},{10,... | collective-permute-start | bytes 589832 | tf_op jit(solution)/shard_map/ppermute | solution.py:17
  146.0 9.3 %collective-permute-done.31 = bf16[2,256,384]{2,1,0:T(8,128)(2,1)S(1)} collective-permute-done((bf16[2,256,384]{2,1,0:T(8,128)(2,1)S(1)}, bf16[2,256,384]{2,1,0:T(8,128)(2,1)S(1)}, u32[]{:S(2)}, u32[]{:S(2)}) %collective-permute-start.31) | collective-permute-done | bytes 393248 | tf_op jit(solution)/shard_map/ppermute | solution.py:17
  155.4 0.5 collective-permute-start.32
  156.1 10.5 %collective-permute-done.32 = bf16[1,256,384]{2,1,0:T(8,128)(2,1)S(1)} collective-permute-done((bf16[1,256,384]{2,1,0:T(8,128)(2,1)S(1)}, bf16[1,256,384]{2,1,0:T(8,128)(2,1)S(1)}, u32[]{:S(2)}, u32[]{:S(2)}) %collective-permute-start.32) | collective-permute-done | bytes 196640 | tf_op jit(solution)/shard_map/ppermute | solution.py:17
  166.9 1.1 copy.13
  (146 shorter events, 5.8 us)
Async XLA Ops:
  0.6 5.5 %copy-start.2 = (f32[2]{0:T(128)S(1)}, f32[2]{0:T(128)}, u32[]{:S(2)}) copy-start(f32[2]{0:T(128)} %param.11) | copy-start | bytes 28
  0.6 6.1 %copy-start.4 = (f32[4]{0:T(128)S(1)}, f32[4]{0:T(128)}, u32[]{:S(2)}) copy-start(f32[4]{0:T(128)} %param.10) | copy-start | bytes 52
  0.7 6.7 %copy-start = (bf16[192,1280]{1,0:T(8,128)(2,1)S(1)}, bf16[192,1280]{1,0:T(8,128)(2,1)}, u32[]{:S(2)}) copy-start(bf16[192,1280]{1,0:T(8,128)(2,1)} %x_ref.3) | copy-start | bytes 1474564
  0.7 10.6 %copy-start.3 = (s32[192]{0:T(256)S(1)}, s32[192]{0:T(256)}, u32[]{:S(2)}) copy-start(s32[192]{0:T(256)} %param.9) | copy-start | bytes 2308
  1.9 22.0 %collective-permute-start.3 = (bf16[1,384,256]{2,1,0:T(8,128)(2,1)S(1)}, bf16[1,384,256]{2,1,0:T(8,128)(2,1)S(1)}, u32[]{:S(2)}, u32[]{:S(2)}) collective-permute-start(bf16[1,384,256]{2,1,0:T(8,128)(2,1)S(1)} %bitcast.119), channel_id=1, source_target_pairs={{0,4},{1,5},{2,6},{3,7},{4,0},{5,1},{6,2},{7,3},{8,12},{9,13},{10,... | collective-permute-start | bytes 589832 | tf_op jit(solution)/shard_map/ppermute | solution.py:17
  6.0 21.2 %collective-permute-start = (bf16[1,384,256]{2,1,0:T(8,128)(2,1)S(1)}, bf16[1,384,256]{2,1,0:T(8,128)(2,1)S(1)}, u32[]{:S(2)}, u32[]{:S(2)}) collective-permute-start(bf16[1,384,256]{2,1,0:T(8,128)(2,1)S(1)} %bitcast.115), channel_id=1, source_target_pairs={{0,4},{1,5},{2,6},{3,7},{4,0},{5,1},{6,2},{7,3},{8,12},{9,13},{10,... | collective-permute-start | bytes 589832 | tf_op jit(solution)/shard_map/ppermute | solution.py:17
  10.5 1.2 collective-permute-start.12
  11.8 3.7 %collective-permute-start.13 = (f32[8,256]{1,0:T(8,128)S(1)}, f32[8,256]{1,0:T(8,128)S(1)}, u32[]{:S(2)}, u32[]{:S(2)}) collective-permute-start(f32[8,256]{1,0:T(8,128)S(1)} %pad_maximum_fusion.10), channel_id=1, source_target_pairs={{0,2},{1,3},{2,0},{3,1},{4,6},{5,7},{6,4},{7,5},{8,10},{9,11},{10,... | collective-permute-start | bytes 24584 | tf_op jit(solution)/shard_map/ppermute | solution.py:17
  15.7 8.3 %collective-permute-start.14 = (f32[8,256]{1,0:T(8,128)S(1)}, f32[8,256]{1,0:T(8,128)S(1)}, u32[]{:S(2)}, u32[]{:S(2)}) collective-permute-start(f32[8,256]{1,0:T(8,128)S(1)} %pad_maximum_fusion.9), channel_id=1, source_target_pairs={{0,4},{1,5},{2,6},{3,7},{4,0},{5,1},{6,2},{7,3},{8,12},{9,13},{10,... | collective-permute-start | bytes 24584 | tf_op jit(solution)/shard_map/ppermute | solution.py:17
  24.0 12.1 %collective-permute-start.4 = (bf16[2,384,256]{2,1,0:T(8,128)(2,1)S(1)}, bf16[2,384,256]{2,1,0:T(8,128)(2,1)S(1)}, u32[]{:S(2)}, u32[]{:S(2)}) collective-permute-start(bf16[2,384,256]{2,1,0:T(8,128)(2,1)S(1)} %pad_maximum_fusion.6), channel_id=1, source_target_pairs={{0,2},{1,3},{2,0},{3,1},{4,6},{5,7},{6,4},{7,5},{8,10},{9,11},{10,... | collective-permute-start | bytes 1179656 | tf_op jit(solution)/shard_map/ppermute | solution.py:17
  27.3 15.5 %collective-permute-start.1 = (bf16[2,384,256]{2,1,0:T(8,128)(2,1)S(1)}, bf16[2,384,256]{2,1,0:T(8,128)(2,1)S(1)}, u32[]{:S(2)}, u32[]{:S(2)}) collective-permute-start(bf16[2,384,256]{2,1,0:T(8,128)(2,1)S(1)} %pad_maximum_fusion.5), channel_id=1, source_target_pairs={{0,2},{1,3},{2,0},{3,1},{4,6},{5,7},{6,4},{7,5},{8,10},{9,11},{10,... | collective-permute-start | bytes 1179656 | tf_op jit(solution)/shard_map/ppermute | solution.py:17
  36.1 9.6 %slice-start = ((s8[5242880]{0:T(1024)(128)(4,1)}), s8[4194304]{0:T(1024)(128)(4,1)S(1)}, s32[]{:S(2)}) async-start(s8[5242880]{0:T(1024)(128)(4,1)} %bitcast.110), calls=%async_computation | async-start | bytes 8388608
  36.2 6.8 %collective-permute-start.5 = (bf16[4,384,256]{2,1,0:T(8,128)(2,1)S(1)}, bf16[4,384,256]{2,1,0:T(8,128)(2,1)S(1)}, u32[]{:S(2)}, u32[]{:S(2)}) collective-permute-start(bf16[4,384,256]{2,1,0:T(8,128)(2,1)S(1)} %pad_maximum_fusion.3), channel_id=1, source_target_pairs={{0,1},{1,0},{2,3},{3,2},{4,5},{5,4},{6,7},{7,6},{8,9},{9,8},{10,11... | collective-permute-start | bytes 2359304 | tf_op jit(solution)/shard_map/ppermute | solution.py:17
  36.4 6.6 %copy-start.1 = (bf16[8,384,256]{2,1,0:T(8,128)(2,1)S(1)}, bf16[8,384,256]{2,1,0:T(8,128)(2,1)}, u32[]{:S(2)}) copy-start(bf16[8,384,256]{2,1,0:T(8,128)(2,1)} %constant_dynamic-update-slice_fusion.7) | copy-start | bytes 4718596
  42.9 2.4 %collective-permute-start.2 = (bf16[4,384,256]{2,1,0:T(8,128)(2,1)S(1)}, bf16[4,384,256]{2,1,0:T(8,128)(2,1)S(1)}, u32[]{:S(2)}, u32[]{:S(2)}) collective-permute-start(bf16[4,384,256]{2,1,0:T(8,128)(2,1)S(1)} %pad_maximum_fusion.2), channel_id=1, source_target_pairs={{0,1},{1,0},{2,3},{3,2},{4,5},{5,4},{6,7},{7,6},{8,9},{9,8},{10,11... | collective-permute-start | bytes 2359304 | tf_op jit(solution)/shard_map/ppermute | solution.py:17
  43.1 2.6 %slice-start.1 = ((s8[5242880]{0:T(1024)(128)(4,1)}), s8[1048576]{0:T(1024)(128)(4,1)S(1)}, s32[]{:S(2)}) async-start(s8[5242880]{0:T(1024)(128)(4,1)} %bitcast.110), calls=%async_computation.1 | async-start | bytes 2097152
  48.2 9.8 %collective-permute-start.8 = (f16[96,1280]{1,0:T(8,128)(2,1)S(1)}, f16[96,1280]{1,0:T(8,128)(2,1)S(1)}, u32[]{:S(2)}, u32[]{:S(2)}) collective-permute-start(f16[96,1280]{1,0:T(8,128)(2,1)S(1)} %get-tuple-element.64), channel_id=1, source_target_pairs={{0,24},{8,16},{16,8},{24,0},{1,25},{9,17},{17,9},{25,1},{2,26},{10... | collective-permute-start | bytes 737288 | tf_op jit(solution)/shard_map/ppermute | solution.py:17
  50.5 12.0 %collective-permute-start.7 = (f16[96,1280]{1,0:T(8,128)(2,1)S(1)}, f16[96,1280]{1,0:T(8,128)(2,1)S(1)}, u32[]{:S(2)}, u32[]{:S(2)}) collective-permute-start(f16[96,1280]{1,0:T(8,128)(2,1)S(1)} %get-tuple-element.65), channel_id=1, source_target_pairs={{0,16},{8,24},{16,0},{24,8},{1,17},{9,25},{17,1},{25,9},{2,18},{10... | collective-permute-start | bytes 737288 | tf_op jit(solution)/shard_map/ppermute | solution.py:17
  51.0 11.5 %collective-permute-start.6 = (f16[96,1280]{1,0:T(8,128)(2,1)S(1)}, f16[96,1280]{1,0:T(8,128)(2,1)S(1)}, u32[]{:S(2)}, u32[]{:S(2)}) collective-permute-start(f16[96,1280]{1,0:T(8,128)(2,1)S(1)} %get-tuple-element.63), channel_id=1, source_target_pairs={{0,8},{8,0},{16,24},{24,16},{1,9},{9,1},{17,25},{25,17},{2,10},{10... | collective-permute-start | bytes 737288 | tf_op jit(solution)/shard_map/ppermute | solution.py:17
  64.5 1.2 collective-permute-start.9
  65.8 4.0 %collective-permute-start.10 = (f32[8,128]{1,0:T(8,128)S(1)}, f32[8,128]{1,0:T(8,128)S(1)}, u32[]{:S(2)}, u32[]{:S(2)}) collective-permute-start(f32[8,128]{1,0:T(8,128)S(1)} %pad_maximum_fusion.14), channel_id=1, source_target_pairs={{0,2},{1,3},{2,0},{3,1},{4,6},{5,7},{6,4},{7,5},{8,10},{9,11},{10,... | collective-permute-start | bytes 12296 | tf_op jit(solution)/shard_map/ppermute | solution.py:17
  70.0 7.1 %collective-permute-start.11 = (f32[8,128]{1,0:T(8,128)S(1)}, f32[8,128]{1,0:T(8,128)S(1)}, u32[]{:S(2)}, u32[]{:S(2)}) collective-permute-start(f32[8,128]{1,0:T(8,128)S(1)} %pad_maximum_fusion.13), channel_id=1, source_target_pairs={{0,4},{1,5},{2,6},{3,7},{4,0},{5,1},{6,2},{7,3},{8,12},{9,13},{10,... | collective-permute-start | bytes 12296 | tf_op jit(solution)/shard_map/ppermute | solution.py:17
  73.5 8.9 %collective-permute-start.15 = (f16[96,1280]{1,0:T(8,128)(2,1)S(1)}, f16[96,1280]{1,0:T(8,128)(2,1)S(1)}, u32[]{:S(2)}, u32[]{:S(2)}) collective-permute-start(f16[96,1280]{1,0:T(8,128)(2,1)S(1)} %get-tuple-element.62), channel_id=1, source_target_pairs={{0,8},{8,0},{16,24},{24,16},{1,9},{9,1},{17,25},{25,17},{2,10},{10... | collective-permute-start | bytes 737288 | tf_op jit(solution)/shard_map/ppermute | solution.py:17
  75.1 12.5 %collective-permute-start.16 = (f16[96,1280]{1,0:T(8,128)(2,1)S(1)}, f16[96,1280]{1,0:T(8,128)(2,1)S(1)}, u32[]{:S(2)}, u32[]{:S(2)}) collective-permute-start(f16[96,1280]{1,0:T(8,128)(2,1)S(1)} %get-tuple-element.61), channel_id=1, source_target_pairs={{0,16},{8,24},{16,0},{24,8},{1,17},{9,25},{17,1},{25,9},{2,18},{10... | collective-permute-start | bytes 737288 | tf_op jit(solution)/shard_map/ppermute | solution.py:17
  75.8 11.7 %collective-permute-start.17 = (f16[96,1280]{1,0:T(8,128)(2,1)S(1)}, f16[96,1280]{1,0:T(8,128)(2,1)S(1)}, u32[]{:S(2)}, u32[]{:S(2)}) collective-permute-start(f16[96,1280]{1,0:T(8,128)(2,1)S(1)} %get-tuple-element.60), channel_id=1, source_target_pairs={{0,24},{8,16},{16,8},{24,0},{1,25},{9,17},{17,9},{25,1},{2,26},{10... | collective-permute-start | bytes 737288 | tf_op jit(solution)/shard_map/ppermute | solution.py:17
  89.6 1.2 collective-permute-start.18
  90.9 3.7 %collective-permute-start.19 = (f32[8,128]{1,0:T(8,128)S(1)}, f32[8,128]{1,0:T(8,128)S(1)}, u32[]{:S(2)}, u32[]{:S(2)}) collective-permute-start(f32[8,128]{1,0:T(8,128)S(1)} %pad_maximum_fusion.17), channel_id=1, source_target_pairs={{0,2},{1,3},{2,0},{3,1},{4,6},{5,7},{6,4},{7,5},{8,10},{9,11},{10,... | collective-permute-start | bytes 12296 | tf_op jit(solution)/shard_map/ppermute | solution.py:17
  94.7 4.6 %collective-permute-start.20 = (f32[8,128]{1,0:T(8,128)S(1)}, f32[8,128]{1,0:T(8,128)S(1)}, u32[]{:S(2)}, u32[]{:S(2)}) collective-permute-start(f32[8,128]{1,0:T(8,128)S(1)} %pad_maximum_fusion.16), channel_id=1, source_target_pairs={{0,4},{1,5},{2,6},{3,7},{4,0},{5,1},{6,2},{7,3},{8,12},{9,13},{10,... | collective-permute-start | bytes 12296 | tf_op jit(solution)/shard_map/ppermute | solution.py:17
  95.0 8.9 %collective-permute-start.21 = (bf16[96,1280]{1,0:T(8,128)(2,1)S(1)}, bf16[96,1280]{1,0:T(8,128)(2,1)S(1)}, u32[]{:S(2)}, u32[]{:S(2)}) collective-permute-start(bf16[96,1280]{1,0:T(8,128)(2,1)S(1)} %grad.2), channel_id=1, source_target_pairs={{0,8},{8,0},{16,24},{24,16},{1,9},{9,1},{17,25},{25,17},{2,10},{10... | collective-permute-start | bytes 737288 | tf_op jit(solution)/shard_map/ppermute | solution.py:17
  95.6 8.6 %collective-permute-start.22 = (bf16[96,1280]{1,0:T(8,128)(2,1)S(1)}, bf16[96,1280]{1,0:T(8,128)(2,1)S(1)}, u32[]{:S(2)}, u32[]{:S(2)}) collective-permute-start(bf16[96,1280]{1,0:T(8,128)(2,1)S(1)} %grad.2), channel_id=1, source_target_pairs={{0,16},{8,24},{16,0},{24,8},{1,17},{9,25},{17,1},{25,9},{2,18},{10... | collective-permute-start | bytes 737288 | tf_op jit(solution)/shard_map/ppermute | solution.py:17
  97.0 10.2 %collective-permute-start.23 = (bf16[96,1280]{1,0:T(8,128)(2,1)S(1)}, bf16[96,1280]{1,0:T(8,128)(2,1)S(1)}, u32[]{:S(2)}, u32[]{:S(2)}) collective-permute-start(bf16[96,1280]{1,0:T(8,128)(2,1)S(1)} %grad.2), channel_id=1, source_target_pairs={{0,24},{8,16},{16,8},{24,0},{1,25},{9,17},{17,9},{25,1},{2,26},{10... | collective-permute-start | bytes 737288 | tf_op jit(solution)/shard_map/ppermute | solution.py:17
  107.2 9.3 %collective-permute-start.29 = (bf16[96,1280]{1,0:T(8,128)(2,1)S(1)}, bf16[96,1280]{1,0:T(8,128)(2,1)S(1)}, u32[]{:S(2)}, u32[]{:S(2)}) collective-permute-start(bf16[96,1280]{1,0:T(8,128)(2,1)S(1)} %grad.3), channel_id=1, source_target_pairs={{0,24},{8,16},{16,8},{24,0},{1,25},{9,17},{17,9},{25,1},{2,26},{10... | collective-permute-start | bytes 737288 | tf_op jit(solution)/shard_map/ppermute | solution.py:17
  108.9 10.1 %collective-permute-start.28 = (bf16[96,1280]{1,0:T(8,128)(2,1)S(1)}, bf16[96,1280]{1,0:T(8,128)(2,1)S(1)}, u32[]{:S(2)}, u32[]{:S(2)}) collective-permute-start(bf16[96,1280]{1,0:T(8,128)(2,1)S(1)} %grad.3), channel_id=1, source_target_pairs={{0,16},{8,24},{16,0},{24,8},{1,17},{9,25},{17,1},{25,9},{2,18},{10... | collective-permute-start | bytes 737288 | tf_op jit(solution)/shard_map/ppermute | solution.py:17
  110.2 8.8 %collective-permute-start.27 = (bf16[96,1280]{1,0:T(8,128)(2,1)S(1)}, bf16[96,1280]{1,0:T(8,128)(2,1)S(1)}, u32[]{:S(2)}, u32[]{:S(2)}) collective-permute-start(bf16[96,1280]{1,0:T(8,128)(2,1)S(1)} %grad.3), channel_id=1, source_target_pairs={{0,8},{8,0},{16,24},{24,16},{1,9},{9,1},{17,25},{25,17},{2,10},{10... | collective-permute-start | bytes 737288 | tf_op jit(solution)/shard_map/ppermute | solution.py:17
  113.6 17.4 %collective-permute-start.24 = (bf16[4,256,384]{2,1,0:T(8,128)(2,1)S(1)}, bf16[4,256,384]{2,1,0:T(8,128)(2,1)S(1)}, u32[]{:S(2)}, u32[]{:S(2)}) collective-permute-start(bf16[4,256,384]{2,1,0:T(8,128)(2,1)S(1)} %get-tuple-element.26), channel_id=1, source_target_pairs={{0,1},{1,0},{2,3},{3,2},{4,5},{5,4},{6,7},{7,6},{8,9},{9,8},{10,11... | collective-permute-start | bytes 2359304 | tf_op jit(solution)/shard_map/ppermute | solution.py:17
  124.6 7.3 %collective-permute-start.30 = (bf16[4,256,384]{2,1,0:T(8,128)(2,1)S(1)}, bf16[4,256,384]{2,1,0:T(8,128)(2,1)S(1)}, u32[]{:S(2)}, u32[]{:S(2)}) collective-permute-start(bf16[4,256,384]{2,1,0:T(8,128)(2,1)S(1)} %get-tuple-element.29), channel_id=1, source_target_pairs={{0,1},{1,0},{2,3},{3,2},{4,5},{5,4},{6,7},{7,6},{8,9},{9,8},{10,11... | collective-permute-start | bytes 2359304 | tf_op jit(solution)/shard_map/ppermute | solution.py:17
  131.3 12.0 %collective-permute-start.25 = (bf16[2,256,384]{2,1,0:T(8,128)(2,1)S(1)}, bf16[2,256,384]{2,1,0:T(8,128)(2,1)S(1)}, u32[]{:S(2)}, u32[]{:S(2)}) collective-permute-start(bf16[2,256,384]{2,1,0:T(8,128)(2,1)S(1)} %pad_maximum_fusion.7), channel_id=1, source_target_pairs={{0,2},{1,3},{2,0},{3,1},{4,6},{5,7},{6,4},{7,5},{8,10},{9,11},{10,... | collective-permute-start | bytes 1179656 | tf_op jit(solution)/shard_map/ppermute | solution.py:17
  132.2 23.2 %collective-permute-start.31 = (bf16[2,256,384]{2,1,0:T(8,128)(2,1)S(1)}, bf16[2,256,384]{2,1,0:T(8,128)(2,1)S(1)}, u32[]{:S(2)}, u32[]{:S(2)}) collective-permute-start(bf16[2,256,384]{2,1,0:T(8,128)(2,1)S(1)} %pad_maximum_fusion.8), channel_id=1, source_target_pairs={{0,2},{1,3},{2,0},{3,1},{4,6},{5,7},{6,4},{7,5},{8,10},{9,11},{10,... | collective-permute-start | bytes 1179656 | tf_op jit(solution)/shard_map/ppermute | solution.py:17
  143.4 12.5 %collective-permute-start.26 = (bf16[1,256,384]{2,1,0:T(8,128)(2,1)S(1)}, bf16[1,256,384]{2,1,0:T(8,128)(2,1)S(1)}, u32[]{:S(2)}, u32[]{:S(2)}) collective-permute-start(bf16[1,256,384]{2,1,0:T(8,128)(2,1)S(1)} %slice.351), channel_id=1, source_target_pairs={{0,4},{1,5},{2,6},{3,7},{4,0},{5,1},{6,2},{7,3},{8,12},{9,13},{10,... | collective-permute-start | bytes 589832 | tf_op jit(solution)/shard_map/ppermute | solution.py:17
  155.4 11.2 %collective-permute-start.32 = (bf16[1,256,384]{2,1,0:T(8,128)(2,1)S(1)}, bf16[1,256,384]{2,1,0:T(8,128)(2,1)S(1)}, u32[]{:S(2)}, u32[]{:S(2)}) collective-permute-start(bf16[1,256,384]{2,1,0:T(8,128)(2,1)S(1)} %slice.350), channel_id=1, source_target_pairs={{0,4},{1,5},{2,6},{3,7},{4,0},{5,1},{6,2},{7,3},{8,12},{9,13},{10,... | collective-permute-start | bytes 589832 | tf_op jit(solution)/shard_map/ppermute | solution.py:17

commit v3 on v0

v3 whole, which is shorter than its diff:
```python
import functools

import jax
import jax.numpy as jnp
from jax import lax
from jax.experimental import pallas as pl
from jax.experimental.pallas import tpu as pltpu
from jax.sharding import PartitionSpec as P

CHUNKS = 2
STRIP = 16
LANES = 128


def swap(value, axis, mask):
    count = lax.axis_size(axis)
    return lax.ppermute(value, axis, [(k, k ^ mask) for k in range(count)])


def masks_far_first(count):
    mask = count // 2
    while mask:
        yield mask
        mask //= 2


def pick(parts, place, axis=0):
    return lax.dynamic_index_in_dim(parts, place, axis, keepdims=False)


def padded(count):
    return -(-count // LANES) * LANES


VMEM = pl.BlockSpec(memory_space=pltpu.VMEM)
SMEM = pl.BlockSpec(memory_space=pltpu.SMEM)


def stats_kernel(heats, pieces, inverse_ref, *refs):
    *values, out_ref, column = refs
    column[...] = jnp.zeros_like(column)
    lane = lax.broadcasted_iota(jnp.int32, (STRIP, LANES), 1)
    chunks = len(values) * pieces
    part = values[0].shape[0] // pieces
    for chunk in range(chunks):
        x_ref, start = values[chunk // pieces], chunk % pieces * part
        base = chunk * padded(part)

        @pl.loop(0, part // STRIP)
        def _(strip):
            row = pl.multiple_of(strip * STRIP, STRIP)
            x = x_ref[pl.ds(start + row, STRIP), :].astype(jnp.float32)
            peak = jnp.max(x, axis=1, keepdims=True)
            x = x - peak
            record = jnp.where(lane == 0, peak, 0.0)
            for k in range(heats):
                total = jnp.sum(jnp.exp(x * inverse_ref[k]), axis=1, keepdims=True)
                record = jnp.where(lane == k + 1, total, record)
            column[pl.ds(base + row, STRIP), :] = record

    out_ref[...] = column[...].T[: out_ref.shape[0], :]


def local_stats(values, pieces, inverse):
    tokens, heats = values[0].shape[0] // pieces, inverse.shape[0]
    lanes = len(values) * pieces * padded(tokens)
    size = len(values) * values[0].size
    return pl.pallas_call(
        functools.partial(stats_kernel, heats, pieces),
        out_shape=jax.ShapeDtypeStruct((8, lanes), jnp.float32),
        in_specs=[SMEM] + [VMEM] * len(values),
        out_specs=VMEM,
        scratch_shapes=[pltpu.VMEM((lanes, LANES), jnp.float32)],
        compiler_params=pltpu.CompilerParams(vmem_limit_bytes=16 << 20),
        cost_estimate=pl.CostEstimate(flops=2 * heats * size, bytes_accessed=2 * size, transcendentals=heats * size),
        name="stats",
    )(inverse, *values)


def grad_kernel(heats, chunk, x_ref, teacher_ref, stats_ref, scalars_ref, out_ref, column):
    part, width = x_ref.shape
    column[...] = stats_ref[...].T
    lane = lax.broadcasted_iota(jnp.int32, (STRIP, width), 1).astype(jnp.float32)

    @pl.loop(0, part // STRIP)
    def _(strip):
        row = pl.multiple_of(strip * STRIP, STRIP)
        record = column[pl.ds(row, STRIP), :]
        x = x_ref[pl.ds(row, STRIP), :] - record[:, 0:1]
        t = teacher_ref[pl.ds(chunk * part + row, STRIP), :].astype(jnp.float32) - record[:, 8:9]
        result = jnp.exp(x) * (scalars_ref[1, 0] / record[:, 1:2])
        result = result - jnp.where(lane == record[:, 15:16], scalars_ref[1, 0], 0.0)
        for k in range(1, heats + 1):
            scale, factor = scalars_ref[0, k], scalars_ref[1, k]
            result = result + jnp.exp(x * scale) * (factor / record[:, k + 1 : k + 2])
            result = result - jnp.exp(t * scale) * (factor / record[:, k + 8 : k + 9])
        out_ref[pl.ds(row, STRIP), :] = result.astype(out_ref.dtype)


def logit_grad(chunk, logits, teacher, stats, scalars):
    heats = scalars.shape[1] - 1
    return pl.pallas_call(
        functools.partial(grad_kernel, heats, chunk),
        out_shape=jax.ShapeDtypeStruct(logits.shape, jnp.bfloat16),
        in_specs=[VMEM, VMEM, VMEM, SMEM],
        out_specs=VMEM,
        scratch_shapes=[pltpu.VMEM((padded(logits.shape[0]), stats.shape[0]), jnp.float32)],
        compiler_params=pltpu.CompilerParams(vmem_limit_bytes=16 << 20),
        cost_estimate=pl.CostEstimate(
            flops=6 * heats * logits.size, bytes_accessed=8 * logits.size, transcendentals=2 * heats * logits.size
        ),
        name="grad",
    )(logits, teacher, stats, scalars)


def merge(mine, other, inverse):
    heats = inverse.shape[0]
    highest = jnp.maximum(mine[0:1], other[0:1])
    total = mine[1 : heats + 1] * jnp.exp((mine[0:1] - highest) * inverse) + other[1 : heats + 1] * jnp.exp(
        (other[0:1] - highest) * inverse
    )
    return jnp.concatenate([highest, total, mine[heats + 1 :]], axis=0)


def copy_kernel(rows, order_ref, in_ref, *refs):
    *out_refs, held, come, gone = refs
    inward, outward = [], []
    for side, out_ref in enumerate(out_refs):
        for k in range(out_ref.shape[0]):
            start = pl.multiple_of(order_ref[side, k] * rows, rows)
            slot = side * out_ref.shape[0] + k
            inward.append(pltpu.make_async_copy(in_ref.at[pl.ds(start, rows)], held.at[slot], come.at[slot]))
            outward.append(pltpu.make_async_copy(held.at[slot], out_ref.at[k], gone.at[slot]))
    for copy in inward:
        copy.start()
    for come_copy, gone_copy in zip(inward, outward):
        come_copy.wait()
        gone_copy.start()
    for copy in outward:
        copy.wait()


def row_blocks(array, order, rows):
    sides, count = order.shape
    block = jax.ShapeDtypeStruct((count, rows, array.shape[1]), array.dtype)
    hbm = pl.BlockSpec(memory_space=pltpu.HBM)
    return pl.pallas_call(
        functools.partial(copy_kernel, rows),
        out_shape=[block] * sides,
        in_specs=[SMEM, hbm],
        out_specs=[hbm] * sides,
        scratch_shapes=[
            pltpu.VMEM((sides * count, rows, array.shape[1]), array.dtype),
            pltpu.SemaphoreType.DMA((sides * count,)),
            pltpu.SemaphoreType.DMA((sides * count,)),
        ],
        compiler_params=pltpu.CompilerParams(vmem_limit_bytes=16 << 20),
        cost_estimate=pl.CostEstimate(flops=0, bytes_accessed=4 * array.size, transcendentals=0),
        name="row_blocks",
    )(order, array)


def shards(hidden_t, head, teacher, labels, temps, mix):
    count_dp, count_vocab = lax.axis_size("dp"), lax.axis_size("vocab")
    me_dp, me_vocab = lax.axis_index("dp"), lax.axis_index("vocab")
    rows = hidden_t.shape[0]
    tokens, width = teacher.shape
    part = tokens // CHUNKS
    heats = temps.shape[0]
    far = list(masks_far_first(count_vocab))
    near = far[::-1]
    dp_masks = list(masks_far_first(count_dp))

    own = hidden_t.T.reshape(count_dp, CHUNKS, part, rows).transpose(1, 0, 2, 3).reshape(-1, rows)

    inverse = 1.0 / temps
    weights = mix[1] * temps
    student_inverse = jnp.concatenate([jnp.ones((1,), jnp.float32), inverse])
    scalars = jnp.stack([student_inverse, jnp.concatenate([mix[:1], weights])])
    relative = jnp.arange(0, count_vocab, 2, dtype=jnp.int32)
    keep_order = me_vocab ^ relative
    send_order = me_vocab ^ (relative + 1)

    def partial_logits(gathered):
        partial = jnp.dot(gathered, head, preferred_element_type=jnp.float32)
        return partial.reshape(*[2] * len(dp_masks), part, width)

    def reduced(partial, masks):
        left = dp_masks
        for mask in masks:
            axis, bit = left.index(mask), (me_dp // mask) % 2
            other = swap(pick(partial, 1 - bit, axis).astype(jnp.float16), "dp", mask)
            partial = pick(partial, bit, axis) + other.astype(jnp.float32)
            left = [m for m in left if m != mask]
        return partial

    def merged(student, fixed):
        stats = jnp.concatenate([student, fixed])
        for mask in near:
            other = swap(stats, "vocab", mask)
            stats = jnp.concatenate(
                [
                    merge(stats[:8], other[:8], student_inverse[:, None]),
                    merge(stats[8:], other[8:], inverse[:, None]),
                ]
            )
        return stats

    def products(blocks, grad):
        return lax.dot_general(blocks, grad, (((2,), (1,)), ((), ())), preferred_element_type=jnp.float32)

    def folded(keep, send):
        keep = keep + send.astype(jnp.float32)
        rest = [keep[k][None] for k in range(keep.shape[0])]
        if len(rest) == 1:
            return keep, None
        return jnp.concatenate(rest[0::2]), jnp.concatenate(rest[1::2]).astype(jnp.bfloat16)

    have, cross = [], []
    for c in range(CHUNKS):
        block = own[c * count_dp * part : (c + 1) * count_dp * part][None]
        have.append({0: block})
        cross.append({1: swap(block, "vocab", 1)})
    own_stats = local_stats([teacher], CHUNKS, inverse)
    for step in range(len(far) - 1):
        arrived = []
        for c in range(CHUNKS):
            mask = far[:-1][step] if c % 2 else near[1:][step]
            keys = sorted(have[c])
            arrived.append((keys, mask, swap(jnp.concatenate([have[c][k] for k in keys]), "vocab", mask)))
        for c, (keys, mask, other) in enumerate(arrived):
            other_cross = swap(other, "vocab", 1)
            for place, k in enumerate(keys):
                have[c][k ^ mask] = other[place : place + 1]
                cross[c][k ^ mask ^ 1] = other_cross[place : place + 1]
        if step == 0:
            own_stats, have = lax.optimization_barrier((own_stats, have))
            head_send, head_keep = row_blocks(head, jnp.stack([send_order, keep_order]), rows)

    (head_send, head_keep), have, cross = lax.optimization_barrier(((head_send, head_keep), have, cross))
    gathered, partials = [], []
    for c in range(CHUNKS):
        found = have[c] | cross[c]
        found = jnp.concatenate([found[k] for k in range(count_vocab)])
        gathered.append(jnp.concatenate([pick(found, me_vocab ^ n) for n in range(count_vocab)], axis=1))
        partials.append(partial_logits(gathered[c]))
    logits = [
        reduced(partials[c], dp_masks if c % 2 else dp_masks[::-1]) for c in range(CHUNKS)
    ]
    place = (labels - me_vocab * width).astype(jnp.float32).reshape(CHUNKS, part)
    place = jnp.pad(place, ((0, 0), (0, padded(part) - part))).reshape(1, -1)
    stats = merged(local_stats(logits, 1, student_inverse), own_stats)
    stats = jnp.split(jnp.concatenate([stats[:15], place]), CHUNKS, axis=1)

    grads, arrived = [], []
    for c in range(CHUNKS):
        grad = logit_grad(c, logits[c], teacher, stats[c], scalars)
        if c + 1 < CHUNKS:
            grad, logits[c + 1] = lax.optimization_barrier((grad, logits[c + 1]))
        grads.append(grad)
        arrived.append([swap(grad, "dp", r) for r in range(1, count_dp)])

    all_grads, state = [], []
    for c in range(CHUNKS):
        if c + 1 < CHUNKS:
            grads[c + 1], arrived[c] = lax.optimization_barrier((grads[c + 1], arrived[c]))
            arrived[c + 1] = [swap(grads[c + 1], "dp", r) for r in range(1, count_dp)]
        found = jnp.stack([grads[c]] + arrived[c])
        grad_all = jnp.concatenate([pick(found, me_dp ^ n) for n in range(count_dp)])
        grad_all = lax.optimization_barrier(grad_all)
        all_grads.append(grad_all)
        crossed = swap(products(head_send, grad_all).astype(jnp.bfloat16), "vocab", 1)
        if c + 1 < CHUNKS:
            pass
        else:
            state[c - 1], crossed = lax.optimization_barrier((state[c - 1], crossed))
        state.append(folded(products(head_keep, grad_all), crossed))
        if c + 1 < CHUNKS:
            keep, send = state[c]
            state[c] = folded(keep, swap(send, "vocab", near[1]))
            arrived[c + 1], state[c] = lax.optimization_barrier((arrived[c + 1], state[c]))
    (state, all_grads) = lax.optimization_barrier((state, all_grads))
    head_grad = lax.dot_general(
        jnp.concatenate(gathered, axis=0),
        jnp.concatenate(all_grads, axis=0),
        (((0,), (0,)), ((), ())),
        preferred_element_type=jnp.float32,
    ).astype(jnp.bfloat16)
    for place, mask in enumerate(near[1:]):
        for c in range(CHUNKS):
            if place == 0 and c + 1 < CHUNKS:
                continue
            keep, send = state[c]
            state[c] = folded(keep, swap(send, "vocab", mask))
    hidden_parts = [keep[0] for keep, _ in state]
    hidden_grad = jnp.stack([p.reshape(rows, count_dp, part) for p in hidden_parts], axis=2)
    return (hidden_grad.reshape(rows, count_dp * tokens), head_grad)


def solution(mesh):
    placed = (P(("dp", "vocab"), None), P("dp", "vocab"), P("dp", "vocab"), P("dp"), P(), P())
    return jax.shard_map(
        shards,
        mesh=mesh,
        in_specs=placed,
        out_specs=(P(("dp", "vocab"), None), P("dp", "vocab")),
        check_vma=False,
    )
```

time: 276 us -> 153 us (0.55)
  waiting for transfers between devices: 178 us -> 76.3 us
  blocking collectives: 28.1 us -> 0 us
  starting transfers between devices: 0.34 us -> 26.3 us
  Pallas kernels: 0 us -> 14.4 us
  matrix products: 29.5 us -> 16.8 us
  between operations: 13.9 us -> 1.47 us
  other arithmetic: 11.9 us -> 4.86 us
    reduce_scatter x2 -> x0, waiting for transfers between devices: 101 us -> none  [the longest x1 52.6 us: shards(): lax.psum_scatter(lax.dot_general(head, grad_all, (((1,), (1,)), ((), ()))...]
    all_gather x2 -> x0, waiting for transfers between devices: 76.8 us -> none  [the longest x1 42.7 us: shards(): h_block = lax.all_gather(hidden_t, 'vocab', axis=0, tiled=True)]
    ppermute x0 -> x29, waiting for transfers between devices: none -> 76.3 us  [swap(): return lax.ppermute(value, axis, [(k, k ^ mask) for k in range(count)])]
    all_gather x2 -> x0, blocking collectives: 28.1 us -> none  [merged(): pieces = jax.tree.map(lambda part: lax.all_gather(part, axis), value)]
    ppermute x0 -> x29, starting transfers between devices: none -> 26.3 us  [swap(): return lax.ppermute(value, axis, [(k, k ^ mask) for k in range(count)])]
    pallas_call x0 -> x5, Pallas kernels: none -> 14.4 us  [the longest x2 6.41 us: local_stats(): pl.pallas_call(functools.partial(stats_kernel, heats, pieces), out_shape=...]
    dot_general x4 -> x7, matrix products: 29.5 us -> 16.8 us  [the longest x4 6.2 us: products(): lax.dot_general(blocks, grad, (((2,), (1,)), ((), ())), preferred_element...]
    div x2 -> x0, other arithmetic: 4.62 us -> none  [the longest x1 4.61 us: shards(): softmaxes = jnp.exp(stacked - highest[:, :, None]) / summed[:, :, None]]
  transfers between devices with their start and end apart: 4 -> 29, of which waited for: 4 -> 21; matrix products, arithmetic and copies ran while one was open for 6% -> 8% of each run, Pallas kernels for 0% -> 6%
where the time goes in v3:
time: 153 us
  waiting for transfers between devices  76.3 us (50%)
  starting transfers between devices  26.3 us (17%)
  matrix products  16.8 us (11%)
  Pallas kernels  14.4 us (9%)
  local copies, waits for them, and re-layouts  12.7 us (8%)
  other arithmetic  4.86 us (3%)
    ppermute x29, waiting for transfers between devices, swap(): return lax.ppermute(value, axis, [(k, k ^ mask) for k in range(count)])  76.3 us
    ppermute x29, starting transfers between devices, swap(): return lax.ppermute(value, axis, [(k, k ^ mask) for k in range(count)])  26.3 us
    unnamed x58, local copies, waits for them, and re-layouts  10.9 us
    pallas_call x2, Pallas kernels, local_stats(): pl.pallas_call(functools.partial(stats_kernel, heats, pieces), out_shape=...  6.41 us
    dot_general x4, matrix products, products(): lax.dot_general(blocks, grad, (((2,), (1,)), ((), ())), preferred_element...  6.2 us
    dot_general x1, matrix products, shards(): lax.dot_general(jnp.concatenate(gathered, axis=0), jnp.concatenate(all_gr...  6.18 us
    dot_general x2, matrix products, partial_logits(): partial = jnp.dot(gathered, head, preferred_element_type=jnp.float32)  4.43 us
    pallas_call x1, Pallas kernels, row_blocks(): pl.pallas_call(functools.partial(copy_kernel, rows), out_shape=[block] *...  4 us
  transfers between devices with their start and end apart: 29, of which 21 were waited for; matrix products, arithmetic and copies ran while one was open for 8% of the time, Pallas kernels for 6%

profile of v3, /device:TPU:0, one launch (start us, length us, event | category | flops | bytes accessed | tf_op | source)
XLA Modules:
  0.0 152.8 jit_solution(4646403609143483553)
XLA Ops:
  0.7 1.2 copy.9
  1.9 3.1 %collective-permute-start = (bf16[1,384,256]{2,1,0:T(8,128)(2,1)S(1)}, bf16[1,384,256]{2,1,0:T(8,128)(2,1)S(1)}, u32[]{:S(2)}, u32[]{:S(2)}) collective-permute-start(bf16[1,384,256]{2,1,0:T(8,128)(2,1)S(1)} %bitcast.138), channel_id=1, source_target_pairs={{0,2},{1,3},{2,0},{3,1},{4,6},{5,7},{6,4},{7,5},{8,10},{9,11},{10,... | collective-permute-start | bytes 589832 | tf_op jit(solution)/shard_map/ppermute | solution.py:17
  5.0 2.6 %collective-permute-start.1 = (bf16[1,384,256]{2,1,0:T(8,128)(2,1)S(1)}, bf16[1,384,256]{2,1,0:T(8,128)(2,1)S(1)}, u32[]{:S(2)}, u32[]{:S(2)}) collective-permute-start(bf16[1,384,256]{2,1,0:T(8,128)(2,1)S(1)} %bitcast.142), channel_id=1, source_target_pairs={{0,4},{1,5},{2,6},{3,7},{4,0},{5,1},{6,2},{7,3},{8,12},{9,13},{10,... | collective-permute-start | bytes 589832 | tf_op jit(solution)/shard_map/ppermute | solution.py:17
  7.6 0.6 fusion.37
  8.2 0.6 broadcast_multiply_fusion
  8.9 3.1 %stats.2 = f32[8,256]{1,0:T(8,128)S(1)} custom-call(f32[4]{0:T(128)S(1)} %get-tuple-element.151.inverse_ref, bf16[192,1280]{1,0:T(8,128)(2,1)S(1)} %copy-done.5), custom_call_target="tpu_custom_call" | custom-call | flops 1966080 | bytes 491520 | tf_op jit(solution)/shard_map/stats/pallas_call | solution.py:68
  12.0 2.0 %collective-permute-done = bf16[1,384,256]{2,1,0:T(8,128)(2,1)S(1)} collective-permute-done((bf16[1,384,256]{2,1,0:T(8,128)(2,1)S(1)}, bf16[1,384,256]{2,1,0:T(8,128)(2,1)S(1)}, u32[]{:S(2)}, u32[]{:S(2)}) %collective-permute-start) | collective-permute-done | bytes 196640 | tf_op jit(solution)/shard_map/ppermute | solution.py:17
  14.0 2.5 %collective-permute-done.1 = bf16[1,384,256]{2,1,0:T(8,128)(2,1)S(1)} collective-permute-done((bf16[1,384,256]{2,1,0:T(8,128)(2,1)S(1)}, bf16[1,384,256]{2,1,0:T(8,128)(2,1)S(1)}, u32[]{:S(2)}, u32[]{:S(2)}) %collective-permute-start.1) | collective-permute-done | bytes 196640 | tf_op jit(solution)/shard_map/ppermute | solution.py:17
  16.5 0.8 pad_maximum_fusion.7
  17.3 0.4 collective-permute-start.3
  17.8 0.8 pad_maximum_fusion.6
  18.6 2.6 %collective-permute-start.2 = (bf16[2,384,256]{2,1,0:T(8,128)(2,1)}, bf16[2,384,256]{2,1,0:T(8,128)(2,1)S(1)}, u32[]{:S(2)}, u32[]{:S(2)}) collective-permute-start(bf16[2,384,256]{2,1,0:T(8,128)(2,1)} %pad_maximum_fusion.6), channel_id=1, source_target_pairs={{0,4},{1,5},{2,6},{3,7},{4,0},{5,1},{6,2},{7,3},{8,12},{9,13},{10,... | collective-permute-start | bytes 1179656 | tf_op jit(solution)/shard_map/ppermute | solution.py:17
  21.2 0.5 collective-permute-start.7
  21.7 2.5 %copy-done = bf16[2048,1280]{1,0:T(8,128)(2,1)S(1)} copy-done((bf16[2048,1280]{1,0:T(8,128)(2,1)S(1)}, bf16[2048,1280]{1,0:T(8,128)(2,1)}, u32[]{:S(2)}) %copy-start) | copy-done | bytes 5242904
  24.2 4.0 %row_blocks.1 = (bf16[4,256,1280]{2,1,0:T(8,128)(2,1)S(1)}, bf16[4,256,1280]{2,1,0:T(8,128)(2,1)S(1)}) custom-call(s32[2,4]{1,0:T(2,128)S(1)} %pad_add_fusion.order_ref, bf16[2048,1280]{1,0:T(8,128)(2,1)S(1)} %copy-done), custom_call_target="tpu_custom_call" | custom-call | bytes 10485760 | tf_op jit(solution)/shard_map/row_blocks/pallas_call | solution.py:147
  28.2 1.5 copy-done.1
  29.6 1.5 copy-done.3
  31.2 1.3 collective-permute-done.3
  32.5 5.3 %collective-permute-done.2 = bf16[2,384,256]{2,1,0:T(8,128)(2,1)S(1)} collective-permute-done((bf16[2,384,256]{2,1,0:T(8,128)(2,1)}, bf16[2,384,256]{2,1,0:T(8,128)(2,1)S(1)}, u32[]{:S(2)}, u32[]{:S(2)}) %collective-permute-start.2) | collective-permute-done | bytes 393248 | tf_op jit(solution)/shard_map/ppermute | solution.py:17
  37.9 0.6 collective-permute-start.9
  38.5 1.0 collective-permute-done.6
  39.6 0.2 collective-permute-done.9
  39.8 0.9 constant_dynamic-update-slice_fusion.14
  41.2 2.2 %fusion.41 = f32[384,1280]{1,0:T(8,128)S(1)} fusion(bf16[384,2048]{1,0:T(8,128)(2,1)S(1)} %bitcast_dynamic-update-slice_fusion, bf16[2048,1280]{1,0:T(8,128)(2,1)S(1)} %bitcast.130), kind=kOutput, calls=%fused_computation.144 | convolution fusion | flops 2013265920 | bytes 8781824 | tf_op jit(solution)/shard_map/dot_general | solution.py:185
  43.5 1.6 %collective-permute-start.12 = (f16[2,96,1280]{2,1,0:T(8,128)(2,1)S(1)}, f16[2,96,1280]{2,1,0:T(8,128)(2,1)S(1)}, u32[]{:S(2)}, u32[]{:S(2)}) collective-permute-start(f16[2,96,1280]{2,1,0:T(8,128)(2,1)S(1)} %fusion.10), channel_id=1, source_target_pairs={{0,16},{8,24},{16,0},{24,8},{1,17},{9,25},{17,1},{25,9},{2,18},{10... | collective-permute-start | bytes 1474568 | tf_op jit(solution)/shard_map/ppermute | solution.py:17
  45.5 2.2 %fusion.40 = f32[384,1280]{1,0:T(8,128)S(1)} fusion(bf16[384,2048]{1,0:T(8,128)(2,1)S(1)} %bitcast_dynamic-update-slice_fusion.8, bf16[2048,1280]{1,0:T(8,128)(2,1)S(1)} %bitcast.130), kind=kOutput, calls=%fused_computation.143 | convolution fusion | flops 2013265920 | bytes 8781824 | tf_op jit(solution)/shard_map/dot_general | solution.py:185
  47.8 1.6 %collective-permute-start.10 = (f16[2,96,1280]{2,1,0:T(8,128)(2,1)S(1)}, f16[2,96,1280]{2,1,0:T(8,128)(2,1)S(1)}, u32[]{:S(2)}, u32[]{:S(2)}) collective-permute-start(f16[2,96,1280]{2,1,0:T(8,128)(2,1)S(1)} %fusion.11), channel_id=1, source_target_pairs={{0,8},{8,0},{16,24},{24,16},{1,9},{9,1},{17,25},{25,17},{2,10},{10... | collective-permute-start | bytes 1474568 | tf_op jit(solution)/shard_map/ppermute | solution.py:17
  49.3 7.5 %collective-permute-done.12 = f16[2,96,1280]{2,1,0:T(8,128)(2,1)S(1)} collective-permute-done((f16[2,96,1280]{2,1,0:T(8,128)(2,1)S(1)}, f16[2,96,1280]{2,1,0:T(8,128)(2,1)S(1)}, u32[]{:S(2)}, u32[]{:S(2)}) %collective-permute-start.12) | collective-permute-done | bytes 491552 | tf_op jit(solution)/shard_map/ppermute | solution.py:17
  57.0 1.6 %collective-permute-start.13 = (f16[96,1280]{1,0:T(8,128)(2,1)S(1)}, f16[96,1280]{1,0:T(8,128)(2,1)S(1)}, u32[]{:S(2)}, u32[]{:S(2)}) collective-permute-start(f16[96,1280]{1,0:T(8,128)(2,1)S(1)} %fusion.13), channel_id=1, source_target_pairs={{0,8},{8,0},{16,24},{24,16},{1,9},{9,1},{17,25},{25,17},{2,10},{10... | collective-permute-start | bytes 737288 | tf_op jit(solution)/shard_map/ppermute | solution.py:17
  58.5 3.4 %collective-permute-done.10 = f16[2,96,1280]{2,1,0:T(8,128)(2,1)S(1)} collective-permute-done((f16[2,96,1280]{2,1,0:T(8,128)(2,1)S(1)}, f16[2,96,1280]{2,1,0:T(8,128)(2,1)S(1)}, u32[]{:S(2)}, u32[]{:S(2)}) %collective-permute-start.10) | collective-permute-done | bytes 491552 | tf_op jit(solution)/shard_map/ppermute | solution.py:17
  62.1 0.3 collective-permute-start.11
  62.4 3.7 %collective-permute-done.13 = f16[96,1280]{1,0:T(8,128)(2,1)S(1)} collective-permute-done((f16[96,1280]{1,0:T(8,128)(2,1)S(1)}, f16[96,1280]{1,0:T(8,128)(2,1)S(1)}, u32[]{:S(2)}, u32[]{:S(2)}) %collective-permute-start.13) | collective-permute-done | bytes 245792 | tf_op jit(solution)/shard_map/ppermute | solution.py:17
  66.2 2.2 %collective-permute-done.11 = f16[96,1280]{1,0:T(8,128)(2,1)S(1)} collective-permute-done((f16[96,1280]{1,0:T(8,128)(2,1)S(1)}, f16[96,1280]{1,0:T(8,128)(2,1)S(1)}, u32[]{:S(2)}, u32[]{:S(2)}) %collective-permute-start.11) | collective-permute-done | bytes 245792 | tf_op jit(solution)/shard_map/ppermute | solution.py:17
  68.5 3.3 %stats.3 = f32[8,256]{1,0:T(8,128)S(1)} custom-call(f32[5]{0:T(128)S(1)} %get-tuple-element.147.inverse_ref, f32[96,1280]{1,0:T(8,128)S(1)} %bitcast_add_fusion.3.refs_0_.x_ref, f32[96,1280]{1,0:T(8,128)S(1)} %bitcast_add_fusion.2.refs_1_.x_ref), custom_call_target="tpu_custom_call" | custom-call | flops 2457600 | bytes 491520 | tf_op jit(solution)/shard_map/stats/pallas_call | solution.py:68
  71.9 1.1 collective-permute-done.14
  73.3 0.6 maximum_bitcast_fusion
  73.9 3.1 %collective-permute-done.15 = f32[16,256]{1,0:T(8,128)S(1)} collective-permute-done((f32[16,256]{1,0:T(8,128)S(1)}, f32[16,256]{1,0:T(8,128)S(1)}, u32[]{:S(2)}, u32[]{:S(2)}) %collective-permute-start.15) | collective-permute-done | bytes 16416 | tf_op jit(solution)/shard_map/ppermute | solution.py:17
  77.4 4.5 %collective-permute-done.16 = f32[16,256]{1,0:T(8,128)S(1)} collective-permute-done((f32[16,256]{1,0:T(8,128)S(1)}, f32[16,256]{1,0:T(8,128)S(1)}, u32[]{:S(2)}, u32[]{:S(2)}) %collective-permute-start.16) | collective-permute-done | bytes 16416 | tf_op jit(solution)/shard_map/ppermute | solution.py:17
  82.2 1.9 %grad.2 = bf16[96,1280]{1,0:T(8,128)(2,1)S(1)} custom-call(f32[96,1280]{1,0:T(8,128)S(1)} %bitcast_add_fusion.3.refs_0_.x_ref, bf16[192,1280]{1,0:T(8,128)(2,1)S(1)} %copy-done.5, f32[16,128]{1,0:T(8,128)S(1)} %get-tuple-element.133.stats_ref, f32[2,5]{1,0:T(2,128)S(1)} %pad_maximum_fusion.12.scalars_ref), custom_call_target="tpu_custom_call" | custom-call | flops 2949120 | bytes 983040 | tf_op jit(solution)/shard_map/grad/pallas_call | solution.py:102
  84.1 1.6 %collective-permute-start.17 = (bf16[96,1280]{1,0:T(8,128)(2,1)S(1)}, bf16[96,1280]{1,0:T(8,128)(2,1)S(1)}, u32[]{:S(2)}, u32[]{:S(2)}) collective-permute-start(bf16[96,1280]{1,0:T(8,128)(2,1)S(1)} %grad.2), channel_id=1, source_target_pairs={{0,8},{8,0},{16,24},{24,16},{1,9},{9,1},{17,25},{25,17},{2,10},{10... | collective-permute-start | bytes 737288 | tf_op jit(solution)/shard_map/ppermute | solution.py:17
  85.8 1.8 %collective-permute-start.19 = (bf16[96,1280]{1,0:T(8,128)(2,1)S(1)}, bf16[96,1280]{1,0:T(8,128)(2,1)S(1)}, u32[]{:S(2)}, u32[]{:S(2)}) collective-permute-start(bf16[96,1280]{1,0:T(8,128)(2,1)S(1)} %grad.2), channel_id=1, source_target_pairs={{0,24},{8,16},{16,8},{24,0},{1,25},{9,17},{17,9},{25,1},{2,26},{10... | collective-permute-start | bytes 737288 | tf_op jit(solution)/shard_map/ppermute | solution.py:17
  87.6 2.1 %grad.3 = bf16[96,1280]{1,0:T(8,128)(2,1)S(1)} custom-call(f32[96,1280]{1,0:T(8,128)S(1)} %bitcast_add_fusion.2.refs_1_.x_ref, bf16[192,1280]{1,0:T(8,128)(2,1)S(1)} %copy-done.5, f32[16,128]{1,0:T(8,128)S(1)} %get-tuple-element.132.stats_ref, f32[2,5]{1,0:T(2,128)S(1)} %pad_maximum_fusion.12.scalars_ref), custom_call_target="tpu_custom_call" | custom-call | flops 2949120 | bytes 983040 | tf_op jit(solution)/shard_map/grad/pallas_call | solution.py:102
  89.7 2.8 %collective-permute-done.17 = bf16[96,1280]{1,0:T(8,128)(2,1)S(1)} collective-permute-done((bf16[96,1280]{1,0:T(8,128)(2,1)S(1)}, bf16[96,1280]{1,0:T(8,128)(2,1)S(1)}, u32[]{:S(2)}, u32[]{:S(2)}) %collective-permute-start.17) | collective-permute-done | bytes 245792 | tf_op jit(solution)/shard_map/ppermute | solution.py:17
  92.5 3.9 %collective-permute-done.18 = bf16[96,1280]{1,0:T(8,128)(2,1)S(1)} collective-permute-done((bf16[96,1280]{1,0:T(8,128)(2,1)S(1)}, bf16[96,1280]{1,0:T(8,128)(2,1)S(1)}, u32[]{:S(2)}, u32[]{:S(2)}) %collective-permute-start.18) | collective-permute-done | bytes 245792 | tf_op jit(solution)/shard_map/ppermute | solution.py:17
  96.6 1.6 %copy-done.4 = bf16[4,256,1280]{2,1,0:T(8,128)(2,1)S(1)} copy-done((bf16[4,256,1280]{2,1,0:T(8,128)(2,1)S(1)}, bf16[4,256,1280]{2,1,0:T(8,128)(2,1)}, u32[]{:S(2)}) %copy-start.4) | copy-done | bytes 2621464
  98.2 1.5 %convolution_convert_fusion.2 = bf16[4,256,384]{2,1,0:T(8,128)(2,1)S(1)} fusion(bf16[4,256,1280]{2,1,0:T(8,128)(2,1)S(1)} %copy-done.4, bf16[384,1280]{1,0:T(8,128)(2,1)S(1)} %pad_maximum_fusion.1), kind=kOutput, calls=%fused_computation.10 | convolution fusion | flops 1007026176 | bytes 4390912 | tf_op jit(solution)/shard_map/dot_general | solution.py:210
  99.8 2.3 %collective-permute-done.23 = bf16[4,256,384]{2,1,0:T(8,128)(2,1)S(1)} collective-permute-done((bf16[4,256,384]{2,1,0:T(8,128)(2,1)S(1)}, bf16[4,256,384]{2,1,0:T(8,128)(2,1)S(1)}, u32[]{:S(2)}, u32[]{:S(2)}) %collective-permute-start.23) | collective-permute-done | bytes 786464 | tf_op jit(solution)/shard_map/ppermute | solution.py:17
  102.1 1.6 %fusion.38 = (bf16[4,256,384]{2,1,0:T(8,128)(2,1)S(1)}, f32[4,256,384]{2,1,0:T(8,128)S(1)}) fusion(bf16[4,256,384]{2,1,0:T(8,128)(2,1)S(1)} %collective-permute-done.23, bf16[4,256,1280]{2,1,0:T(8,128)(2,1)S(1)} %copy-done.2, bf16[384,1280]{1,0:T(8,128)(2,1)S(1)} %pad_maximum_fusion.1), kind=kOutput, calls=%fused_computation.141 | convolution fusion | flops 1007812608 | bytes 6750208 | tf_op jit(solution)/shard_map/dot_general | solution.py:210
  103.8 0.3 collective-permute-start.24
  104.1 0.5 collective-permute-start.20
  104.7 1.2 collective-permute-start.21
  105.9 1.7 %collective-permute-start.22 = (bf16[96,1280]{1,0:T(8,128)(2,1)S(1)}, bf16[96,1280]{1,0:T(8,128)(2,1)S(1)}, u32[]{:S(2)}, u32[]{:S(2)}) collective-permute-start(bf16[96,1280]{1,0:T(8,128)(2,1)S(1)} %grad.3), channel_id=1, source_target_pairs={{0,24},{8,16},{16,8},{24,0},{1,25},{9,17},{17,9},{25,1},{2,26},{10... | collective-permute-start | bytes 737288 | tf_op jit(solution)/shard_map/ppermute | solution.py:17
  107.7 7.3 %collective-permute-done.24 = bf16[2,256,384]{2,1,0:T(8,128)(2,1)S(1)} collective-permute-done((bf16[2,256,384]{2,1,0:T(8,128)(2,1)S(1)}, bf16[2,256,384]{2,1,0:T(8,128)(2,1)S(1)}, u32[]{:S(2)}, u32[]{:S(2)}) %collective-permute-start.24) | collective-permute-done | bytes 393248 | tf_op jit(solution)/shard_map/ppermute | solution.py:17
  115.1 2.3 %collective-permute-done.21 = bf16[96,1280]{1,0:T(8,128)(2,1)S(1)} collective-permute-done((bf16[96,1280]{1,0:T(8,128)(2,1)S(1)}, bf16[96,1280]{1,0:T(8,128)(2,1)S(1)}, u32[]{:S(2)}, u32[]{:S(2)}) %collective-permute-start.21) | collective-permute-done | bytes 245792 | tf_op jit(solution)/shard_map/ppermute | solution.py:17
  117.7 1.5 %convolution_convert_fusion.1 = bf16[4,256,384]{2,1,0:T(8,128)(2,1)S(1)} fusion(bf16[4,256,1280]{2,1,0:T(8,128)(2,1)S(1)} %copy-done.4, bf16[384,1280]{1,0:T(8,128)(2,1)S(1)} %pad_maximum_fusion.3), kind=kOutput, calls=%fused_computation.9 | convolution fusion | flops 1007026176 | bytes 4390912 | tf_op jit(solution)/shard_map/dot_general | solution.py:210
  119.4 2.3 %collective-permute-done.25 = bf16[4,256,384]{2,1,0:T(8,128)(2,1)S(1)} collective-permute-done((bf16[4,256,384]{2,1,0:T(8,128)(2,1)S(1)}, bf16[4,256,384]{2,1,0:T(8,128)(2,1)S(1)}, u32[]{:S(2)}, u32[]{:S(2)}) %collective-permute-start.25) | collective-permute-done | bytes 786464 | tf_op jit(solution)/shard_map/ppermute | solution.py:17
  121.6 1.6 %fusion.39 = (bf16[4,256,384]{2,1,0:T(8,128)(2,1)S(1)}, f32[4,256,384]{2,1,0:T(8,128)S(1)}) fusion(bf16[4,256,384]{2,1,0:T(8,128)(2,1)S(1)} %collective-permute-done.25, bf16[4,256,1280]{2,1,0:T(8,128)(2,1)S(1)} %copy-done.2, bf16[384,1280]{1,0:T(8,128)(2,1)S(1)} %pad_maximum_fusion.3), kind=kOutput, calls=%fused_computation.142 | convolution fusion | flops 1007812608 | bytes 6750208 | tf_op jit(solution)/shard_map/dot_general | solution.py:210
  123.4 1.6 %collective-permute-start.26 = (bf16[1,256,384]{2,1,0:T(8,128)(2,1)S(1)}, bf16[1,256,384]{2,1,0:T(8,128)(2,1)S(1)}, u32[]{:S(2)}, u32[]{:S(2)}) collective-permute-start(bf16[1,256,384]{2,1,0:T(8,128)(2,1)S(1)} %slice.286), channel_id=1, source_target_pairs={{0,4},{1,5},{2,6},{3,7},{4,0},{5,1},{6,2},{7,3},{8,12},{9,13},{10,... | collective-permute-start | bytes 589832 | tf_op jit(solution)/shard_map/ppermute | solution.py:17
  125.1 0.4 collective-permute-start.27
  125.5 6.2 %convolution_convert_fusion = bf16[2048,1280]{1,0:T(8,128)(2,1)} fusion(bf16[384,2048]{1,0:T(8,128)(2,1)S(1)} %copy-done.8, bf16[384,2048]{1,0:T(8,128)(2,1)S(1)} %bitcast_dynamic-update-slice_fusion.8, bf16[384,1280]{1,0:T(8,128)(2,1)S(1)} %pad_maximum_fusion.3, bf16[384,1280]{1,0:T(8,128)(2,1)S(1)} %pad_maximum_fusion.1), kind=kOutput, calls=%fused_computation | convolution fusion | flops 4039376896 | bytes 10354688 | tf_op jit(solution)/shard_map/dot_general | solution.py:283
  131.7 8.1 %collective-permute-done.27 = bf16[2,256,384]{2,1,0:T(8,128)(2,1)S(1)} collective-permute-done((bf16[2,256,384]{2,1,0:T(8,128)(2,1)S(1)}, bf16[2,256,384]{2,1,0:T(8,128)(2,1)S(1)}, u32[]{:S(2)}, u32[]{:S(2)}) %collective-permute-start.27) | collective-permute-done | bytes 393248 | tf_op jit(solution)/shard_map/ppermute | solution.py:17
  139.9 1.8 %collective-permute-start.28 = (bf16[1,256,384]{2,1,0:T(8,128)(2,1)S(1)}, bf16[1,256,384]{2,1,0:T(8,128)(2,1)S(1)}, u32[]{:S(2)}, u32[]{:S(2)}) collective-permute-start(bf16[1,256,384]{2,1,0:T(8,128)(2,1)S(1)} %slice.285), channel_id=1, source_target_pairs={{0,4},{1,5},{2,6},{3,7},{4,0},{5,1},{6,2},{7,3},{8,12},{9,13},{10,... | collective-permute-start | bytes 589832 | tf_op jit(solution)/shard_map/ppermute | solution.py:17
  141.9 9.4 %collective-permute-done.28 = bf16[1,256,384]{2,1,0:T(8,128)(2,1)S(1)} collective-permute-done((bf16[1,256,384]{2,1,0:T(8,128)(2,1)S(1)}, bf16[1,256,384]{2,1,0:T(8,128)(2,1)S(1)}, u32[]{:S(2)}, u32[]{:S(2)}) %collective-permute-start.28) | collective-permute-done | bytes 196640 | tf_op jit(solution)/shard_map/ppermute | solution.py:17
  151.6 1.1 copy.14
  (138 shorter events, 4.3 us)
Async XLA Ops:
  0.6 7.0 %copy-start.9 = (f32[2]{0:T(128)S(1)}, f32[2]{0:T(128)}, u32[]{:S(2)}) copy-start(f32[2]{0:T(128)} %param.11) | copy-start | bytes 28
  0.6 7.5 %copy-start.11 = (f32[4]{0:T(128)S(1)}, f32[4]{0:T(128)}, u32[]{:S(2)}) copy-start(f32[4]{0:T(128)} %param.10) | copy-start | bytes 52
  0.7 8.2 %copy-start.5 = (bf16[192,1280]{1,0:T(8,128)(2,1)S(1)}, bf16[192,1280]{1,0:T(8,128)(2,1)}, u32[]{:S(2)}) copy-start(bf16[192,1280]{1,0:T(8,128)(2,1)} %teacher_ref.3) | copy-start | bytes 1474564
  1.9 12.1 %collective-permute-start = (bf16[1,384,256]{2,1,0:T(8,128)(2,1)S(1)}, bf16[1,384,256]{2,1,0:T(8,128)(2,1)S(1)}, u32[]{:S(2)}, u32[]{:S(2)}) collective-permute-start(bf16[1,384,256]{2,1,0:T(8,128)(2,1)S(1)} %bitcast.138), channel_id=1, source_target_pairs={{0,2},{1,3},{2,0},{3,1},{4,6},{5,7},{6,4},{7,5},{8,10},{9,11},{10,... | collective-permute-start | bytes 589832 | tf_op jit(solution)/shard_map/ppermute | solution.py:17
  5.0 11.5 %collective-permute-start.1 = (bf16[1,384,256]{2,1,0:T(8,128)(2,1)S(1)}, bf16[1,384,256]{2,1,0:T(8,128)(2,1)S(1)}, u32[]{:S(2)}, u32[]{:S(2)}) collective-permute-start(bf16[1,384,256]{2,1,0:T(8,128)(2,1)S(1)} %bitcast.142), channel_id=1, source_target_pairs={{0,4},{1,5},{2,6},{3,7},{4,0},{5,1},{6,2},{7,3},{8,12},{9,13},{10,... | collective-permute-start | bytes 589832 | tf_op jit(solution)/shard_map/ppermute | solution.py:17
  17.3 15.2 %collective-permute-start.3 = (bf16[2,384,256]{2,1,0:T(8,128)(2,1)}, bf16[2,384,256]{2,1,0:T(8,128)(2,1)S(1)}, u32[]{:S(2)}, u32[]{:S(2)}) collective-permute-start(bf16[2,384,256]{2,1,0:T(8,128)(2,1)} %pad_maximum_fusion.7), channel_id=1, source_target_pairs={{0,2},{1,3},{2,0},{3,1},{4,6},{5,7},{6,4},{7,5},{8,10},{9,11},{10,... | collective-permute-start | bytes 1179656 | tf_op jit(solution)/shard_map/ppermute | solution.py:17
  18.6 19.2 %collective-permute-start.2 = (bf16[2,384,256]{2,1,0:T(8,128)(2,1)}, bf16[2,384,256]{2,1,0:T(8,128)(2,1)S(1)}, u32[]{:S(2)}, u32[]{:S(2)}) collective-permute-start(bf16[2,384,256]{2,1,0:T(8,128)(2,1)} %pad_maximum_fusion.6), channel_id=1, source_target_pairs={{0,4},{1,5},{2,6},{3,7},{4,0},{5,1},{6,2},{7,3},{8,12},{9,13},{10,... | collective-permute-start | bytes 1179656 | tf_op jit(solution)/shard_map/ppermute | solution.py:17
  21.2 18.4 %collective-permute-start.4 = (bf16[1,384,256]{2,1,0:T(8,128)(2,1)S(1)}, bf16[1,384,256]{2,1,0:T(8,128)(2,1)S(1)}, u32[]{:S(2)}, u32[]{:S(2)}) collective-permute-start(bf16[1,384,256]{2,1,0:T(8,128)(2,1)S(1)} %bitcast.140), channel_id=1, source_target_pairs={{0,1},{1,0},{2,3},{3,2},{4,5},{5,4},{6,7},{7,6},{8,9},{9,8},{10,11... | collective-permute-start | bytes 589832 | tf_op jit(solution)/shard_map/ppermute | solution.py:17
  21.2 18.4 %collective-permute-start.7 = (bf16[1,384,256]{2,1,0:T(8,128)(2,1)S(1)}, bf16[1,384,256]{2,1,0:T(8,128)(2,1)}, u32[]{:S(2)}, u32[]{:S(2)}) collective-permute-start(bf16[1,384,256]{2,1,0:T(8,128)(2,1)S(1)} %bitcast.144), channel_id=1, source_target_pairs={{0,1},{1,0},{2,3},{3,2},{4,5},{5,4},{6,7},{7,6},{8,9},{9,8},{10,11... | collective-permute-start | bytes 589832 | tf_op jit(solution)/shard_map/ppermute | solution.py:17
  21.7 2.5 %copy-start = (bf16[2048,1280]{1,0:T(8,128)(2,1)S(1)}, bf16[2048,1280]{1,0:T(8,128)(2,1)}, u32[]{:S(2)}) copy-start(bf16[2048,1280]{1,0:T(8,128)(2,1)} %in_ref.1) | copy-start | bytes 15728644
  24.2 17.0 %slice-start = ((s8[5242880]{0:T(1024)(128)(4,1)}), s8[1048576]{0:T(1024)(128)(4,1)S(1)}, s32[]{:S(2)}) async-start(s8[5242880]{0:T(1024)(128)(4,1)} %bitcast.129), calls=%async_computation | async-start | bytes 2097152
  28.2 1.5 copy-start.1
  29.6 1.5 copy-start.3
  31.2 8.4 %collective-permute-start.5 = (bf16[1,384,256]{2,1,0:T(8,128)(2,1)S(1)}, bf16[1,384,256]{2,1,0:T(8,128)(2,1)S(1)}, u32[]{:S(2)}, u32[]{:S(2)}) collective-permute-start(bf16[1,384,256]{2,1,0:T(8,128)(2,1)S(1)} %collective-permute-done), channel_id=1, source_target_pairs={{0,1},{1,0},{2,3},{3,2},{4,5},{5,4},{6,7},{7,6},{8,9},{9,8},{10,11... | collective-permute-start | bytes 589832 | tf_op jit(solution)/shard_map/ppermute | solution.py:17
  32.5 5.3 %collective-permute-start.8 = (bf16[2,384,256]{2,1,0:T(8,128)(2,1)S(1)}, bf16[2,384,256]{2,1,0:T(8,128)(2,1)S(1)}, u32[]{:S(2)}, u32[]{:S(2)}) collective-permute-start(bf16[2,384,256]{2,1,0:T(8,128)(2,1)S(1)} %collective-permute-done.3), channel_id=1, source_target_pairs={{0,1},{1,0},{2,3},{3,2},{4,5},{5,4},{6,7},{7,6},{8,9},{9,8},{10,11... | collective-permute-start | bytes 1179656 | tf_op jit(solution)/shard_map/ppermute | solution.py:17
  37.8 1.7 %collective-permute-start.6 = (bf16[2,384,256]{2,1,0:T(8,128)(2,1)S(1)}, bf16[2,384,256]{2,1,0:T(8,128)(2,1)S(1)}, u32[]{:S(2)}, u32[]{:S(2)}) collective-permute-start(bf16[2,384,256]{2,1,0:T(8,128)(2,1)S(1)} %collective-permute-done.2), channel_id=1, source_target_pairs={{0,1},{1,0},{2,3},{3,2},{4,5},{5,4},{6,7},{7,6},{8,9},{9,8},{10,11... | collective-permute-start | bytes 1179656 | tf_op jit(solution)/shard_map/ppermute | solution.py:17
  37.9 3.3 %slice-start.1 = ((s8[5242880]{0:T(1024)(128)(4,1)}), s8[4194304]{0:T(1024)(128)(4,1)S(1)}, s32[]{:S(2)}) async-start(s8[5242880]{0:T(1024)(128)(4,1)} %bitcast.129), calls=%async_computation.1 | async-start | bytes 8388608
  37.9 1.9 %collective-permute-start.9 = (bf16[1,384,256]{2,1,0:T(8,128)(2,1)S(1)}, bf16[1,384,256]{2,1,0:T(8,128)(2,1)S(1)}, u32[]{:S(2)}, u32[]{:S(2)}) collective-permute-start(bf16[1,384,256]{2,1,0:T(8,128)(2,1)S(1)} %collective-permute-done.1), channel_id=1, source_target_pairs={{0,1},{1,0},{2,3},{3,2},{4,5},{5,4},{6,7},{7,6},{8,9},{9,8},{10,11... | collective-permute-start | bytes 589832 | tf_op jit(solution)/shard_map/ppermute | solution.py:17
  41.2 2.2 %copy-start.7 = (bf16[384,2048]{1,0:T(8,128)(2,1)}, bf16[384,2048]{1,0:T(8,128)(2,1)S(1)}, u32[]{:S(2)}) copy-start(bf16[384,2048]{1,0:T(8,128)(2,1)S(1)} %bitcast_dynamic-update-slice_fusion) | copy-start | bytes 4718596
  43.5 13.3 %collective-permute-start.12 = (f16[2,96,1280]{2,1,0:T(8,128)(2,1)S(1)}, f16[2,96,1280]{2,1,0:T(8,128)(2,1)S(1)}, u32[]{:S(2)}, u32[]{:S(2)}) collective-permute-start(f16[2,96,1280]{2,1,0:T(8,128)(2,1)S(1)} %fusion.10), channel_id=1, source_target_pairs={{0,16},{8,24},{16,0},{24,8},{1,17},{9,25},{17,1},{25,9},{2,18},{10... | collective-permute-start | bytes 1474568 | tf_op jit(solution)/shard_map/ppermute | solution.py:17
  47.8 14.2 %collective-permute-start.10 = (f16[2,96,1280]{2,1,0:T(8,128)(2,1)S(1)}, f16[2,96,1280]{2,1,0:T(8,128)(2,1)S(1)}, u32[]{:S(2)}, u32[]{:S(2)}) collective-permute-start(f16[2,96,1280]{2,1,0:T(8,128)(2,1)S(1)} %fusion.11), channel_id=1, source_target_pairs={{0,8},{8,0},{16,24},{24,16},{1,9},{9,1},{17,25},{25,17},{2,10},{10... | collective-permute-start | bytes 1474568 | tf_op jit(solution)/shard_map/ppermute | solution.py:17
  57.0 9.1 %collective-permute-start.13 = (f16[96,1280]{1,0:T(8,128)(2,1)S(1)}, f16[96,1280]{1,0:T(8,128)(2,1)S(1)}, u32[]{:S(2)}, u32[]{:S(2)}) collective-permute-start(f16[96,1280]{1,0:T(8,128)(2,1)S(1)} %fusion.13), channel_id=1, source_target_pairs={{0,8},{8,0},{16,24},{24,16},{1,9},{9,1},{17,25},{25,17},{2,10},{10... | collective-permute-start | bytes 737288 | tf_op jit(solution)/shard_map/ppermute | solution.py:17
  62.1 6.3 %collective-permute-start.11 = (f16[96,1280]{1,0:T(8,128)(2,1)S(1)}, f16[96,1280]{1,0:T(8,128)(2,1)S(1)}, u32[]{:S(2)}, u32[]{:S(2)}) collective-permute-start(f16[96,1280]{1,0:T(8,128)(2,1)S(1)} %fusion.12), channel_id=1, source_target_pairs={{0,16},{8,24},{16,0},{24,8},{1,17},{9,25},{17,1},{25,9},{2,18},{10... | collective-permute-start | bytes 737288 | tf_op jit(solution)/shard_map/ppermute | solution.py:17
  66.2 5.7 %copy-start.10 = (s32[192]{0:T(256)S(1)}, s32[192]{0:T(256)}, u32[]{:S(2)}) copy-start(s32[192]{0:T(256)} %param.9) | copy-start | bytes 2308
  71.8 1.2 collective-permute-start.14
  73.2 3.8 %collective-permute-start.15 = (f32[16,256]{1,0:T(8,128)S(1)}, f32[16,256]{1,0:T(8,128)S(1)}, u32[]{:S(2)}, u32[]{:S(2)}) collective-permute-start(f32[16,256]{1,0:T(8,128)S(1)} %concatenate.73), channel_id=1, source_target_pairs={{0,2},{1,3},{2,0},{3,1},{4,6},{5,7},{6,4},{7,5},{8,10},{9,11},{10,... | collective-permute-start | bytes 49160 | tf_op jit(solution)/shard_map/ppermute | solution.py:17
  77.2 4.7 %collective-permute-start.16 = (f32[16,256]{1,0:T(8,128)S(1)}, f32[16,256]{1,0:T(8,128)S(1)}, u32[]{:S(2)}, u32[]{:S(2)}) collective-permute-start(f32[16,256]{1,0:T(8,128)S(1)} %concatenate.74), channel_id=1, source_target_pairs={{0,4},{1,5},{2,6},{3,7},{4,0},{5,1},{6,2},{7,3},{8,12},{9,13},{10,... | collective-permute-start | bytes 49160 | tf_op jit(solution)/shard_map/ppermute | solution.py:17
  84.1 8.4 %collective-permute-start.17 = (bf16[96,1280]{1,0:T(8,128)(2,1)S(1)}, bf16[96,1280]{1,0:T(8,128)(2,1)S(1)}, u32[]{:S(2)}, u32[]{:S(2)}) collective-permute-start(bf16[96,1280]{1,0:T(8,128)(2,1)S(1)} %grad.2), channel_id=1, source_target_pairs={{0,8},{8,0},{16,24},{24,16},{1,9},{9,1},{17,25},{25,17},{2,10},{10... | collective-permute-start | bytes 737288 | tf_op jit(solution)/shard_map/ppermute | solution.py:17
  85.6 10.7 %collective-permute-start.18 = (bf16[96,1280]{1,0:T(8,128)(2,1)S(1)}, bf16[96,1280]{1,0:T(8,128)(2,1)S(1)}, u32[]{:S(2)}, u32[]{:S(2)}) collective-permute-start(bf16[96,1280]{1,0:T(8,128)(2,1)S(1)} %grad.2), channel_id=1, source_target_pairs={{0,16},{8,24},{16,0},{24,8},{1,17},{9,25},{17,1},{25,9},{2,18},{10... | collective-permute-start | bytes 737288 | tf_op jit(solution)/shard_map/ppermute | solution.py:17
  85.8 10.5 %collective-permute-start.19 = (bf16[96,1280]{1,0:T(8,128)(2,1)S(1)}, bf16[96,1280]{1,0:T(8,128)(2,1)S(1)}, u32[]{:S(2)}, u32[]{:S(2)}) collective-permute-start(bf16[96,1280]{1,0:T(8,128)(2,1)S(1)} %grad.2), channel_id=1, source_target_pairs={{0,24},{8,16},{16,8},{24,0},{1,25},{9,17},{17,9},{25,1},{2,26},{10... | collective-permute-start | bytes 737288 | tf_op jit(solution)/shard_map/ppermute | solution.py:17
  96.5 1.7 %copy-start.4 = (bf16[4,256,1280]{2,1,0:T(8,128)(2,1)S(1)}, bf16[4,256,1280]{2,1,0:T(8,128)(2,1)}, u32[]{:S(2)}) copy-start(bf16[4,256,1280]{2,1,0:T(8,128)(2,1)} %copy-done.3) | copy-start | bytes 7864324
  98.2 3.9 %copy-start.2 = (bf16[4,256,1280]{2,1,0:T(8,128)(2,1)S(1)}, bf16[4,256,1280]{2,1,0:T(8,128)(2,1)}, u32[]{:S(2)}) copy-start(bf16[4,256,1280]{2,1,0:T(8,128)(2,1)} %copy-done.1) | copy-start | bytes 7864324
  99.8 2.4 %collective-permute-start.23 = (bf16[4,256,384]{2,1,0:T(8,128)(2,1)S(1)}, bf16[4,256,384]{2,1,0:T(8,128)(2,1)S(1)}, u32[]{:S(2)}, u32[]{:S(2)}) collective-permute-start(bf16[4,256,384]{2,1,0:T(8,128)(2,1)S(1)} %convolution_convert_fusion.2), channel_id=1, source_target_pairs={{0,1},{1,0},{2,3},{3,2},{4,5},{5,4},{6,7},{7,6},{8,9},{9,8},{10,11... | collective-permute-start | bytes 2359304 | tf_op jit(solution)/shard_map/ppermute | solution.py:17
  103.8 11.2 %collective-permute-start.24 = (bf16[2,256,384]{2,1,0:T(8,128)(2,1)S(1)}, bf16[2,256,384]{2,1,0:T(8,128)(2,1)S(1)}, u32[]{:S(2)}, u32[]{:S(2)}) collective-permute-start(bf16[2,256,384]{2,1,0:T(8,128)(2,1)S(1)} %pad_maximum_fusion.8), channel_id=1, source_target_pairs={{0,2},{1,3},{2,0},{3,1},{4,6},{5,7},{6,4},{7,5},{8,10},{9,11},{10,... | collective-permute-start | bytes 1179656 | tf_op jit(solution)/shard_map/ppermute | solution.py:17
  104.1 11.0 %collective-permute-start.20 = (bf16[96,1280]{1,0:T(8,128)(2,1)S(1)}, bf16[96,1280]{1,0:T(8,128)(2,1)S(1)}, u32[]{:S(2)}, u32[]{:S(2)}) collective-permute-start(bf16[96,1280]{1,0:T(8,128)(2,1)S(1)} %grad.3), channel_id=1, source_target_pairs={{0,8},{8,0},{16,24},{24,16},{1,9},{9,1},{17,25},{25,17},{2,10},{10... | collective-permute-start | bytes 737288 | tf_op jit(solution)/shard_map/ppermute | solution.py:17
  104.7 12.8 %collective-permute-start.21 = (bf16[96,1280]{1,0:T(8,128)(2,1)S(1)}, bf16[96,1280]{1,0:T(8,128)(2,1)S(1)}, u32[]{:S(2)}, u32[]{:S(2)}) collective-permute-start(bf16[96,1280]{1,0:T(8,128)(2,1)S(1)} %grad.3), channel_id=1, source_target_pairs={{0,16},{8,24},{16,0},{24,8},{1,17},{9,25},{17,1},{25,9},{2,18},{10... | collective-permute-start | bytes 737288 | tf_op jit(solution)/shard_map/ppermute | solution.py:17
  105.9 11.6 %collective-permute-start.22 = (bf16[96,1280]{1,0:T(8,128)(2,1)S(1)}, bf16[96,1280]{1,0:T(8,128)(2,1)S(1)}, u32[]{:S(2)}, u32[]{:S(2)}) collective-permute-start(bf16[96,1280]{1,0:T(8,128)(2,1)S(1)} %grad.3), channel_id=1, source_target_pairs={{0,24},{8,16},{16,8},{24,0},{1,25},{9,17},{17,9},{25,1},{2,26},{10... | collective-permute-start | bytes 737288 | tf_op jit(solution)/shard_map/ppermute | solution.py:17
  115.1 2.5 %copy-start.6 = (f32[2,256,384]{2,1,0:T(8,128)}, f32[2,256,384]{2,1,0:T(8,128)S(1)}, u32[]{:S(2)}) copy-start(f32[2,256,384]{2,1,0:T(8,128)S(1)} %maximum_add_fusion) | copy-start | bytes 2359300
  119.3 2.4 %collective-permute-start.25 = (bf16[4,256,384]{2,1,0:T(8,128)(2,1)S(1)}, bf16[4,256,384]{2,1,0:T(8,128)(2,1)S(1)}, u32[]{:S(2)}, u32[]{:S(2)}) collective-permute-start(bf16[4,256,384]{2,1,0:T(8,128)(2,1)S(1)} %convolution_convert_fusion.1), channel_id=1, source_target_pairs={{0,1},{1,0},{2,3},{3,2},{4,5},{5,4},{6,7},{7,6},{8,9},{9,8},{10,11... | collective-permute-start | bytes 2359304 | tf_op jit(solution)/shard_map/ppermute | solution.py:17
  123.3 2.1 %copy-start.8 = (bf16[384,2048]{1,0:T(8,128)(2,1)S(1)}, bf16[384,2048]{1,0:T(8,128)(2,1)}, u32[]{:S(2)}) copy-start(bf16[384,2048]{1,0:T(8,128)(2,1)} %copy-done.7) | copy-start | bytes 4718596
  123.4 18.2 %collective-permute-start.26 = (bf16[1,256,384]{2,1,0:T(8,128)(2,1)S(1)}, bf16[1,256,384]{2,1,0:T(8,128)(2,1)S(1)}, u32[]{:S(2)}, u32[]{:S(2)}) collective-permute-start(bf16[1,256,384]{2,1,0:T(8,128)(2,1)S(1)} %slice.286), channel_id=1, source_target_pairs={{0,4},{1,5},{2,6},{3,7},{4,0},{5,1},{6,2},{7,3},{8,12},{9,13},{10,... | collective-permute-start | bytes 589832 | tf_op jit(solution)/shard_map/ppermute | solution.py:17
  125.1 14.7 %collective-permute-start.27 = (bf16[2,256,384]{2,1,0:T(8,128)(2,1)S(1)}, bf16[2,256,384]{2,1,0:T(8,128)(2,1)S(1)}, u32[]{:S(2)}, u32[]{:S(2)}) collective-permute-start(bf16[2,256,384]{2,1,0:T(8,128)(2,1)S(1)} %pad_maximum_fusion.9), channel_id=1, source_target_pairs={{0,2},{1,3},{2,0},{3,1},{4,6},{5,7},{6,4},{7,5},{8,10},{9,11},{10,... | collective-permute-start | bytes 1179656 | tf_op jit(solution)/shard_map/ppermute | solution.py:17
  131.7 10.0 %slice-start.2 = ((f32[2,256,384]{2,1,0:T(8,128)}), f32[1,256,384]{2,1,0:T(8,128)S(1)}, s32[]{:S(2)}) async-start(f32[2,256,384]{2,1,0:T(8,128)} %copy-done.6), calls=%async_computation.2 | async-start | bytes 786432 | tf_op jit(solution)/shard_map/slice | solution.py:214
  139.9 11.4 %collective-permute-start.28 = (bf16[1,256,384]{2,1,0:T(8,128)(2,1)S(1)}, bf16[1,256,384]{2,1,0:T(8,128)(2,1)S(1)}, u32[]{:S(2)}, u32[]{:S(2)}) collective-permute-start(bf16[1,256,384]{2,1,0:T(8,128)(2,1)S(1)} %slice.285), channel_id=1, source_target_pairs={{0,4},{1,5},{2,6},{3,7},{4,0},{5,1},{6,2},{7,3},{8,12},{9,13},{10,... | collective-permute-start | bytes 589832 | tf_op jit(solution)/shard_map/ppermute | solution.py:17

commit v4 on v3

--- a/solution.py
+++ b/solution.py
@@ -8,8 +8,10 @@
 from jax.sharding import PartitionSpec as P
 
 CHUNKS = 2
-STRIP = 16
+FIRST = 64
+STRIP = 32
 LANES = 128
+LOG2E = 1.4426950408889634
 
 
 def swap(value, axis, mask):
@@ -54,7 +56,7 @@
             x = x - peak
             record = jnp.where(lane == 0, peak, 0.0)
             for k in range(heats):
-                total = jnp.sum(jnp.exp(x * inverse_ref[k]), axis=1, keepdims=True)
+                total = jnp.sum(jnp.exp2(x * inverse_ref[k]), axis=1, keepdims=True)
                 record = jnp.where(lane == k + 1, total, record)
             column[pl.ds(base + row, STRIP), :] = record
 
@@ -71,52 +73,67 @@
         in_specs=[SMEM] + [VMEM] * len(values),
         out_specs=VMEM,
         scratch_shapes=[pltpu.VMEM((lanes, LANES), jnp.float32)],
-        compiler_params=pltpu.CompilerParams(vmem_limit_bytes=16 << 20),
+        compiler_params=pltpu.CompilerParams(vmem_limit_bytes=4 << 20),
         cost_estimate=pl.CostEstimate(flops=2 * heats * size, bytes_accessed=2 * size, transcendentals=heats * size),
         name="stats",
     )(inverse, *values)
 
 
-def grad_kernel(heats, chunk, x_ref, teacher_ref, stats_ref, scalars_ref, out_ref, column):
-    part, width = x_ref.shape
-    column[...] = stats_ref[...].T
+def grad_kernel(heats, pieces, scalars_ref, teacher_ref, *refs):
+    values, stats, (out_ref, column) = refs[: len(pieces)], refs[len(pieces) : -2], refs[-2:]
+    width = teacher_ref.shape[1]
     lane = lax.broadcasted_iota(jnp.int32, (STRIP, width), 1).astype(jnp.float32)
-
-    @pl.loop(0, part // STRIP)
-    def _(strip):
-        row = pl.multiple_of(strip * STRIP, STRIP)
-        record = column[pl.ds(row, STRIP), :]
-        x = x_ref[pl.ds(row, STRIP), :] - record[:, 0:1]
-        t = teacher_ref[pl.ds(chunk * part + row, STRIP), :].astype(jnp.float32) - record[:, 8:9]
-        result = jnp.exp(x) * (scalars_ref[1, 0] / record[:, 1:2])
-        result = result - jnp.where(lane == record[:, 15:16], scalars_ref[1, 0], 0.0)
-        for k in range(1, heats + 1):
-            scale, factor = scalars_ref[0, k], scalars_ref[1, k]
-            result = result + jnp.exp(x * scale) * (factor / record[:, k + 1 : k + 2])
-            result = result - jnp.exp(t * scale) * (factor / record[:, k + 8 : k + 9])
-        out_ref[pl.ds(row, STRIP), :] = result.astype(out_ref.dtype)
-
-
-def logit_grad(chunk, logits, teacher, stats, scalars):
+    done = 0
+    for x_ref, stats_ref, (start, token, count) in zip(values, stats, pieces):
+        column[...] = stats_ref[...].T
+        base = done
+
+        @pl.loop(0, count // STRIP)
+        def _(strip):
+            row = pl.multiple_of(strip * STRIP, STRIP)
+            record = column[pl.ds(start + row, STRIP), :]
+            x = x_ref[pl.ds(start + row, STRIP), :] - record[:, 0:1]
+            t = teacher_ref[pl.ds(token + row, STRIP), :].astype(jnp.float32) - record[:, 8:9]
+            result = jnp.exp2(x * scalars_ref[0, 0]) * (scalars_ref[1, 0] / record[:, 1:2])
+            result = result - jnp.where(lane == record[:, 15:16], scalars_ref[1, 0], 0.0)
+            for k in range(1, heats + 1):
+                scale, factor = scalars_ref[0, k], scalars_ref[1, k]
+                result = result + jnp.exp2(x * scale) * (factor / record[:, k + 1 : k + 2])
+                result = result - jnp.exp2(t * scale) * (factor / record[:, k + 8 : k + 9])
+            out_ref[pl.ds(base + row, STRIP), :] = result.astype(out_ref.dtype)
+
+        done += count
+
+
+def logit_grad(first, last, logits, teacher, stats, scalars):
     heats = scalars.shape[1] - 1
+    part, width = logits[0].shape
+    pieces, values, records = [], [], []
+    for c in range(len(logits)):
+        low, high = max(first, c * part), min(last, (c + 1) * part)
+        if low < high:
+            pieces.append((low - c * part, low, high - low))
+            values.append(logits[c])
+            records.append(stats[c])
+    size = (last - first) * width
     return pl.pallas_call(
-        functools.partial(grad_kernel, heats, chunk),
-        out_shape=jax.ShapeDtypeStruct(logits.shape, jnp.bfloat16),
-        in_specs=[VMEM, VMEM, VMEM, SMEM],
+        functools.partial(grad_kernel, heats, pieces),
+        out_shape=jax.ShapeDtypeStruct((last - first, width), jnp.bfloat16),
+        in_specs=[SMEM] + [VMEM] * (1 + 2 * len(pieces)),
         out_specs=VMEM,
-        scratch_shapes=[pltpu.VMEM((padded(logits.shape[0]), stats.shape[0]), jnp.float32)],
-        compiler_params=pltpu.CompilerParams(vmem_limit_bytes=16 << 20),
+        scratch_shapes=[pltpu.VMEM((padded(part), stats[0].shape[0]), jnp.float32)],
+        compiler_params=pltpu.CompilerParams(vmem_limit_bytes=4 << 20),
         cost_estimate=pl.CostEstimate(
-            flops=6 * heats * logits.size, bytes_accessed=8 * logits.size, transcendentals=2 * heats * logits.size
+            flops=6 * heats * size, bytes_accessed=8 * size, transcendentals=2 * heats * size
         ),
         name="grad",
-    )(logits, teacher, stats, scalars)
+    )(scalars, teacher, *values, *records)
 
 
 def merge(mine, other, inverse):
     heats = inverse.shape[0]
     highest = jnp.maximum(mine[0:1], other[0:1])
-    total = mine[1 : heats + 1] * jnp.exp((mine[0:1] - highest) * inverse) + other[1 : heats + 1] * jnp.exp(
+    total = mine[1 : heats + 1] * jnp.exp2((mine[0:1] - highest) * inverse) + other[1 : heats + 1] * jnp.exp2(
         (other[0:1] - highest) * inverse
     )
     return jnp.concatenate([highest, total, mine[heats + 1 :]], axis=0)
@@ -154,7 +171,7 @@
             pltpu.SemaphoreType.DMA((sides * count,)),
             pltpu.SemaphoreType.DMA((sides * count,)),
         ],
-        compiler_params=pltpu.CompilerParams(vmem_limit_bytes=16 << 20),
+        compiler_params=pltpu.CompilerParams(vmem_limit_bytes=8 << 20),
         cost_estimate=pl.CostEstimate(flops=0, bytes_accessed=4 * array.size, transcendentals=0),
         name="row_blocks",
     )(order, array)
@@ -173,9 +190,9 @@
 
     own = hidden_t.T.reshape(count_dp, CHUNKS, part, rows).transpose(1, 0, 2, 3).reshape(-1, rows)
 
-    inverse = 1.0 / temps
+    inverse = LOG2E / temps
     weights = mix[1] * temps
-    student_inverse = jnp.concatenate([jnp.ones((1,), jnp.float32), inverse])
+    student_inverse = jnp.concatenate([jnp.full((1,), LOG2E, jnp.float32), inverse])
     scalars = jnp.stack([student_inverse, jnp.concatenate([mix[:1], weights])])
     relative = jnp.arange(0, count_vocab, 2, dtype=jnp.int32)
     keep_order = me_vocab ^ relative
@@ -209,12 +226,16 @@
     def products(blocks, grad):
         return lax.dot_general(blocks, grad, (((2,), (1,)), ((), ())), preferred_element_type=jnp.float32)
 
-    def folded(keep, send):
-        keep = keep + send.astype(jnp.float32)
-        rest = [keep[k][None] for k in range(keep.shape[0])]
-        if len(rest) == 1:
-            return keep, None
-        return jnp.concatenate(rest[0::2]), jnp.concatenate(rest[1::2]).astype(jnp.bfloat16)
+    def folded(blocks, mask):
+        sent = [k for k in sorted(blocks) if k & mask]
+        other = swap(jnp.stack([blocks[k].astype(jnp.bfloat16) for k in sent]), "vocab", mask)
+        return {k ^ mask: blocks[k ^ mask] + other[n].astype(jnp.float32) for n, k in enumerate(sent)}
+
+    def split(blocks):
+        return [{k: blocks[k][: rows // 2] for k in blocks}, {k: blocks[k][rows // 2 :] for k in blocks}]
+
+    def both(sides, masks):
+        return [folded(side, mask) for side, mask in zip(sides, masks)]
 
     have, cross = [], []
     for c in range(CHUNKS):
@@ -252,48 +273,49 @@
     stats = merged(local_stats(logits, 1, student_inverse), own_stats)
     stats = jnp.split(jnp.concatenate([stats[:15], place]), CHUNKS, axis=1)
 
+    cuts = [0, FIRST, tokens]
     grads, arrived = [], []
-    for c in range(CHUNKS):
-        grad = logit_grad(c, logits[c], teacher, stats[c], scalars)
-        if c + 1 < CHUNKS:
-            grad, logits[c + 1] = lax.optimization_barrier((grad, logits[c + 1]))
-        grads.append(grad)
-        arrived.append([swap(grad, "dp", r) for r in range(1, count_dp)])
-
-    all_grads, state = [], []
-    for c in range(CHUNKS):
-        if c + 1 < CHUNKS:
-            grads[c + 1], arrived[c] = lax.optimization_barrier((grads[c + 1], arrived[c]))
-            arrived[c + 1] = [swap(grads[c + 1], "dp", r) for r in range(1, count_dp)]
+    for first, last in zip(cuts, cuts[1:]):
+        if grads:
+            grads[-1], logits = lax.optimization_barrier((grads[-1], logits))
+        grads.append(logit_grad(first, last, logits, teacher, stats, scalars))
+    arrived = [[swap(grad, "dp", r) for r in range(1, count_dp)] for grad in grads]
+
+    def summed(c):
         found = jnp.stack([grads[c]] + arrived[c])
         grad_all = jnp.concatenate([pick(found, me_dp ^ n) for n in range(count_dp)])
         grad_all = lax.optimization_barrier(grad_all)
-        all_grads.append(grad_all)
         crossed = swap(products(head_send, grad_all).astype(jnp.bfloat16), "vocab", 1)
-        if c + 1 < CHUNKS:
-            pass
-        else:
-            state[c - 1], crossed = lax.optimization_barrier((state[c - 1], crossed))
-        state.append(folded(products(head_keep, grad_all), crossed))
-        if c + 1 < CHUNKS:
-            keep, send = state[c]
-            state[c] = folded(keep, swap(send, "vocab", near[1]))
-            arrived[c + 1], state[c] = lax.optimization_barrier((arrived[c + 1], state[c]))
-    (state, all_grads) = lax.optimization_barrier((state, all_grads))
+        keep = products(head_keep, grad_all)
+        return grad_all, {
+            2 * k: keep[k] + crossed[k].astype(jnp.float32) for k in range(count_vocab // 2)
+        }
+
+    grads[1], arrived[0] = lax.optimization_barrier((grads[1], arrived[0]))
+    arrived[1] = [swap(grads[1], "dp", r) for r in range(1, count_dp)]
+    all_grads = [None, None]
+    all_grads[0], early = summed(0)
+    steps = list(zip(near[1:], far))
+    early = split(early)
+    for step in steps:
+        early = both(early, step)
+    arrived[1], early = lax.optimization_barrier((arrived[1], early))
+    all_grads[1], late = summed(1)
+    early, late, all_grads = lax.optimization_barrier((early, late, all_grads))
     head_grad = lax.dot_general(
         jnp.concatenate(gathered, axis=0),
-        jnp.concatenate(all_grads, axis=0),
+        jnp.concatenate([g.reshape(count_dp, -1, width) for g in all_grads], axis=1)
+        .reshape(count_dp, CHUNKS, part, width)
+        .transpose(1, 0, 2, 3)
+        .reshape(-1, width),
         (((0,), (0,)), ((), ())),
         preferred_element_type=jnp.float32,
     ).astype(jnp.bfloat16)
-    for place, mask in enumerate(near[1:]):
-        for c in range(CHUNKS):
-            if place == 0 and c + 1 < CHUNKS:
-                continue
-            keep, send = state[c]
-            state[c] = folded(keep, swap(send, "vocab", mask))
-    hidden_parts = [keep[0] for keep, _ in state]
-    hidden_grad = jnp.stack([p.reshape(rows, count_dp, part) for p in hidden_parts], axis=2)
+    late = split(late)
+    for step in steps:
+        late = both(late, step)
+    hidden_parts = [jnp.concatenate([side[0] for side in sides]) for sides in (early, late)]
+    hidden_grad = jnp.concatenate([p.reshape(rows, count_dp, -1) for p in hidden_parts], axis=2)
     return (hidden_grad.reshape(rows, count_dp * tokens), head_grad)
 
 

time: 153 us -> 146 us (0.954)
  waiting for transfers between devices: 76.3 us -> 67.8 us
  starting transfers between devices: 26.3 us -> 29.9 us
  Pallas kernels: 14.4 us -> 12 us
    ppermute x29 -> x33, waiting for transfers between devices: 76.3 us -> 67.8 us  [swap(): return lax.ppermute(value, axis, [(k, k ^ mask) for k in range(count)])]
    ppermute x29 -> x33, starting transfers between devices: 26.3 us -> 29.9 us  [swap(): return lax.ppermute(value, axis, [(k, k ^ mask) for k in range(count)])]
    pallas_call x2, Pallas kernels: 6.41 us -> 4.4 us  [local_stats(): pl.pallas_call(functools.partial(stats_kernel, heats, pieces), out_shape=...]
    unnamed x58 -> x60, local copies, waits for them, and re-layouts: 10.9 us -> 11.7 us
  transfers between devices with their start and end apart: 29 -> 33, of which waited for: 21 -> 22; matrix products, arithmetic and copies ran while one was open for 8% -> 10% of each run, Pallas kernels for 6% -> 6%
where the time goes in v4:
time: 146 us
  waiting for transfers between devices  67.8 us (46%)
  starting transfers between devices  29.9 us (20%)
  matrix products  15.4 us (11%)
  local copies, waits for them, and re-layouts  13.4 us (9%)
  Pallas kernels  12 us (8%)
  other arithmetic  5.56 us (4%)
  between operations  1.56 us (1%)
    ppermute x33, waiting for transfers between devices, swap(): return lax.ppermute(value, axis, [(k, k ^ mask) for k in range(count)])  67.8 us
    ppermute x33, starting transfers between devices, swap(): return lax.ppermute(value, axis, [(k, k ^ mask) for k in range(count)])  29.9 us
    unnamed x60, local copies, waits for them, and re-layouts  11.7 us
    dot_general x1, matrix products, shards(): lax.dot_general(jnp.concatenate(gathered, axis=0), jnp.concatenate([g.res...  6.16 us
    dot_general x4, matrix products, products(): lax.dot_general(blocks, grad, (((2,), (1,)), ((), ())), preferred_element...  4.84 us
    dot_general x2, matrix products, partial_logits(): partial = jnp.dot(gathered, head, preferred_element_type=jnp.float32)  4.45 us
    pallas_call x2, Pallas kernels, local_stats(): pl.pallas_call(functools.partial(stats_kernel, heats, pieces), out_shape=...  4.4 us
    pallas_call x1, Pallas kernels, row_blocks(): pl.pallas_call(functools.partial(copy_kernel, rows), out_shape=[block] *...  4 us
  transfers between devices with their start and end apart: 33, of which 22 were waited for; matrix products, arithmetic and copies ran while one was open for 10% of the time, Pallas kernels for 6%

profile of v4, /device:TPU:0, one launch (start us, length us, event | category | flops | bytes accessed | tf_op | source)
XLA Modules:
  0.0 145.7 jit_solution(12609259419860371903)
XLA Ops:
  0.7 1.2 copy.13
  1.9 3.1 %collective-permute-start = (bf16[1,384,256]{2,1,0:T(8,128)(2,1)S(1)}, bf16[1,384,256]{2,1,0:T(8,128)(2,1)S(1)}, u32[]{:S(2)}, u32[]{:S(2)}) collective-permute-start(bf16[1,384,256]{2,1,0:T(8,128)(2,1)S(1)} %bitcast.196), channel_id=1, source_target_pairs={{0,2},{1,3},{2,0},{3,1},{4,6},{5,7},{6,4},{7,5},{8,10},{9,11},{10,... | collective-permute-start | bytes 589832 | tf_op jit(solution)/shard_map/ppermute | solution.py:19
  5.0 2.6 %collective-permute-start.1 = (bf16[1,384,256]{2,1,0:T(8,128)(2,1)S(1)}, bf16[1,384,256]{2,1,0:T(8,128)(2,1)S(1)}, u32[]{:S(2)}, u32[]{:S(2)}) collective-permute-start(bf16[1,384,256]{2,1,0:T(8,128)(2,1)S(1)} %bitcast.200), channel_id=1, source_target_pairs={{0,4},{1,5},{2,6},{3,7},{4,0},{5,1},{6,2},{7,3},{8,12},{9,13},{10,... | collective-permute-start | bytes 589832 | tf_op jit(solution)/shard_map/ppermute | solution.py:19
  7.6 0.6 fusion.50
  8.2 0.6 broadcast_divide_fusion
  8.9 2.1 %stats.2 = f32[8,256]{1,0:T(8,128)S(1)} custom-call(f32[4]{0:T(128)S(1)} %get-tuple-element.157.inverse_ref, bf16[192,1280]{1,0:T(8,128)(2,1)S(1)} %copy-done.5), custom_call_target="tpu_custom_call" | custom-call | flops 1966080 | bytes 491520 | tf_op jit(solution)/shard_map/stats/pallas_call | solution.py:70
  11.0 3.0 %collective-permute-done = bf16[1,384,256]{2,1,0:T(8,128)(2,1)S(1)} collective-permute-done((bf16[1,384,256]{2,1,0:T(8,128)(2,1)S(1)}, bf16[1,384,256]{2,1,0:T(8,128)(2,1)S(1)}, u32[]{:S(2)}, u32[]{:S(2)}) %collective-permute-start) | collective-permute-done | bytes 196640 | tf_op jit(solution)/shard_map/ppermute | solution.py:19
  14.0 2.5 %collective-permute-done.1 = bf16[1,384,256]{2,1,0:T(8,128)(2,1)S(1)} collective-permute-done((bf16[1,384,256]{2,1,0:T(8,128)(2,1)S(1)}, bf16[1,384,256]{2,1,0:T(8,128)(2,1)S(1)}, u32[]{:S(2)}, u32[]{:S(2)}) %collective-permute-start.1) | collective-permute-done | bytes 196640 | tf_op jit(solution)/shard_map/ppermute | solution.py:19
  16.5 0.8 pad_maximum_fusion.8
  17.3 0.4 collective-permute-start.3
  17.8 0.8 pad_maximum_fusion.7
  18.5 2.6 %collective-permute-start.2 = (bf16[2,384,256]{2,1,0:T(8,128)(2,1)}, bf16[2,384,256]{2,1,0:T(8,128)(2,1)S(1)}, u32[]{:S(2)}, u32[]{:S(2)}) collective-permute-start(bf16[2,384,256]{2,1,0:T(8,128)(2,1)} %pad_maximum_fusion.7), channel_id=1, source_target_pairs={{0,4},{1,5},{2,6},{3,7},{4,0},{5,1},{6,2},{7,3},{8,12},{9,13},{10,... | collective-permute-start | bytes 1179656 | tf_op jit(solution)/shard_map/ppermute | solution.py:19
  21.1 0.5 collective-permute-start.7
  21.7 2.5 %copy-done = bf16[2048,1280]{1,0:T(8,128)(2,1)S(1)} copy-done((bf16[2048,1280]{1,0:T(8,128)(2,1)S(1)}, bf16[2048,1280]{1,0:T(8,128)(2,1)}, u32[]{:S(2)}) %copy-start) | copy-done | bytes 5242904
  24.2 4.0 %row_blocks.1 = (bf16[4,256,1280]{2,1,0:T(8,128)(2,1)S(1)}, bf16[4,256,1280]{2,1,0:T(8,128)(2,1)S(1)}) custom-call(s32[2,4]{1,0:T(2,128)S(1)} %pad_add_fusion.order_ref, bf16[2048,1280]{1,0:T(8,128)(2,1)S(1)} %copy-done), custom_call_target="tpu_custom_call" | custom-call | bytes 10485760 | tf_op jit(solution)/shard_map/row_blocks/pallas_call | solution.py:164
  28.2 1.5 %copy-done.1 = bf16[4,256,1280]{2,1,0:T(8,128)(2,1)} copy-done((bf16[4,256,1280]{2,1,0:T(8,128)(2,1)}, bf16[4,256,1280]{2,1,0:T(8,128)(2,1)S(1)}, u32[]{:S(2)}) %copy-start.1) | copy-done | bytes 2621464
  29.7 1.5 %copy-done.3 = bf16[4,256,1280]{2,1,0:T(8,128)(2,1)} copy-done((bf16[4,256,1280]{2,1,0:T(8,128)(2,1)}, bf16[4,256,1280]{2,1,0:T(8,128)(2,1)S(1)}, u32[]{:S(2)}) %copy-start.3) | copy-done | bytes 2621464
  31.2 1.3 collective-permute-done.3
  32.6 5.2 %collective-permute-done.2 = bf16[2,384,256]{2,1,0:T(8,128)(2,1)S(1)} collective-permute-done((bf16[2,384,256]{2,1,0:T(8,128)(2,1)}, bf16[2,384,256]{2,1,0:T(8,128)(2,1)S(1)}, u32[]{:S(2)}, u32[]{:S(2)}) %collective-permute-start.2) | collective-permute-done | bytes 393248 | tf_op jit(solution)/shard_map/ppermute | solution.py:19
  37.9 0.6 collective-permute-start.9
  38.5 1.0 collective-permute-done.6
  39.8 0.9 constant_dynamic-update-slice_fusion.14
  41.2 2.2 %fusion.52 = f32[384,1280]{1,0:T(8,128)S(1)} fusion(bf16[384,2048]{1,0:T(8,128)(2,1)S(1)} %bitcast_dynamic-update-slice_fusion, bf16[2048,1280]{1,0:T(8,128)(2,1)S(1)} %bitcast.183), kind=kOutput, calls=%fused_computation.179 | convolution fusion | flops 2013265920 | bytes 8781824 | tf_op jit(solution)/shard_map/dot_general | solution.py:202
  43.5 1.6 %collective-permute-start.12 = (f16[2,96,1280]{2,1,0:T(8,128)(2,1)S(1)}, f16[2,96,1280]{2,1,0:T(8,128)(2,1)S(1)}, u32[]{:S(2)}, u32[]{:S(2)}) collective-permute-start(f16[2,96,1280]{2,1,0:T(8,128)(2,1)S(1)} %fusion.13), channel_id=1, source_target_pairs={{0,16},{8,24},{16,0},{24,8},{1,17},{9,25},{17,1},{25,9},{2,18},{10... | collective-permute-start | bytes 1474568 | tf_op jit(solution)/shard_map/ppermute | solution.py:19
  45.5 2.2 %fusion.51 = f32[384,1280]{1,0:T(8,128)S(1)} fusion(bf16[384,2048]{1,0:T(8,128)(2,1)S(1)} %bitcast_dynamic-update-slice_fusion.8, bf16[2048,1280]{1,0:T(8,128)(2,1)S(1)} %bitcast.183), kind=kOutput, calls=%fused_computation.178 | convolution fusion | flops 2013265920 | bytes 8781824 | tf_op jit(solution)/shard_map/dot_general | solution.py:202
  47.8 1.5 %collective-permute-start.10 = (f16[2,96,1280]{2,1,0:T(8,128)(2,1)S(1)}, f16[2,96,1280]{2,1,0:T(8,128)(2,1)S(1)}, u32[]{:S(2)}, u32[]{:S(2)}) collective-permute-start(f16[2,96,1280]{2,1,0:T(8,128)(2,1)S(1)} %fusion.14), channel_id=1, source_target_pairs={{0,8},{8,0},{16,24},{24,16},{1,9},{9,1},{17,25},{25,17},{2,10},{10... | collective-permute-start | bytes 1474568 | tf_op jit(solution)/shard_map/ppermute | solution.py:19
  49.4 7.5 %collective-permute-done.12 = f16[2,96,1280]{2,1,0:T(8,128)(2,1)S(1)} collective-permute-done((f16[2,96,1280]{2,1,0:T(8,128)(2,1)S(1)}, f16[2,96,1280]{2,1,0:T(8,128)(2,1)S(1)}, u32[]{:S(2)}, u32[]{:S(2)}) %collective-permute-start.12) | collective-permute-done | bytes 491552 | tf_op jit(solution)/shard_map/ppermute | solution.py:19
  57.0 1.6 %collective-permute-start.13 = (f16[96,1280]{1,0:T(8,128)(2,1)S(1)}, f16[96,1280]{1,0:T(8,128)(2,1)S(1)}, u32[]{:S(2)}, u32[]{:S(2)}) collective-permute-start(f16[96,1280]{1,0:T(8,128)(2,1)S(1)} %fusion.19), channel_id=1, source_target_pairs={{0,8},{8,0},{16,24},{24,16},{1,9},{9,1},{17,25},{25,17},{2,10},{10... | collective-permute-start | bytes 737288 | tf_op jit(solution)/shard_map/ppermute | solution.py:19
  58.5 3.5 %collective-permute-done.10 = f16[2,96,1280]{2,1,0:T(8,128)(2,1)S(1)} collective-permute-done((f16[2,96,1280]{2,1,0:T(8,128)(2,1)S(1)}, f16[2,96,1280]{2,1,0:T(8,128)(2,1)S(1)}, u32[]{:S(2)}, u32[]{:S(2)}) %collective-permute-start.10) | collective-permute-done | bytes 491552 | tf_op jit(solution)/shard_map/ppermute | solution.py:19
  62.5 3.7 %collective-permute-done.13 = f16[96,1280]{1,0:T(8,128)(2,1)S(1)} collective-permute-done((f16[96,1280]{1,0:T(8,128)(2,1)S(1)}, f16[96,1280]{1,0:T(8,128)(2,1)S(1)}, u32[]{:S(2)}, u32[]{:S(2)}) %collective-permute-start.13) | collective-permute-done | bytes 245792 | tf_op jit(solution)/shard_map/ppermute | solution.py:19
  66.2 2.2 %collective-permute-done.11 = f16[96,1280]{1,0:T(8,128)(2,1)S(1)} collective-permute-done((f16[96,1280]{1,0:T(8,128)(2,1)S(1)}, f16[96,1280]{1,0:T(8,128)(2,1)S(1)}, u32[]{:S(2)}, u32[]{:S(2)}) %collective-permute-start.11) | collective-permute-done | bytes 245792 | tf_op jit(solution)/shard_map/ppermute | solution.py:19
  68.5 2.3 %stats.3 = f32[8,256]{1,0:T(8,128)S(1)} custom-call(f32[5]{0:T(128)S(1)} %get-tuple-element.155.inverse_ref, f32[96,1280]{1,0:T(8,128)S(1)} %bitcast_add_fusion.3.refs_0_, f32[96,1280]{1,0:T(8,128)S(1)} %bitcast_add_fusion.2.refs_1_), custom_call_target="tpu_custom_call" | custom-call | flops 2457600 | bytes 491520 | tf_op jit(solution)/shard_map/stats/pallas_call | solution.py:70
  70.9 1.1 collective-permute-done.14
  72.3 0.7 maximum_bitcast_fusion
  73.0 3.0 %collective-permute-done.15 = f32[16,256]{1,0:T(8,128)S(1)} collective-permute-done((f32[16,256]{1,0:T(8,128)S(1)}, f32[16,256]{1,0:T(8,128)S(1)}, u32[]{:S(2)}, u32[]{:S(2)}) %collective-permute-start.15) | collective-permute-done | bytes 16416 | tf_op jit(solution)/shard_map/ppermute | solution.py:19
  76.4 4.5 %collective-permute-done.16 = f32[16,256]{1,0:T(8,128)S(1)} collective-permute-done((f32[16,256]{1,0:T(8,128)S(1)}, f32[16,256]{1,0:T(8,128)S(1)}, u32[]{:S(2)}, u32[]{:S(2)}) %collective-permute-start.16) | collective-permute-done | bytes 16416 | tf_op jit(solution)/shard_map/ppermute | solution.py:19
  81.2 1.4 grad.2
  82.5 1.5 %collective-permute-start.17 = (bf16[64,1280]{1,0:T(8,128)(2,1)S(1)}, bf16[64,1280]{1,0:T(8,128)(2,1)S(1)}, u32[]{:S(2)}, u32[]{:S(2)}) collective-permute-start(bf16[64,1280]{1,0:T(8,128)(2,1)S(1)} %grad.2), channel_id=1, source_target_pairs={{0,8},{8,0},{16,24},{24,16},{1,9},{9,1},{17,25},{25,17},{2,10},{10... | collective-permute-start | bytes 491528 | tf_op jit(solution)/shard_map/ppermute | solution.py:19
  84.3 1.8 %collective-permute-start.19 = (bf16[64,1280]{1,0:T(8,128)(2,1)S(1)}, bf16[64,1280]{1,0:T(8,128)(2,1)S(1)}, u32[]{:S(2)}, u32[]{:S(2)}) collective-permute-start(bf16[64,1280]{1,0:T(8,128)(2,1)S(1)} %grad.2), channel_id=1, source_target_pairs={{0,24},{8,16},{16,8},{24,0},{1,25},{9,17},{17,9},{25,1},{2,26},{10... | collective-permute-start | bytes 491528 | tf_op jit(solution)/shard_map/ppermute | solution.py:19
  86.1 2.2 %grad.3 = bf16[128,1280]{1,0:T(8,128)(2,1)S(1)} custom-call(f32[2,5]{1,0:T(2,128)S(1)} %pad_maximum_fusion.16.scalars_ref, bf16[192,1280]{1,0:T(8,128)(2,1)S(1)} %copy-done.5, f32[96,1280]{1,0:T(8,128)S(1)} %bitcast_add_fusion.3.refs_0_, f32[96,1280]{1,0:T(8,128)S(1)} %bitcast_add_fusion.2.refs_1_, f32[16,128]{1,0:T(8,128)S(1)} %get-tuple-element.142.refs_1_.refs_2_, ...), custom_call_target="tpu_custom_call" | custom-call | flops 3932160 | bytes 1310720 | tf_op jit(solution)/shard_map/grad/pallas_call | solution.py:119
  88.3 0.6 collective-permute-done.17
  89.0 2.4 %collective-permute-done.18 = bf16[64,1280]{1,0:T(8,128)(2,1)S(1)} collective-permute-done((bf16[64,1280]{1,0:T(8,128)(2,1)S(1)}, bf16[64,1280]{1,0:T(8,128)(2,1)S(1)}, u32[]{:S(2)}, u32[]{:S(2)}) %collective-permute-start.18) | collective-permute-done | bytes 163872 | tf_op jit(solution)/shard_map/ppermute | solution.py:19
  91.6 1.6 %copy-done.4 = bf16[4,256,1280]{2,1,0:T(8,128)(2,1)S(1)} copy-done((bf16[4,256,1280]{2,1,0:T(8,128)(2,1)S(1)}, bf16[4,256,1280]{2,1,0:T(8,128)(2,1)}, u32[]{:S(2)}) %copy-start.4) | copy-done | bytes 2621464
  93.2 0.9 convolution_convert_fusion.2
  94.2 0.8 copy-done.2
  95.0 0.9 fusion.7
  96.3 0.4 collective-permute-start.24
  96.7 0.4 collective-permute-start.20
  97.1 1.2 collective-permute-start.21
  98.3 1.9 %collective-permute-start.22 = (bf16[128,1280]{1,0:T(8,128)(2,1)S(1)}, bf16[128,1280]{1,0:T(8,128)(2,1)S(1)}, u32[]{:S(2)}, u32[]{:S(2)}) collective-permute-start(bf16[128,1280]{1,0:T(8,128)(2,1)S(1)} %grad.3), channel_id=1, source_target_pairs={{0,24},{8,16},{16,8},{24,0},{1,25},{9,17},{17,9},{25,1},{2,26},{10... | collective-permute-start | bytes 983048 | tf_op jit(solution)/shard_map/ppermute | solution.py:19
  100.2 1.7 %collective-permute-start.26 = (bf16[2,128,256]{2,1,0:T(8,128)(2,1)S(1)}, bf16[2,128,256]{2,1,0:T(8,128)(2,1)S(1)}, u32[]{:S(2)}, u32[]{:S(2)}) collective-permute-start(bf16[2,128,256]{2,1,0:T(8,128)(2,1)S(1)} %pad_maximum_fusion.13), channel_id=1, source_target_pairs={{0,4},{1,5},{2,6},{3,7},{4,0},{5,1},{6,2},{7,3},{8,12},{9,13},{10,... | collective-permute-start | bytes 393224 | tf_op jit(solution)/shard_map/ppermute | solution.py:19
  101.9 1.4 collective-permute-start.25
  103.3 7.3 %collective-permute-done.26 = bf16[2,128,256]{2,1,0:T(8,128)(2,1)S(1)} collective-permute-done((bf16[2,128,256]{2,1,0:T(8,128)(2,1)S(1)}, bf16[2,128,256]{2,1,0:T(8,128)(2,1)S(1)}, u32[]{:S(2)}, u32[]{:S(2)}) %collective-permute-start.26) | collective-permute-done | bytes 131104 | tf_op jit(solution)/shard_map/ppermute | solution.py:19
  110.6 0.6 collective-permute-done.25
  111.2 3.6 %collective-permute-done.27 = bf16[1,128,256]{2,1,0:T(8,128)(2,1)S(1)} collective-permute-done((bf16[1,128,256]{2,1,0:T(8,128)(2,1)S(1)}, bf16[1,128,256]{2,1,0:T(8,128)(2,1)S(1)}, u32[]{:S(2)}, u32[]{:S(2)}) %collective-permute-start.27) | collective-permute-done | bytes 65568 | tf_op jit(solution)/shard_map/ppermute | solution.py:19
  115.3 1.5 %convolution_convert_fusion.1 = bf16[4,256,512]{2,1,0:T(8,128)(2,1)S(1)} fusion(bf16[4,256,1280]{2,1,0:T(8,128)(2,1)S(1)} %copy-done.4, bf16[512,1280]{1,0:T(8,128)(2,1)S(1)} %pad_maximum_fusion.2), kind=kOutput, calls=%fused_computation.5 | convolution fusion | flops 1342701568 | bytes 4980736 | tf_op jit(solution)/shard_map/dot_general | solution.py:227
  117.0 1.5 %fusion.4 = f32[4,256,512]{2,1,0:T(8,128)S(1)} fusion(bf16[4,256,1280]{2,1,0:T(8,128)(2,1)S(1)} %copy-done.2, bf16[512,1280]{1,0:T(8,128)(2,1)S(1)} %pad_maximum_fusion.2), kind=kOutput, calls=%fused_computation.9 | convolution fusion | flops 1342177280 | bytes 6029312 | tf_op jit(solution)/shard_map/dot_general | solution.py:227
  118.5 1.1 collective-permute-done.28
  120.4 1.8 %collective-permute-start.29 = (bf16[2,128,512]{2,1,0:T(8,128)(2,1)S(1)}, bf16[2,128,512]{2,1,0:T(8,128)(2,1)S(1)}, u32[]{:S(2)}, u32[]{:S(2)}) collective-permute-start(bf16[2,128,512]{2,1,0:T(8,128)(2,1)S(1)} %pad_maximum_fusion.10), channel_id=1, source_target_pairs={{0,2},{1,3},{2,0},{3,1},{4,6},{5,7},{6,4},{7,5},{8,10},{9,11},{10,... | collective-permute-start | bytes 786440 | tf_op jit(solution)/shard_map/ppermute | solution.py:19
  122.5 12.2 %collective-permute-done.31 = bf16[2,128,512]{2,1,0:T(8,128)(2,1)S(1)} collective-permute-done((bf16[2,128,512]{2,1,0:T(8,128)(2,1)S(1)}, bf16[2,128,512]{2,1,0:T(8,128)(2,1)S(1)}, u32[]{:S(2)}, u32[]{:S(2)}) %collective-permute-start.31) | collective-permute-done | bytes 262176 | tf_op jit(solution)/shard_map/ppermute | solution.py:19
  134.9 2.2 %collective-permute-start.30 = (bf16[1,128,512]{2,1,0:T(8,128)(2,1)S(1)}, bf16[1,128,512]{2,1,0:T(8,128)(2,1)S(1)}, u32[]{:S(2)}, u32[]{:S(2)}) collective-permute-start(bf16[1,128,512]{2,1,0:T(8,128)(2,1)S(1)} %fusion.20), channel_id=1, source_target_pairs={{0,4},{1,5},{2,6},{3,7},{4,0},{5,1},{6,2},{7,3},{8,12},{9,13},{10,... | collective-permute-start | bytes 393224 | tf_op jit(solution)/shard_map/ppermute | solution.py:19
  137.1 6.2 %convolution_convert_fusion = bf16[2048,1280]{1,0:T(8,128)(2,1)} fusion(bf16[768,1280]{1,0:T(8,128)(2,1)S(1)} %bitcast.193, bf16[384,2048]{1,0:T(8,128)(2,1)S(1)} %copy-done.9, bf16[384,2048]{1,0:T(8,128)(2,1)S(1)} %copy-done.7), kind=kOutput, calls=%fused_computation | convolution fusion | flops 4035444736 | bytes 10354688 | tf_op jit(solution)/shard_map/dot_general | solution.py:305
  143.4 0.8 collective-permute-done.30
  144.6 1.1 copy.18
  (155 shorter events, 6.2 us)
Async XLA Ops:
  0.6 7.0 %copy-start.10 = (f32[2]{0:T(128)S(1)}, f32[2]{0:T(128)}, u32[]{:S(2)}) copy-start(f32[2]{0:T(128)} %param.11) | copy-start | bytes 28
  0.6 7.5 %copy-start.12 = (f32[4]{0:T(128)S(1)}, f32[4]{0:T(128)}, u32[]{:S(2)}) copy-start(f32[4]{0:T(128)} %param.10) | copy-start | bytes 52
  0.7 8.2 %copy-start.5 = (bf16[192,1280]{1,0:T(8,128)(2,1)S(1)}, bf16[192,1280]{1,0:T(8,128)(2,1)}, u32[]{:S(2)}) copy-start(bf16[192,1280]{1,0:T(8,128)(2,1)} %teacher_ref.3) | copy-start | bytes 1474564
  1.9 12.1 %collective-permute-start = (bf16[1,384,256]{2,1,0:T(8,128)(2,1)S(1)}, bf16[1,384,256]{2,1,0:T(8,128)(2,1)S(1)}, u32[]{:S(2)}, u32[]{:S(2)}) collective-permute-start(bf16[1,384,256]{2,1,0:T(8,128)(2,1)S(1)} %bitcast.196), channel_id=1, source_target_pairs={{0,2},{1,3},{2,0},{3,1},{4,6},{5,7},{6,4},{7,5},{8,10},{9,11},{10,... | collective-permute-start | bytes 589832 | tf_op jit(solution)/shard_map/ppermute | solution.py:19
  5.0 11.5 %collective-permute-start.1 = (bf16[1,384,256]{2,1,0:T(8,128)(2,1)S(1)}, bf16[1,384,256]{2,1,0:T(8,128)(2,1)S(1)}, u32[]{:S(2)}, u32[]{:S(2)}) collective-permute-start(bf16[1,384,256]{2,1,0:T(8,128)(2,1)S(1)} %bitcast.200), channel_id=1, source_target_pairs={{0,4},{1,5},{2,6},{3,7},{4,0},{5,1},{6,2},{7,3},{8,12},{9,13},{10,... | collective-permute-start | bytes 589832 | tf_op jit(solution)/shard_map/ppermute | solution.py:19
  17.3 15.2 %collective-permute-start.3 = (bf16[2,384,256]{2,1,0:T(8,128)(2,1)}, bf16[2,384,256]{2,1,0:T(8,128)(2,1)S(1)}, u32[]{:S(2)}, u32[]{:S(2)}) collective-permute-start(bf16[2,384,256]{2,1,0:T(8,128)(2,1)} %pad_maximum_fusion.8), channel_id=1, source_target_pairs={{0,2},{1,3},{2,0},{3,1},{4,6},{5,7},{6,4},{7,5},{8,10},{9,11},{10,... | collective-permute-start | bytes 1179656 | tf_op jit(solution)/shard_map/ppermute | solution.py:19
  18.5 19.2 %collective-permute-start.2 = (bf16[2,384,256]{2,1,0:T(8,128)(2,1)}, bf16[2,384,256]{2,1,0:T(8,128)(2,1)S(1)}, u32[]{:S(2)}, u32[]{:S(2)}) collective-permute-start(bf16[2,384,256]{2,1,0:T(8,128)(2,1)} %pad_maximum_fusion.7), channel_id=1, source_target_pairs={{0,4},{1,5},{2,6},{3,7},{4,0},{5,1},{6,2},{7,3},{8,12},{9,13},{10,... | collective-permute-start | bytes 1179656 | tf_op jit(solution)/shard_map/ppermute | solution.py:19
  21.1 18.4 %collective-permute-start.4 = (bf16[1,384,256]{2,1,0:T(8,128)(2,1)S(1)}, bf16[1,384,256]{2,1,0:T(8,128)(2,1)S(1)}, u32[]{:S(2)}, u32[]{:S(2)}) collective-permute-start(bf16[1,384,256]{2,1,0:T(8,128)(2,1)S(1)} %bitcast.198), channel_id=1, source_target_pairs={{0,1},{1,0},{2,3},{3,2},{4,5},{5,4},{6,7},{7,6},{8,9},{9,8},{10,11... | collective-permute-start | bytes 589832 | tf_op jit(solution)/shard_map/ppermute | solution.py:19
  21.1 18.4 %collective-permute-start.7 = (bf16[1,384,256]{2,1,0:T(8,128)(2,1)S(1)}, bf16[1,384,256]{2,1,0:T(8,128)(2,1)}, u32[]{:S(2)}, u32[]{:S(2)}) collective-permute-start(bf16[1,384,256]{2,1,0:T(8,128)(2,1)S(1)} %bitcast.202), channel_id=1, source_target_pairs={{0,1},{1,0},{2,3},{3,2},{4,5},{5,4},{6,7},{7,6},{8,9},{9,8},{10,11... | collective-permute-start | bytes 589832 | tf_op jit(solution)/shard_map/ppermute | solution.py:19
  21.7 2.5 %copy-start = (bf16[2048,1280]{1,0:T(8,128)(2,1)S(1)}, bf16[2048,1280]{1,0:T(8,128)(2,1)}, u32[]{:S(2)}) copy-start(bf16[2048,1280]{1,0:T(8,128)(2,1)} %in_ref.1) | copy-start | bytes 15728644
  24.2 17.0 %slice-start = ((s8[5242880]{0:T(1024)(128)(4,1)}), s8[1048576]{0:T(1024)(128)(4,1)S(1)}, s32[]{:S(2)}) async-start(s8[5242880]{0:T(1024)(128)(4,1)} %bitcast.182), calls=%async_computation | async-start | bytes 2097152
  28.2 1.5 %copy-start.1 = (bf16[4,256,1280]{2,1,0:T(8,128)(2,1)}, bf16[4,256,1280]{2,1,0:T(8,128)(2,1)S(1)}, u32[]{:S(2)}) copy-start(bf16[4,256,1280]{2,1,0:T(8,128)(2,1)S(1)} %get-tuple-element.74) | copy-start | bytes 7864324
  29.7 1.5 %copy-start.3 = (bf16[4,256,1280]{2,1,0:T(8,128)(2,1)}, bf16[4,256,1280]{2,1,0:T(8,128)(2,1)S(1)}, u32[]{:S(2)}) copy-start(bf16[4,256,1280]{2,1,0:T(8,128)(2,1)S(1)} %get-tuple-element.78) | copy-start | bytes 7864324
  31.2 8.3 %collective-permute-start.5 = (bf16[1,384,256]{2,1,0:T(8,128)(2,1)S(1)}, bf16[1,384,256]{2,1,0:T(8,128)(2,1)S(1)}, u32[]{:S(2)}, u32[]{:S(2)}) collective-permute-start(bf16[1,384,256]{2,1,0:T(8,128)(2,1)S(1)} %collective-permute-done), channel_id=1, source_target_pairs={{0,1},{1,0},{2,3},{3,2},{4,5},{5,4},{6,7},{7,6},{8,9},{9,8},{10,11... | collective-permute-start | bytes 589832 | tf_op jit(solution)/shard_map/ppermute | solution.py:19
  32.6 5.3 %collective-permute-start.8 = (bf16[2,384,256]{2,1,0:T(8,128)(2,1)S(1)}, bf16[2,384,256]{2,1,0:T(8,128)(2,1)S(1)}, u32[]{:S(2)}, u32[]{:S(2)}) collective-permute-start(bf16[2,384,256]{2,1,0:T(8,128)(2,1)S(1)} %collective-permute-done.3), channel_id=1, source_target_pairs={{0,1},{1,0},{2,3},{3,2},{4,5},{5,4},{6,7},{7,6},{8,9},{9,8},{10,11... | collective-permute-start | bytes 1179656 | tf_op jit(solution)/shard_map/ppermute | solution.py:19
  37.8 1.7 %collective-permute-start.6 = (bf16[2,384,256]{2,1,0:T(8,128)(2,1)S(1)}, bf16[2,384,256]{2,1,0:T(8,128)(2,1)S(1)}, u32[]{:S(2)}, u32[]{:S(2)}) collective-permute-start(bf16[2,384,256]{2,1,0:T(8,128)(2,1)S(1)} %collective-permute-done.2), channel_id=1, source_target_pairs={{0,1},{1,0},{2,3},{3,2},{4,5},{5,4},{6,7},{7,6},{8,9},{9,8},{10,11... | collective-permute-start | bytes 1179656 | tf_op jit(solution)/shard_map/ppermute | solution.py:19
  37.9 3.3 %slice-start.1 = ((s8[5242880]{0:T(1024)(128)(4,1)}), s8[4194304]{0:T(1024)(128)(4,1)S(1)}, s32[]{:S(2)}) async-start(s8[5242880]{0:T(1024)(128)(4,1)} %bitcast.182), calls=%async_computation.1 | async-start | bytes 8388608
  37.9 1.9 %collective-permute-start.9 = (bf16[1,384,256]{2,1,0:T(8,128)(2,1)S(1)}, bf16[1,384,256]{2,1,0:T(8,128)(2,1)S(1)}, u32[]{:S(2)}, u32[]{:S(2)}) collective-permute-start(bf16[1,384,256]{2,1,0:T(8,128)(2,1)S(1)} %collective-permute-done.1), channel_id=1, source_target_pairs={{0,1},{1,0},{2,3},{3,2},{4,5},{5,4},{6,7},{7,6},{8,9},{9,8},{10,11... | collective-permute-start | bytes 589832 | tf_op jit(solution)/shard_map/ppermute | solution.py:19
  41.2 2.2 %copy-start.8 = (bf16[384,2048]{1,0:T(8,128)(2,1)}, bf16[384,2048]{1,0:T(8,128)(2,1)S(1)}, u32[]{:S(2)}) copy-start(bf16[384,2048]{1,0:T(8,128)(2,1)S(1)} %bitcast_dynamic-update-slice_fusion) | copy-start | bytes 4718596
  43.5 13.3 %collective-permute-start.12 = (f16[2,96,1280]{2,1,0:T(8,128)(2,1)S(1)}, f16[2,96,1280]{2,1,0:T(8,128)(2,1)S(1)}, u32[]{:S(2)}, u32[]{:S(2)}) collective-permute-start(f16[2,96,1280]{2,1,0:T(8,128)(2,1)S(1)} %fusion.13), channel_id=1, source_target_pairs={{0,16},{8,24},{16,0},{24,8},{1,17},{9,25},{17,1},{25,9},{2,18},{10... | collective-permute-start | bytes 1474568 | tf_op jit(solution)/shard_map/ppermute | solution.py:19
  45.5 2.2 %copy-start.6 = (bf16[384,2048]{1,0:T(8,128)(2,1)}, bf16[384,2048]{1,0:T(8,128)(2,1)S(1)}, u32[]{:S(2)}) copy-start(bf16[384,2048]{1,0:T(8,128)(2,1)S(1)} %bitcast_dynamic-update-slice_fusion.8) | copy-start | bytes 4718596
  47.8 14.2 %collective-permute-start.10 = (f16[2,96,1280]{2,1,0:T(8,128)(2,1)S(1)}, f16[2,96,1280]{2,1,0:T(8,128)(2,1)S(1)}, u32[]{:S(2)}, u32[]{:S(2)}) collective-permute-start(f16[2,96,1280]{2,1,0:T(8,128)(2,1)S(1)} %fusion.14), channel_id=1, source_target_pairs={{0,8},{8,0},{16,24},{24,16},{1,9},{9,1},{17,25},{25,17},{2,10},{10... | collective-permute-start | bytes 1474568 | tf_op jit(solution)/shard_map/ppermute | solution.py:19
  57.0 9.2 %collective-permute-start.13 = (f16[96,1280]{1,0:T(8,128)(2,1)S(1)}, f16[96,1280]{1,0:T(8,128)(2,1)S(1)}, u32[]{:S(2)}, u32[]{:S(2)}) collective-permute-start(f16[96,1280]{1,0:T(8,128)(2,1)S(1)} %fusion.19), channel_id=1, source_target_pairs={{0,8},{8,0},{16,24},{24,16},{1,9},{9,1},{17,25},{25,17},{2,10},{10... | collective-permute-start | bytes 737288 | tf_op jit(solution)/shard_map/ppermute | solution.py:19
  62.2 6.3 %collective-permute-start.11 = (f16[96,1280]{1,0:T(8,128)(2,1)S(1)}, f16[96,1280]{1,0:T(8,128)(2,1)S(1)}, u32[]{:S(2)}, u32[]{:S(2)}) collective-permute-start(f16[96,1280]{1,0:T(8,128)(2,1)S(1)} %fusion.18), channel_id=1, source_target_pairs={{0,16},{8,24},{16,0},{24,8},{1,17},{9,25},{17,1},{25,9},{2,18},{10... | collective-permute-start | bytes 737288 | tf_op jit(solution)/shard_map/ppermute | solution.py:19
  66.2 4.7 %copy-start.11 = (s32[192]{0:T(256)S(1)}, s32[192]{0:T(256)}, u32[]{:S(2)}) copy-start(s32[192]{0:T(256)} %param.9) | copy-start | bytes 2308
  70.8 1.2 collective-permute-start.14
  72.2 3.8 %collective-permute-start.15 = (f32[16,256]{1,0:T(8,128)S(1)}, f32[16,256]{1,0:T(8,128)S(1)}, u32[]{:S(2)}, u32[]{:S(2)}) collective-permute-start(f32[16,256]{1,0:T(8,128)S(1)} %concatenate.69), channel_id=1, source_target_pairs={{0,2},{1,3},{2,0},{3,1},{4,6},{5,7},{6,4},{7,5},{8,10},{9,11},{10,... | collective-permute-start | bytes 49160 | tf_op jit(solution)/shard_map/ppermute | solution.py:19
  76.2 4.7 %collective-permute-start.16 = (f32[16,256]{1,0:T(8,128)S(1)}, f32[16,256]{1,0:T(8,128)S(1)}, u32[]{:S(2)}, u32[]{:S(2)}) collective-permute-start(f32[16,256]{1,0:T(8,128)S(1)} %concatenate.70), channel_id=1, source_target_pairs={{0,4},{1,5},{2,6},{3,7},{4,0},{5,1},{6,2},{7,3},{8,12},{9,13},{10,... | collective-permute-start | bytes 49160 | tf_op jit(solution)/shard_map/ppermute | solution.py:19
  82.5 6.4 %collective-permute-start.17 = (bf16[64,1280]{1,0:T(8,128)(2,1)S(1)}, bf16[64,1280]{1,0:T(8,128)(2,1)S(1)}, u32[]{:S(2)}, u32[]{:S(2)}) collective-permute-start(bf16[64,1280]{1,0:T(8,128)(2,1)S(1)} %grad.2), channel_id=1, source_target_pairs={{0,8},{8,0},{16,24},{24,16},{1,9},{9,1},{17,25},{25,17},{2,10},{10... | collective-permute-start | bytes 491528 | tf_op jit(solution)/shard_map/ppermute | solution.py:19
  84.1 7.3 %collective-permute-start.18 = (bf16[64,1280]{1,0:T(8,128)(2,1)S(1)}, bf16[64,1280]{1,0:T(8,128)(2,1)S(1)}, u32[]{:S(2)}, u32[]{:S(2)}) collective-permute-start(bf16[64,1280]{1,0:T(8,128)(2,1)S(1)} %grad.2), channel_id=1, source_target_pairs={{0,16},{8,24},{16,0},{24,8},{1,17},{9,25},{17,1},{25,9},{2,18},{10... | collective-permute-start | bytes 491528 | tf_op jit(solution)/shard_map/ppermute | solution.py:19
  84.3 7.1 %collective-permute-start.19 = (bf16[64,1280]{1,0:T(8,128)(2,1)S(1)}, bf16[64,1280]{1,0:T(8,128)(2,1)S(1)}, u32[]{:S(2)}, u32[]{:S(2)}) collective-permute-start(bf16[64,1280]{1,0:T(8,128)(2,1)S(1)} %grad.2), channel_id=1, source_target_pairs={{0,24},{8,16},{16,8},{24,0},{1,25},{9,17},{17,9},{25,1},{2,26},{10... | collective-permute-start | bytes 491528 | tf_op jit(solution)/shard_map/ppermute | solution.py:19
  91.5 1.7 %copy-start.4 = (bf16[4,256,1280]{2,1,0:T(8,128)(2,1)S(1)}, bf16[4,256,1280]{2,1,0:T(8,128)(2,1)}, u32[]{:S(2)}) copy-start(bf16[4,256,1280]{2,1,0:T(8,128)(2,1)} %copy-done.3) | copy-start | bytes 7864324
  93.2 1.7 %copy-start.2 = (bf16[4,256,1280]{2,1,0:T(8,128)(2,1)S(1)}, bf16[4,256,1280]{2,1,0:T(8,128)(2,1)}, u32[]{:S(2)}) copy-start(bf16[4,256,1280]{2,1,0:T(8,128)(2,1)} %copy-done.1) | copy-start | bytes 7864324
  94.1 2.0 %collective-permute-start.23 = (bf16[4,256,256]{2,1,0:T(8,128)(2,1)S(1)}, bf16[4,256,256]{2,1,0:T(8,128)(2,1)S(1)}, u32[]{:S(2)}, u32[]{:S(2)}) collective-permute-start(bf16[4,256,256]{2,1,0:T(8,128)(2,1)S(1)} %convolution_convert_fusion.2), channel_id=1, source_target_pairs={{0,1},{1,0},{2,3},{3,2},{4,5},{5,4},{6,7},{7,6},{8,9},{9,8},{10,11... | collective-permute-start | bytes 1572872 | tf_op jit(solution)/shard_map/ppermute | solution.py:19
  96.3 5.6 %collective-permute-start.24 = (bf16[2,128,256]{2,1,0:T(8,128)(2,1)S(1)}, bf16[2,128,256]{2,1,0:T(8,128)(2,1)S(1)}, u32[]{:S(2)}, u32[]{:S(2)}) collective-permute-start(bf16[2,128,256]{2,1,0:T(8,128)(2,1)S(1)} %pad_maximum_fusion.12), channel_id=1, source_target_pairs={{0,2},{1,3},{2,0},{3,1},{4,6},{5,7},{6,4},{7,5},{8,10},{9,11},{10,... | collective-permute-start | bytes 393224 | tf_op jit(solution)/shard_map/ppermute | solution.py:19
  96.7 18.3 %collective-permute-start.20 = (bf16[128,1280]{1,0:T(8,128)(2,1)S(1)}, bf16[128,1280]{1,0:T(8,128)(2,1)S(1)}, u32[]{:S(2)}, u32[]{:S(2)}) collective-permute-start(bf16[128,1280]{1,0:T(8,128)(2,1)S(1)} %grad.3), channel_id=1, source_target_pairs={{0,8},{8,0},{16,24},{24,16},{1,9},{9,1},{17,25},{25,17},{2,10},{10... | collective-permute-start | bytes 983048 | tf_op jit(solution)/shard_map/ppermute | solution.py:19
  97.1 17.8 %collective-permute-start.21 = (bf16[128,1280]{1,0:T(8,128)(2,1)S(1)}, bf16[128,1280]{1,0:T(8,128)(2,1)S(1)}, u32[]{:S(2)}, u32[]{:S(2)}) collective-permute-start(bf16[128,1280]{1,0:T(8,128)(2,1)S(1)} %grad.3), channel_id=1, source_target_pairs={{0,16},{8,24},{16,0},{24,8},{1,17},{9,25},{17,1},{25,9},{2,18},{10... | collective-permute-start | bytes 983048 | tf_op jit(solution)/shard_map/ppermute | solution.py:19
  98.3 16.7 %collective-permute-start.22 = (bf16[128,1280]{1,0:T(8,128)(2,1)S(1)}, bf16[128,1280]{1,0:T(8,128)(2,1)S(1)}, u32[]{:S(2)}, u32[]{:S(2)}) collective-permute-start(bf16[128,1280]{1,0:T(8,128)(2,1)S(1)} %grad.3), channel_id=1, source_target_pairs={{0,24},{8,16},{16,8},{24,0},{1,25},{9,17},{17,9},{25,1},{2,26},{10... | collective-permute-start | bytes 983048 | tf_op jit(solution)/shard_map/ppermute | solution.py:19
  100.2 10.4 %collective-permute-start.26 = (bf16[2,128,256]{2,1,0:T(8,128)(2,1)S(1)}, bf16[2,128,256]{2,1,0:T(8,128)(2,1)S(1)}, u32[]{:S(2)}, u32[]{:S(2)}) collective-permute-start(bf16[2,128,256]{2,1,0:T(8,128)(2,1)S(1)} %pad_maximum_fusion.13), channel_id=1, source_target_pairs={{0,4},{1,5},{2,6},{3,7},{4,0},{5,1},{6,2},{7,3},{8,12},{9,13},{10,... | collective-permute-start | bytes 393224 | tf_op jit(solution)/shard_map/ppermute | solution.py:19
  101.9 9.3 %collective-permute-start.25 = (bf16[1,128,256]{2,1,0:T(8,128)(2,1)S(1)}, bf16[1,128,256]{2,1,0:T(8,128)(2,1)S(1)}, u32[]{:S(2)}, u32[]{:S(2)}) collective-permute-start(bf16[1,128,256]{2,1,0:T(8,128)(2,1)S(1)} %fusion.27), channel_id=1, source_target_pairs={{0,4},{1,5},{2,6},{3,7},{4,0},{5,1},{6,2},{7,3},{8,12},{9,13},{10,... | collective-permute-start | bytes 196616 | tf_op jit(solution)/shard_map/ppermute | solution.py:19
  110.5 4.3 %collective-permute-start.27 = (bf16[1,128,256]{2,1,0:T(8,128)(2,1)S(1)}, bf16[1,128,256]{2,1,0:T(8,128)(2,1)S(1)}, u32[]{:S(2)}, u32[]{:S(2)}) collective-permute-start(bf16[1,128,256]{2,1,0:T(8,128)(2,1)S(1)} %fusion.24), channel_id=1, source_target_pairs={{0,2},{1,3},{2,0},{3,1},{4,6},{5,7},{6,4},{7,5},{8,10},{9,11},{10,... | collective-permute-start | bytes 196616 | tf_op jit(solution)/shard_map/ppermute | solution.py:19
  116.9 2.7 %collective-permute-start.28 = (bf16[4,256,512]{2,1,0:T(8,128)(2,1)S(1)}, bf16[4,256,512]{2,1,0:T(8,128)(2,1)S(1)}, u32[]{:S(2)}, u32[]{:S(2)}) collective-permute-start(bf16[4,256,512]{2,1,0:T(8,128)(2,1)S(1)} %convolution_convert_fusion.1), channel_id=1, source_target_pairs={{0,1},{1,0},{2,3},{3,2},{4,5},{5,4},{6,7},{7,6},{8,9},{9,8},{10,11... | collective-permute-start | bytes 3145736 | tf_op jit(solution)/shard_map/ppermute | solution.py:19
  120.1 14.7 %collective-permute-start.31 = (bf16[2,128,512]{2,1,0:T(8,128)(2,1)S(1)}, bf16[2,128,512]{2,1,0:T(8,128)(2,1)S(1)}, u32[]{:S(2)}, u32[]{:S(2)}) collective-permute-start(bf16[2,128,512]{2,1,0:T(8,128)(2,1)S(1)} %pad_maximum_fusion.11), channel_id=1, source_target_pairs={{0,4},{1,5},{2,6},{3,7},{4,0},{5,1},{6,2},{7,3},{8,12},{9,13},{10,... | collective-permute-start | bytes 786440 | tf_op jit(solution)/shard_map/ppermute | solution.py:19
  120.4 14.5 %collective-permute-start.29 = (bf16[2,128,512]{2,1,0:T(8,128)(2,1)S(1)}, bf16[2,128,512]{2,1,0:T(8,128)(2,1)S(1)}, u32[]{:S(2)}, u32[]{:S(2)}) collective-permute-start(bf16[2,128,512]{2,1,0:T(8,128)(2,1)S(1)} %pad_maximum_fusion.10), channel_id=1, source_target_pairs={{0,2},{1,3},{2,0},{3,1},{4,6},{5,7},{6,4},{7,5},{8,10},{9,11},{10,... | collective-permute-start | bytes 786440 | tf_op jit(solution)/shard_map/ppermute | solution.py:19
  122.4 14.7 %copy-start.7 = (bf16[384,2048]{1,0:T(8,128)(2,1)S(1)}, bf16[384,2048]{1,0:T(8,128)(2,1)}, u32[]{:S(2)}) copy-start(bf16[384,2048]{1,0:T(8,128)(2,1)} %copy-done.6) | copy-start | bytes 4718596
  122.4 14.7 %copy-start.9 = (bf16[384,2048]{1,0:T(8,128)(2,1)S(1)}, bf16[384,2048]{1,0:T(8,128)(2,1)}, u32[]{:S(2)}) copy-start(bf16[384,2048]{1,0:T(8,128)(2,1)} %copy-done.8) | copy-start | bytes 4718596
  134.8 8.6 %collective-permute-start.32 = (bf16[1,128,512]{2,1,0:T(8,128)(2,1)S(1)}, bf16[1,128,512]{2,1,0:T(8,128)(2,1)S(1)}, u32[]{:S(2)}, u32[]{:S(2)}) collective-permute-start(bf16[1,128,512]{2,1,0:T(8,128)(2,1)S(1)} %fusion.21), channel_id=1, source_target_pairs={{0,2},{1,3},{2,0},{3,1},{4,6},{5,7},{6,4},{7,5},{8,10},{9,11},{10,... | collective-permute-start | bytes 393224 | tf_op jit(solution)/shard_map/ppermute | solution.py:19
  134.9 9.3 %collective-permute-start.30 = (bf16[1,128,512]{2,1,0:T(8,128)(2,1)S(1)}, bf16[1,128,512]{2,1,0:T(8,128)(2,1)S(1)}, u32[]{:S(2)}, u32[]{:S(2)}) collective-permute-start(bf16[1,128,512]{2,1,0:T(8,128)(2,1)S(1)} %fusion.20), channel_id=1, source_target_pairs={{0,4},{1,5},{2,6},{3,7},{4,0},{5,1},{6,2},{7,3},{8,12},{9,13},{10,... | collective-permute-start | bytes 393224 | tf_op jit(solution)/shard_map/ppermute | solution.py:19

commit v5 on v4

--- a/solution.py
+++ b/solution.py
@@ -8,7 +8,7 @@
 from jax.sharding import PartitionSpec as P
 
 CHUNKS = 2
-FIRST = 64
+FIRST = 96
 STRIP = 32
 LANES = 128
 LOG2E = 1.4426950408889634
@@ -226,16 +226,20 @@
     def products(blocks, grad):
         return lax.dot_general(blocks, grad, (((2,), (1,)), ((), ())), preferred_element_type=jnp.float32)
 
-    def folded(blocks, mask):
-        sent = [k for k in sorted(blocks) if k & mask]
-        other = swap(jnp.stack([blocks[k].astype(jnp.bfloat16) for k in sent]), "vocab", mask)
-        return {k ^ mask: blocks[k ^ mask] + other[n].astype(jnp.float32) for n, k in enumerate(sent)}
+    def folded(sides, masks):
+        sent = [[k for k in sorted(side) if k & mask] for side, mask in zip(sides, masks)]
+        others = [
+            swap(jnp.stack([side[k].astype(jnp.bfloat16) for k in keys]), "vocab", mask)
+            for side, keys, mask in zip(sides, sent, masks)
+        ]
+        others = lax.optimization_barrier(others)
+        return [
+            {k ^ mask: side[k ^ mask] + other[n].astype(jnp.float32) for n, k in enumerate(keys)}
+            for side, keys, mask, other in zip(sides, sent, masks, others)
+        ]
 
     def split(blocks):
         return [{k: blocks[k][: rows // 2] for k in blocks}, {k: blocks[k][rows // 2 :] for k in blocks}]
-
-    def both(sides, masks):
-        return [folded(side, mask) for side, mask in zip(sides, masks)]
 
     have, cross = [], []
     for c in range(CHUNKS):
@@ -279,29 +283,35 @@
         if grads:
             grads[-1], logits = lax.optimization_barrier((grads[-1], logits))
         grads.append(logit_grad(first, last, logits, teacher, stats, scalars))
-    arrived = [[swap(grad, "dp", r) for r in range(1, count_dp)] for grad in grads]
-
-    def summed(c):
-        found = jnp.stack([grads[c]] + arrived[c])
+
+    def crossing(c):
+        found = jnp.stack([grads[c]] + [arrived[c][r] for r in range(1, count_dp)])
         grad_all = jnp.concatenate([pick(found, me_dp ^ n) for n in range(count_dp)])
         grad_all = lax.optimization_barrier(grad_all)
         crossed = swap(products(head_send, grad_all).astype(jnp.bfloat16), "vocab", 1)
+        return crossed, grad_all
+
+    def kept(crossed, grad_all):
         keep = products(head_keep, grad_all)
-        return grad_all, {
-            2 * k: keep[k] + crossed[k].astype(jnp.float32) for k in range(count_vocab // 2)
-        }
-
+        return {2 * k: keep[k] + crossed[k].astype(jnp.float32) for k in range(count_vocab // 2)}
+
+    arrived = [None, None]
+    exchange = lambda grad: {r: swap(grad, "dp", r) for r in range(1, count_dp)}
+    arrived[0] = exchange(grads[0])
     grads[1], arrived[0] = lax.optimization_barrier((grads[1], arrived[0]))
-    arrived[1] = [swap(grads[1], "dp", r) for r in range(1, count_dp)]
+    arrived[1] = exchange(grads[1])
+    steps = list(zip(near[1:], far))
     all_grads = [None, None]
-    all_grads[0], early = summed(0)
-    steps = list(zip(near[1:], far))
+    crossed, all_grads[0] = crossing(0)
+    early = kept(crossed, all_grads[0])
+    early, arrived[1][1] = lax.optimization_barrier((early, arrived[1][1]))
     early = split(early)
-    for step in steps:
-        early = both(early, step)
-    arrived[1], early = lax.optimization_barrier((arrived[1], early))
-    all_grads[1], late = summed(1)
+    early = folded(early, steps[0])
+    crossed, all_grads[1] = crossing(1)
+    late = kept(crossed, all_grads[1])
     early, late, all_grads = lax.optimization_barrier((early, late, all_grads))
+    for step in steps[1:]:
+        early = folded(early, step)
     head_grad = lax.dot_general(
         jnp.concatenate(gathered, axis=0),
         jnp.concatenate([g.reshape(count_dp, -1, width) for g in all_grads], axis=1)
@@ -313,7 +323,7 @@
     ).astype(jnp.bfloat16)
     late = split(late)
     for step in steps:
-        late = both(late, step)
+        late = folded(late, step)
     hidden_parts = [jnp.concatenate([side[0] for side in sides]) for sides in (early, late)]
     hidden_grad = jnp.concatenate([p.reshape(rows, count_dp, -1) for p in hidden_parts], axis=2)
     return (hidden_grad.reshape(rows, count_dp * tokens), head_grad)

time: 146 us -> 141 us (0.966)
  waiting for transfers between devices: 67.8 us -> 55.5 us
  starting transfers between devices: 29.9 us -> 36 us
    ppermute x33, waiting for transfers between devices: 67.8 us -> 55.5 us  [swap(): return lax.ppermute(value, axis, [(k, k ^ mask) for k in range(count)])]
    ppermute x33, starting transfers between devices: 29.9 us -> 36 us  [swap(): return lax.ppermute(value, axis, [(k, k ^ mask) for k in range(count)])]
    unnamed x60 -> x56, local copies, waits for them, and re-layouts: 11.7 us -> 12.1 us
  transfers between devices with their start and end apart: 33 -> 33, of which waited for: 22 -> 24; matrix products, arithmetic and copies ran while one was open for 10% -> 13% of each run, Pallas kernels for 6% -> 6%
where the time goes in v5:
time: 141 us
  waiting for transfers between devices  55.5 us (39%)
  starting transfers between devices  36 us (26%)
  matrix products  16.8 us (12%)
  local copies, waits for them, and re-layouts  13.9 us (10%)
  Pallas kernels  12 us (9%)
  other arithmetic  5.49 us (4%)
  between operations  1.48 us (1%)
    ppermute x33, waiting for transfers between devices, swap(): return lax.ppermute(value, axis, [(k, k ^ mask) for k in range(count)])  55.5 us
    ppermute x33, starting transfers between devices, swap(): return lax.ppermute(value, axis, [(k, k ^ mask) for k in range(count)])  36 us
    unnamed x56, local copies, waits for them, and re-layouts  12.1 us
    dot_general x1, matrix products, shards(): lax.dot_general(jnp.concatenate(gathered, axis=0), jnp.concatenate([g.res...  6.17 us
    dot_general x4, matrix products, products(): lax.dot_general(blocks, grad, (((2,), (1,)), ((), ())), preferred_element...  6.16 us
    dot_general x2, matrix products, partial_logits(): partial = jnp.dot(gathered, head, preferred_element_type=jnp.float32)  4.44 us
    pallas_call x2, Pallas kernels, local_stats(): pl.pallas_call(functools.partial(stats_kernel, heats, pieces), out_shape=...  4.4 us
    pallas_call x1, Pallas kernels, row_blocks(): pl.pallas_call(functools.partial(copy_kernel, rows), out_shape=[block] *...  4 us
  transfers between devices with their start and end apart: 33, of which 24 were waited for; matrix products, arithmetic and copies ran while one was open for 13% of the time, Pallas kernels for 6%

profile of v5, /device:TPU:0, one launch (start us, length us, event | category | flops | bytes accessed | tf_op | source)
XLA Modules:
  0.0 141.1 jit_solution(4560255404612132753)
XLA Ops:
  0.7 1.2 copy.13
  1.9 3.1 %collective-permute-start = (bf16[1,384,256]{2,1,0:T(8,128)(2,1)S(1)}, bf16[1,384,256]{2,1,0:T(8,128)(2,1)S(1)}, u32[]{:S(2)}, u32[]{:S(2)}) collective-permute-start(bf16[1,384,256]{2,1,0:T(8,128)(2,1)S(1)} %bitcast.227), channel_id=1, source_target_pairs={{0,2},{1,3},{2,0},{3,1},{4,6},{5,7},{6,4},{7,5},{8,10},{9,11},{10,... | collective-permute-start | bytes 589832 | tf_op jit(solution)/shard_map/ppermute | solution.py:19
  5.0 2.6 %collective-permute-start.1 = (bf16[1,384,256]{2,1,0:T(8,128)(2,1)S(1)}, bf16[1,384,256]{2,1,0:T(8,128)(2,1)S(1)}, u32[]{:S(2)}, u32[]{:S(2)}) collective-permute-start(bf16[1,384,256]{2,1,0:T(8,128)(2,1)S(1)} %bitcast.223), channel_id=1, source_target_pairs={{0,4},{1,5},{2,6},{3,7},{4,0},{5,1},{6,2},{7,3},{8,12},{9,13},{10,... | collective-permute-start | bytes 589832 | tf_op jit(solution)/shard_map/ppermute | solution.py:19
  7.6 0.6 fusion.48
  8.2 0.7 broadcast_multiply_fusion
  8.9 2.1 %stats.2 = f32[8,256]{1,0:T(8,128)S(1)} custom-call(f32[4]{0:T(128)S(1)} %get-tuple-element.177.inverse_ref, bf16[192,1280]{1,0:T(8,128)(2,1)S(1)} %copy-done.5), custom_call_target="tpu_custom_call" | custom-call | flops 1966080 | bytes 491520 | tf_op jit(solution)/shard_map/stats/pallas_call | solution.py:70
  11.0 3.0 %collective-permute-done = bf16[1,384,256]{2,1,0:T(8,128)(2,1)S(1)} collective-permute-done((bf16[1,384,256]{2,1,0:T(8,128)(2,1)S(1)}, bf16[1,384,256]{2,1,0:T(8,128)(2,1)S(1)}, u32[]{:S(2)}, u32[]{:S(2)}) %collective-permute-start) | collective-permute-done | bytes 196640 | tf_op jit(solution)/shard_map/ppermute | solution.py:19
  14.0 2.5 %collective-permute-done.1 = bf16[1,384,256]{2,1,0:T(8,128)(2,1)S(1)} collective-permute-done((bf16[1,384,256]{2,1,0:T(8,128)(2,1)S(1)}, bf16[1,384,256]{2,1,0:T(8,128)(2,1)S(1)}, u32[]{:S(2)}, u32[]{:S(2)}) %collective-permute-start.1) | collective-permute-done | bytes 196640 | tf_op jit(solution)/shard_map/ppermute | solution.py:19
  16.5 0.8 pad_maximum_fusion.6
  17.7 0.8 pad_maximum_fusion.7
  18.4 2.7 %collective-permute-start.3 = (bf16[2,384,256]{2,1,0:T(8,128)(2,1)}, bf16[2,384,256]{2,1,0:T(8,128)(2,1)S(1)}, u32[]{:S(2)}, u32[]{:S(2)}) collective-permute-start(bf16[2,384,256]{2,1,0:T(8,128)(2,1)} %pad_maximum_fusion.7), channel_id=1, source_target_pairs={{0,2},{1,3},{2,0},{3,1},{4,6},{5,7},{6,4},{7,5},{8,10},{9,11},{10,... | collective-permute-start | bytes 1179656 | tf_op jit(solution)/shard_map/ppermute | solution.py:19
  21.7 2.5 %copy-done = bf16[2048,1280]{1,0:T(8,128)(2,1)S(1)} copy-done((bf16[2048,1280]{1,0:T(8,128)(2,1)S(1)}, bf16[2048,1280]{1,0:T(8,128)(2,1)}, u32[]{:S(2)}) %copy-start) | copy-done | bytes 5242904
  24.2 4.0 %row_blocks.1 = (bf16[4,256,1280]{2,1,0:T(8,128)(2,1)S(1)}, bf16[4,256,1280]{2,1,0:T(8,128)(2,1)S(1)}) custom-call(s32[2,4]{1,0:T(2,128)S(1)} %pad_add_fusion.order_ref, bf16[2048,1280]{1,0:T(8,128)(2,1)S(1)} %copy-done), custom_call_target="tpu_custom_call" | custom-call | bytes 10485760 | tf_op jit(solution)/shard_map/row_blocks/pallas_call | solution.py:164
  28.2 1.5 %copy-done.1 = bf16[4,256,1280]{2,1,0:T(8,128)(2,1)} copy-done((bf16[4,256,1280]{2,1,0:T(8,128)(2,1)}, bf16[4,256,1280]{2,1,0:T(8,128)(2,1)S(1)}, u32[]{:S(2)}) %copy-start.1) | copy-done | bytes 2621464
  29.7 1.5 %copy-done.3 = bf16[4,256,1280]{2,1,0:T(8,128)(2,1)} copy-done((bf16[4,256,1280]{2,1,0:T(8,128)(2,1)}, bf16[4,256,1280]{2,1,0:T(8,128)(2,1)S(1)}, u32[]{:S(2)}) %copy-start.3) | copy-done | bytes 2621464
  31.2 3.3 %collective-permute-done.2 = bf16[2,384,256]{2,1,0:T(8,128)(2,1)S(1)} collective-permute-done((bf16[2,384,256]{2,1,0:T(8,128)(2,1)}, bf16[2,384,256]{2,1,0:T(8,128)(2,1)S(1)}, u32[]{:S(2)}, u32[]{:S(2)}) %collective-permute-start.2) | collective-permute-done | bytes 393248 | tf_op jit(solution)/shard_map/ppermute | solution.py:19
  35.1 1.1 collective-permute-done.6
  36.8 0.8 collective-permute-done.9
  37.7 0.9 constant_dynamic-update-slice_fusion.6
  39.0 2.2 %fusion.49 = f32[384,1280]{1,0:T(8,128)S(1)} fusion(bf16[384,2048]{1,0:T(8,128)(2,1)S(1)} %bitcast_dynamic-update-slice_fusion.8, bf16[2048,1280]{1,0:T(8,128)(2,1)S(1)} %bitcast.211), kind=kOutput, calls=%fused_computation.178 | convolution fusion | flops 2013265920 | bytes 8781824 | tf_op jit(solution)/shard_map/dot_general | solution.py:202
  41.4 1.6 %collective-permute-start.10 = (f16[2,96,1280]{2,1,0:T(8,128)(2,1)S(1)}, f16[2,96,1280]{2,1,0:T(8,128)(2,1)S(1)}, u32[]{:S(2)}, u32[]{:S(2)}) collective-permute-start(f16[2,96,1280]{2,1,0:T(8,128)(2,1)S(1)} %fusion.10), channel_id=1, source_target_pairs={{0,8},{8,0},{16,24},{24,16},{1,9},{9,1},{17,25},{25,17},{2,10},{10... | collective-permute-start | bytes 1474568 | tf_op jit(solution)/shard_map/ppermute | solution.py:19
  43.3 2.2 %fusion.50 = f32[384,1280]{1,0:T(8,128)S(1)} fusion(bf16[384,2048]{1,0:T(8,128)(2,1)S(1)} %bitcast_dynamic-update-slice_fusion, bf16[2048,1280]{1,0:T(8,128)(2,1)S(1)} %bitcast.211), kind=kOutput, calls=%fused_computation.179 | convolution fusion | flops 2013265920 | bytes 8781824 | tf_op jit(solution)/shard_map/dot_general | solution.py:202
  45.6 1.6 %collective-permute-start.12 = (f16[2,96,1280]{2,1,0:T(8,128)(2,1)S(1)}, f16[2,96,1280]{2,1,0:T(8,128)(2,1)S(1)}, u32[]{:S(2)}, u32[]{:S(2)}) collective-permute-start(f16[2,96,1280]{2,1,0:T(8,128)(2,1)S(1)} %fusion.9), channel_id=1, source_target_pairs={{0,16},{8,24},{16,0},{24,8},{1,17},{9,25},{17,1},{25,9},{2,18},{10... | collective-permute-start | bytes 1474568 | tf_op jit(solution)/shard_map/ppermute | solution.py:19
  47.2 7.5 %collective-permute-done.10 = f16[2,96,1280]{2,1,0:T(8,128)(2,1)S(1)} collective-permute-done((f16[2,96,1280]{2,1,0:T(8,128)(2,1)S(1)}, f16[2,96,1280]{2,1,0:T(8,128)(2,1)S(1)}, u32[]{:S(2)}, u32[]{:S(2)}) %collective-permute-start.10) | collective-permute-done | bytes 491552 | tf_op jit(solution)/shard_map/ppermute | solution.py:19
  54.8 1.6 %collective-permute-start.11 = (f16[96,1280]{1,0:T(8,128)(2,1)S(1)}, f16[96,1280]{1,0:T(8,128)(2,1)S(1)}, u32[]{:S(2)}, u32[]{:S(2)}) collective-permute-start(f16[96,1280]{1,0:T(8,128)(2,1)S(1)} %fusion.19), channel_id=1, source_target_pairs={{0,16},{8,24},{16,0},{24,8},{1,17},{9,25},{17,1},{25,9},{2,18},{10... | collective-permute-start | bytes 737288 | tf_op jit(solution)/shard_map/ppermute | solution.py:19
  56.4 3.4 %collective-permute-done.12 = f16[2,96,1280]{2,1,0:T(8,128)(2,1)S(1)} collective-permute-done((f16[2,96,1280]{2,1,0:T(8,128)(2,1)S(1)}, f16[2,96,1280]{2,1,0:T(8,128)(2,1)S(1)}, u32[]{:S(2)}, u32[]{:S(2)}) %collective-permute-start.12) | collective-permute-done | bytes 491552 | tf_op jit(solution)/shard_map/ppermute | solution.py:19
  60.3 3.6 %collective-permute-done.11 = f16[96,1280]{1,0:T(8,128)(2,1)S(1)} collective-permute-done((f16[96,1280]{1,0:T(8,128)(2,1)S(1)}, f16[96,1280]{1,0:T(8,128)(2,1)S(1)}, u32[]{:S(2)}, u32[]{:S(2)}) %collective-permute-start.11) | collective-permute-done | bytes 245792 | tf_op jit(solution)/shard_map/ppermute | solution.py:19
  64.0 2.2 %collective-permute-done.13 = f16[96,1280]{1,0:T(8,128)(2,1)S(1)} collective-permute-done((f16[96,1280]{1,0:T(8,128)(2,1)S(1)}, f16[96,1280]{1,0:T(8,128)(2,1)S(1)}, u32[]{:S(2)}, u32[]{:S(2)}) %collective-permute-start.13) | collective-permute-done | bytes 245792 | tf_op jit(solution)/shard_map/ppermute | solution.py:19
  66.3 2.3 %stats.3 = f32[8,256]{1,0:T(8,128)S(1)} custom-call(f32[5]{0:T(128)S(1)} %get-tuple-element.172.inverse_ref, f32[96,1280]{1,0:T(8,128)S(1)} %bitcast_add_fusion.3.refs_0_, f32[96,1280]{1,0:T(8,128)S(1)} %bitcast_add_fusion.2.refs_1_.refs_0_), custom_call_target="tpu_custom_call" | custom-call | flops 2457600 | bytes 491520 | tf_op jit(solution)/shard_map/stats/pallas_call | solution.py:70
  68.7 1.1 collective-permute-done.14
  70.0 0.7 collective-permute-start.15
  70.7 0.8 maximum_bitcast_fusion
  71.5 2.4 %collective-permute-done.15 = f32[16,256]{1,0:T(8,128)S(1)} collective-permute-done((f32[16,256]{1,0:T(8,128)S(1)}, f32[16,256]{1,0:T(8,128)S(1)}, u32[]{:S(2)}, u32[]{:S(2)}) %collective-permute-start.15) | collective-permute-done | bytes 16416 | tf_op jit(solution)/shard_map/ppermute | solution.py:19
  74.0 1.7 %collective-permute-start.16 = (f32[16,256]{1,0:T(8,128)S(1)}, f32[16,256]{1,0:T(8,128)S(1)}, u32[]{:S(2)}, u32[]{:S(2)}) collective-permute-start(f32[16,256]{1,0:T(8,128)S(1)} %concatenate.70), channel_id=1, source_target_pairs={{0,4},{1,5},{2,6},{3,7},{4,0},{5,1},{6,2},{7,3},{8,12},{9,13},{10,... | collective-permute-start | bytes 49160 | tf_op jit(solution)/shard_map/ppermute | solution.py:19
  75.8 3.1 %collective-permute-done.16 = f32[16,256]{1,0:T(8,128)S(1)} collective-permute-done((f32[16,256]{1,0:T(8,128)S(1)}, f32[16,256]{1,0:T(8,128)S(1)}, u32[]{:S(2)}, u32[]{:S(2)}) %collective-permute-start.16) | collective-permute-done | bytes 16416 | tf_op jit(solution)/shard_map/ppermute | solution.py:19
  79.1 1.7 %grad.2 = bf16[96,1280]{1,0:T(8,128)(2,1)S(1)} custom-call(f32[2,5]{1,0:T(2,128)S(1)} %pad_maximum_fusion.16.scalars_ref, bf16[192,1280]{1,0:T(8,128)(2,1)S(1)} %copy-done.5, f32[96,1280]{1,0:T(8,128)S(1)} %bitcast_add_fusion.3.refs_0_, f32[16,128]{1,0:T(8,128)S(1)} %get-tuple-element.159.refs_1_), custom_call_target="tpu_custom_call" | custom-call | flops 2949120 | bytes 983040 | tf_op jit(solution)/shard_map/grad/pallas_call | solution.py:119
  81.2 1.5 %collective-permute-start.18 = (bf16[96,1280]{1,0:T(8,128)(2,1)S(1)}, bf16[96,1280]{1,0:T(8,128)(2,1)S(1)}, u32[]{:S(2)}, u32[]{:S(2)}) collective-permute-start(bf16[96,1280]{1,0:T(8,128)(2,1)S(1)} %grad.2), channel_id=1, source_target_pairs={{0,16},{8,24},{16,0},{24,8},{1,17},{9,25},{17,1},{25,9},{2,18},{10... | collective-permute-start | bytes 737288 | tf_op jit(solution)/shard_map/ppermute | solution.py:19
  82.7 1.7 %collective-permute-start.19 = (bf16[96,1280]{1,0:T(8,128)(2,1)S(1)}, bf16[96,1280]{1,0:T(8,128)(2,1)S(1)}, u32[]{:S(2)}, u32[]{:S(2)}) collective-permute-start(bf16[96,1280]{1,0:T(8,128)(2,1)S(1)} %grad.2), channel_id=1, source_target_pairs={{0,24},{8,16},{16,8},{24,0},{1,25},{9,17},{17,9},{25,1},{2,26},{10... | collective-permute-start | bytes 737288 | tf_op jit(solution)/shard_map/ppermute | solution.py:19
  84.4 1.9 %grad.3 = bf16[96,1280]{1,0:T(8,128)(2,1)S(1)} custom-call(f32[2,5]{1,0:T(2,128)S(1)} %pad_maximum_fusion.16.scalars_ref, bf16[192,1280]{1,0:T(8,128)(2,1)S(1)} %copy-done.5, f32[96,1280]{1,0:T(8,128)S(1)} %bitcast_add_fusion.2.refs_1_.refs_0_, f32[16,128]{1,0:T(8,128)S(1)} %get-tuple-element.158.refs_1_), custom_call_target="tpu_custom_call" | custom-call | flops 2949120 | bytes 983040 | tf_op jit(solution)/shard_map/grad/pallas_call | solution.py:119
  86.3 3.0 %collective-permute-done.17 = bf16[96,1280]{1,0:T(8,128)(2,1)S(1)} collective-permute-done((bf16[96,1280]{1,0:T(8,128)(2,1)S(1)}, bf16[96,1280]{1,0:T(8,128)(2,1)S(1)}, u32[]{:S(2)}, u32[]{:S(2)}) %collective-permute-start.17) | collective-permute-done | bytes 245792 | tf_op jit(solution)/shard_map/ppermute | solution.py:19
  89.3 0.7 collective-permute-done.18
  90.0 2.9 %collective-permute-done.19 = bf16[96,1280]{1,0:T(8,128)(2,1)S(1)} collective-permute-done((bf16[96,1280]{1,0:T(8,128)(2,1)S(1)}, bf16[96,1280]{1,0:T(8,128)(2,1)S(1)}, u32[]{:S(2)}, u32[]{:S(2)}) %collective-permute-start.19) | collective-permute-done | bytes 245792 | tf_op jit(solution)/shard_map/ppermute | solution.py:19
  93.2 1.6 %copy-done.4 = bf16[4,256,1280]{2,1,0:T(8,128)(2,1)S(1)} copy-done((bf16[4,256,1280]{2,1,0:T(8,128)(2,1)S(1)}, bf16[4,256,1280]{2,1,0:T(8,128)(2,1)}, u32[]{:S(2)}) %copy-start.4) | copy-done | bytes 2621464
  94.8 1.5 %convolution_convert_fusion.2 = bf16[4,256,384]{2,1,0:T(8,128)(2,1)S(1)} fusion(bf16[4,256,1280]{2,1,0:T(8,128)(2,1)S(1)} %copy-done.4, bf16[384,1280]{1,0:T(8,128)(2,1)S(1)} %pad_maximum_fusion.2), kind=kOutput, calls=%fused_computation.6 | convolution fusion | flops 1007026176 | bytes 4390912 | tf_op jit(solution)/shard_map/dot_general | solution.py:227
  96.4 0.9 collective-permute-start.21
  97.2 1.3 collective-permute-start.25
  98.5 1.4 collective-permute-start.24
  99.9 1.5 %fusion.7 = f32[4,256,384]{2,1,0:T(8,128)S(1)} fusion(bf16[4,256,1280]{2,1,0:T(8,128)(2,1)S(1)} %copy-done.2, bf16[384,1280]{1,0:T(8,128)(2,1)S(1)} %pad_maximum_fusion.2), kind=kOutput, calls=%fused_computation.16 | convolution fusion | flops 1006632960 | bytes 5177344 | tf_op jit(solution)/shard_map/dot_general | solution.py:227
  101.7 3.5 %collective-permute-done.21 = bf16[96,1280]{1,0:T(8,128)(2,1)S(1)} collective-permute-done((bf16[96,1280]{1,0:T(8,128)(2,1)S(1)}, bf16[96,1280]{1,0:T(8,128)(2,1)S(1)}, u32[]{:S(2)}, u32[]{:S(2)}) %collective-permute-start.21) | collective-permute-done | bytes 245792 | tf_op jit(solution)/shard_map/ppermute | solution.py:19
  105.3 0.6 collective-permute-start.22
  105.9 2.6 %collective-permute-start.23 = (bf16[2,128,384]{2,1,0:T(8,128)(2,1)S(1)}, bf16[2,128,384]{2,1,0:T(8,128)(2,1)S(1)}, u32[]{:S(2)}, u32[]{:S(2)}) collective-permute-start(bf16[2,128,384]{2,1,0:T(8,128)(2,1)S(1)} %pad_maximum_fusion.11), channel_id=1, source_target_pairs={{0,4},{1,5},{2,6},{3,7},{4,0},{5,1},{6,2},{7,3},{8,12},{9,13},{10,... | collective-permute-start | bytes 589832 | tf_op jit(solution)/shard_map/ppermute | solution.py:19
  108.6 1.6 %collective-permute-done.25 = bf16[96,1280]{1,0:T(8,128)(2,1)S(1)} collective-permute-done((bf16[96,1280]{1,0:T(8,128)(2,1)S(1)}, bf16[96,1280]{1,0:T(8,128)(2,1)S(1)}, u32[]{:S(2)}, u32[]{:S(2)}) %collective-permute-start.25) | collective-permute-done | bytes 245792 | tf_op jit(solution)/shard_map/ppermute | solution.py:19
  110.2 1.4 collective-permute-done.24
  111.8 1.5 %convolution_convert_fusion.1 = bf16[4,256,384]{2,1,0:T(8,128)(2,1)S(1)} fusion(bf16[4,256,1280]{2,1,0:T(8,128)(2,1)S(1)} %copy-done.4, bf16[384,1280]{1,0:T(8,128)(2,1)S(1)} %pad_maximum_fusion.4), kind=kOutput, calls=%fused_computation.5 | convolution fusion | flops 1007026176 | bytes 4390912 | tf_op jit(solution)/shard_map/dot_general | solution.py:227
  113.5 1.5 %fusion.4 = f32[4,256,384]{2,1,0:T(8,128)S(1)} fusion(bf16[4,256,1280]{2,1,0:T(8,128)(2,1)S(1)} %copy-done.2, bf16[384,1280]{1,0:T(8,128)(2,1)S(1)} %pad_maximum_fusion.4), kind=kOutput, calls=%fused_computation.13 | convolution fusion | flops 1006632960 | bytes 5177344 | tf_op jit(solution)/shard_map/dot_general | solution.py:227
  115.2 1.6 %collective-permute-done.23 = bf16[2,128,384]{2,1,0:T(8,128)(2,1)S(1)} collective-permute-done((bf16[2,128,384]{2,1,0:T(8,128)(2,1)S(1)}, bf16[2,128,384]{2,1,0:T(8,128)(2,1)S(1)}, u32[]{:S(2)}, u32[]{:S(2)}) %collective-permute-start.23) | collective-permute-done | bytes 196640 | tf_op jit(solution)/shard_map/ppermute | solution.py:19
  117.6 2.8 %collective-permute-start.30 = (bf16[2,128,384]{2,1,0:T(8,128)(2,1)S(1)}, bf16[2,128,384]{2,1,0:T(8,128)(2,1)S(1)}, u32[]{:S(2)}, u32[]{:S(2)}) collective-permute-start(bf16[2,128,384]{2,1,0:T(8,128)(2,1)S(1)} %pad_maximum_fusion.13), channel_id=1, source_target_pairs={{0,4},{1,5},{2,6},{3,7},{4,0},{5,1},{6,2},{7,3},{8,12},{9,13},{10,... | collective-permute-start | bytes 589832 | tf_op jit(solution)/shard_map/ppermute | solution.py:19
  120.6 1.8 %collective-permute-start.28 = (bf16[1,128,384]{2,1,0:T(8,128)(2,1)S(1)}, bf16[1,128,384]{2,1,0:T(8,128)(2,1)S(1)}, u32[]{:S(2)}, u32[]{:S(2)}) collective-permute-start(bf16[1,128,384]{2,1,0:T(8,128)(2,1)S(1)} %bitcast.240), channel_id=1, source_target_pairs={{0,2},{1,3},{2,0},{3,1},{4,6},{5,7},{6,4},{7,5},{8,10},{9,11},{10,... | collective-permute-start | bytes 294920 | tf_op jit(solution)/shard_map/ppermute | solution.py:19
  122.7 1.3 copy-done.7
  123.9 6.2 %convolution_convert_fusion = bf16[2048,1280]{1,0:T(8,128)(2,1)} fusion(bf16[768,1280]{1,0:T(8,128)(2,1)S(1)} %bitcast.222, bf16[384,2048]{1,0:T(8,128)(2,1)S(1)} %bitcast_dynamic-update-slice_fusion, bf16[384,2048]{1,0:T(8,128)(2,1)S(1)} %copy-done.7), kind=kOutput, calls=%fused_computation | convolution fusion | flops 4035444736 | bytes 10354688 | tf_op jit(solution)/shard_map/dot_general | solution.py:315
  130.1 2.6 %collective-permute-done.27 = bf16[1,128,384]{2,1,0:T(8,128)(2,1)S(1)} collective-permute-done((bf16[1,128,384]{2,1,0:T(8,128)(2,1)S(1)}, bf16[1,128,384]{2,1,0:T(8,128)(2,1)S(1)}, u32[]{:S(2)}, u32[]{:S(2)}) %collective-permute-start.27) | collective-permute-done | bytes 98336 | tf_op jit(solution)/shard_map/ppermute | solution.py:19
  133.1 2.8 %collective-permute-start.32 = (bf16[1,128,384]{2,1,0:T(8,128)(2,1)S(1)}, bf16[1,128,384]{2,1,0:T(8,128)(2,1)S(1)}, u32[]{:S(2)}, u32[]{:S(2)}) collective-permute-start(bf16[1,128,384]{2,1,0:T(8,128)(2,1)S(1)} %fusion.24), channel_id=1, source_target_pairs={{0,2},{1,3},{2,0},{3,1},{4,6},{5,7},{6,4},{7,5},{8,10},{9,11},{10,... | collective-permute-start | bytes 294920 | tf_op jit(solution)/shard_map/ppermute | solution.py:19
  136.2 2.9 %collective-permute-done.31 = bf16[1,128,384]{2,1,0:T(8,128)(2,1)S(1)} collective-permute-done((bf16[1,128,384]{2,1,0:T(8,128)(2,1)S(1)}, bf16[1,128,384]{2,1,0:T(8,128)(2,1)S(1)}, u32[]{:S(2)}, u32[]{:S(2)}) %collective-permute-start.31) | collective-permute-done | bytes 98336 | tf_op jit(solution)/shard_map/ppermute | solution.py:19
  139.9 1.1 copy.18
  (154 shorter events, 8.4 us)
Async XLA Ops:
  0.6 7.0 %copy-start.8 = (f32[2]{0:T(128)S(1)}, f32[2]{0:T(128)}, u32[]{:S(2)}) copy-start(f32[2]{0:T(128)} %param.11) | copy-start | bytes 28
  0.6 7.6 %copy-start.10 = (f32[4]{0:T(128)S(1)}, f32[4]{0:T(128)}, u32[]{:S(2)}) copy-start(f32[4]{0:T(128)} %param.10) | copy-start | bytes 52
  0.7 8.2 %copy-start.5 = (bf16[192,1280]{1,0:T(8,128)(2,1)S(1)}, bf16[192,1280]{1,0:T(8,128)(2,1)}, u32[]{:S(2)}) copy-start(bf16[192,1280]{1,0:T(8,128)(2,1)} %teacher_ref.3) | copy-start | bytes 1474564
  1.9 12.1 %collective-permute-start = (bf16[1,384,256]{2,1,0:T(8,128)(2,1)S(1)}, bf16[1,384,256]{2,1,0:T(8,128)(2,1)S(1)}, u32[]{:S(2)}, u32[]{:S(2)}) collective-permute-start(bf16[1,384,256]{2,1,0:T(8,128)(2,1)S(1)} %bitcast.227), channel_id=1, source_target_pairs={{0,2},{1,3},{2,0},{3,1},{4,6},{5,7},{6,4},{7,5},{8,10},{9,11},{10,... | collective-permute-start | bytes 589832 | tf_op jit(solution)/shard_map/ppermute | solution.py:19
  5.0 11.5 %collective-permute-start.1 = (bf16[1,384,256]{2,1,0:T(8,128)(2,1)S(1)}, bf16[1,384,256]{2,1,0:T(8,128)(2,1)S(1)}, u32[]{:S(2)}, u32[]{:S(2)}) collective-permute-start(bf16[1,384,256]{2,1,0:T(8,128)(2,1)S(1)} %bitcast.223), channel_id=1, source_target_pairs={{0,4},{1,5},{2,6},{3,7},{4,0},{5,1},{6,2},{7,3},{8,12},{9,13},{10,... | collective-permute-start | bytes 589832 | tf_op jit(solution)/shard_map/ppermute | solution.py:19
  17.3 17.2 %collective-permute-start.2 = (bf16[2,384,256]{2,1,0:T(8,128)(2,1)}, bf16[2,384,256]{2,1,0:T(8,128)(2,1)S(1)}, u32[]{:S(2)}, u32[]{:S(2)}) collective-permute-start(bf16[2,384,256]{2,1,0:T(8,128)(2,1)} %pad_maximum_fusion.6), channel_id=1, source_target_pairs={{0,4},{1,5},{2,6},{3,7},{4,0},{5,1},{6,2},{7,3},{8,12},{9,13},{10,... | collective-permute-start | bytes 1179656 | tf_op jit(solution)/shard_map/ppermute | solution.py:19
  18.4 16.1 %collective-permute-start.3 = (bf16[2,384,256]{2,1,0:T(8,128)(2,1)}, bf16[2,384,256]{2,1,0:T(8,128)(2,1)S(1)}, u32[]{:S(2)}, u32[]{:S(2)}) collective-permute-start(bf16[2,384,256]{2,1,0:T(8,128)(2,1)} %pad_maximum_fusion.7), channel_id=1, source_target_pairs={{0,2},{1,3},{2,0},{3,1},{4,6},{5,7},{6,4},{7,5},{8,10},{9,11},{10,... | collective-permute-start | bytes 1179656 | tf_op jit(solution)/shard_map/ppermute | solution.py:19
  21.1 15.7 %collective-permute-start.4 = (bf16[1,384,256]{2,1,0:T(8,128)(2,1)S(1)}, bf16[1,384,256]{2,1,0:T(8,128)(2,1)}, u32[]{:S(2)}, u32[]{:S(2)}) collective-permute-start(bf16[1,384,256]{2,1,0:T(8,128)(2,1)S(1)} %bitcast.229), channel_id=1, source_target_pairs={{0,1},{1,0},{2,3},{3,2},{4,5},{5,4},{6,7},{7,6},{8,9},{9,8},{10,11... | collective-permute-start | bytes 589832 | tf_op jit(solution)/shard_map/ppermute | solution.py:19
  21.2 15.7 %collective-permute-start.7 = (bf16[1,384,256]{2,1,0:T(8,128)(2,1)S(1)}, bf16[1,384,256]{2,1,0:T(8,128)(2,1)S(1)}, u32[]{:S(2)}, u32[]{:S(2)}) collective-permute-start(bf16[1,384,256]{2,1,0:T(8,128)(2,1)S(1)} %bitcast.225), channel_id=1, source_target_pairs={{0,1},{1,0},{2,3},{3,2},{4,5},{5,4},{6,7},{7,6},{8,9},{9,8},{10,11... | collective-permute-start | bytes 589832 | tf_op jit(solution)/shard_map/ppermute | solution.py:19
  21.7 2.5 %copy-start = (bf16[2048,1280]{1,0:T(8,128)(2,1)S(1)}, bf16[2048,1280]{1,0:T(8,128)(2,1)}, u32[]{:S(2)}) copy-start(bf16[2048,1280]{1,0:T(8,128)(2,1)} %in_ref.1) | copy-start | bytes 15728644
  24.2 14.8 %slice-start = ((s8[5242880]{0:T(1024)(128)(4,1)}), s8[1048576]{0:T(1024)(128)(4,1)S(1)}, s32[]{:S(2)}) async-start(s8[5242880]{0:T(1024)(128)(4,1)} %bitcast.210), calls=%async_computation | async-start | bytes 2097152
  28.2 1.5 %copy-start.1 = (bf16[4,256,1280]{2,1,0:T(8,128)(2,1)}, bf16[4,256,1280]{2,1,0:T(8,128)(2,1)S(1)}, u32[]{:S(2)}) copy-start(bf16[4,256,1280]{2,1,0:T(8,128)(2,1)S(1)} %get-tuple-element.62) | copy-start | bytes 7864324
  29.7 1.5 %copy-start.3 = (bf16[4,256,1280]{2,1,0:T(8,128)(2,1)}, bf16[4,256,1280]{2,1,0:T(8,128)(2,1)S(1)}, u32[]{:S(2)}) copy-start(bf16[4,256,1280]{2,1,0:T(8,128)(2,1)S(1)} %get-tuple-element.85) | copy-start | bytes 7864324
  31.2 5.6 %collective-permute-start.5 = (bf16[1,384,256]{2,1,0:T(8,128)(2,1)S(1)}, bf16[1,384,256]{2,1,0:T(8,128)(2,1)S(1)}, u32[]{:S(2)}, u32[]{:S(2)}) collective-permute-start(bf16[1,384,256]{2,1,0:T(8,128)(2,1)S(1)} %collective-permute-done), channel_id=1, source_target_pairs={{0,1},{1,0},{2,3},{3,2},{4,5},{5,4},{6,7},{7,6},{8,9},{9,8},{10,11... | collective-permute-start | bytes 589832 | tf_op jit(solution)/shard_map/ppermute | solution.py:19
  34.5 1.7 %collective-permute-start.6 = (bf16[2,384,256]{2,1,0:T(8,128)(2,1)S(1)}, bf16[2,384,256]{2,1,0:T(8,128)(2,1)S(1)}, u32[]{:S(2)}, u32[]{:S(2)}) collective-permute-start(bf16[2,384,256]{2,1,0:T(8,128)(2,1)S(1)} %collective-permute-done.2), channel_id=1, source_target_pairs={{0,1},{1,0},{2,3},{3,2},{4,5},{5,4},{6,7},{7,6},{8,9},{9,8},{10,11... | collective-permute-start | bytes 1179656 | tf_op jit(solution)/shard_map/ppermute | solution.py:19
  34.5 2.3 %collective-permute-start.8 = (bf16[2,384,256]{2,1,0:T(8,128)(2,1)S(1)}, bf16[2,384,256]{2,1,0:T(8,128)(2,1)S(1)}, u32[]{:S(2)}, u32[]{:S(2)}) collective-permute-start(bf16[2,384,256]{2,1,0:T(8,128)(2,1)S(1)} %collective-permute-done.3), channel_id=1, source_target_pairs={{0,1},{1,0},{2,3},{3,2},{4,5},{5,4},{6,7},{7,6},{8,9},{9,8},{10,11... | collective-permute-start | bytes 1179656 | tf_op jit(solution)/shard_map/ppermute | solution.py:19
  35.1 3.9 %slice-start.1 = ((s8[5242880]{0:T(1024)(128)(4,1)}), s8[4194304]{0:T(1024)(128)(4,1)S(1)}, s32[]{:S(2)}) async-start(s8[5242880]{0:T(1024)(128)(4,1)} %bitcast.210), calls=%async_computation.1 | async-start | bytes 8388608
  36.2 1.4 %collective-permute-start.9 = (bf16[1,384,256]{2,1,0:T(8,128)(2,1)S(1)}, bf16[1,384,256]{2,1,0:T(8,128)(2,1)S(1)}, u32[]{:S(2)}, u32[]{:S(2)}) collective-permute-start(bf16[1,384,256]{2,1,0:T(8,128)(2,1)S(1)} %collective-permute-done.1), channel_id=1, source_target_pairs={{0,1},{1,0},{2,3},{3,2},{4,5},{5,4},{6,7},{7,6},{8,9},{9,8},{10,11... | collective-permute-start | bytes 589832 | tf_op jit(solution)/shard_map/ppermute | solution.py:19
  39.0 2.2 %copy-start.6 = (bf16[384,2048]{1,0:T(8,128)(2,1)}, bf16[384,2048]{1,0:T(8,128)(2,1)S(1)}, u32[]{:S(2)}) copy-start(bf16[384,2048]{1,0:T(8,128)(2,1)S(1)} %bitcast_dynamic-update-slice_fusion.8) | copy-start | bytes 4718596
  41.4 13.3 %collective-permute-start.10 = (f16[2,96,1280]{2,1,0:T(8,128)(2,1)S(1)}, f16[2,96,1280]{2,1,0:T(8,128)(2,1)S(1)}, u32[]{:S(2)}, u32[]{:S(2)}) collective-permute-start(f16[2,96,1280]{2,1,0:T(8,128)(2,1)S(1)} %fusion.10), channel_id=1, source_target_pairs={{0,8},{8,0},{16,24},{24,16},{1,9},{9,1},{17,25},{25,17},{2,10},{10... | collective-permute-start | bytes 1474568 | tf_op jit(solution)/shard_map/ppermute | solution.py:19
  45.6 14.2 %collective-permute-start.12 = (f16[2,96,1280]{2,1,0:T(8,128)(2,1)S(1)}, f16[2,96,1280]{2,1,0:T(8,128)(2,1)S(1)}, u32[]{:S(2)}, u32[]{:S(2)}) collective-permute-start(f16[2,96,1280]{2,1,0:T(8,128)(2,1)S(1)} %fusion.9), channel_id=1, source_target_pairs={{0,16},{8,24},{16,0},{24,8},{1,17},{9,25},{17,1},{25,9},{2,18},{10... | collective-permute-start | bytes 1474568 | tf_op jit(solution)/shard_map/ppermute | solution.py:19
  54.8 9.1 %collective-permute-start.11 = (f16[96,1280]{1,0:T(8,128)(2,1)S(1)}, f16[96,1280]{1,0:T(8,128)(2,1)S(1)}, u32[]{:S(2)}, u32[]{:S(2)}) collective-permute-start(f16[96,1280]{1,0:T(8,128)(2,1)S(1)} %fusion.19), channel_id=1, source_target_pairs={{0,16},{8,24},{16,0},{24,8},{1,17},{9,25},{17,1},{25,9},{2,18},{10... | collective-permute-start | bytes 737288 | tf_op jit(solution)/shard_map/ppermute | solution.py:19
  60.0 6.3 %collective-permute-start.13 = (f16[96,1280]{1,0:T(8,128)(2,1)S(1)}, f16[96,1280]{1,0:T(8,128)(2,1)S(1)}, u32[]{:S(2)}, u32[]{:S(2)}) collective-permute-start(f16[96,1280]{1,0:T(8,128)(2,1)S(1)} %fusion.20), channel_id=1, source_target_pairs={{0,8},{8,0},{16,24},{24,16},{1,9},{9,1},{17,25},{25,17},{2,10},{10... | collective-permute-start | bytes 737288 | tf_op jit(solution)/shard_map/ppermute | solution.py:19
  64.0 4.6 %copy-start.9 = (s32[192]{0:T(256)S(1)}, s32[192]{0:T(256)}, u32[]{:S(2)}) copy-start(s32[192]{0:T(256)} %param.9) | copy-start | bytes 2308
  68.6 1.2 collective-permute-start.14
  70.0 3.8 %collective-permute-start.15 = (f32[16,256]{1,0:T(8,128)S(1)}, f32[16,256]{1,0:T(8,128)S(1)}, u32[]{:S(2)}, u32[]{:S(2)}) collective-permute-start(f32[16,256]{1,0:T(8,128)S(1)} %concatenate.69), channel_id=1, source_target_pairs={{0,2},{1,3},{2,0},{3,1},{4,6},{5,7},{6,4},{7,5},{8,10},{9,11},{10,... | collective-permute-start | bytes 49160 | tf_op jit(solution)/shard_map/ppermute | solution.py:19
  74.0 4.9 %collective-permute-start.16 = (f32[16,256]{1,0:T(8,128)S(1)}, f32[16,256]{1,0:T(8,128)S(1)}, u32[]{:S(2)}, u32[]{:S(2)}) collective-permute-start(f32[16,256]{1,0:T(8,128)S(1)} %concatenate.70), channel_id=1, source_target_pairs={{0,4},{1,5},{2,6},{3,7},{4,0},{5,1},{6,2},{7,3},{8,12},{9,13},{10,... | collective-permute-start | bytes 49160 | tf_op jit(solution)/shard_map/ppermute | solution.py:19
  80.9 8.4 %collective-permute-start.17 = (bf16[96,1280]{1,0:T(8,128)(2,1)S(1)}, bf16[96,1280]{1,0:T(8,128)(2,1)S(1)}, u32[]{:S(2)}, u32[]{:S(2)}) collective-permute-start(bf16[96,1280]{1,0:T(8,128)(2,1)S(1)} %grad.2), channel_id=1, source_target_pairs={{0,8},{8,0},{16,24},{24,16},{1,9},{9,1},{17,25},{25,17},{2,10},{10... | collective-permute-start | bytes 737288 | tf_op jit(solution)/shard_map/ppermute | solution.py:19
  81.2 8.8 %collective-permute-start.18 = (bf16[96,1280]{1,0:T(8,128)(2,1)S(1)}, bf16[96,1280]{1,0:T(8,128)(2,1)S(1)}, u32[]{:S(2)}, u32[]{:S(2)}) collective-permute-start(bf16[96,1280]{1,0:T(8,128)(2,1)S(1)} %grad.2), channel_id=1, source_target_pairs={{0,16},{8,24},{16,0},{24,8},{1,17},{9,25},{17,1},{25,9},{2,18},{10... | collective-permute-start | bytes 737288 | tf_op jit(solution)/shard_map/ppermute | solution.py:19
  82.7 10.2 %collective-permute-start.19 = (bf16[96,1280]{1,0:T(8,128)(2,1)S(1)}, bf16[96,1280]{1,0:T(8,128)(2,1)S(1)}, u32[]{:S(2)}, u32[]{:S(2)}) collective-permute-start(bf16[96,1280]{1,0:T(8,128)(2,1)S(1)} %grad.2), channel_id=1, source_target_pairs={{0,24},{8,16},{16,8},{24,0},{1,25},{9,17},{17,9},{25,1},{2,26},{10... | collective-permute-start | bytes 737288 | tf_op jit(solution)/shard_map/ppermute | solution.py:19
  93.0 1.7 %copy-start.4 = (bf16[4,256,1280]{2,1,0:T(8,128)(2,1)S(1)}, bf16[4,256,1280]{2,1,0:T(8,128)(2,1)}, u32[]{:S(2)}) copy-start(bf16[4,256,1280]{2,1,0:T(8,128)(2,1)} %copy-done.3) | copy-start | bytes 7864324
  94.8 5.2 %copy-start.2 = (bf16[4,256,1280]{2,1,0:T(8,128)(2,1)S(1)}, bf16[4,256,1280]{2,1,0:T(8,128)(2,1)}, u32[]{:S(2)}) copy-start(bf16[4,256,1280]{2,1,0:T(8,128)(2,1)} %copy-done.1) | copy-start | bytes 7864324
  96.3 5.2 %collective-permute-start.20 = (bf16[4,256,384]{2,1,0:T(8,128)(2,1)S(1)}, bf16[4,256,384]{2,1,0:T(8,128)(2,1)S(1)}, u32[]{:S(2)}, u32[]{:S(2)}) collective-permute-start(bf16[4,256,384]{2,1,0:T(8,128)(2,1)S(1)} %convolution_convert_fusion.2), channel_id=1, source_target_pairs={{0,1},{1,0},{2,3},{3,2},{4,5},{5,4},{6,7},{7,6},{8,9},{9,8},{10,11... | collective-permute-start | bytes 2359304 | tf_op jit(solution)/shard_map/ppermute | solution.py:19
  96.4 8.8 %collective-permute-start.21 = (bf16[96,1280]{1,0:T(8,128)(2,1)S(1)}, bf16[96,1280]{1,0:T(8,128)(2,1)S(1)}, u32[]{:S(2)}, u32[]{:S(2)}) collective-permute-start(bf16[96,1280]{1,0:T(8,128)(2,1)S(1)} %grad.3), channel_id=1, source_target_pairs={{0,8},{8,0},{16,24},{24,16},{1,9},{9,1},{17,25},{25,17},{2,10},{10... | collective-permute-start | bytes 737288 | tf_op jit(solution)/shard_map/ppermute | solution.py:19
  97.2 13.0 %collective-permute-start.25 = (bf16[96,1280]{1,0:T(8,128)(2,1)S(1)}, bf16[96,1280]{1,0:T(8,128)(2,1)S(1)}, u32[]{:S(2)}, u32[]{:S(2)}) collective-permute-start(bf16[96,1280]{1,0:T(8,128)(2,1)S(1)} %grad.3), channel_id=1, source_target_pairs={{0,24},{8,16},{16,8},{24,0},{1,25},{9,17},{17,9},{25,1},{2,26},{10... | collective-permute-start | bytes 737288 | tf_op jit(solution)/shard_map/ppermute | solution.py:19
  98.5 13.0 %collective-permute-start.24 = (bf16[96,1280]{1,0:T(8,128)(2,1)S(1)}, bf16[96,1280]{1,0:T(8,128)(2,1)S(1)}, u32[]{:S(2)}, u32[]{:S(2)}) collective-permute-start(bf16[96,1280]{1,0:T(8,128)(2,1)S(1)} %grad.3), channel_id=1, source_target_pairs={{0,16},{8,24},{16,0},{24,8},{1,17},{9,25},{17,1},{25,9},{2,18},{10... | collective-permute-start | bytes 737288 | tf_op jit(solution)/shard_map/ppermute | solution.py:19
  105.3 10.0 %collective-permute-start.22 = (bf16[2,128,384]{2,1,0:T(8,128)(2,1)S(1)}, bf16[2,128,384]{2,1,0:T(8,128)(2,1)S(1)}, u32[]{:S(2)}, u32[]{:S(2)}) collective-permute-start(bf16[2,128,384]{2,1,0:T(8,128)(2,1)S(1)} %pad_maximum_fusion.10), channel_id=1, source_target_pairs={{0,2},{1,3},{2,0},{3,1},{4,6},{5,7},{6,4},{7,5},{8,10},{9,11},{10,... | collective-permute-start | bytes 589832 | tf_op jit(solution)/shard_map/ppermute | solution.py:19
  105.9 11.0 %collective-permute-start.23 = (bf16[2,128,384]{2,1,0:T(8,128)(2,1)S(1)}, bf16[2,128,384]{2,1,0:T(8,128)(2,1)S(1)}, u32[]{:S(2)}, u32[]{:S(2)}) collective-permute-start(bf16[2,128,384]{2,1,0:T(8,128)(2,1)S(1)} %pad_maximum_fusion.11), channel_id=1, source_target_pairs={{0,4},{1,5},{2,6},{3,7},{4,0},{5,1},{6,2},{7,3},{8,12},{9,13},{10,... | collective-permute-start | bytes 589832 | tf_op jit(solution)/shard_map/ppermute | solution.py:19
  113.4 3.6 %collective-permute-start.26 = (bf16[4,256,384]{2,1,0:T(8,128)(2,1)S(1)}, bf16[4,256,384]{2,1,0:T(8,128)(2,1)S(1)}, u32[]{:S(2)}, u32[]{:S(2)}) collective-permute-start(bf16[4,256,384]{2,1,0:T(8,128)(2,1)S(1)} %convolution_convert_fusion.1), channel_id=1, source_target_pairs={{0,1},{1,0},{2,3},{3,2},{4,5},{5,4},{6,7},{7,6},{8,9},{9,8},{10,11... | collective-permute-start | bytes 2359304 | tf_op jit(solution)/shard_map/ppermute | solution.py:19
  117.3 15.5 %collective-permute-start.29 = (bf16[2,128,384]{2,1,0:T(8,128)(2,1)S(1)}, bf16[2,128,384]{2,1,0:T(8,128)(2,1)S(1)}, u32[]{:S(2)}, u32[]{:S(2)}) collective-permute-start(bf16[2,128,384]{2,1,0:T(8,128)(2,1)S(1)} %pad_maximum_fusion.12), channel_id=1, source_target_pairs={{0,2},{1,3},{2,0},{3,1},{4,6},{5,7},{6,4},{7,5},{8,10},{9,11},{10,... | collective-permute-start | bytes 589832 | tf_op jit(solution)/shard_map/ppermute | solution.py:19
  117.6 15.2 %collective-permute-start.30 = (bf16[2,128,384]{2,1,0:T(8,128)(2,1)S(1)}, bf16[2,128,384]{2,1,0:T(8,128)(2,1)S(1)}, u32[]{:S(2)}, u32[]{:S(2)}) collective-permute-start(bf16[2,128,384]{2,1,0:T(8,128)(2,1)S(1)} %pad_maximum_fusion.13), channel_id=1, source_target_pairs={{0,4},{1,5},{2,6},{3,7},{4,0},{5,1},{6,2},{7,3},{8,12},{9,13},{10,... | collective-permute-start | bytes 589832 | tf_op jit(solution)/shard_map/ppermute | solution.py:19
  120.4 12.4 %collective-permute-start.27 = (bf16[1,128,384]{2,1,0:T(8,128)(2,1)S(1)}, bf16[1,128,384]{2,1,0:T(8,128)(2,1)S(1)}, u32[]{:S(2)}, u32[]{:S(2)}) collective-permute-start(bf16[1,128,384]{2,1,0:T(8,128)(2,1)S(1)} %bitcast.241), channel_id=1, source_target_pairs={{0,4},{1,5},{2,6},{3,7},{4,0},{5,1},{6,2},{7,3},{8,12},{9,13},{10,... | collective-permute-start | bytes 294920 | tf_op jit(solution)/shard_map/ppermute | solution.py:19
  120.6 12.1 %collective-permute-start.28 = (bf16[1,128,384]{2,1,0:T(8,128)(2,1)S(1)}, bf16[1,128,384]{2,1,0:T(8,128)(2,1)S(1)}, u32[]{:S(2)}, u32[]{:S(2)}) collective-permute-start(bf16[1,128,384]{2,1,0:T(8,128)(2,1)S(1)} %bitcast.240), channel_id=1, source_target_pairs={{0,2},{1,3},{2,0},{3,1},{4,6},{5,7},{6,4},{7,5},{8,10},{9,11},{10,... | collective-permute-start | bytes 294920 | tf_op jit(solution)/shard_map/ppermute | solution.py:19
  122.5 1.4 copy-start.7
  132.9 6.2 %collective-permute-start.31 = (bf16[1,128,384]{2,1,0:T(8,128)(2,1)S(1)}, bf16[1,128,384]{2,1,0:T(8,128)(2,1)S(1)}, u32[]{:S(2)}, u32[]{:S(2)}) collective-permute-start(bf16[1,128,384]{2,1,0:T(8,128)(2,1)S(1)} %fusion.23), channel_id=1, source_target_pairs={{0,4},{1,5},{2,6},{3,7},{4,0},{5,1},{6,2},{7,3},{8,12},{9,13},{10,... | collective-permute-start | bytes 294920 | tf_op jit(solution)/shard_map/ppermute | solution.py:19
  133.1 6.5 %collective-permute-start.32 = (bf16[1,128,384]{2,1,0:T(8,128)(2,1)S(1)}, bf16[1,128,384]{2,1,0:T(8,128)(2,1)S(1)}, u32[]{:S(2)}, u32[]{:S(2)}) collective-permute-start(bf16[1,128,384]{2,1,0:T(8,128)(2,1)S(1)} %fusion.24), channel_id=1, source_target_pairs={{0,2},{1,3},{2,0},{3,1},{4,6},{5,7},{6,4},{7,5},{8,10},{9,11},{10,... | collective-permute-start | bytes 294920 | tf_op jit(solution)/shard_map/ppermute | solution.py:19

commit v6 on v5

--- a/solution.py
+++ b/solution.py
@@ -9,7 +9,7 @@
 
 CHUNKS = 2
 FIRST = 96
-STRIP = 32
+STRIP = 96
 LANES = 128
 LOG2E = 1.4426950408889634
 

time: 141 us -> 140 us (level)
  Pallas kernels: 12 us -> 9.58 us
    pallas_call x2, Pallas kernels: 4.4 us -> 2.66 us  [local_stats(): pl.pallas_call(functools.partial(stats_kernel, heats, pieces), out_shape=...]
  transfers between devices with their start and end apart: 33 -> 33, of which waited for: 24 -> 23; matrix products, arithmetic and copies ran while one was open for 13% -> 13% of each run, Pallas kernels for 6% -> 5%
where the time goes in v6:
time: 140 us
  waiting for transfers between devices  56.8 us (41%)
  starting transfers between devices  35.9 us (26%)
  matrix products  16.9 us (12%)
  local copies, waits for them, and re-layouts  13.9 us (10%)
  Pallas kernels  9.58 us (7%)
  other arithmetic  5.49 us (4%)
  between operations  1.48 us (1%)
    ppermute x33, waiting for transfers between devices, swap(): return lax.ppermute(value, axis, [(k, k ^ mask) for k in range(count)])  56.8 us
    ppermute x33, starting transfers between devices, swap(): return lax.ppermute(value, axis, [(k, k ^ mask) for k in range(count)])  35.9 us
    unnamed x56, local copies, waits for them, and re-layouts  12.1 us
    dot_general x4, matrix products, products(): lax.dot_general(blocks, grad, (((2,), (1,)), ((), ())), preferred_element...  6.33 us
    dot_general x1, matrix products, shards(): lax.dot_general(jnp.concatenate(gathered, axis=0), jnp.concatenate([g.res...  6.17 us
    dot_general x2, matrix products, partial_logits(): partial = jnp.dot(gathered, head, preferred_element_type=jnp.float32)  4.44 us
    pallas_call x1, Pallas kernels, row_blocks(): pl.pallas_call(functools.partial(copy_kernel, rows), out_shape=[block] *...  4 us
    pallas_call x2, Pallas kernels, logit_grad(): pl.pallas_call(functools.partial(grad_kernel, heats, pieces), out_shape=j...  2.93 us
  transfers between devices with their start and end apart: 33, of which 23 were waited for; matrix products, arithmetic and copies ran while one was open for 13% of the time, Pallas kernels for 5%

profile of v6, /device:TPU:0, one launch (start us, length us, event | category | flops | bytes accessed | tf_op | source)
XLA Modules:
  0.0 140.1 jit_solution(8652308426715310415)
XLA Ops:
  0.7 1.2 copy.13
  1.9 3.1 %collective-permute-start = (bf16[1,384,256]{2,1,0:T(8,128)(2,1)S(1)}, bf16[1,384,256]{2,1,0:T(8,128)(2,1)S(1)}, u32[]{:S(2)}, u32[]{:S(2)}) collective-permute-start(bf16[1,384,256]{2,1,0:T(8,128)(2,1)S(1)} %bitcast.227), channel_id=1, source_target_pairs={{0,2},{1,3},{2,0},{3,1},{4,6},{5,7},{6,4},{7,5},{8,10},{9,11},{10,... | collective-permute-start | bytes 589832 | tf_op jit(solution)/shard_map/ppermute | solution.py:19
  5.0 2.6 %collective-permute-start.1 = (bf16[1,384,256]{2,1,0:T(8,128)(2,1)S(1)}, bf16[1,384,256]{2,1,0:T(8,128)(2,1)S(1)}, u32[]{:S(2)}, u32[]{:S(2)}) collective-permute-start(bf16[1,384,256]{2,1,0:T(8,128)(2,1)S(1)} %bitcast.223), channel_id=1, source_target_pairs={{0,4},{1,5},{2,6},{3,7},{4,0},{5,1},{6,2},{7,3},{8,12},{9,13},{10,... | collective-permute-start | bytes 589832 | tf_op jit(solution)/shard_map/ppermute | solution.py:19
  7.6 0.6 fusion.48
  8.2 0.7 broadcast_multiply_fusion
  8.9 1.3 stats.2
  10.1 3.9 %collective-permute-done = bf16[1,384,256]{2,1,0:T(8,128)(2,1)S(1)} collective-permute-done((bf16[1,384,256]{2,1,0:T(8,128)(2,1)S(1)}, bf16[1,384,256]{2,1,0:T(8,128)(2,1)S(1)}, u32[]{:S(2)}, u32[]{:S(2)}) %collective-permute-start) | collective-permute-done | bytes 196640 | tf_op jit(solution)/shard_map/ppermute | solution.py:19
  14.0 2.5 %collective-permute-done.1 = bf16[1,384,256]{2,1,0:T(8,128)(2,1)S(1)} collective-permute-done((bf16[1,384,256]{2,1,0:T(8,128)(2,1)S(1)}, bf16[1,384,256]{2,1,0:T(8,128)(2,1)S(1)}, u32[]{:S(2)}, u32[]{:S(2)}) %collective-permute-start.1) | collective-permute-done | bytes 196640 | tf_op jit(solution)/shard_map/ppermute | solution.py:19
  16.5 0.8 pad_maximum_fusion.6
  17.7 0.8 pad_maximum_fusion.7
  18.4 2.7 %collective-permute-start.3 = (bf16[2,384,256]{2,1,0:T(8,128)(2,1)}, bf16[2,384,256]{2,1,0:T(8,128)(2,1)S(1)}, u32[]{:S(2)}, u32[]{:S(2)}) collective-permute-start(bf16[2,384,256]{2,1,0:T(8,128)(2,1)} %pad_maximum_fusion.7), channel_id=1, source_target_pairs={{0,2},{1,3},{2,0},{3,1},{4,6},{5,7},{6,4},{7,5},{8,10},{9,11},{10,... | collective-permute-start | bytes 1179656 | tf_op jit(solution)/shard_map/ppermute | solution.py:19
  21.7 2.5 %copy-done = bf16[2048,1280]{1,0:T(8,128)(2,1)S(1)} copy-done((bf16[2048,1280]{1,0:T(8,128)(2,1)S(1)}, bf16[2048,1280]{1,0:T(8,128)(2,1)}, u32[]{:S(2)}) %copy-start) | copy-done | bytes 5242904
  24.2 4.0 %row_blocks.1 = (bf16[4,256,1280]{2,1,0:T(8,128)(2,1)S(1)}, bf16[4,256,1280]{2,1,0:T(8,128)(2,1)S(1)}) custom-call(s32[2,4]{1,0:T(2,128)S(1)} %pad_add_fusion.order_ref, bf16[2048,1280]{1,0:T(8,128)(2,1)S(1)} %copy-done), custom_call_target="tpu_custom_call" | custom-call | bytes 10485760 | tf_op jit(solution)/shard_map/row_blocks/pallas_call | solution.py:164
  28.2 1.5 %copy-done.1 = bf16[4,256,1280]{2,1,0:T(8,128)(2,1)} copy-done((bf16[4,256,1280]{2,1,0:T(8,128)(2,1)}, bf16[4,256,1280]{2,1,0:T(8,128)(2,1)S(1)}, u32[]{:S(2)}) %copy-start.1) | copy-done | bytes 2621464
  29.7 1.5 %copy-done.3 = bf16[4,256,1280]{2,1,0:T(8,128)(2,1)} copy-done((bf16[4,256,1280]{2,1,0:T(8,128)(2,1)}, bf16[4,256,1280]{2,1,0:T(8,128)(2,1)S(1)}, u32[]{:S(2)}) %copy-start.3) | copy-done | bytes 2621464
  31.2 3.3 %collective-permute-done.2 = bf16[2,384,256]{2,1,0:T(8,128)(2,1)S(1)} collective-permute-done((bf16[2,384,256]{2,1,0:T(8,128)(2,1)}, bf16[2,384,256]{2,1,0:T(8,128)(2,1)S(1)}, u32[]{:S(2)}, u32[]{:S(2)}) %collective-permute-start.2) | collective-permute-done | bytes 393248 | tf_op jit(solution)/shard_map/ppermute | solution.py:19
  35.1 1.1 collective-permute-done.6
  36.8 0.8 collective-permute-done.9
  37.7 0.9 constant_dynamic-update-slice_fusion.6
  39.0 2.2 %fusion.49 = f32[384,1280]{1,0:T(8,128)S(1)} fusion(bf16[384,2048]{1,0:T(8,128)(2,1)S(1)} %bitcast_dynamic-update-slice_fusion.8, bf16[2048,1280]{1,0:T(8,128)(2,1)S(1)} %bitcast.211), kind=kOutput, calls=%fused_computation.178 | convolution fusion | flops 2013265920 | bytes 8781824 | tf_op jit(solution)/shard_map/dot_general | solution.py:202
  41.4 1.6 %collective-permute-start.10 = (f16[2,96,1280]{2,1,0:T(8,128)(2,1)S(1)}, f16[2,96,1280]{2,1,0:T(8,128)(2,1)S(1)}, u32[]{:S(2)}, u32[]{:S(2)}) collective-permute-start(f16[2,96,1280]{2,1,0:T(8,128)(2,1)S(1)} %fusion.10), channel_id=1, source_target_pairs={{0,8},{8,0},{16,24},{24,16},{1,9},{9,1},{17,25},{25,17},{2,10},{10... | collective-permute-start | bytes 1474568 | tf_op jit(solution)/shard_map/ppermute | solution.py:19
  43.3 2.2 %fusion.50 = f32[384,1280]{1,0:T(8,128)S(1)} fusion(bf16[384,2048]{1,0:T(8,128)(2,1)S(1)} %bitcast_dynamic-update-slice_fusion, bf16[2048,1280]{1,0:T(8,128)(2,1)S(1)} %bitcast.211), kind=kOutput, calls=%fused_computation.179 | convolution fusion | flops 2013265920 | bytes 8781824 | tf_op jit(solution)/shard_map/dot_general | solution.py:202
  45.6 1.6 %collective-permute-start.12 = (f16[2,96,1280]{2,1,0:T(8,128)(2,1)S(1)}, f16[2,96,1280]{2,1,0:T(8,128)(2,1)S(1)}, u32[]{:S(2)}, u32[]{:S(2)}) collective-permute-start(f16[2,96,1280]{2,1,0:T(8,128)(2,1)S(1)} %fusion.9), channel_id=1, source_target_pairs={{0,16},{8,24},{16,0},{24,8},{1,17},{9,25},{17,1},{25,9},{2,18},{10... | collective-permute-start | bytes 1474568 | tf_op jit(solution)/shard_map/ppermute | solution.py:19
  47.2 7.5 %collective-permute-done.10 = f16[2,96,1280]{2,1,0:T(8,128)(2,1)S(1)} collective-permute-done((f16[2,96,1280]{2,1,0:T(8,128)(2,1)S(1)}, f16[2,96,1280]{2,1,0:T(8,128)(2,1)S(1)}, u32[]{:S(2)}, u32[]{:S(2)}) %collective-permute-start.10) | collective-permute-done | bytes 491552 | tf_op jit(solution)/shard_map/ppermute | solution.py:19
  54.8 1.6 %collective-permute-start.11 = (f16[96,1280]{1,0:T(8,128)(2,1)S(1)}, f16[96,1280]{1,0:T(8,128)(2,1)S(1)}, u32[]{:S(2)}, u32[]{:S(2)}) collective-permute-start(f16[96,1280]{1,0:T(8,128)(2,1)S(1)} %fusion.19), channel_id=1, source_target_pairs={{0,16},{8,24},{16,0},{24,8},{1,17},{9,25},{17,1},{25,9},{2,18},{10... | collective-permute-start | bytes 737288 | tf_op jit(solution)/shard_map/ppermute | solution.py:19
  56.4 3.4 %collective-permute-done.12 = f16[2,96,1280]{2,1,0:T(8,128)(2,1)S(1)} collective-permute-done((f16[2,96,1280]{2,1,0:T(8,128)(2,1)S(1)}, f16[2,96,1280]{2,1,0:T(8,128)(2,1)S(1)}, u32[]{:S(2)}, u32[]{:S(2)}) %collective-permute-start.12) | collective-permute-done | bytes 491552 | tf_op jit(solution)/shard_map/ppermute | solution.py:19
  60.3 3.6 %collective-permute-done.11 = f16[96,1280]{1,0:T(8,128)(2,1)S(1)} collective-permute-done((f16[96,1280]{1,0:T(8,128)(2,1)S(1)}, f16[96,1280]{1,0:T(8,128)(2,1)S(1)}, u32[]{:S(2)}, u32[]{:S(2)}) %collective-permute-start.11) | collective-permute-done | bytes 245792 | tf_op jit(solution)/shard_map/ppermute | solution.py:19
  64.0 2.2 %collective-permute-done.13 = f16[96,1280]{1,0:T(8,128)(2,1)S(1)} collective-permute-done((f16[96,1280]{1,0:T(8,128)(2,1)S(1)}, f16[96,1280]{1,0:T(8,128)(2,1)S(1)}, u32[]{:S(2)}, u32[]{:S(2)}) %collective-permute-start.13) | collective-permute-done | bytes 245792 | tf_op jit(solution)/shard_map/ppermute | solution.py:19
  66.3 1.4 stats.3
  67.8 1.1 collective-permute-done.14
  69.1 0.7 collective-permute-start.15
  69.8 0.8 maximum_bitcast_fusion
  70.6 2.4 %collective-permute-done.15 = f32[16,256]{1,0:T(8,128)S(1)} collective-permute-done((f32[16,256]{1,0:T(8,128)S(1)}, f32[16,256]{1,0:T(8,128)S(1)}, u32[]{:S(2)}, u32[]{:S(2)}) %collective-permute-start.15) | collective-permute-done | bytes 16416 | tf_op jit(solution)/shard_map/ppermute | solution.py:19
  73.1 1.7 %collective-permute-start.16 = (f32[16,256]{1,0:T(8,128)S(1)}, f32[16,256]{1,0:T(8,128)S(1)}, u32[]{:S(2)}, u32[]{:S(2)}) collective-permute-start(f32[16,256]{1,0:T(8,128)S(1)} %concatenate.70), channel_id=1, source_target_pairs={{0,4},{1,5},{2,6},{3,7},{4,0},{5,1},{6,2},{7,3},{8,12},{9,13},{10,... | collective-permute-start | bytes 49160 | tf_op jit(solution)/shard_map/ppermute | solution.py:19
  74.9 3.1 %collective-permute-done.16 = f32[16,256]{1,0:T(8,128)S(1)} collective-permute-done((f32[16,256]{1,0:T(8,128)S(1)}, f32[16,256]{1,0:T(8,128)S(1)}, u32[]{:S(2)}, u32[]{:S(2)}) %collective-permute-start.16) | collective-permute-done | bytes 16416 | tf_op jit(solution)/shard_map/ppermute | solution.py:19
  78.2 1.5 %grad.2 = bf16[96,1280]{1,0:T(8,128)(2,1)S(1)} custom-call(f32[2,5]{1,0:T(2,128)S(1)} %pad_maximum_fusion.16.scalars_ref, bf16[192,1280]{1,0:T(8,128)(2,1)S(1)} %copy-done.5, f32[96,1280]{1,0:T(8,128)S(1)} %bitcast_add_fusion.3.refs_0_, f32[16,128]{1,0:T(8,128)S(1)} %get-tuple-element.159.refs_1_), custom_call_target="tpu_custom_call" | custom-call | flops 2949120 | bytes 983040 | tf_op jit(solution)/shard_map/grad/pallas_call | solution.py:119
  80.0 1.5 %collective-permute-start.18 = (bf16[96,1280]{1,0:T(8,128)(2,1)S(1)}, bf16[96,1280]{1,0:T(8,128)(2,1)S(1)}, u32[]{:S(2)}, u32[]{:S(2)}) collective-permute-start(bf16[96,1280]{1,0:T(8,128)(2,1)S(1)} %grad.2), channel_id=1, source_target_pairs={{0,16},{8,24},{16,0},{24,8},{1,17},{9,25},{17,1},{25,9},{2,18},{10... | collective-permute-start | bytes 737288 | tf_op jit(solution)/shard_map/ppermute | solution.py:19
  81.6 1.7 %collective-permute-start.19 = (bf16[96,1280]{1,0:T(8,128)(2,1)S(1)}, bf16[96,1280]{1,0:T(8,128)(2,1)S(1)}, u32[]{:S(2)}, u32[]{:S(2)}) collective-permute-start(bf16[96,1280]{1,0:T(8,128)(2,1)S(1)} %grad.2), channel_id=1, source_target_pairs={{0,24},{8,16},{16,8},{24,0},{1,25},{9,17},{17,9},{25,1},{2,26},{10... | collective-permute-start | bytes 737288 | tf_op jit(solution)/shard_map/ppermute | solution.py:19
  83.3 1.5 %grad.3 = bf16[96,1280]{1,0:T(8,128)(2,1)S(1)} custom-call(f32[2,5]{1,0:T(2,128)S(1)} %pad_maximum_fusion.16.scalars_ref, bf16[192,1280]{1,0:T(8,128)(2,1)S(1)} %copy-done.5, f32[96,1280]{1,0:T(8,128)S(1)} %bitcast_add_fusion.2.refs_1_.refs_0_, f32[16,128]{1,0:T(8,128)S(1)} %get-tuple-element.158.refs_1_), custom_call_target="tpu_custom_call" | custom-call | flops 2949120 | bytes 983040 | tf_op jit(solution)/shard_map/grad/pallas_call | solution.py:119
  84.7 3.4 %collective-permute-done.17 = bf16[96,1280]{1,0:T(8,128)(2,1)S(1)} collective-permute-done((bf16[96,1280]{1,0:T(8,128)(2,1)S(1)}, bf16[96,1280]{1,0:T(8,128)(2,1)S(1)}, u32[]{:S(2)}, u32[]{:S(2)}) %collective-permute-start.17) | collective-permute-done | bytes 245792 | tf_op jit(solution)/shard_map/ppermute | solution.py:19
  88.1 0.7 collective-permute-done.18
  88.9 2.9 %collective-permute-done.19 = bf16[96,1280]{1,0:T(8,128)(2,1)S(1)} collective-permute-done((bf16[96,1280]{1,0:T(8,128)(2,1)S(1)}, bf16[96,1280]{1,0:T(8,128)(2,1)S(1)}, u32[]{:S(2)}, u32[]{:S(2)}) %collective-permute-start.19) | collective-permute-done | bytes 245792 | tf_op jit(solution)/shard_map/ppermute | solution.py:19
  92.0 1.6 %copy-done.4 = bf16[4,256,1280]{2,1,0:T(8,128)(2,1)S(1)} copy-done((bf16[4,256,1280]{2,1,0:T(8,128)(2,1)S(1)}, bf16[4,256,1280]{2,1,0:T(8,128)(2,1)}, u32[]{:S(2)}) %copy-start.4) | copy-done | bytes 2621464
  93.6 1.5 %convolution_convert_fusion.2 = bf16[4,256,384]{2,1,0:T(8,128)(2,1)S(1)} fusion(bf16[4,256,1280]{2,1,0:T(8,128)(2,1)S(1)} %copy-done.4, bf16[384,1280]{1,0:T(8,128)(2,1)S(1)} %pad_maximum_fusion.2), kind=kOutput, calls=%fused_computation.6 | convolution fusion | flops 1007026176 | bytes 4390912 | tf_op jit(solution)/shard_map/dot_general | solution.py:227
  95.2 0.9 collective-permute-start.21
  96.1 1.3 collective-permute-start.25
  97.4 1.4 collective-permute-start.24
  98.8 1.5 %fusion.7 = f32[4,256,384]{2,1,0:T(8,128)S(1)} fusion(bf16[4,256,1280]{2,1,0:T(8,128)(2,1)S(1)} %copy-done.2, bf16[384,1280]{1,0:T(8,128)(2,1)S(1)} %pad_maximum_fusion.2), kind=kOutput, calls=%fused_computation.16 | convolution fusion | flops 1006632960 | bytes 5177344 | tf_op jit(solution)/shard_map/dot_general | solution.py:227
  100.5 3.5 %collective-permute-done.21 = bf16[96,1280]{1,0:T(8,128)(2,1)S(1)} collective-permute-done((bf16[96,1280]{1,0:T(8,128)(2,1)S(1)}, bf16[96,1280]{1,0:T(8,128)(2,1)S(1)}, u32[]{:S(2)}, u32[]{:S(2)}) %collective-permute-start.21) | collective-permute-done | bytes 245792 | tf_op jit(solution)/shard_map/ppermute | solution.py:19
  104.1 0.6 collective-permute-start.22
  104.8 2.6 %collective-permute-start.23 = (bf16[2,128,384]{2,1,0:T(8,128)(2,1)S(1)}, bf16[2,128,384]{2,1,0:T(8,128)(2,1)S(1)}, u32[]{:S(2)}, u32[]{:S(2)}) collective-permute-start(bf16[2,128,384]{2,1,0:T(8,128)(2,1)S(1)} %pad_maximum_fusion.11), channel_id=1, source_target_pairs={{0,4},{1,5},{2,6},{3,7},{4,0},{5,1},{6,2},{7,3},{8,12},{9,13},{10,... | collective-permute-start | bytes 589832 | tf_op jit(solution)/shard_map/ppermute | solution.py:19
  107.4 1.7 %collective-permute-done.25 = bf16[96,1280]{1,0:T(8,128)(2,1)S(1)} collective-permute-done((bf16[96,1280]{1,0:T(8,128)(2,1)S(1)}, bf16[96,1280]{1,0:T(8,128)(2,1)S(1)}, u32[]{:S(2)}, u32[]{:S(2)}) %collective-permute-start.25) | collective-permute-done | bytes 245792 | tf_op jit(solution)/shard_map/ppermute | solution.py:19
  109.0 1.4 collective-permute-done.24
  110.7 1.7 %convolution_convert_fusion.1 = bf16[4,256,384]{2,1,0:T(8,128)(2,1)S(1)} fusion(bf16[4,256,1280]{2,1,0:T(8,128)(2,1)S(1)} %copy-done.4, bf16[384,1280]{1,0:T(8,128)(2,1)S(1)} %pad_maximum_fusion.4), kind=kOutput, calls=%fused_computation.5 | convolution fusion | flops 1007026176 | bytes 4390912 | tf_op jit(solution)/shard_map/dot_general | solution.py:227
  112.5 1.5 %fusion.4 = f32[4,256,384]{2,1,0:T(8,128)S(1)} fusion(bf16[4,256,1280]{2,1,0:T(8,128)(2,1)S(1)} %copy-done.2, bf16[384,1280]{1,0:T(8,128)(2,1)S(1)} %pad_maximum_fusion.4), kind=kOutput, calls=%fused_computation.13 | convolution fusion | flops 1006632960 | bytes 5177344 | tf_op jit(solution)/shard_map/dot_general | solution.py:227
  114.1 1.7 %collective-permute-done.23 = bf16[2,128,384]{2,1,0:T(8,128)(2,1)S(1)} collective-permute-done((bf16[2,128,384]{2,1,0:T(8,128)(2,1)S(1)}, bf16[2,128,384]{2,1,0:T(8,128)(2,1)S(1)}, u32[]{:S(2)}, u32[]{:S(2)}) %collective-permute-start.23) | collective-permute-done | bytes 196640 | tf_op jit(solution)/shard_map/ppermute | solution.py:19
  116.5 2.8 %collective-permute-start.30 = (bf16[2,128,384]{2,1,0:T(8,128)(2,1)S(1)}, bf16[2,128,384]{2,1,0:T(8,128)(2,1)S(1)}, u32[]{:S(2)}, u32[]{:S(2)}) collective-permute-start(bf16[2,128,384]{2,1,0:T(8,128)(2,1)S(1)} %pad_maximum_fusion.13), channel_id=1, source_target_pairs={{0,4},{1,5},{2,6},{3,7},{4,0},{5,1},{6,2},{7,3},{8,12},{9,13},{10,... | collective-permute-start | bytes 589832 | tf_op jit(solution)/shard_map/ppermute | solution.py:19
  119.4 1.8 %collective-permute-start.28 = (bf16[1,128,384]{2,1,0:T(8,128)(2,1)S(1)}, bf16[1,128,384]{2,1,0:T(8,128)(2,1)S(1)}, u32[]{:S(2)}, u32[]{:S(2)}) collective-permute-start(bf16[1,128,384]{2,1,0:T(8,128)(2,1)S(1)} %bitcast.240), channel_id=1, source_target_pairs={{0,2},{1,3},{2,0},{3,1},{4,6},{5,7},{6,4},{7,5},{8,10},{9,11},{10,... | collective-permute-start | bytes 294920 | tf_op jit(solution)/shard_map/ppermute | solution.py:19
  121.5 1.3 copy-done.7
  122.8 6.2 %convolution_convert_fusion = bf16[2048,1280]{1,0:T(8,128)(2,1)} fusion(bf16[768,1280]{1,0:T(8,128)(2,1)S(1)} %bitcast.222, bf16[384,2048]{1,0:T(8,128)(2,1)S(1)} %bitcast_dynamic-update-slice_fusion, bf16[384,2048]{1,0:T(8,128)(2,1)S(1)} %copy-done.7), kind=kOutput, calls=%fused_computation | convolution fusion | flops 4035444736 | bytes 10354688 | tf_op jit(solution)/shard_map/dot_general | solution.py:315
  129.0 2.8 %collective-permute-done.27 = bf16[1,128,384]{2,1,0:T(8,128)(2,1)S(1)} collective-permute-done((bf16[1,128,384]{2,1,0:T(8,128)(2,1)S(1)}, bf16[1,128,384]{2,1,0:T(8,128)(2,1)S(1)}, u32[]{:S(2)}, u32[]{:S(2)}) %collective-permute-start.27) | collective-permute-done | bytes 98336 | tf_op jit(solution)/shard_map/ppermute | solution.py:19
  132.1 2.8 %collective-permute-start.32 = (bf16[1,128,384]{2,1,0:T(8,128)(2,1)S(1)}, bf16[1,128,384]{2,1,0:T(8,128)(2,1)S(1)}, u32[]{:S(2)}, u32[]{:S(2)}) collective-permute-start(bf16[1,128,384]{2,1,0:T(8,128)(2,1)S(1)} %fusion.24), channel_id=1, source_target_pairs={{0,2},{1,3},{2,0},{3,1},{4,6},{5,7},{6,4},{7,5},{8,10},{9,11},{10,... | collective-permute-start | bytes 294920 | tf_op jit(solution)/shard_map/ppermute | solution.py:19
  135.2 3.0 %collective-permute-done.31 = bf16[1,128,384]{2,1,0:T(8,128)(2,1)S(1)} collective-permute-done((bf16[1,128,384]{2,1,0:T(8,128)(2,1)S(1)}, bf16[1,128,384]{2,1,0:T(8,128)(2,1)S(1)}, u32[]{:S(2)}, u32[]{:S(2)}) %collective-permute-start.31) | collective-permute-done | bytes 98336 | tf_op jit(solution)/shard_map/ppermute | solution.py:19
  138.9 1.1 copy.18
  (154 shorter events, 8.2 us)
Async XLA Ops:
  0.6 7.0 %copy-start.8 = (f32[2]{0:T(128)S(1)}, f32[2]{0:T(128)}, u32[]{:S(2)}) copy-start(f32[2]{0:T(128)} %param.11) | copy-start | bytes 28
  0.6 7.6 %copy-start.10 = (f32[4]{0:T(128)S(1)}, f32[4]{0:T(128)}, u32[]{:S(2)}) copy-start(f32[4]{0:T(128)} %param.10) | copy-start | bytes 52
  0.7 8.2 %copy-start.5 = (bf16[192,1280]{1,0:T(8,128)(2,1)S(1)}, bf16[192,1280]{1,0:T(8,128)(2,1)}, u32[]{:S(2)}) copy-start(bf16[192,1280]{1,0:T(8,128)(2,1)} %teacher_ref.3) | copy-start | bytes 1474564
  1.9 12.1 %collective-permute-start = (bf16[1,384,256]{2,1,0:T(8,128)(2,1)S(1)}, bf16[1,384,256]{2,1,0:T(8,128)(2,1)S(1)}, u32[]{:S(2)}, u32[]{:S(2)}) collective-permute-start(bf16[1,384,256]{2,1,0:T(8,128)(2,1)S(1)} %bitcast.227), channel_id=1, source_target_pairs={{0,2},{1,3},{2,0},{3,1},{4,6},{5,7},{6,4},{7,5},{8,10},{9,11},{10,... | collective-permute-start | bytes 589832 | tf_op jit(solution)/shard_map/ppermute | solution.py:19
  5.0 11.5 %collective-permute-start.1 = (bf16[1,384,256]{2,1,0:T(8,128)(2,1)S(1)}, bf16[1,384,256]{2,1,0:T(8,128)(2,1)S(1)}, u32[]{:S(2)}, u32[]{:S(2)}) collective-permute-start(bf16[1,384,256]{2,1,0:T(8,128)(2,1)S(1)} %bitcast.223), channel_id=1, source_target_pairs={{0,4},{1,5},{2,6},{3,7},{4,0},{5,1},{6,2},{7,3},{8,12},{9,13},{10,... | collective-permute-start | bytes 589832 | tf_op jit(solution)/shard_map/ppermute | solution.py:19
  17.3 17.2 %collective-permute-start.2 = (bf16[2,384,256]{2,1,0:T(8,128)(2,1)}, bf16[2,384,256]{2,1,0:T(8,128)(2,1)S(1)}, u32[]{:S(2)}, u32[]{:S(2)}) collective-permute-start(bf16[2,384,256]{2,1,0:T(8,128)(2,1)} %pad_maximum_fusion.6), channel_id=1, source_target_pairs={{0,4},{1,5},{2,6},{3,7},{4,0},{5,1},{6,2},{7,3},{8,12},{9,13},{10,... | collective-permute-start | bytes 1179656 | tf_op jit(solution)/shard_map/ppermute | solution.py:19
  18.4 16.1 %collective-permute-start.3 = (bf16[2,384,256]{2,1,0:T(8,128)(2,1)}, bf16[2,384,256]{2,1,0:T(8,128)(2,1)S(1)}, u32[]{:S(2)}, u32[]{:S(2)}) collective-permute-start(bf16[2,384,256]{2,1,0:T(8,128)(2,1)} %pad_maximum_fusion.7), channel_id=1, source_target_pairs={{0,2},{1,3},{2,0},{3,1},{4,6},{5,7},{6,4},{7,5},{8,10},{9,11},{10,... | collective-permute-start | bytes 1179656 | tf_op jit(solution)/shard_map/ppermute | solution.py:19
  21.1 15.7 %collective-permute-start.4 = (bf16[1,384,256]{2,1,0:T(8,128)(2,1)S(1)}, bf16[1,384,256]{2,1,0:T(8,128)(2,1)}, u32[]{:S(2)}, u32[]{:S(2)}) collective-permute-start(bf16[1,384,256]{2,1,0:T(8,128)(2,1)S(1)} %bitcast.229), channel_id=1, source_target_pairs={{0,1},{1,0},{2,3},{3,2},{4,5},{5,4},{6,7},{7,6},{8,9},{9,8},{10,11... | collective-permute-start | bytes 589832 | tf_op jit(solution)/shard_map/ppermute | solution.py:19
  21.2 15.7 %collective-permute-start.7 = (bf16[1,384,256]{2,1,0:T(8,128)(2,1)S(1)}, bf16[1,384,256]{2,1,0:T(8,128)(2,1)S(1)}, u32[]{:S(2)}, u32[]{:S(2)}) collective-permute-start(bf16[1,384,256]{2,1,0:T(8,128)(2,1)S(1)} %bitcast.225), channel_id=1, source_target_pairs={{0,1},{1,0},{2,3},{3,2},{4,5},{5,4},{6,7},{7,6},{8,9},{9,8},{10,11... | collective-permute-start | bytes 589832 | tf_op jit(solution)/shard_map/ppermute | solution.py:19
  21.7 2.5 %copy-start = (bf16[2048,1280]{1,0:T(8,128)(2,1)S(1)}, bf16[2048,1280]{1,0:T(8,128)(2,1)}, u32[]{:S(2)}) copy-start(bf16[2048,1280]{1,0:T(8,128)(2,1)} %in_ref.1) | copy-start | bytes 15728644
  24.2 14.8 %slice-start = ((s8[5242880]{0:T(1024)(128)(4,1)}), s8[1048576]{0:T(1024)(128)(4,1)S(1)}, s32[]{:S(2)}) async-start(s8[5242880]{0:T(1024)(128)(4,1)} %bitcast.210), calls=%async_computation | async-start | bytes 2097152
  28.2 1.5 %copy-start.1 = (bf16[4,256,1280]{2,1,0:T(8,128)(2,1)}, bf16[4,256,1280]{2,1,0:T(8,128)(2,1)S(1)}, u32[]{:S(2)}) copy-start(bf16[4,256,1280]{2,1,0:T(8,128)(2,1)S(1)} %get-tuple-element.62) | copy-start | bytes 7864324
  29.7 1.5 %copy-start.3 = (bf16[4,256,1280]{2,1,0:T(8,128)(2,1)}, bf16[4,256,1280]{2,1,0:T(8,128)(2,1)S(1)}, u32[]{:S(2)}) copy-start(bf16[4,256,1280]{2,1,0:T(8,128)(2,1)S(1)} %get-tuple-element.85) | copy-start | bytes 7864324
  31.2 5.6 %collective-permute-start.5 = (bf16[1,384,256]{2,1,0:T(8,128)(2,1)S(1)}, bf16[1,384,256]{2,1,0:T(8,128)(2,1)S(1)}, u32[]{:S(2)}, u32[]{:S(2)}) collective-permute-start(bf16[1,384,256]{2,1,0:T(8,128)(2,1)S(1)} %collective-permute-done), channel_id=1, source_target_pairs={{0,1},{1,0},{2,3},{3,2},{4,5},{5,4},{6,7},{7,6},{8,9},{9,8},{10,11... | collective-permute-start | bytes 589832 | tf_op jit(solution)/shard_map/ppermute | solution.py:19
  34.5 1.7 %collective-permute-start.6 = (bf16[2,384,256]{2,1,0:T(8,128)(2,1)S(1)}, bf16[2,384,256]{2,1,0:T(8,128)(2,1)S(1)}, u32[]{:S(2)}, u32[]{:S(2)}) collective-permute-start(bf16[2,384,256]{2,1,0:T(8,128)(2,1)S(1)} %collective-permute-done.2), channel_id=1, source_target_pairs={{0,1},{1,0},{2,3},{3,2},{4,5},{5,4},{6,7},{7,6},{8,9},{9,8},{10,11... | collective-permute-start | bytes 1179656 | tf_op jit(solution)/shard_map/ppermute | solution.py:19
  34.5 2.3 %collective-permute-start.8 = (bf16[2,384,256]{2,1,0:T(8,128)(2,1)S(1)}, bf16[2,384,256]{2,1,0:T(8,128)(2,1)S(1)}, u32[]{:S(2)}, u32[]{:S(2)}) collective-permute-start(bf16[2,384,256]{2,1,0:T(8,128)(2,1)S(1)} %collective-permute-done.3), channel_id=1, source_target_pairs={{0,1},{1,0},{2,3},{3,2},{4,5},{5,4},{6,7},{7,6},{8,9},{9,8},{10,11... | collective-permute-start | bytes 1179656 | tf_op jit(solution)/shard_map/ppermute | solution.py:19
  35.1 3.9 %slice-start.1 = ((s8[5242880]{0:T(1024)(128)(4,1)}), s8[4194304]{0:T(1024)(128)(4,1)S(1)}, s32[]{:S(2)}) async-start(s8[5242880]{0:T(1024)(128)(4,1)} %bitcast.210), calls=%async_computation.1 | async-start | bytes 8388608
  36.2 1.4 %collective-permute-start.9 = (bf16[1,384,256]{2,1,0:T(8,128)(2,1)S(1)}, bf16[1,384,256]{2,1,0:T(8,128)(2,1)S(1)}, u32[]{:S(2)}, u32[]{:S(2)}) collective-permute-start(bf16[1,384,256]{2,1,0:T(8,128)(2,1)S(1)} %collective-permute-done.1), channel_id=1, source_target_pairs={{0,1},{1,0},{2,3},{3,2},{4,5},{5,4},{6,7},{7,6},{8,9},{9,8},{10,11... | collective-permute-start | bytes 589832 | tf_op jit(solution)/shard_map/ppermute | solution.py:19
  39.0 2.2 %copy-start.6 = (bf16[384,2048]{1,0:T(8,128)(2,1)}, bf16[384,2048]{1,0:T(8,128)(2,1)S(1)}, u32[]{:S(2)}) copy-start(bf16[384,2048]{1,0:T(8,128)(2,1)S(1)} %bitcast_dynamic-update-slice_fusion.8) | copy-start | bytes 4718596
  41.4 13.3 %collective-permute-start.10 = (f16[2,96,1280]{2,1,0:T(8,128)(2,1)S(1)}, f16[2,96,1280]{2,1,0:T(8,128)(2,1)S(1)}, u32[]{:S(2)}, u32[]{:S(2)}) collective-permute-start(f16[2,96,1280]{2,1,0:T(8,128)(2,1)S(1)} %fusion.10), channel_id=1, source_target_pairs={{0,8},{8,0},{16,24},{24,16},{1,9},{9,1},{17,25},{25,17},{2,10},{10... | collective-permute-start | bytes 1474568 | tf_op jit(solution)/shard_map/ppermute | solution.py:19
  45.6 14.2 %collective-permute-start.12 = (f16[2,96,1280]{2,1,0:T(8,128)(2,1)S(1)}, f16[2,96,1280]{2,1,0:T(8,128)(2,1)S(1)}, u32[]{:S(2)}, u32[]{:S(2)}) collective-permute-start(f16[2,96,1280]{2,1,0:T(8,128)(2,1)S(1)} %fusion.9), channel_id=1, source_target_pairs={{0,16},{8,24},{16,0},{24,8},{1,17},{9,25},{17,1},{25,9},{2,18},{10... | collective-permute-start | bytes 1474568 | tf_op jit(solution)/shard_map/ppermute | solution.py:19
  54.8 9.1 %collective-permute-start.11 = (f16[96,1280]{1,0:T(8,128)(2,1)S(1)}, f16[96,1280]{1,0:T(8,128)(2,1)S(1)}, u32[]{:S(2)}, u32[]{:S(2)}) collective-permute-start(f16[96,1280]{1,0:T(8,128)(2,1)S(1)} %fusion.19), channel_id=1, source_target_pairs={{0,16},{8,24},{16,0},{24,8},{1,17},{9,25},{17,1},{25,9},{2,18},{10... | collective-permute-start | bytes 737288 | tf_op jit(solution)/shard_map/ppermute | solution.py:19
  60.0 6.3 %collective-permute-start.13 = (f16[96,1280]{1,0:T(8,128)(2,1)S(1)}, f16[96,1280]{1,0:T(8,128)(2,1)S(1)}, u32[]{:S(2)}, u32[]{:S(2)}) collective-permute-start(f16[96,1280]{1,0:T(8,128)(2,1)S(1)} %fusion.20), channel_id=1, source_target_pairs={{0,8},{8,0},{16,24},{24,16},{1,9},{9,1},{17,25},{25,17},{2,10},{10... | collective-permute-start | bytes 737288 | tf_op jit(solution)/shard_map/ppermute | solution.py:19
  64.0 3.7 %copy-start.9 = (s32[192]{0:T(256)S(1)}, s32[192]{0:T(256)}, u32[]{:S(2)}) copy-start(s32[192]{0:T(256)} %param.9) | copy-start | bytes 2308
  67.7 1.2 collective-permute-start.14
  69.1 3.8 %collective-permute-start.15 = (f32[16,256]{1,0:T(8,128)S(1)}, f32[16,256]{1,0:T(8,128)S(1)}, u32[]{:S(2)}, u32[]{:S(2)}) collective-permute-start(f32[16,256]{1,0:T(8,128)S(1)} %concatenate.69), channel_id=1, source_target_pairs={{0,2},{1,3},{2,0},{3,1},{4,6},{5,7},{6,4},{7,5},{8,10},{9,11},{10,... | collective-permute-start | bytes 49160 | tf_op jit(solution)/shard_map/ppermute | solution.py:19
  73.1 4.9 %collective-permute-start.16 = (f32[16,256]{1,0:T(8,128)S(1)}, f32[16,256]{1,0:T(8,128)S(1)}, u32[]{:S(2)}, u32[]{:S(2)}) collective-permute-start(f32[16,256]{1,0:T(8,128)S(1)} %concatenate.70), channel_id=1, source_target_pairs={{0,4},{1,5},{2,6},{3,7},{4,0},{5,1},{6,2},{7,3},{8,12},{9,13},{10,... | collective-permute-start | bytes 49160 | tf_op jit(solution)/shard_map/ppermute | solution.py:19
  79.7 8.4 %collective-permute-start.17 = (bf16[96,1280]{1,0:T(8,128)(2,1)S(1)}, bf16[96,1280]{1,0:T(8,128)(2,1)S(1)}, u32[]{:S(2)}, u32[]{:S(2)}) collective-permute-start(bf16[96,1280]{1,0:T(8,128)(2,1)S(1)} %grad.2), channel_id=1, source_target_pairs={{0,8},{8,0},{16,24},{24,16},{1,9},{9,1},{17,25},{25,17},{2,10},{10... | collective-permute-start | bytes 737288 | tf_op jit(solution)/shard_map/ppermute | solution.py:19
  80.0 8.8 %collective-permute-start.18 = (bf16[96,1280]{1,0:T(8,128)(2,1)S(1)}, bf16[96,1280]{1,0:T(8,128)(2,1)S(1)}, u32[]{:S(2)}, u32[]{:S(2)}) collective-permute-start(bf16[96,1280]{1,0:T(8,128)(2,1)S(1)} %grad.2), channel_id=1, source_target_pairs={{0,16},{8,24},{16,0},{24,8},{1,17},{9,25},{17,1},{25,9},{2,18},{10... | collective-permute-start | bytes 737288 | tf_op jit(solution)/shard_map/ppermute | solution.py:19
  81.6 10.2 %collective-permute-start.19 = (bf16[96,1280]{1,0:T(8,128)(2,1)S(1)}, bf16[96,1280]{1,0:T(8,128)(2,1)S(1)}, u32[]{:S(2)}, u32[]{:S(2)}) collective-permute-start(bf16[96,1280]{1,0:T(8,128)(2,1)S(1)} %grad.2), channel_id=1, source_target_pairs={{0,24},{8,16},{16,8},{24,0},{1,25},{9,17},{17,9},{25,1},{2,26},{10... | collective-permute-start | bytes 737288 | tf_op jit(solution)/shard_map/ppermute | solution.py:19
  91.9 1.7 %copy-start.4 = (bf16[4,256,1280]{2,1,0:T(8,128)(2,1)S(1)}, bf16[4,256,1280]{2,1,0:T(8,128)(2,1)}, u32[]{:S(2)}) copy-start(bf16[4,256,1280]{2,1,0:T(8,128)(2,1)} %copy-done.3) | copy-start | bytes 7864324
  93.6 5.2 %copy-start.2 = (bf16[4,256,1280]{2,1,0:T(8,128)(2,1)S(1)}, bf16[4,256,1280]{2,1,0:T(8,128)(2,1)}, u32[]{:S(2)}) copy-start(bf16[4,256,1280]{2,1,0:T(8,128)(2,1)} %copy-done.1) | copy-start | bytes 7864324
  95.1 5.2 %collective-permute-start.20 = (bf16[4,256,384]{2,1,0:T(8,128)(2,1)S(1)}, bf16[4,256,384]{2,1,0:T(8,128)(2,1)S(1)}, u32[]{:S(2)}, u32[]{:S(2)}) collective-permute-start(bf16[4,256,384]{2,1,0:T(8,128)(2,1)S(1)} %convolution_convert_fusion.2), channel_id=1, source_target_pairs={{0,1},{1,0},{2,3},{3,2},{4,5},{5,4},{6,7},{7,6},{8,9},{9,8},{10,11... | collective-permute-start | bytes 2359304 | tf_op jit(solution)/shard_map/ppermute | solution.py:19
  95.2 8.8 %collective-permute-start.21 = (bf16[96,1280]{1,0:T(8,128)(2,1)S(1)}, bf16[96,1280]{1,0:T(8,128)(2,1)S(1)}, u32[]{:S(2)}, u32[]{:S(2)}) collective-permute-start(bf16[96,1280]{1,0:T(8,128)(2,1)S(1)} %grad.3), channel_id=1, source_target_pairs={{0,8},{8,0},{16,24},{24,16},{1,9},{9,1},{17,25},{25,17},{2,10},{10... | collective-permute-start | bytes 737288 | tf_op jit(solution)/shard_map/ppermute | solution.py:19
  96.1 13.0 %collective-permute-start.25 = (bf16[96,1280]{1,0:T(8,128)(2,1)S(1)}, bf16[96,1280]{1,0:T(8,128)(2,1)S(1)}, u32[]{:S(2)}, u32[]{:S(2)}) collective-permute-start(bf16[96,1280]{1,0:T(8,128)(2,1)S(1)} %grad.3), channel_id=1, source_target_pairs={{0,24},{8,16},{16,8},{24,0},{1,25},{9,17},{17,9},{25,1},{2,26},{10... | collective-permute-start | bytes 737288 | tf_op jit(solution)/shard_map/ppermute | solution.py:19
  97.4 13.0 %collective-permute-start.24 = (bf16[96,1280]{1,0:T(8,128)(2,1)S(1)}, bf16[96,1280]{1,0:T(8,128)(2,1)S(1)}, u32[]{:S(2)}, u32[]{:S(2)}) collective-permute-start(bf16[96,1280]{1,0:T(8,128)(2,1)S(1)} %grad.3), channel_id=1, source_target_pairs={{0,16},{8,24},{16,0},{24,8},{1,17},{9,25},{17,1},{25,9},{2,18},{10... | collective-permute-start | bytes 737288 | tf_op jit(solution)/shard_map/ppermute | solution.py:19
  104.1 10.0 %collective-permute-start.22 = (bf16[2,128,384]{2,1,0:T(8,128)(2,1)S(1)}, bf16[2,128,384]{2,1,0:T(8,128)(2,1)S(1)}, u32[]{:S(2)}, u32[]{:S(2)}) collective-permute-start(bf16[2,128,384]{2,1,0:T(8,128)(2,1)S(1)} %pad_maximum_fusion.10), channel_id=1, source_target_pairs={{0,2},{1,3},{2,0},{3,1},{4,6},{5,7},{6,4},{7,5},{8,10},{9,11},{10,... | collective-permute-start | bytes 589832 | tf_op jit(solution)/shard_map/ppermute | solution.py:19
  104.8 11.0 %collective-permute-start.23 = (bf16[2,128,384]{2,1,0:T(8,128)(2,1)S(1)}, bf16[2,128,384]{2,1,0:T(8,128)(2,1)S(1)}, u32[]{:S(2)}, u32[]{:S(2)}) collective-permute-start(bf16[2,128,384]{2,1,0:T(8,128)(2,1)S(1)} %pad_maximum_fusion.11), channel_id=1, source_target_pairs={{0,4},{1,5},{2,6},{3,7},{4,0},{5,1},{6,2},{7,3},{8,12},{9,13},{10,... | collective-permute-start | bytes 589832 | tf_op jit(solution)/shard_map/ppermute | solution.py:19
  112.4 3.4 %collective-permute-start.26 = (bf16[4,256,384]{2,1,0:T(8,128)(2,1)S(1)}, bf16[4,256,384]{2,1,0:T(8,128)(2,1)S(1)}, u32[]{:S(2)}, u32[]{:S(2)}) collective-permute-start(bf16[4,256,384]{2,1,0:T(8,128)(2,1)S(1)} %convolution_convert_fusion.1), channel_id=1, source_target_pairs={{0,1},{1,0},{2,3},{3,2},{4,5},{5,4},{6,7},{7,6},{8,9},{9,8},{10,11... | collective-permute-start | bytes 2359304 | tf_op jit(solution)/shard_map/ppermute | solution.py:19
  116.1 15.7 %collective-permute-start.29 = (bf16[2,128,384]{2,1,0:T(8,128)(2,1)S(1)}, bf16[2,128,384]{2,1,0:T(8,128)(2,1)S(1)}, u32[]{:S(2)}, u32[]{:S(2)}) collective-permute-start(bf16[2,128,384]{2,1,0:T(8,128)(2,1)S(1)} %pad_maximum_fusion.12), channel_id=1, source_target_pairs={{0,2},{1,3},{2,0},{3,1},{4,6},{5,7},{6,4},{7,5},{8,10},{9,11},{10,... | collective-permute-start | bytes 589832 | tf_op jit(solution)/shard_map/ppermute | solution.py:19
  116.5 15.4 %collective-permute-start.30 = (bf16[2,128,384]{2,1,0:T(8,128)(2,1)S(1)}, bf16[2,128,384]{2,1,0:T(8,128)(2,1)S(1)}, u32[]{:S(2)}, u32[]{:S(2)}) collective-permute-start(bf16[2,128,384]{2,1,0:T(8,128)(2,1)S(1)} %pad_maximum_fusion.13), channel_id=1, source_target_pairs={{0,4},{1,5},{2,6},{3,7},{4,0},{5,1},{6,2},{7,3},{8,12},{9,13},{10,... | collective-permute-start | bytes 589832 | tf_op jit(solution)/shard_map/ppermute | solution.py:19
  119.2 12.5 %collective-permute-start.27 = (bf16[1,128,384]{2,1,0:T(8,128)(2,1)S(1)}, bf16[1,128,384]{2,1,0:T(8,128)(2,1)S(1)}, u32[]{:S(2)}, u32[]{:S(2)}) collective-permute-start(bf16[1,128,384]{2,1,0:T(8,128)(2,1)S(1)} %bitcast.241), channel_id=1, source_target_pairs={{0,4},{1,5},{2,6},{3,7},{4,0},{5,1},{6,2},{7,3},{8,12},{9,13},{10,... | collective-permute-start | bytes 294920 | tf_op jit(solution)/shard_map/ppermute | solution.py:19
  119.4 12.3 %collective-permute-start.28 = (bf16[1,128,384]{2,1,0:T(8,128)(2,1)S(1)}, bf16[1,128,384]{2,1,0:T(8,128)(2,1)S(1)}, u32[]{:S(2)}, u32[]{:S(2)}) collective-permute-start(bf16[1,128,384]{2,1,0:T(8,128)(2,1)S(1)} %bitcast.240), channel_id=1, source_target_pairs={{0,2},{1,3},{2,0},{3,1},{4,6},{5,7},{6,4},{7,5},{8,10},{9,11},{10,... | collective-permute-start | bytes 294920 | tf_op jit(solution)/shard_map/ppermute | solution.py:19
  121.4 1.4 %copy-start.7 = (bf16[384,2048]{1,0:T(8,128)(2,1)S(1)}, bf16[384,2048]{1,0:T(8,128)(2,1)}, u32[]{:S(2)}) copy-start(bf16[384,2048]{1,0:T(8,128)(2,1)} %copy-done.6) | copy-start | bytes 4718596
  131.9 6.3 %collective-permute-start.31 = (bf16[1,128,384]{2,1,0:T(8,128)(2,1)S(1)}, bf16[1,128,384]{2,1,0:T(8,128)(2,1)S(1)}, u32[]{:S(2)}, u32[]{:S(2)}) collective-permute-start(bf16[1,128,384]{2,1,0:T(8,128)(2,1)S(1)} %fusion.23), channel_id=1, source_target_pairs={{0,4},{1,5},{2,6},{3,7},{4,0},{5,1},{6,2},{7,3},{8,12},{9,13},{10,... | collective-permute-start | bytes 294920 | tf_op jit(solution)/shard_map/ppermute | solution.py:19
  132.1 6.5 %collective-permute-start.32 = (bf16[1,128,384]{2,1,0:T(8,128)(2,1)S(1)}, bf16[1,128,384]{2,1,0:T(8,128)(2,1)S(1)}, u32[]{:S(2)}, u32[]{:S(2)}) collective-permute-start(bf16[1,128,384]{2,1,0:T(8,128)(2,1)S(1)} %fusion.24), channel_id=1, source_target_pairs={{0,2},{1,3},{2,0},{3,1},{4,6},{5,7},{6,4},{7,5},{8,10},{9,11},{10,... | collective-permute-start | bytes 294920 | tf_op jit(solution)/shard_map/ppermute | solution.py:19

commit v7 on v6

--- a/solution.py
+++ b/solution.py
@@ -285,6 +285,7 @@
         grads.append(logit_grad(first, last, logits, teacher, stats, scalars))
 
     def crossing(c):
+        arrived[c] = lax.optimization_barrier(arrived[c])
         found = jnp.stack([grads[c]] + [arrived[c][r] for r in range(1, count_dp)])
         grad_all = jnp.concatenate([pick(found, me_dp ^ n) for n in range(count_dp)])
         grad_all = lax.optimization_barrier(grad_all)
@@ -296,7 +297,9 @@
         return {2 * k: keep[k] + crossed[k].astype(jnp.float32) for k in range(count_vocab // 2)}
 
     arrived = [None, None]
-    exchange = lambda grad: {r: swap(grad, "dp", r) for r in range(1, count_dp)}
+    def exchange(grad):
+        return {r: swap(grad, "dp", r) for r in range(1, count_dp)}
+
     arrived[0] = exchange(grads[0])
     grads[1], arrived[0] = lax.optimization_barrier((grads[1], arrived[0]))
     arrived[1] = exchange(grads[1])

time: 140 us -> 139 us (level)
  no operation moved by 1% of the time
where the time goes in v7:
time: 139 us
  waiting for transfers between devices  56.2 us (40%)
  starting transfers between devices  35.5 us (26%)
  matrix products  16.9 us (12%)
  local copies, waits for them, and re-layouts  13.9 us (10%)
  Pallas kernels  9.58 us (7%)
  other arithmetic  5.49 us (4%)
  between operations  1.48 us (1%)
    ppermute x33, waiting for transfers between devices, swap(): return lax.ppermute(value, axis, [(k, k ^ mask) for k in range(count)])  56.2 us
    ppermute x33, starting transfers between devices, swap(): return lax.ppermute(value, axis, [(k, k ^ mask) for k in range(count)])  35.5 us
    unnamed x56, local copies, waits for them, and re-layouts  12.1 us
    dot_general x4, matrix products, products(): lax.dot_general(blocks, grad, (((2,), (1,)), ((), ())), preferred_element...  6.33 us
    dot_general x1, matrix products, shards(): lax.dot_general(jnp.concatenate(gathered, axis=0), jnp.concatenate([g.res...  6.17 us
    dot_general x2, matrix products, partial_logits(): partial = jnp.dot(gathered, head, preferred_element_type=jnp.float32)  4.44 us
    pallas_call x1, Pallas kernels, row_blocks(): pl.pallas_call(functools.partial(copy_kernel, rows), out_shape=[block] *...  4 us
    pallas_call x2, Pallas kernels, logit_grad(): pl.pallas_call(functools.partial(grad_kernel, heats, pieces), out_shape=j...  2.93 us
  transfers between devices with their start and end apart: 33, of which 23 were waited for; matrix products, arithmetic and copies ran while one was open for 13% of the time, Pallas kernels for 5%

profile of v7, /device:TPU:0, one launch (start us, length us, event | category | flops | bytes accessed | tf_op | source)
XLA Modules:
  0.0 139.1 jit_solution(13487182425063416859)
XLA Ops:
  0.7 1.2 copy.13
  1.9 3.1 %collective-permute-start = (bf16[1,384,256]{2,1,0:T(8,128)(2,1)S(1)}, bf16[1,384,256]{2,1,0:T(8,128)(2,1)S(1)}, u32[]{:S(2)}, u32[]{:S(2)}) collective-permute-start(bf16[1,384,256]{2,1,0:T(8,128)(2,1)S(1)} %bitcast.227), channel_id=1, source_target_pairs={{0,2},{1,3},{2,0},{3,1},{4,6},{5,7},{6,4},{7,5},{8,10},{9,11},{10,... | collective-permute-start | bytes 589832 | tf_op jit(solution)/shard_map/ppermute | solution.py:19
  5.0 2.6 %collective-permute-start.1 = (bf16[1,384,256]{2,1,0:T(8,128)(2,1)S(1)}, bf16[1,384,256]{2,1,0:T(8,128)(2,1)S(1)}, u32[]{:S(2)}, u32[]{:S(2)}) collective-permute-start(bf16[1,384,256]{2,1,0:T(8,128)(2,1)S(1)} %bitcast.223), channel_id=1, source_target_pairs={{0,4},{1,5},{2,6},{3,7},{4,0},{5,1},{6,2},{7,3},{8,12},{9,13},{10,... | collective-permute-start | bytes 589832 | tf_op jit(solution)/shard_map/ppermute | solution.py:19
  7.6 0.6 fusion.48
  8.2 0.7 broadcast_multiply_fusion
  8.9 1.3 stats.2
  10.1 3.9 %collective-permute-done = bf16[1,384,256]{2,1,0:T(8,128)(2,1)S(1)} collective-permute-done((bf16[1,384,256]{2,1,0:T(8,128)(2,1)S(1)}, bf16[1,384,256]{2,1,0:T(8,128)(2,1)S(1)}, u32[]{:S(2)}, u32[]{:S(2)}) %collective-permute-start) | collective-permute-done | bytes 196640 | tf_op jit(solution)/shard_map/ppermute | solution.py:19
  14.0 2.5 %collective-permute-done.1 = bf16[1,384,256]{2,1,0:T(8,128)(2,1)S(1)} collective-permute-done((bf16[1,384,256]{2,1,0:T(8,128)(2,1)S(1)}, bf16[1,384,256]{2,1,0:T(8,128)(2,1)S(1)}, u32[]{:S(2)}, u32[]{:S(2)}) %collective-permute-start.1) | collective-permute-done | bytes 196640 | tf_op jit(solution)/shard_map/ppermute | solution.py:19
  16.5 0.8 pad_maximum_fusion.6
  17.7 0.8 pad_maximum_fusion.7
  18.4 2.7 %collective-permute-start.3 = (bf16[2,384,256]{2,1,0:T(8,128)(2,1)}, bf16[2,384,256]{2,1,0:T(8,128)(2,1)S(1)}, u32[]{:S(2)}, u32[]{:S(2)}) collective-permute-start(bf16[2,384,256]{2,1,0:T(8,128)(2,1)} %pad_maximum_fusion.7), channel_id=1, source_target_pairs={{0,2},{1,3},{2,0},{3,1},{4,6},{5,7},{6,4},{7,5},{8,10},{9,11},{10,... | collective-permute-start | bytes 1179656 | tf_op jit(solution)/shard_map/ppermute | solution.py:19
  21.7 2.5 %copy-done = bf16[2048,1280]{1,0:T(8,128)(2,1)S(1)} copy-done((bf16[2048,1280]{1,0:T(8,128)(2,1)S(1)}, bf16[2048,1280]{1,0:T(8,128)(2,1)}, u32[]{:S(2)}) %copy-start) | copy-done | bytes 5242904
  24.2 4.0 %row_blocks.1 = (bf16[4,256,1280]{2,1,0:T(8,128)(2,1)S(1)}, bf16[4,256,1280]{2,1,0:T(8,128)(2,1)S(1)}) custom-call(s32[2,4]{1,0:T(2,128)S(1)} %pad_add_fusion.order_ref, bf16[2048,1280]{1,0:T(8,128)(2,1)S(1)} %copy-done), custom_call_target="tpu_custom_call" | custom-call | bytes 10485760 | tf_op jit(solution)/shard_map/row_blocks/pallas_call | solution.py:164
  28.2 1.5 %copy-done.1 = bf16[4,256,1280]{2,1,0:T(8,128)(2,1)} copy-done((bf16[4,256,1280]{2,1,0:T(8,128)(2,1)}, bf16[4,256,1280]{2,1,0:T(8,128)(2,1)S(1)}, u32[]{:S(2)}) %copy-start.1) | copy-done | bytes 2621464
  29.7 1.5 %copy-done.3 = bf16[4,256,1280]{2,1,0:T(8,128)(2,1)} copy-done((bf16[4,256,1280]{2,1,0:T(8,128)(2,1)}, bf16[4,256,1280]{2,1,0:T(8,128)(2,1)S(1)}, u32[]{:S(2)}) %copy-start.3) | copy-done | bytes 2621464
  31.2 3.3 %collective-permute-done.2 = bf16[2,384,256]{2,1,0:T(8,128)(2,1)S(1)} collective-permute-done((bf16[2,384,256]{2,1,0:T(8,128)(2,1)}, bf16[2,384,256]{2,1,0:T(8,128)(2,1)S(1)}, u32[]{:S(2)}, u32[]{:S(2)}) %collective-permute-start.2) | collective-permute-done | bytes 393248 | tf_op jit(solution)/shard_map/ppermute | solution.py:19
  35.1 1.1 collective-permute-done.6
  36.8 0.8 collective-permute-done.9
  37.7 0.9 constant_dynamic-update-slice_fusion.6
  39.0 2.2 %fusion.49 = f32[384,1280]{1,0:T(8,128)S(1)} fusion(bf16[384,2048]{1,0:T(8,128)(2,1)S(1)} %bitcast_dynamic-update-slice_fusion.8, bf16[2048,1280]{1,0:T(8,128)(2,1)S(1)} %bitcast.211), kind=kOutput, calls=%fused_computation.178 | convolution fusion | flops 2013265920 | bytes 8781824 | tf_op jit(solution)/shard_map/dot_general | solution.py:202
  41.4 1.6 %collective-permute-start.10 = (f16[2,96,1280]{2,1,0:T(8,128)(2,1)S(1)}, f16[2,96,1280]{2,1,0:T(8,128)(2,1)S(1)}, u32[]{:S(2)}, u32[]{:S(2)}) collective-permute-start(f16[2,96,1280]{2,1,0:T(8,128)(2,1)S(1)} %fusion.10), channel_id=1, source_target_pairs={{0,8},{8,0},{16,24},{24,16},{1,9},{9,1},{17,25},{25,17},{2,10},{10... | collective-permute-start | bytes 1474568 | tf_op jit(solution)/shard_map/ppermute | solution.py:19
  43.3 2.2 %fusion.50 = f32[384,1280]{1,0:T(8,128)S(1)} fusion(bf16[384,2048]{1,0:T(8,128)(2,1)S(1)} %bitcast_dynamic-update-slice_fusion, bf16[2048,1280]{1,0:T(8,128)(2,1)S(1)} %bitcast.211), kind=kOutput, calls=%fused_computation.179 | convolution fusion | flops 2013265920 | bytes 8781824 | tf_op jit(solution)/shard_map/dot_general | solution.py:202
  45.6 1.6 %collective-permute-start.12 = (f16[2,96,1280]{2,1,0:T(8,128)(2,1)S(1)}, f16[2,96,1280]{2,1,0:T(8,128)(2,1)S(1)}, u32[]{:S(2)}, u32[]{:S(2)}) collective-permute-start(f16[2,96,1280]{2,1,0:T(8,128)(2,1)S(1)} %fusion.9), channel_id=1, source_target_pairs={{0,16},{8,24},{16,0},{24,8},{1,17},{9,25},{17,1},{25,9},{2,18},{10... | collective-permute-start | bytes 1474568 | tf_op jit(solution)/shard_map/ppermute | solution.py:19
  47.2 7.5 %collective-permute-done.10 = f16[2,96,1280]{2,1,0:T(8,128)(2,1)S(1)} collective-permute-done((f16[2,96,1280]{2,1,0:T(8,128)(2,1)S(1)}, f16[2,96,1280]{2,1,0:T(8,128)(2,1)S(1)}, u32[]{:S(2)}, u32[]{:S(2)}) %collective-permute-start.10) | collective-permute-done | bytes 491552 | tf_op jit(solution)/shard_map/ppermute | solution.py:19
  54.8 1.6 %collective-permute-start.11 = (f16[96,1280]{1,0:T(8,128)(2,1)S(1)}, f16[96,1280]{1,0:T(8,128)(2,1)S(1)}, u32[]{:S(2)}, u32[]{:S(2)}) collective-permute-start(f16[96,1280]{1,0:T(8,128)(2,1)S(1)} %fusion.19), channel_id=1, source_target_pairs={{0,16},{8,24},{16,0},{24,8},{1,17},{9,25},{17,1},{25,9},{2,18},{10... | collective-permute-start | bytes 737288 | tf_op jit(solution)/shard_map/ppermute | solution.py:19
  56.4 3.4 %collective-permute-done.12 = f16[2,96,1280]{2,1,0:T(8,128)(2,1)S(1)} collective-permute-done((f16[2,96,1280]{2,1,0:T(8,128)(2,1)S(1)}, f16[2,96,1280]{2,1,0:T(8,128)(2,1)S(1)}, u32[]{:S(2)}, u32[]{:S(2)}) %collective-permute-start.12) | collective-permute-done | bytes 491552 | tf_op jit(solution)/shard_map/ppermute | solution.py:19
  60.3 3.6 %collective-permute-done.11 = f16[96,1280]{1,0:T(8,128)(2,1)S(1)} collective-permute-done((f16[96,1280]{1,0:T(8,128)(2,1)S(1)}, f16[96,1280]{1,0:T(8,128)(2,1)S(1)}, u32[]{:S(2)}, u32[]{:S(2)}) %collective-permute-start.11) | collective-permute-done | bytes 245792 | tf_op jit(solution)/shard_map/ppermute | solution.py:19
  64.0 2.2 %collective-permute-done.13 = f16[96,1280]{1,0:T(8,128)(2,1)S(1)} collective-permute-done((f16[96,1280]{1,0:T(8,128)(2,1)S(1)}, f16[96,1280]{1,0:T(8,128)(2,1)S(1)}, u32[]{:S(2)}, u32[]{:S(2)}) %collective-permute-start.13) | collective-permute-done | bytes 245792 | tf_op jit(solution)/shard_map/ppermute | solution.py:19
  66.3 1.4 stats.3
  67.8 1.1 collective-permute-done.14
  69.1 0.7 collective-permute-start.15
  69.8 0.8 maximum_bitcast_fusion
  70.6 2.4 %collective-permute-done.15 = f32[16,256]{1,0:T(8,128)S(1)} collective-permute-done((f32[16,256]{1,0:T(8,128)S(1)}, f32[16,256]{1,0:T(8,128)S(1)}, u32[]{:S(2)}, u32[]{:S(2)}) %collective-permute-start.15) | collective-permute-done | bytes 16416 | tf_op jit(solution)/shard_map/ppermute | solution.py:19
  73.1 1.7 %collective-permute-start.16 = (f32[16,256]{1,0:T(8,128)S(1)}, f32[16,256]{1,0:T(8,128)S(1)}, u32[]{:S(2)}, u32[]{:S(2)}) collective-permute-start(f32[16,256]{1,0:T(8,128)S(1)} %concatenate.70), channel_id=1, source_target_pairs={{0,4},{1,5},{2,6},{3,7},{4,0},{5,1},{6,2},{7,3},{8,12},{9,13},{10,... | collective-permute-start | bytes 49160 | tf_op jit(solution)/shard_map/ppermute | solution.py:19
  74.9 3.1 %collective-permute-done.16 = f32[16,256]{1,0:T(8,128)S(1)} collective-permute-done((f32[16,256]{1,0:T(8,128)S(1)}, f32[16,256]{1,0:T(8,128)S(1)}, u32[]{:S(2)}, u32[]{:S(2)}) %collective-permute-start.16) | collective-permute-done | bytes 16416 | tf_op jit(solution)/shard_map/ppermute | solution.py:19
  78.2 1.5 %grad.2 = bf16[96,1280]{1,0:T(8,128)(2,1)S(1)} custom-call(f32[2,5]{1,0:T(2,128)S(1)} %pad_maximum_fusion.16.scalars_ref, bf16[192,1280]{1,0:T(8,128)(2,1)S(1)} %copy-done.5, f32[96,1280]{1,0:T(8,128)S(1)} %bitcast_add_fusion.3.refs_0_, f32[16,128]{1,0:T(8,128)S(1)} %get-tuple-element.171.refs_1_), custom_call_target="tpu_custom_call" | custom-call | flops 2949120 | bytes 983040 | tf_op jit(solution)/shard_map/grad/pallas_call | solution.py:119
  80.0 1.5 %collective-permute-start.18 = (bf16[96,1280]{1,0:T(8,128)(2,1)S(1)}, bf16[96,1280]{1,0:T(8,128)(2,1)S(1)}, u32[]{:S(2)}, u32[]{:S(2)}) collective-permute-start(bf16[96,1280]{1,0:T(8,128)(2,1)S(1)} %grad.2), channel_id=1, source_target_pairs={{0,16},{8,24},{16,0},{24,8},{1,17},{9,25},{17,1},{25,9},{2,18},{10... | collective-permute-start | bytes 737288 | tf_op jit(solution)/shard_map/ppermute | solution.py:19
  81.6 1.7 %collective-permute-start.19 = (bf16[96,1280]{1,0:T(8,128)(2,1)S(1)}, bf16[96,1280]{1,0:T(8,128)(2,1)S(1)}, u32[]{:S(2)}, u32[]{:S(2)}) collective-permute-start(bf16[96,1280]{1,0:T(8,128)(2,1)S(1)} %grad.2), channel_id=1, source_target_pairs={{0,24},{8,16},{16,8},{24,0},{1,25},{9,17},{17,9},{25,1},{2,26},{10... | collective-permute-start | bytes 737288 | tf_op jit(solution)/shard_map/ppermute | solution.py:19
  83.3 1.5 %grad.3 = bf16[96,1280]{1,0:T(8,128)(2,1)S(1)} custom-call(f32[2,5]{1,0:T(2,128)S(1)} %pad_maximum_fusion.16.scalars_ref, bf16[192,1280]{1,0:T(8,128)(2,1)S(1)} %copy-done.5, f32[96,1280]{1,0:T(8,128)S(1)} %bitcast_add_fusion.2.refs_1_.refs_0_, f32[16,128]{1,0:T(8,128)S(1)} %get-tuple-element.170.refs_1_), custom_call_target="tpu_custom_call" | custom-call | flops 2949120 | bytes 983040 | tf_op jit(solution)/shard_map/grad/pallas_call | solution.py:119
  84.7 3.4 %collective-permute-done.17 = bf16[96,1280]{1,0:T(8,128)(2,1)S(1)} collective-permute-done((bf16[96,1280]{1,0:T(8,128)(2,1)S(1)}, bf16[96,1280]{1,0:T(8,128)(2,1)S(1)}, u32[]{:S(2)}, u32[]{:S(2)}) %collective-permute-start.17) | collective-permute-done | bytes 245792 | tf_op jit(solution)/shard_map/ppermute | solution.py:19
  88.1 0.7 collective-permute-done.18
  88.9 2.9 %collective-permute-done.19 = bf16[96,1280]{1,0:T(8,128)(2,1)S(1)} collective-permute-done((bf16[96,1280]{1,0:T(8,128)(2,1)S(1)}, bf16[96,1280]{1,0:T(8,128)(2,1)S(1)}, u32[]{:S(2)}, u32[]{:S(2)}) %collective-permute-start.19) | collective-permute-done | bytes 245792 | tf_op jit(solution)/shard_map/ppermute | solution.py:19
  92.0 1.6 %copy-done.4 = bf16[4,256,1280]{2,1,0:T(8,128)(2,1)S(1)} copy-done((bf16[4,256,1280]{2,1,0:T(8,128)(2,1)S(1)}, bf16[4,256,1280]{2,1,0:T(8,128)(2,1)}, u32[]{:S(2)}) %copy-start.4) | copy-done | bytes 2621464
  93.6 1.5 %convolution_convert_fusion.2 = bf16[4,256,384]{2,1,0:T(8,128)(2,1)S(1)} fusion(bf16[4,256,1280]{2,1,0:T(8,128)(2,1)S(1)} %copy-done.4, bf16[384,1280]{1,0:T(8,128)(2,1)S(1)} %pad_maximum_fusion.2), kind=kOutput, calls=%fused_computation.6 | convolution fusion | flops 1007026176 | bytes 4390912 | tf_op jit(solution)/shard_map/dot_general | solution.py:227
  95.2 0.9 collective-permute-start.21
  96.1 1.5 %collective-permute-start.24 = (bf16[96,1280]{1,0:T(8,128)(2,1)S(1)}, bf16[96,1280]{1,0:T(8,128)(2,1)S(1)}, u32[]{:S(2)}, u32[]{:S(2)}) collective-permute-start(bf16[96,1280]{1,0:T(8,128)(2,1)S(1)} %grad.3), channel_id=1, source_target_pairs={{0,16},{8,24},{16,0},{24,8},{1,17},{9,25},{17,1},{25,9},{2,18},{10... | collective-permute-start | bytes 737288 | tf_op jit(solution)/shard_map/ppermute | solution.py:19
  97.6 1.2 collective-permute-start.25
  98.8 1.5 %fusion.7 = f32[4,256,384]{2,1,0:T(8,128)S(1)} fusion(bf16[4,256,1280]{2,1,0:T(8,128)(2,1)S(1)} %copy-done.2, bf16[384,1280]{1,0:T(8,128)(2,1)S(1)} %pad_maximum_fusion.2), kind=kOutput, calls=%fused_computation.16 | convolution fusion | flops 1006632960 | bytes 5177344 | tf_op jit(solution)/shard_map/dot_general | solution.py:227
  100.5 3.5 %collective-permute-done.21 = bf16[96,1280]{1,0:T(8,128)(2,1)S(1)} collective-permute-done((bf16[96,1280]{1,0:T(8,128)(2,1)S(1)}, bf16[96,1280]{1,0:T(8,128)(2,1)S(1)}, u32[]{:S(2)}, u32[]{:S(2)}) %collective-permute-start.21) | collective-permute-done | bytes 245792 | tf_op jit(solution)/shard_map/ppermute | solution.py:19
  104.1 0.6 collective-permute-start.22
  104.8 2.6 %collective-permute-start.23 = (bf16[2,128,384]{2,1,0:T(8,128)(2,1)S(1)}, bf16[2,128,384]{2,1,0:T(8,128)(2,1)S(1)}, u32[]{:S(2)}, u32[]{:S(2)}) collective-permute-start(bf16[2,128,384]{2,1,0:T(8,128)(2,1)S(1)} %pad_maximum_fusion.11), channel_id=1, source_target_pairs={{0,4},{1,5},{2,6},{3,7},{4,0},{5,1},{6,2},{7,3},{8,12},{9,13},{10,... | collective-permute-start | bytes 589832 | tf_op jit(solution)/shard_map/ppermute | solution.py:19
  107.4 2.0 %collective-permute-done.24 = bf16[96,1280]{1,0:T(8,128)(2,1)S(1)} collective-permute-done((bf16[96,1280]{1,0:T(8,128)(2,1)S(1)}, bf16[96,1280]{1,0:T(8,128)(2,1)S(1)}, u32[]{:S(2)}, u32[]{:S(2)}) %collective-permute-start.24) | collective-permute-done | bytes 245792 | tf_op jit(solution)/shard_map/ppermute | solution.py:19
  109.7 1.7 %convolution_convert_fusion.1 = bf16[4,256,384]{2,1,0:T(8,128)(2,1)S(1)} fusion(bf16[4,256,1280]{2,1,0:T(8,128)(2,1)S(1)} %copy-done.4, bf16[384,1280]{1,0:T(8,128)(2,1)S(1)} %pad_maximum_fusion.4), kind=kOutput, calls=%fused_computation.5 | convolution fusion | flops 1007026176 | bytes 4390912 | tf_op jit(solution)/shard_map/dot_general | solution.py:227
  111.5 1.5 %fusion.4 = f32[4,256,384]{2,1,0:T(8,128)S(1)} fusion(bf16[4,256,1280]{2,1,0:T(8,128)(2,1)S(1)} %copy-done.2, bf16[384,1280]{1,0:T(8,128)(2,1)S(1)} %pad_maximum_fusion.4), kind=kOutput, calls=%fused_computation.13 | convolution fusion | flops 1006632960 | bytes 5177344 | tf_op jit(solution)/shard_map/dot_general | solution.py:227
  113.0 1.1 collective-permute-done.22
  114.1 1.7 %collective-permute-done.23 = bf16[2,128,384]{2,1,0:T(8,128)(2,1)S(1)} collective-permute-done((bf16[2,128,384]{2,1,0:T(8,128)(2,1)S(1)}, bf16[2,128,384]{2,1,0:T(8,128)(2,1)S(1)}, u32[]{:S(2)}, u32[]{:S(2)}) %collective-permute-start.23) | collective-permute-done | bytes 196640 | tf_op jit(solution)/shard_map/ppermute | solution.py:19
  116.5 2.8 %collective-permute-start.30 = (bf16[2,128,384]{2,1,0:T(8,128)(2,1)S(1)}, bf16[2,128,384]{2,1,0:T(8,128)(2,1)S(1)}, u32[]{:S(2)}, u32[]{:S(2)}) collective-permute-start(bf16[2,128,384]{2,1,0:T(8,128)(2,1)S(1)} %pad_maximum_fusion.13), channel_id=1, source_target_pairs={{0,4},{1,5},{2,6},{3,7},{4,0},{5,1},{6,2},{7,3},{8,12},{9,13},{10,... | collective-permute-start | bytes 589832 | tf_op jit(solution)/shard_map/ppermute | solution.py:19
  119.4 1.8 %collective-permute-start.28 = (bf16[1,128,384]{2,1,0:T(8,128)(2,1)S(1)}, bf16[1,128,384]{2,1,0:T(8,128)(2,1)S(1)}, u32[]{:S(2)}, u32[]{:S(2)}) collective-permute-start(bf16[1,128,384]{2,1,0:T(8,128)(2,1)S(1)} %bitcast.240), channel_id=1, source_target_pairs={{0,2},{1,3},{2,0},{3,1},{4,6},{5,7},{6,4},{7,5},{8,10},{9,11},{10,... | collective-permute-start | bytes 294920 | tf_op jit(solution)/shard_map/ppermute | solution.py:19
  121.5 1.3 copy-done.7
  122.8 6.2 %convolution_convert_fusion = bf16[2048,1280]{1,0:T(8,128)(2,1)} fusion(bf16[768,1280]{1,0:T(8,128)(2,1)S(1)} %bitcast.222, bf16[384,2048]{1,0:T(8,128)(2,1)S(1)} %bitcast_dynamic-update-slice_fusion, bf16[384,2048]{1,0:T(8,128)(2,1)S(1)} %copy-done.7), kind=kOutput, calls=%fused_computation | convolution fusion | flops 4035444736 | bytes 10354688 | tf_op jit(solution)/shard_map/dot_general | solution.py:318
  129.0 2.2 %collective-permute-done.27 = bf16[1,128,384]{2,1,0:T(8,128)(2,1)S(1)} collective-permute-done((bf16[1,128,384]{2,1,0:T(8,128)(2,1)S(1)}, bf16[1,128,384]{2,1,0:T(8,128)(2,1)S(1)}, u32[]{:S(2)}, u32[]{:S(2)}) %collective-permute-start.27) | collective-permute-done | bytes 98336 | tf_op jit(solution)/shard_map/ppermute | solution.py:19
  131.4 2.5 %collective-permute-start.32 = (bf16[1,128,384]{2,1,0:T(8,128)(2,1)S(1)}, bf16[1,128,384]{2,1,0:T(8,128)(2,1)S(1)}, u32[]{:S(2)}, u32[]{:S(2)}) collective-permute-start(bf16[1,128,384]{2,1,0:T(8,128)(2,1)S(1)} %fusion.24), channel_id=1, source_target_pairs={{0,2},{1,3},{2,0},{3,1},{4,6},{5,7},{6,4},{7,5},{8,10},{9,11},{10,... | collective-permute-start | bytes 294920 | tf_op jit(solution)/shard_map/ppermute | solution.py:19
  134.2 2.9 %collective-permute-done.31 = bf16[1,128,384]{2,1,0:T(8,128)(2,1)S(1)} collective-permute-done((bf16[1,128,384]{2,1,0:T(8,128)(2,1)S(1)}, bf16[1,128,384]{2,1,0:T(8,128)(2,1)S(1)}, u32[]{:S(2)}, u32[]{:S(2)}) %collective-permute-start.31) | collective-permute-done | bytes 98336 | tf_op jit(solution)/shard_map/ppermute | solution.py:19
  137.9 1.1 copy.18
  (154 shorter events, 8.1 us)
Async XLA Ops:
  0.6 7.0 %copy-start.8 = (f32[2]{0:T(128)S(1)}, f32[2]{0:T(128)}, u32[]{:S(2)}) copy-start(f32[2]{0:T(128)} %param.11) | copy-start | bytes 28
  0.6 7.6 %copy-start.10 = (f32[4]{0:T(128)S(1)}, f32[4]{0:T(128)}, u32[]{:S(2)}) copy-start(f32[4]{0:T(128)} %param.10) | copy-start | bytes 52
  0.7 8.2 %copy-start.5 = (bf16[192,1280]{1,0:T(8,128)(2,1)S(1)}, bf16[192,1280]{1,0:T(8,128)(2,1)}, u32[]{:S(2)}) copy-start(bf16[192,1280]{1,0:T(8,128)(2,1)} %teacher_ref.3) | copy-start | bytes 1474564
  1.9 12.1 %collective-permute-start = (bf16[1,384,256]{2,1,0:T(8,128)(2,1)S(1)}, bf16[1,384,256]{2,1,0:T(8,128)(2,1)S(1)}, u32[]{:S(2)}, u32[]{:S(2)}) collective-permute-start(bf16[1,384,256]{2,1,0:T(8,128)(2,1)S(1)} %bitcast.227), channel_id=1, source_target_pairs={{0,2},{1,3},{2,0},{3,1},{4,6},{5,7},{6,4},{7,5},{8,10},{9,11},{10,... | collective-permute-start | bytes 589832 | tf_op jit(solution)/shard_map/ppermute | solution.py:19
  5.0 11.5 %collective-permute-start.1 = (bf16[1,384,256]{2,1,0:T(8,128)(2,1)S(1)}, bf16[1,384,256]{2,1,0:T(8,128)(2,1)S(1)}, u32[]{:S(2)}, u32[]{:S(2)}) collective-permute-start(bf16[1,384,256]{2,1,0:T(8,128)(2,1)S(1)} %bitcast.223), channel_id=1, source_target_pairs={{0,4},{1,5},{2,6},{3,7},{4,0},{5,1},{6,2},{7,3},{8,12},{9,13},{10,... | collective-permute-start | bytes 589832 | tf_op jit(solution)/shard_map/ppermute | solution.py:19
  17.3 17.2 %collective-permute-start.2 = (bf16[2,384,256]{2,1,0:T(8,128)(2,1)}, bf16[2,384,256]{2,1,0:T(8,128)(2,1)S(1)}, u32[]{:S(2)}, u32[]{:S(2)}) collective-permute-start(bf16[2,384,256]{2,1,0:T(8,128)(2,1)} %pad_maximum_fusion.6), channel_id=1, source_target_pairs={{0,4},{1,5},{2,6},{3,7},{4,0},{5,1},{6,2},{7,3},{8,12},{9,13},{10,... | collective-permute-start | bytes 1179656 | tf_op jit(solution)/shard_map/ppermute | solution.py:19
  18.4 16.1 %collective-permute-start.3 = (bf16[2,384,256]{2,1,0:T(8,128)(2,1)}, bf16[2,384,256]{2,1,0:T(8,128)(2,1)S(1)}, u32[]{:S(2)}, u32[]{:S(2)}) collective-permute-start(bf16[2,384,256]{2,1,0:T(8,128)(2,1)} %pad_maximum_fusion.7), channel_id=1, source_target_pairs={{0,2},{1,3},{2,0},{3,1},{4,6},{5,7},{6,4},{7,5},{8,10},{9,11},{10,... | collective-permute-start | bytes 1179656 | tf_op jit(solution)/shard_map/ppermute | solution.py:19
  21.1 15.7 %collective-permute-start.4 = (bf16[1,384,256]{2,1,0:T(8,128)(2,1)S(1)}, bf16[1,384,256]{2,1,0:T(8,128)(2,1)}, u32[]{:S(2)}, u32[]{:S(2)}) collective-permute-start(bf16[1,384,256]{2,1,0:T(8,128)(2,1)S(1)} %bitcast.229), channel_id=1, source_target_pairs={{0,1},{1,0},{2,3},{3,2},{4,5},{5,4},{6,7},{7,6},{8,9},{9,8},{10,11... | collective-permute-start | bytes 589832 | tf_op jit(solution)/shard_map/ppermute | solution.py:19
  21.2 15.7 %collective-permute-start.7 = (bf16[1,384,256]{2,1,0:T(8,128)(2,1)S(1)}, bf16[1,384,256]{2,1,0:T(8,128)(2,1)S(1)}, u32[]{:S(2)}, u32[]{:S(2)}) collective-permute-start(bf16[1,384,256]{2,1,0:T(8,128)(2,1)S(1)} %bitcast.225), channel_id=1, source_target_pairs={{0,1},{1,0},{2,3},{3,2},{4,5},{5,4},{6,7},{7,6},{8,9},{9,8},{10,11... | collective-permute-start | bytes 589832 | tf_op jit(solution)/shard_map/ppermute | solution.py:19
  21.7 2.5 %copy-start = (bf16[2048,1280]{1,0:T(8,128)(2,1)S(1)}, bf16[2048,1280]{1,0:T(8,128)(2,1)}, u32[]{:S(2)}) copy-start(bf16[2048,1280]{1,0:T(8,128)(2,1)} %in_ref.1) | copy-start | bytes 15728644
  24.2 14.8 %slice-start = ((s8[5242880]{0:T(1024)(128)(4,1)}), s8[1048576]{0:T(1024)(128)(4,1)S(1)}, s32[]{:S(2)}) async-start(s8[5242880]{0:T(1024)(128)(4,1)} %bitcast.210), calls=%async_computation | async-start | bytes 2097152
  28.2 1.5 %copy-start.1 = (bf16[4,256,1280]{2,1,0:T(8,128)(2,1)}, bf16[4,256,1280]{2,1,0:T(8,128)(2,1)S(1)}, u32[]{:S(2)}) copy-start(bf16[4,256,1280]{2,1,0:T(8,128)(2,1)S(1)} %get-tuple-element.68) | copy-start | bytes 7864324
  29.7 1.5 %copy-start.3 = (bf16[4,256,1280]{2,1,0:T(8,128)(2,1)}, bf16[4,256,1280]{2,1,0:T(8,128)(2,1)S(1)}, u32[]{:S(2)}) copy-start(bf16[4,256,1280]{2,1,0:T(8,128)(2,1)S(1)} %get-tuple-element.94) | copy-start | bytes 7864324
  31.2 5.6 %collective-permute-start.5 = (bf16[1,384,256]{2,1,0:T(8,128)(2,1)S(1)}, bf16[1,384,256]{2,1,0:T(8,128)(2,1)S(1)}, u32[]{:S(2)}, u32[]{:S(2)}) collective-permute-start(bf16[1,384,256]{2,1,0:T(8,128)(2,1)S(1)} %collective-permute-done), channel_id=1, source_target_pairs={{0,1},{1,0},{2,3},{3,2},{4,5},{5,4},{6,7},{7,6},{8,9},{9,8},{10,11... | collective-permute-start | bytes 589832 | tf_op jit(solution)/shard_map/ppermute | solution.py:19
  34.5 1.7 %collective-permute-start.6 = (bf16[2,384,256]{2,1,0:T(8,128)(2,1)S(1)}, bf16[2,384,256]{2,1,0:T(8,128)(2,1)S(1)}, u32[]{:S(2)}, u32[]{:S(2)}) collective-permute-start(bf16[2,384,256]{2,1,0:T(8,128)(2,1)S(1)} %collective-permute-done.2), channel_id=1, source_target_pairs={{0,1},{1,0},{2,3},{3,2},{4,5},{5,4},{6,7},{7,6},{8,9},{9,8},{10,11... | collective-permute-start | bytes 1179656 | tf_op jit(solution)/shard_map/ppermute | solution.py:19
  34.5 2.3 %collective-permute-start.8 = (bf16[2,384,256]{2,1,0:T(8,128)(2,1)S(1)}, bf16[2,384,256]{2,1,0:T(8,128)(2,1)S(1)}, u32[]{:S(2)}, u32[]{:S(2)}) collective-permute-start(bf16[2,384,256]{2,1,0:T(8,128)(2,1)S(1)} %collective-permute-done.3), channel_id=1, source_target_pairs={{0,1},{1,0},{2,3},{3,2},{4,5},{5,4},{6,7},{7,6},{8,9},{9,8},{10,11... | collective-permute-start | bytes 1179656 | tf_op jit(solution)/shard_map/ppermute | solution.py:19
  35.1 3.9 %slice-start.1 = ((s8[5242880]{0:T(1024)(128)(4,1)}), s8[4194304]{0:T(1024)(128)(4,1)S(1)}, s32[]{:S(2)}) async-start(s8[5242880]{0:T(1024)(128)(4,1)} %bitcast.210), calls=%async_computation.1 | async-start | bytes 8388608
  36.2 1.4 %collective-permute-start.9 = (bf16[1,384,256]{2,1,0:T(8,128)(2,1)S(1)}, bf16[1,384,256]{2,1,0:T(8,128)(2,1)S(1)}, u32[]{:S(2)}, u32[]{:S(2)}) collective-permute-start(bf16[1,384,256]{2,1,0:T(8,128)(2,1)S(1)} %collective-permute-done.1), channel_id=1, source_target_pairs={{0,1},{1,0},{2,3},{3,2},{4,5},{5,4},{6,7},{7,6},{8,9},{9,8},{10,11... | collective-permute-start | bytes 589832 | tf_op jit(solution)/shard_map/ppermute | solution.py:19
  39.0 2.2 %copy-start.6 = (bf16[384,2048]{1,0:T(8,128)(2,1)}, bf16[384,2048]{1,0:T(8,128)(2,1)S(1)}, u32[]{:S(2)}) copy-start(bf16[384,2048]{1,0:T(8,128)(2,1)S(1)} %bitcast_dynamic-update-slice_fusion.8) | copy-start | bytes 4718596
  41.4 13.3 %collective-permute-start.10 = (f16[2,96,1280]{2,1,0:T(8,128)(2,1)S(1)}, f16[2,96,1280]{2,1,0:T(8,128)(2,1)S(1)}, u32[]{:S(2)}, u32[]{:S(2)}) collective-permute-start(f16[2,96,1280]{2,1,0:T(8,128)(2,1)S(1)} %fusion.10), channel_id=1, source_target_pairs={{0,8},{8,0},{16,24},{24,16},{1,9},{9,1},{17,25},{25,17},{2,10},{10... | collective-permute-start | bytes 1474568 | tf_op jit(solution)/shard_map/ppermute | solution.py:19
  45.6 14.2 %collective-permute-start.12 = (f16[2,96,1280]{2,1,0:T(8,128)(2,1)S(1)}, f16[2,96,1280]{2,1,0:T(8,128)(2,1)S(1)}, u32[]{:S(2)}, u32[]{:S(2)}) collective-permute-start(f16[2,96,1280]{2,1,0:T(8,128)(2,1)S(1)} %fusion.9), channel_id=1, source_target_pairs={{0,16},{8,24},{16,0},{24,8},{1,17},{9,25},{17,1},{25,9},{2,18},{10... | collective-permute-start | bytes 1474568 | tf_op jit(solution)/shard_map/ppermute | solution.py:19
  54.8 9.1 %collective-permute-start.11 = (f16[96,1280]{1,0:T(8,128)(2,1)S(1)}, f16[96,1280]{1,0:T(8,128)(2,1)S(1)}, u32[]{:S(2)}, u32[]{:S(2)}) collective-permute-start(f16[96,1280]{1,0:T(8,128)(2,1)S(1)} %fusion.19), channel_id=1, source_target_pairs={{0,16},{8,24},{16,0},{24,8},{1,17},{9,25},{17,1},{25,9},{2,18},{10... | collective-permute-start | bytes 737288 | tf_op jit(solution)/shard_map/ppermute | solution.py:19
  60.0 6.3 %collective-permute-start.13 = (f16[96,1280]{1,0:T(8,128)(2,1)S(1)}, f16[96,1280]{1,0:T(8,128)(2,1)S(1)}, u32[]{:S(2)}, u32[]{:S(2)}) collective-permute-start(f16[96,1280]{1,0:T(8,128)(2,1)S(1)} %fusion.20), channel_id=1, source_target_pairs={{0,8},{8,0},{16,24},{24,16},{1,9},{9,1},{17,25},{25,17},{2,10},{10... | collective-permute-start | bytes 737288 | tf_op jit(solution)/shard_map/ppermute | solution.py:19
  64.0 3.7 %copy-start.9 = (s32[192]{0:T(256)S(1)}, s32[192]{0:T(256)}, u32[]{:S(2)}) copy-start(s32[192]{0:T(256)} %param.9) | copy-start | bytes 2308
  67.7 1.2 collective-permute-start.14
  69.1 3.8 %collective-permute-start.15 = (f32[16,256]{1,0:T(8,128)S(1)}, f32[16,256]{1,0:T(8,128)S(1)}, u32[]{:S(2)}, u32[]{:S(2)}) collective-permute-start(f32[16,256]{1,0:T(8,128)S(1)} %concatenate.69), channel_id=1, source_target_pairs={{0,2},{1,3},{2,0},{3,1},{4,6},{5,7},{6,4},{7,5},{8,10},{9,11},{10,... | collective-permute-start | bytes 49160 | tf_op jit(solution)/shard_map/ppermute | solution.py:19
  73.1 4.9 %collective-permute-start.16 = (f32[16,256]{1,0:T(8,128)S(1)}, f32[16,256]{1,0:T(8,128)S(1)}, u32[]{:S(2)}, u32[]{:S(2)}) collective-permute-start(f32[16,256]{1,0:T(8,128)S(1)} %concatenate.70), channel_id=1, source_target_pairs={{0,4},{1,5},{2,6},{3,7},{4,0},{5,1},{6,2},{7,3},{8,12},{9,13},{10,... | collective-permute-start | bytes 49160 | tf_op jit(solution)/shard_map/ppermute | solution.py:19
  79.7 8.4 %collective-permute-start.17 = (bf16[96,1280]{1,0:T(8,128)(2,1)S(1)}, bf16[96,1280]{1,0:T(8,128)(2,1)S(1)}, u32[]{:S(2)}, u32[]{:S(2)}) collective-permute-start(bf16[96,1280]{1,0:T(8,128)(2,1)S(1)} %grad.2), channel_id=1, source_target_pairs={{0,8},{8,0},{16,24},{24,16},{1,9},{9,1},{17,25},{25,17},{2,10},{10... | collective-permute-start | bytes 737288 | tf_op jit(solution)/shard_map/ppermute | solution.py:19
  80.0 8.8 %collective-permute-start.18 = (bf16[96,1280]{1,0:T(8,128)(2,1)S(1)}, bf16[96,1280]{1,0:T(8,128)(2,1)S(1)}, u32[]{:S(2)}, u32[]{:S(2)}) collective-permute-start(bf16[96,1280]{1,0:T(8,128)(2,1)S(1)} %grad.2), channel_id=1, source_target_pairs={{0,16},{8,24},{16,0},{24,8},{1,17},{9,25},{17,1},{25,9},{2,18},{10... | collective-permute-start | bytes 737288 | tf_op jit(solution)/shard_map/ppermute | solution.py:19
  81.6 10.2 %collective-permute-start.19 = (bf16[96,1280]{1,0:T(8,128)(2,1)S(1)}, bf16[96,1280]{1,0:T(8,128)(2,1)S(1)}, u32[]{:S(2)}, u32[]{:S(2)}) collective-permute-start(bf16[96,1280]{1,0:T(8,128)(2,1)S(1)} %grad.2), channel_id=1, source_target_pairs={{0,24},{8,16},{16,8},{24,0},{1,25},{9,17},{17,9},{25,1},{2,26},{10... | collective-permute-start | bytes 737288 | tf_op jit(solution)/shard_map/ppermute | solution.py:19
  91.9 1.7 %copy-start.4 = (bf16[4,256,1280]{2,1,0:T(8,128)(2,1)S(1)}, bf16[4,256,1280]{2,1,0:T(8,128)(2,1)}, u32[]{:S(2)}) copy-start(bf16[4,256,1280]{2,1,0:T(8,128)(2,1)} %copy-done.3) | copy-start | bytes 7864324
  93.6 5.2 %copy-start.2 = (bf16[4,256,1280]{2,1,0:T(8,128)(2,1)S(1)}, bf16[4,256,1280]{2,1,0:T(8,128)(2,1)}, u32[]{:S(2)}) copy-start(bf16[4,256,1280]{2,1,0:T(8,128)(2,1)} %copy-done.1) | copy-start | bytes 7864324
  95.1 5.2 %collective-permute-start.20 = (bf16[4,256,384]{2,1,0:T(8,128)(2,1)S(1)}, bf16[4,256,384]{2,1,0:T(8,128)(2,1)S(1)}, u32[]{:S(2)}, u32[]{:S(2)}) collective-permute-start(bf16[4,256,384]{2,1,0:T(8,128)(2,1)S(1)} %convolution_convert_fusion.2), channel_id=1, source_target_pairs={{0,1},{1,0},{2,3},{3,2},{4,5},{5,4},{6,7},{7,6},{8,9},{9,8},{10,11... | collective-permute-start | bytes 2359304 | tf_op jit(solution)/shard_map/ppermute | solution.py:19
  95.2 8.8 %collective-permute-start.21 = (bf16[96,1280]{1,0:T(8,128)(2,1)S(1)}, bf16[96,1280]{1,0:T(8,128)(2,1)S(1)}, u32[]{:S(2)}, u32[]{:S(2)}) collective-permute-start(bf16[96,1280]{1,0:T(8,128)(2,1)S(1)} %grad.3), channel_id=1, source_target_pairs={{0,8},{8,0},{16,24},{24,16},{1,9},{9,1},{17,25},{25,17},{2,10},{10... | collective-permute-start | bytes 737288 | tf_op jit(solution)/shard_map/ppermute | solution.py:19
  96.1 13.3 %collective-permute-start.24 = (bf16[96,1280]{1,0:T(8,128)(2,1)S(1)}, bf16[96,1280]{1,0:T(8,128)(2,1)S(1)}, u32[]{:S(2)}, u32[]{:S(2)}) collective-permute-start(bf16[96,1280]{1,0:T(8,128)(2,1)S(1)} %grad.3), channel_id=1, source_target_pairs={{0,16},{8,24},{16,0},{24,8},{1,17},{9,25},{17,1},{25,9},{2,18},{10... | collective-permute-start | bytes 737288 | tf_op jit(solution)/shard_map/ppermute | solution.py:19
  97.6 11.8 %collective-permute-start.25 = (bf16[96,1280]{1,0:T(8,128)(2,1)S(1)}, bf16[96,1280]{1,0:T(8,128)(2,1)S(1)}, u32[]{:S(2)}, u32[]{:S(2)}) collective-permute-start(bf16[96,1280]{1,0:T(8,128)(2,1)S(1)} %grad.3), channel_id=1, source_target_pairs={{0,24},{8,16},{16,8},{24,0},{1,25},{9,17},{17,9},{25,1},{2,26},{10... | collective-permute-start | bytes 737288 | tf_op jit(solution)/shard_map/ppermute | solution.py:19
  104.1 10.0 %collective-permute-start.22 = (bf16[2,128,384]{2,1,0:T(8,128)(2,1)S(1)}, bf16[2,128,384]{2,1,0:T(8,128)(2,1)S(1)}, u32[]{:S(2)}, u32[]{:S(2)}) collective-permute-start(bf16[2,128,384]{2,1,0:T(8,128)(2,1)S(1)} %pad_maximum_fusion.10), channel_id=1, source_target_pairs={{0,2},{1,3},{2,0},{3,1},{4,6},{5,7},{6,4},{7,5},{8,10},{9,11},{10,... | collective-permute-start | bytes 589832 | tf_op jit(solution)/shard_map/ppermute | solution.py:19
  104.8 11.0 %collective-permute-start.23 = (bf16[2,128,384]{2,1,0:T(8,128)(2,1)S(1)}, bf16[2,128,384]{2,1,0:T(8,128)(2,1)S(1)}, u32[]{:S(2)}, u32[]{:S(2)}) collective-permute-start(bf16[2,128,384]{2,1,0:T(8,128)(2,1)S(1)} %pad_maximum_fusion.11), channel_id=1, source_target_pairs={{0,4},{1,5},{2,6},{3,7},{4,0},{5,1},{6,2},{7,3},{8,12},{9,13},{10,... | collective-permute-start | bytes 589832 | tf_op jit(solution)/shard_map/ppermute | solution.py:19
  111.4 4.5 %collective-permute-start.26 = (bf16[4,256,384]{2,1,0:T(8,128)(2,1)S(1)}, bf16[4,256,384]{2,1,0:T(8,128)(2,1)S(1)}, u32[]{:S(2)}, u32[]{:S(2)}) collective-permute-start(bf16[4,256,384]{2,1,0:T(8,128)(2,1)S(1)} %convolution_convert_fusion.1), channel_id=1, source_target_pairs={{0,1},{1,0},{2,3},{3,2},{4,5},{5,4},{6,7},{7,6},{8,9},{9,8},{10,11... | collective-permute-start | bytes 2359304 | tf_op jit(solution)/shard_map/ppermute | solution.py:19
  116.1 15.2 %collective-permute-start.29 = (bf16[2,128,384]{2,1,0:T(8,128)(2,1)S(1)}, bf16[2,128,384]{2,1,0:T(8,128)(2,1)S(1)}, u32[]{:S(2)}, u32[]{:S(2)}) collective-permute-start(bf16[2,128,384]{2,1,0:T(8,128)(2,1)S(1)} %pad_maximum_fusion.12), channel_id=1, source_target_pairs={{0,2},{1,3},{2,0},{3,1},{4,6},{5,7},{6,4},{7,5},{8,10},{9,11},{10,... | collective-permute-start | bytes 589832 | tf_op jit(solution)/shard_map/ppermute | solution.py:19
  116.5 14.8 %collective-permute-start.30 = (bf16[2,128,384]{2,1,0:T(8,128)(2,1)S(1)}, bf16[2,128,384]{2,1,0:T(8,128)(2,1)S(1)}, u32[]{:S(2)}, u32[]{:S(2)}) collective-permute-start(bf16[2,128,384]{2,1,0:T(8,128)(2,1)S(1)} %pad_maximum_fusion.13), channel_id=1, source_target_pairs={{0,4},{1,5},{2,6},{3,7},{4,0},{5,1},{6,2},{7,3},{8,12},{9,13},{10,... | collective-permute-start | bytes 589832 | tf_op jit(solution)/shard_map/ppermute | solution.py:19
  119.2 12.0 %collective-permute-start.27 = (bf16[1,128,384]{2,1,0:T(8,128)(2,1)S(1)}, bf16[1,128,384]{2,1,0:T(8,128)(2,1)S(1)}, u32[]{:S(2)}, u32[]{:S(2)}) collective-permute-start(bf16[1,128,384]{2,1,0:T(8,128)(2,1)S(1)} %bitcast.241), channel_id=1, source_target_pairs={{0,4},{1,5},{2,6},{3,7},{4,0},{5,1},{6,2},{7,3},{8,12},{9,13},{10,... | collective-permute-start | bytes 294920 | tf_op jit(solution)/shard_map/ppermute | solution.py:19
  119.4 11.8 %collective-permute-start.28 = (bf16[1,128,384]{2,1,0:T(8,128)(2,1)S(1)}, bf16[1,128,384]{2,1,0:T(8,128)(2,1)S(1)}, u32[]{:S(2)}, u32[]{:S(2)}) collective-permute-start(bf16[1,128,384]{2,1,0:T(8,128)(2,1)S(1)} %bitcast.240), channel_id=1, source_target_pairs={{0,2},{1,3},{2,0},{3,1},{4,6},{5,7},{6,4},{7,5},{8,10},{9,11},{10,... | collective-permute-start | bytes 294920 | tf_op jit(solution)/shard_map/ppermute | solution.py:19
  121.4 1.4 %copy-start.7 = (bf16[384,2048]{1,0:T(8,128)(2,1)S(1)}, bf16[384,2048]{1,0:T(8,128)(2,1)}, u32[]{:S(2)}) copy-start(bf16[384,2048]{1,0:T(8,128)(2,1)} %copy-done.6) | copy-start | bytes 4718596
  131.3 5.8 %collective-permute-start.31 = (bf16[1,128,384]{2,1,0:T(8,128)(2,1)S(1)}, bf16[1,128,384]{2,1,0:T(8,128)(2,1)S(1)}, u32[]{:S(2)}, u32[]{:S(2)}) collective-permute-start(bf16[1,128,384]{2,1,0:T(8,128)(2,1)S(1)} %fusion.23), channel_id=1, source_target_pairs={{0,4},{1,5},{2,6},{3,7},{4,0},{5,1},{6,2},{7,3},{8,12},{9,13},{10,... | collective-permute-start | bytes 294920 | tf_op jit(solution)/shard_map/ppermute | solution.py:19
  131.4 6.2 %collective-permute-start.32 = (bf16[1,128,384]{2,1,0:T(8,128)(2,1)S(1)}, bf16[1,128,384]{2,1,0:T(8,128)(2,1)S(1)}, u32[]{:S(2)}, u32[]{:S(2)}) collective-permute-start(bf16[1,128,384]{2,1,0:T(8,128)(2,1)S(1)} %fusion.24), channel_id=1, source_target_pairs={{0,2},{1,3},{2,0},{3,1},{4,6},{5,7},{6,4},{7,5},{8,10},{9,11},{10,... | collective-permute-start | bytes 294920 | tf_op jit(solution)/shard_map/ppermute | solution.py:19

commit v8 on v7

--- a/solution.py
+++ b/solution.py
@@ -260,9 +260,7 @@
                 cross[c][k ^ mask ^ 1] = other_cross[place : place + 1]
         if step == 0:
             own_stats, have = lax.optimization_barrier((own_stats, have))
-            head_send, head_keep = row_blocks(head, jnp.stack([send_order, keep_order]), rows)
-
-    (head_send, head_keep), have, cross = lax.optimization_barrier(((head_send, head_keep), have, cross))
+
     gathered, partials = [], []
     for c in range(CHUNKS):
         found = have[c] | cross[c]
@@ -301,7 +299,9 @@
         return {r: swap(grad, "dp", r) for r in range(1, count_dp)}
 
     arrived[0] = exchange(grads[0])
-    grads[1], arrived[0] = lax.optimization_barrier((grads[1], arrived[0]))
+    grads[1], head = lax.optimization_barrier((grads[1], head))
+    head_send, head_keep = row_blocks(head, jnp.stack([send_order, keep_order]), rows)
+    grads[1], head_send, head_keep, arrived[0] = lax.optimization_barrier((grads[1], head_send, head_keep, arrived[0]))
     arrived[1] = exchange(grads[1])
     steps = list(zip(near[1:], far))
     all_grads = [None, None]

time: 139 us -> 137 us (0.986)
  waiting for transfers between devices: 56.2 us -> 62.7 us
  local copies, waits for them, and re-layouts: 13.9 us -> 8.35 us
  starting transfers between devices: 35.5 us -> 33.9 us
  other arithmetic: 5.49 us -> 3.9 us
    ppermute x33, waiting for transfers between devices: 56.2 us -> 62.7 us  [swap(): return lax.ppermute(value, axis, [(k, k ^ mask) for k in range(count)])]
    unnamed x56 -> x47, local copies, waits for them, and re-layouts: 12.1 us -> 6.74 us
    ppermute x33, starting transfers between devices: 35.5 us -> 33.9 us  [swap(): return lax.ppermute(value, axis, [(k, k ^ mask) for k in range(count)])]
    concatenate x2, other arithmetic: 1.58 us -> 0.08 us  [shards(): jnp.concatenate([have[c][k] for k in keys])]
  transfers between devices with their start and end apart: 33 -> 33, of which waited for: 23 -> 21; matrix products, arithmetic and copies ran while one was open for 13% -> 13% of each run, Pallas kernels for 5% -> 5%
where the time goes in v8:
time: 137 us
  waiting for transfers between devices  62.7 us (46%)
  starting transfers between devices  33.9 us (25%)
  matrix products  16.7 us (12%)
  Pallas kernels  9.76 us (7%)
  local copies, waits for them, and re-layouts  8.35 us (6%)
  other arithmetic  3.9 us (3%)
  between operations  1.54 us (1%)
    ppermute x33, waiting for transfers between devices, swap(): return lax.ppermute(value, axis, [(k, k ^ mask) for k in range(count)])  62.7 us
    ppermute x33, starting transfers between devices, swap(): return lax.ppermute(value, axis, [(k, k ^ mask) for k in range(count)])  33.9 us
    unnamed x47, local copies, waits for them, and re-layouts  6.74 us
    dot_general x1, matrix products, shards(): lax.dot_general(jnp.concatenate(gathered, axis=0), jnp.concatenate([g.res...  6.17 us
    dot_general x4, matrix products, products(): lax.dot_general(blocks, grad, (((2,), (1,)), ((), ())), preferred_element...  6.16 us
    dot_general x2, matrix products, partial_logits(): partial = jnp.dot(gathered, head, preferred_element_type=jnp.float32)  4.4 us
    pallas_call x1, Pallas kernels, row_blocks(): pl.pallas_call(functools.partial(copy_kernel, rows), out_shape=[block] *...  4.18 us
    pallas_call x2, Pallas kernels, logit_grad(): pl.pallas_call(functools.partial(grad_kernel, heats, pieces), out_shape=j...  2.93 us
  transfers between devices with their start and end apart: 33, of which 21 were waited for; matrix products, arithmetic and copies ran while one was open for 13% of the time, Pallas kernels for 5%

profile of v8, /device:TPU:0, one launch (start us, length us, event | category | flops | bytes accessed | tf_op | source)
XLA Modules:
  0.0 136.9 jit_solution(9091944946314062654)
XLA Ops:
  0.7 1.3 copy.13
  2.0 4.1 %collective-permute-start.1 = (bf16[1,384,256]{2,1,0:T(8,128)(2,1)S(1)}, bf16[1,384,256]{2,1,0:T(8,128)(2,1)S(1)}, u32[]{:S(2)}, u32[]{:S(2)}) collective-permute-start(bf16[1,384,256]{2,1,0:T(8,128)(2,1)S(1)} %bitcast.223), channel_id=1, source_target_pairs={{0,4},{1,5},{2,6},{3,7},{4,0},{5,1},{6,2},{7,3},{8,12},{9,13},{10,... | collective-permute-start | bytes 589832 | tf_op jit(solution)/shard_map/ppermute | solution.py:19
  6.1 1.6 %collective-permute-start = (bf16[1,384,256]{2,1,0:T(8,128)(2,1)S(1)}, bf16[1,384,256]{2,1,0:T(8,128)(2,1)S(1)}, u32[]{:S(2)}, u32[]{:S(2)}) collective-permute-start(bf16[1,384,256]{2,1,0:T(8,128)(2,1)S(1)} %bitcast.227), channel_id=1, source_target_pairs={{0,2},{1,3},{2,0},{3,1},{4,6},{5,7},{6,4},{7,5},{8,10},{9,11},{10,... | collective-permute-start | bytes 589832 | tf_op jit(solution)/shard_map/ppermute | solution.py:19
  7.7 0.2 collective-permute-start.2
  7.9 0.6 fusion.44
  8.5 0.6 broadcast_divide_fusion
  9.2 1.3 stats.2
  10.6 5.9 %collective-permute-done = bf16[1,384,256]{2,1,0:T(8,128)(2,1)S(1)} collective-permute-done((bf16[1,384,256]{2,1,0:T(8,128)(2,1)S(1)}, bf16[1,384,256]{2,1,0:T(8,128)(2,1)S(1)}, u32[]{:S(2)}, u32[]{:S(2)}) %collective-permute-start) | collective-permute-done | bytes 196640 | tf_op jit(solution)/shard_map/ppermute | solution.py:19
  16.5 0.6 collective-permute-start.9
  17.1 2.6 %collective-permute-start.4 = (bf16[2,384,256]{2,1,0:T(8,128)(2,1)S(1)}, bf16[2,384,256]{2,1,0:T(8,128)(2,1)S(1)}, u32[]{:S(2)}, u32[]{:S(2)}) collective-permute-start(bf16[2,384,256]{2,1,0:T(8,128)(2,1)S(1)} %pad_maximum_fusion.6), channel_id=1, source_target_pairs={{0,4},{1,5},{2,6},{3,7},{4,0},{5,1},{6,2},{7,3},{8,12},{9,13},{10,... | collective-permute-start | bytes 1179656 | tf_op jit(solution)/shard_map/ppermute | solution.py:19
  19.8 0.6 collective-permute-start.3
  20.5 1.0 collective-permute-done.3
  21.5 13.9 %collective-permute-done.9 = bf16[2,384,256]{2,1,0:T(8,128)(2,1)S(1)} collective-permute-done((bf16[2,384,256]{2,1,0:T(8,128)(2,1)S(1)}, bf16[2,384,256]{2,1,0:T(8,128)(2,1)S(1)}, u32[]{:S(2)}, u32[]{:S(2)}) %collective-permute-start.9) | collective-permute-done | bytes 393248 | tf_op jit(solution)/shard_map/ppermute | solution.py:19
  35.4 1.6 %collective-permute-done.4 = bf16[2,384,256]{2,1,0:T(8,128)(2,1)S(1)} collective-permute-done((bf16[2,384,256]{2,1,0:T(8,128)(2,1)S(1)}, bf16[2,384,256]{2,1,0:T(8,128)(2,1)S(1)}, u32[]{:S(2)}, u32[]{:S(2)}) %collective-permute-start.4) | collective-permute-done | bytes 393248 | tf_op jit(solution)/shard_map/ppermute | solution.py:19
  37.3 1.5 %collective-permute-done.5 = bf16[2,384,256]{2,1,0:T(8,128)(2,1)S(1)} collective-permute-done((bf16[2,384,256]{2,1,0:T(8,128)(2,1)S(1)}, bf16[2,384,256]{2,1,0:T(8,128)(2,1)S(1)}, u32[]{:S(2)}, u32[]{:S(2)}) %collective-permute-start.5) | collective-permute-done | bytes 393248 | tf_op jit(solution)/shard_map/ppermute | solution.py:19
  39.2 2.2 %fusion.45 = f32[384,1280]{1,0:T(8,128)S(1)} fusion(bf16[384,2048]{1,0:T(8,128)(2,1)S(1)} %bitcast_dynamic-update-slice_fusion.8, bf16[2048,1280]{1,0:T(8,128)(2,1)S(1)} %bitcast.211), kind=kOutput, calls=%fused_computation.174 | convolution fusion | flops 2013265920 | bytes 8781824 | tf_op jit(solution)/shard_map/dot_general | solution.py:202
  41.4 1.6 %collective-permute-start.6 = (f16[2,96,1280]{2,1,0:T(8,128)(2,1)S(1)}, f16[2,96,1280]{2,1,0:T(8,128)(2,1)S(1)}, u32[]{:S(2)}, u32[]{:S(2)}) collective-permute-start(f16[2,96,1280]{2,1,0:T(8,128)(2,1)S(1)} %fusion.10), channel_id=1, source_target_pairs={{0,8},{8,0},{16,24},{24,16},{1,9},{9,1},{17,25},{25,17},{2,10},{10... | collective-permute-start | bytes 1474568 | tf_op jit(solution)/shard_map/ppermute | solution.py:19
  43.2 2.2 %fusion.46 = f32[384,1280]{1,0:T(8,128)S(1)} fusion(bf16[384,2048]{1,0:T(8,128)(2,1)S(1)} %bitcast_dynamic-update-slice_fusion, bf16[2048,1280]{1,0:T(8,128)(2,1)S(1)} %bitcast.211), kind=kOutput, calls=%fused_computation.175 | convolution fusion | flops 2013265920 | bytes 8781824 | tf_op jit(solution)/shard_map/dot_general | solution.py:202
  45.5 1.6 %collective-permute-start.12 = (f16[2,96,1280]{2,1,0:T(8,128)(2,1)S(1)}, f16[2,96,1280]{2,1,0:T(8,128)(2,1)S(1)}, u32[]{:S(2)}, u32[]{:S(2)}) collective-permute-start(f16[2,96,1280]{2,1,0:T(8,128)(2,1)S(1)} %fusion.9), channel_id=1, source_target_pairs={{0,16},{8,24},{16,0},{24,8},{1,17},{9,25},{17,1},{25,9},{2,18},{10... | collective-permute-start | bytes 1474568 | tf_op jit(solution)/shard_map/ppermute | solution.py:19
  47.1 7.7 %collective-permute-done.6 = f16[2,96,1280]{2,1,0:T(8,128)(2,1)S(1)} collective-permute-done((f16[2,96,1280]{2,1,0:T(8,128)(2,1)S(1)}, f16[2,96,1280]{2,1,0:T(8,128)(2,1)S(1)}, u32[]{:S(2)}, u32[]{:S(2)}) %collective-permute-start.6) | collective-permute-done | bytes 491552 | tf_op jit(solution)/shard_map/ppermute | solution.py:19
  54.9 1.6 %collective-permute-start.7 = (f16[96,1280]{1,0:T(8,128)(2,1)S(1)}, f16[96,1280]{1,0:T(8,128)(2,1)S(1)}, u32[]{:S(2)}, u32[]{:S(2)}) collective-permute-start(f16[96,1280]{1,0:T(8,128)(2,1)S(1)} %fusion.19), channel_id=1, source_target_pairs={{0,16},{8,24},{16,0},{24,8},{1,17},{9,25},{17,1},{25,9},{2,18},{10... | collective-permute-start | bytes 737288 | tf_op jit(solution)/shard_map/ppermute | solution.py:19
  56.5 3.1 %collective-permute-done.12 = f16[2,96,1280]{2,1,0:T(8,128)(2,1)S(1)} collective-permute-done((f16[2,96,1280]{2,1,0:T(8,128)(2,1)S(1)}, f16[2,96,1280]{2,1,0:T(8,128)(2,1)S(1)}, u32[]{:S(2)}, u32[]{:S(2)}) %collective-permute-start.12) | collective-permute-done | bytes 491552 | tf_op jit(solution)/shard_map/ppermute | solution.py:19
  59.9 3.9 %collective-permute-done.7 = f16[96,1280]{1,0:T(8,128)(2,1)S(1)} collective-permute-done((f16[96,1280]{1,0:T(8,128)(2,1)S(1)}, f16[96,1280]{1,0:T(8,128)(2,1)S(1)}, u32[]{:S(2)}, u32[]{:S(2)}) %collective-permute-start.7) | collective-permute-done | bytes 245792 | tf_op jit(solution)/shard_map/ppermute | solution.py:19
  63.9 2.2 %collective-permute-done.13 = f16[96,1280]{1,0:T(8,128)(2,1)S(1)} collective-permute-done((f16[96,1280]{1,0:T(8,128)(2,1)S(1)}, f16[96,1280]{1,0:T(8,128)(2,1)S(1)}, u32[]{:S(2)}, u32[]{:S(2)}) %collective-permute-start.13) | collective-permute-done | bytes 245792 | tf_op jit(solution)/shard_map/ppermute | solution.py:19
  66.1 1.4 %stats.3 = f32[8,256]{1,0:T(8,128)S(1)} custom-call(f32[5]{0:T(128)S(1)} %get-tuple-element.148.inverse_ref, f32[96,1280]{1,0:T(8,128)S(1)} %bitcast_add_fusion.3.refs_0_, f32[96,1280]{1,0:T(8,128)S(1)} %bitcast_add_fusion.2.refs_1_.refs_0_), custom_call_target="tpu_custom_call" | custom-call | flops 2457600 | bytes 491520 | tf_op jit(solution)/shard_map/stats/pallas_call | solution.py:70
  67.6 1.1 collective-permute-done.14
  68.9 0.3 collective-permute-start.15
  69.2 0.7 maximum_bitcast_fusion
  69.9 2.8 %collective-permute-done.15 = f32[16,256]{1,0:T(8,128)S(1)} collective-permute-done((f32[16,256]{1,0:T(8,128)S(1)}, f32[16,256]{1,0:T(8,128)S(1)}, u32[]{:S(2)}, u32[]{:S(2)}) %collective-permute-start.15) | collective-permute-done | bytes 16416 | tf_op jit(solution)/shard_map/ppermute | solution.py:19
  72.9 1.0 collective-permute-start.16
  74.0 3.6 %collective-permute-done.16 = f32[16,256]{1,0:T(8,128)S(1)} collective-permute-done((f32[16,256]{1,0:T(8,128)S(1)}, f32[16,256]{1,0:T(8,128)S(1)}, u32[]{:S(2)}, u32[]{:S(2)}) %collective-permute-start.16) | collective-permute-done | bytes 16416 | tf_op jit(solution)/shard_map/ppermute | solution.py:19
  77.9 1.5 %grad.2 = bf16[96,1280]{1,0:T(8,128)(2,1)S(1)} custom-call(f32[2,5]{1,0:T(2,128)S(1)} %pad_maximum_fusion.16.scalars_ref, bf16[192,1280]{1,0:T(8,128)(2,1)S(1)} %copy-done.1, f32[96,1280]{1,0:T(8,128)S(1)} %bitcast_add_fusion.3.refs_0_, f32[16,128]{1,0:T(8,128)S(1)} %get-tuple-element.135.refs_1_), custom_call_target="tpu_custom_call" | custom-call | flops 2949120 | bytes 983040 | tf_op jit(solution)/shard_map/grad/pallas_call | solution.py:119
  79.5 1.5 %collective-permute-start.18 = (bf16[96,1280]{1,0:T(8,128)(2,1)S(1)}, bf16[96,1280]{1,0:T(8,128)(2,1)S(1)}, u32[]{:S(2)}, u32[]{:S(2)}) collective-permute-start(bf16[96,1280]{1,0:T(8,128)(2,1)S(1)} %grad.2), channel_id=1, source_target_pairs={{0,16},{8,24},{16,0},{24,8},{1,17},{9,25},{17,1},{25,9},{2,18},{10... | collective-permute-start | bytes 737288 | tf_op jit(solution)/shard_map/ppermute | solution.py:19
  81.0 1.9 %collective-permute-start.19 = (bf16[96,1280]{1,0:T(8,128)(2,1)S(1)}, bf16[96,1280]{1,0:T(8,128)(2,1)S(1)}, u32[]{:S(2)}, u32[]{:S(2)}) collective-permute-start(bf16[96,1280]{1,0:T(8,128)(2,1)S(1)} %grad.2), channel_id=1, source_target_pairs={{0,24},{8,16},{16,8},{24,0},{1,25},{9,17},{17,9},{25,1},{2,26},{10... | collective-permute-start | bytes 737288 | tf_op jit(solution)/shard_map/ppermute | solution.py:19
  82.9 1.5 %grad.3 = bf16[96,1280]{1,0:T(8,128)(2,1)S(1)} custom-call(f32[2,5]{1,0:T(2,128)S(1)} %pad_maximum_fusion.16.scalars_ref, bf16[192,1280]{1,0:T(8,128)(2,1)S(1)} %copy-done.1, f32[96,1280]{1,0:T(8,128)S(1)} %bitcast_add_fusion.2.refs_1_.refs_0_, f32[16,128]{1,0:T(8,128)S(1)} %get-tuple-element.134.refs_1_), custom_call_target="tpu_custom_call" | custom-call | flops 2949120 | bytes 983040 | tf_op jit(solution)/shard_map/grad/pallas_call | solution.py:119
  84.4 2.5 %copy-done = bf16[2048,1280]{1,0:T(8,128)(2,1)S(1)} copy-done((bf16[2048,1280]{1,0:T(8,128)(2,1)S(1)}, bf16[2048,1280]{1,0:T(8,128)(2,1)}, u32[]{:S(2)}) %copy-start) | copy-done | bytes 5242904
  86.9 4.2 %row_blocks.1 = (bf16[4,256,1280]{2,1,0:T(8,128)(2,1)S(1)}, bf16[4,256,1280]{2,1,0:T(8,128)(2,1)S(1)}) custom-call(s32[2,4]{1,0:T(2,128)S(1)} %pad_add_fusion.order_ref, bf16[2048,1280]{1,0:T(8,128)(2,1)S(1)} %copy-done), custom_call_target="tpu_custom_call" | custom-call | bytes 10485760 | tf_op jit(solution)/shard_map/row_blocks/pallas_call | solution.py:164
  91.1 0.3 collective-permute-done.19
  91.7 1.5 %convolution_convert_fusion.2 = bf16[4,256,384]{2,1,0:T(8,128)(2,1)S(1)} fusion(bf16[4,256,1280]{2,1,0:T(8,128)(2,1)S(1)} %get-tuple-element.66, bf16[384,1280]{1,0:T(8,128)(2,1)S(1)} %pad_maximum_fusion.2), kind=kOutput, calls=%fused_computation.6 | convolution fusion | flops 1007026176 | bytes 4390912 | tf_op jit(solution)/shard_map/dot_general | solution.py:227
  93.3 0.9 collective-permute-start.21
  94.1 1.5 %collective-permute-start.24 = (bf16[96,1280]{1,0:T(8,128)(2,1)S(1)}, bf16[96,1280]{1,0:T(8,128)(2,1)S(1)}, u32[]{:S(2)}, u32[]{:S(2)}) collective-permute-start(bf16[96,1280]{1,0:T(8,128)(2,1)S(1)} %grad.3), channel_id=1, source_target_pairs={{0,16},{8,24},{16,0},{24,8},{1,17},{9,25},{17,1},{25,9},{2,18},{10... | collective-permute-start | bytes 737288 | tf_op jit(solution)/shard_map/ppermute | solution.py:19
  95.7 1.2 collective-permute-start.25
  96.8 1.5 %fusion.7 = f32[4,256,384]{2,1,0:T(8,128)S(1)} fusion(bf16[4,256,1280]{2,1,0:T(8,128)(2,1)S(1)} %get-tuple-element.59, bf16[384,1280]{1,0:T(8,128)(2,1)S(1)} %pad_maximum_fusion.2), kind=kOutput, calls=%fused_computation.16 | convolution fusion | flops 1006632960 | bytes 5177344 | tf_op jit(solution)/shard_map/dot_general | solution.py:227
  98.6 3.5 %collective-permute-done.21 = bf16[96,1280]{1,0:T(8,128)(2,1)S(1)} collective-permute-done((bf16[96,1280]{1,0:T(8,128)(2,1)S(1)}, bf16[96,1280]{1,0:T(8,128)(2,1)S(1)}, u32[]{:S(2)}, u32[]{:S(2)}) %collective-permute-start.21) | collective-permute-done | bytes 245792 | tf_op jit(solution)/shard_map/ppermute | solution.py:19
  102.2 0.4 collective-permute-start.22
  102.6 2.7 %collective-permute-start.23 = (bf16[2,128,384]{2,1,0:T(8,128)(2,1)S(1)}, bf16[2,128,384]{2,1,0:T(8,128)(2,1)S(1)}, u32[]{:S(2)}, u32[]{:S(2)}) collective-permute-start(bf16[2,128,384]{2,1,0:T(8,128)(2,1)S(1)} %pad_maximum_fusion.11), channel_id=1, source_target_pairs={{0,4},{1,5},{2,6},{3,7},{4,0},{5,1},{6,2},{7,3},{8,12},{9,13},{10,... | collective-permute-start | bytes 589832 | tf_op jit(solution)/shard_map/ppermute | solution.py:19
  105.3 1.2 collective-permute-done.24
  106.5 1.1 collective-permute-done.25
  107.9 1.5 %convolution_convert_fusion.1 = bf16[4,256,384]{2,1,0:T(8,128)(2,1)S(1)} fusion(bf16[4,256,1280]{2,1,0:T(8,128)(2,1)S(1)} %get-tuple-element.66, bf16[384,1280]{1,0:T(8,128)(2,1)S(1)} %pad_maximum_fusion.4), kind=kOutput, calls=%fused_computation.5 | convolution fusion | flops 1007026176 | bytes 4390912 | tf_op jit(solution)/shard_map/dot_general | solution.py:227
  109.5 1.5 %fusion.4 = f32[4,256,384]{2,1,0:T(8,128)S(1)} fusion(bf16[4,256,1280]{2,1,0:T(8,128)(2,1)S(1)} %get-tuple-element.59, bf16[384,1280]{1,0:T(8,128)(2,1)S(1)} %pad_maximum_fusion.4), kind=kOutput, calls=%fused_computation.13 | convolution fusion | flops 1006632960 | bytes 5177344 | tf_op jit(solution)/shard_map/dot_general | solution.py:227
  111.1 1.1 collective-permute-done.22
  112.1 1.4 %collective-permute-done.23 = bf16[2,128,384]{2,1,0:T(8,128)(2,1)S(1)} collective-permute-done((bf16[2,128,384]{2,1,0:T(8,128)(2,1)S(1)}, bf16[2,128,384]{2,1,0:T(8,128)(2,1)S(1)}, u32[]{:S(2)}, u32[]{:S(2)}) %collective-permute-start.23) | collective-permute-done | bytes 196640 | tf_op jit(solution)/shard_map/ppermute | solution.py:19
  113.9 0.3 collective-permute-start.29
  114.2 2.8 %collective-permute-start.30 = (bf16[2,128,384]{2,1,0:T(8,128)(2,1)S(1)}, bf16[2,128,384]{2,1,0:T(8,128)(2,1)S(1)}, u32[]{:S(2)}, u32[]{:S(2)}) collective-permute-start(bf16[2,128,384]{2,1,0:T(8,128)(2,1)S(1)} %pad_maximum_fusion.13), channel_id=1, source_target_pairs={{0,4},{1,5},{2,6},{3,7},{4,0},{5,1},{6,2},{7,3},{8,12},{9,13},{10,... | collective-permute-start | bytes 589832 | tf_op jit(solution)/shard_map/ppermute | solution.py:19
  117.0 0.2 collective-permute-start.27
  117.2 1.8 %collective-permute-start.28 = (bf16[1,128,384]{2,1,0:T(8,128)(2,1)S(1)}, bf16[1,128,384]{2,1,0:T(8,128)(2,1)S(1)}, u32[]{:S(2)}, u32[]{:S(2)}) collective-permute-start(bf16[1,128,384]{2,1,0:T(8,128)(2,1)S(1)} %bitcast.240), channel_id=1, source_target_pairs={{0,2},{1,3},{2,0},{3,1},{4,6},{5,7},{6,4},{7,5},{8,10},{9,11},{10,... | collective-permute-start | bytes 294920 | tf_op jit(solution)/shard_map/ppermute | solution.py:19
  119.3 1.3 copy-done.3
  120.6 6.2 %convolution_convert_fusion = bf16[2048,1280]{1,0:T(8,128)(2,1)} fusion(bf16[768,1280]{1,0:T(8,128)(2,1)S(1)} %bitcast.222, bf16[384,2048]{1,0:T(8,128)(2,1)S(1)} %bitcast_dynamic-update-slice_fusion, bf16[384,2048]{1,0:T(8,128)(2,1)S(1)} %copy-done.3), kind=kOutput, calls=%fused_computation | convolution fusion | flops 4035444736 | bytes 10354688 | tf_op jit(solution)/shard_map/dot_general | solution.py:318
  126.8 2.1 %collective-permute-done.27 = bf16[1,128,384]{2,1,0:T(8,128)(2,1)S(1)} collective-permute-done((bf16[1,128,384]{2,1,0:T(8,128)(2,1)S(1)}, bf16[1,128,384]{2,1,0:T(8,128)(2,1)S(1)}, u32[]{:S(2)}, u32[]{:S(2)}) %collective-permute-start.27) | collective-permute-done | bytes 98336 | tf_op jit(solution)/shard_map/ppermute | solution.py:19
  129.1 2.6 %collective-permute-start.32 = (bf16[1,128,384]{2,1,0:T(8,128)(2,1)S(1)}, bf16[1,128,384]{2,1,0:T(8,128)(2,1)S(1)}, u32[]{:S(2)}, u32[]{:S(2)}) collective-permute-start(bf16[1,128,384]{2,1,0:T(8,128)(2,1)S(1)} %fusion.24), channel_id=1, source_target_pairs={{0,2},{1,3},{2,0},{3,1},{4,6},{5,7},{6,4},{7,5},{8,10},{9,11},{10,... | collective-permute-start | bytes 294920 | tf_op jit(solution)/shard_map/ppermute | solution.py:19
  131.8 0.2 copy.15
  132.0 2.9 %collective-permute-done.31 = bf16[1,128,384]{2,1,0:T(8,128)(2,1)S(1)} collective-permute-done((bf16[1,128,384]{2,1,0:T(8,128)(2,1)S(1)}, bf16[1,128,384]{2,1,0:T(8,128)(2,1)S(1)}, u32[]{:S(2)}, u32[]{:S(2)}) %collective-permute-start.31) | collective-permute-done | bytes 98336 | tf_op jit(solution)/shard_map/ppermute | solution.py:19
  134.9 0.5 collective-permute-done.32
  135.7 1.1 copy.18
  (141 shorter events, 4.5 us)
Async XLA Ops:
  0.6 7.3 %copy-start.4 = (f32[2]{0:T(128)S(1)}, f32[2]{0:T(128)}, u32[]{:S(2)}) copy-start(f32[2]{0:T(128)} %param.11) | copy-start | bytes 28
  0.6 7.9 %copy-start.6 = (f32[4]{0:T(128)S(1)}, f32[4]{0:T(128)}, u32[]{:S(2)}) copy-start(f32[4]{0:T(128)} %param.10) | copy-start | bytes 52
  0.7 8.6 %copy-start.1 = (bf16[192,1280]{1,0:T(8,128)(2,1)S(1)}, bf16[192,1280]{1,0:T(8,128)(2,1)}, u32[]{:S(2)}) copy-start(bf16[192,1280]{1,0:T(8,128)(2,1)} %teacher_ref.3) | copy-start | bytes 1474564
  0.7 38.5 %slice-start = ((s8[5242880]{0:T(1024)(128)(4,1)}), s8[1048576]{0:T(1024)(128)(4,1)S(1)}, s32[]{:S(2)}) async-start(s8[5242880]{0:T(1024)(128)(4,1)} %bitcast.210), calls=%async_computation | async-start | bytes 2097152
  2.0 14.5 %collective-permute-start.1 = (bf16[1,384,256]{2,1,0:T(8,128)(2,1)S(1)}, bf16[1,384,256]{2,1,0:T(8,128)(2,1)S(1)}, u32[]{:S(2)}, u32[]{:S(2)}) collective-permute-start(bf16[1,384,256]{2,1,0:T(8,128)(2,1)S(1)} %bitcast.223), channel_id=1, source_target_pairs={{0,4},{1,5},{2,6},{3,7},{4,0},{5,1},{6,2},{7,3},{8,12},{9,13},{10,... | collective-permute-start | bytes 589832 | tf_op jit(solution)/shard_map/ppermute | solution.py:19
  6.1 14.3 %collective-permute-start.8 = (bf16[1,384,256]{2,1,0:T(8,128)(2,1)S(1)}, bf16[1,384,256]{2,1,0:T(8,128)(2,1)S(1)}, u32[]{:S(2)}, u32[]{:S(2)}) collective-permute-start(bf16[1,384,256]{2,1,0:T(8,128)(2,1)S(1)} %bitcast.224), channel_id=1, source_target_pairs={{0,1},{1,0},{2,3},{3,2},{4,5},{5,4},{6,7},{7,6},{8,9},{9,8},{10,11... | collective-permute-start | bytes 589832 | tf_op jit(solution)/shard_map/ppermute | solution.py:19
  6.1 10.4 %collective-permute-start = (bf16[1,384,256]{2,1,0:T(8,128)(2,1)S(1)}, bf16[1,384,256]{2,1,0:T(8,128)(2,1)S(1)}, u32[]{:S(2)}, u32[]{:S(2)}) collective-permute-start(bf16[1,384,256]{2,1,0:T(8,128)(2,1)S(1)} %bitcast.227), channel_id=1, source_target_pairs={{0,2},{1,3},{2,0},{3,1},{4,6},{5,7},{6,4},{7,5},{8,10},{9,11},{10,... | collective-permute-start | bytes 589832 | tf_op jit(solution)/shard_map/ppermute | solution.py:19
  7.7 12.1 %collective-permute-start.2 = (bf16[1,384,256]{2,1,0:T(8,128)(2,1)S(1)}, bf16[1,384,256]{2,1,0:T(8,128)(2,1)S(1)}, u32[]{:S(2)}, u32[]{:S(2)}) collective-permute-start(bf16[1,384,256]{2,1,0:T(8,128)(2,1)S(1)} %bitcast.228), channel_id=1, source_target_pairs={{0,1},{1,0},{2,3},{3,2},{4,5},{5,4},{6,7},{7,6},{8,9},{9,8},{10,11... | collective-permute-start | bytes 589832 | tf_op jit(solution)/shard_map/ppermute | solution.py:19
  16.5 18.9 %collective-permute-start.9 = (bf16[2,384,256]{2,1,0:T(8,128)(2,1)S(1)}, bf16[2,384,256]{2,1,0:T(8,128)(2,1)S(1)}, u32[]{:S(2)}, u32[]{:S(2)}) collective-permute-start(bf16[2,384,256]{2,1,0:T(8,128)(2,1)S(1)} %pad_maximum_fusion.7), channel_id=1, source_target_pairs={{0,2},{1,3},{2,0},{3,1},{4,6},{5,7},{6,4},{7,5},{8,10},{9,11},{10,... | collective-permute-start | bytes 1179656 | tf_op jit(solution)/shard_map/ppermute | solution.py:19
  17.1 19.9 %collective-permute-start.4 = (bf16[2,384,256]{2,1,0:T(8,128)(2,1)S(1)}, bf16[2,384,256]{2,1,0:T(8,128)(2,1)S(1)}, u32[]{:S(2)}, u32[]{:S(2)}) collective-permute-start(bf16[2,384,256]{2,1,0:T(8,128)(2,1)S(1)} %pad_maximum_fusion.6), channel_id=1, source_target_pairs={{0,4},{1,5},{2,6},{3,7},{4,0},{5,1},{6,2},{7,3},{8,12},{9,13},{10,... | collective-permute-start | bytes 1179656 | tf_op jit(solution)/shard_map/ppermute | solution.py:19
  19.8 17.4 %collective-permute-start.11 = (bf16[1,384,256]{2,1,0:T(8,128)(2,1)S(1)}, bf16[1,384,256]{2,1,0:T(8,128)(2,1)S(1)}, u32[]{:S(2)}, u32[]{:S(2)}) collective-permute-start(bf16[1,384,256]{2,1,0:T(8,128)(2,1)S(1)} %collective-permute-done.1), channel_id=1, source_target_pairs={{0,1},{1,0},{2,3},{3,2},{4,5},{5,4},{6,7},{7,6},{8,9},{9,8},{10,11... | collective-permute-start | bytes 589832 | tf_op jit(solution)/shard_map/ppermute | solution.py:19
  19.8 1.7 %collective-permute-start.3 = (bf16[1,384,256]{2,1,0:T(8,128)(2,1)S(1)}, bf16[1,384,256]{2,1,0:T(8,128)(2,1)S(1)}, u32[]{:S(2)}, u32[]{:S(2)}) collective-permute-start(bf16[1,384,256]{2,1,0:T(8,128)(2,1)S(1)} %collective-permute-done), channel_id=1, source_target_pairs={{0,1},{1,0},{2,3},{3,2},{4,5},{5,4},{6,7},{7,6},{8,9},{9,8},{10,11... | collective-permute-start | bytes 589832 | tf_op jit(solution)/shard_map/ppermute | solution.py:19
  20.4 18.7 %slice-start.1 = ((s8[5242880]{0:T(1024)(128)(4,1)}), s8[4194304]{0:T(1024)(128)(4,1)S(1)}, s32[]{:S(2)}) async-start(s8[5242880]{0:T(1024)(128)(4,1)} %bitcast.210), calls=%async_computation.1 | async-start | bytes 8388608
  35.4 1.7 %collective-permute-start.10 = (bf16[2,384,256]{2,1,0:T(8,128)(2,1)S(1)}, bf16[2,384,256]{2,1,0:T(8,128)(2,1)S(1)}, u32[]{:S(2)}, u32[]{:S(2)}) collective-permute-start(bf16[2,384,256]{2,1,0:T(8,128)(2,1)S(1)} %collective-permute-done.9), channel_id=1, source_target_pairs={{0,1},{1,0},{2,3},{3,2},{4,5},{5,4},{6,7},{7,6},{8,9},{9,8},{10,11... | collective-permute-start | bytes 1179656 | tf_op jit(solution)/shard_map/ppermute | solution.py:19
  37.1 1.7 %collective-permute-start.5 = (bf16[2,384,256]{2,1,0:T(8,128)(2,1)S(1)}, bf16[2,384,256]{2,1,0:T(8,128)(2,1)S(1)}, u32[]{:S(2)}, u32[]{:S(2)}) collective-permute-start(bf16[2,384,256]{2,1,0:T(8,128)(2,1)S(1)} %collective-permute-done.4), channel_id=1, source_target_pairs={{0,1},{1,0},{2,3},{3,2},{4,5},{5,4},{6,7},{7,6},{8,9},{9,8},{10,11... | collective-permute-start | bytes 1179656 | tf_op jit(solution)/shard_map/ppermute | solution.py:19
  39.1 2.2 %copy-start.2 = (bf16[384,2048]{1,0:T(8,128)(2,1)}, bf16[384,2048]{1,0:T(8,128)(2,1)S(1)}, u32[]{:S(2)}) copy-start(bf16[384,2048]{1,0:T(8,128)(2,1)S(1)} %bitcast_dynamic-update-slice_fusion.8) | copy-start | bytes 4718596
  41.4 13.3 %collective-permute-start.6 = (f16[2,96,1280]{2,1,0:T(8,128)(2,1)S(1)}, f16[2,96,1280]{2,1,0:T(8,128)(2,1)S(1)}, u32[]{:S(2)}, u32[]{:S(2)}) collective-permute-start(f16[2,96,1280]{2,1,0:T(8,128)(2,1)S(1)} %fusion.10), channel_id=1, source_target_pairs={{0,8},{8,0},{16,24},{24,16},{1,9},{9,1},{17,25},{25,17},{2,10},{10... | collective-permute-start | bytes 1474568 | tf_op jit(solution)/shard_map/ppermute | solution.py:19
  45.5 14.2 %collective-permute-start.12 = (f16[2,96,1280]{2,1,0:T(8,128)(2,1)S(1)}, f16[2,96,1280]{2,1,0:T(8,128)(2,1)S(1)}, u32[]{:S(2)}, u32[]{:S(2)}) collective-permute-start(f16[2,96,1280]{2,1,0:T(8,128)(2,1)S(1)} %fusion.9), channel_id=1, source_target_pairs={{0,16},{8,24},{16,0},{24,8},{1,17},{9,25},{17,1},{25,9},{2,18},{10... | collective-permute-start | bytes 1474568 | tf_op jit(solution)/shard_map/ppermute | solution.py:19
  54.9 8.9 %collective-permute-start.7 = (f16[96,1280]{1,0:T(8,128)(2,1)S(1)}, f16[96,1280]{1,0:T(8,128)(2,1)S(1)}, u32[]{:S(2)}, u32[]{:S(2)}) collective-permute-start(f16[96,1280]{1,0:T(8,128)(2,1)S(1)} %fusion.19), channel_id=1, source_target_pairs={{0,16},{8,24},{16,0},{24,8},{1,17},{9,25},{17,1},{25,9},{2,18},{10... | collective-permute-start | bytes 737288 | tf_op jit(solution)/shard_map/ppermute | solution.py:19
  59.8 6.3 %collective-permute-start.13 = (f16[96,1280]{1,0:T(8,128)(2,1)S(1)}, f16[96,1280]{1,0:T(8,128)(2,1)S(1)}, u32[]{:S(2)}, u32[]{:S(2)}) collective-permute-start(f16[96,1280]{1,0:T(8,128)(2,1)S(1)} %fusion.20), channel_id=1, source_target_pairs={{0,8},{8,0},{16,24},{24,16},{1,9},{9,1},{17,25},{25,17},{2,10},{10... | collective-permute-start | bytes 737288 | tf_op jit(solution)/shard_map/ppermute | solution.py:19
  63.8 3.7 %copy-start.5 = (s32[192]{0:T(256)S(1)}, s32[192]{0:T(256)}, u32[]{:S(2)}) copy-start(s32[192]{0:T(256)} %param.9) | copy-start | bytes 2308
  67.5 1.2 collective-permute-start.14
  68.9 3.8 %collective-permute-start.15 = (f32[16,256]{1,0:T(8,128)S(1)}, f32[16,256]{1,0:T(8,128)S(1)}, u32[]{:S(2)}, u32[]{:S(2)}) collective-permute-start(f32[16,256]{1,0:T(8,128)S(1)} %concatenate.69), channel_id=1, source_target_pairs={{0,2},{1,3},{2,0},{3,1},{4,6},{5,7},{6,4},{7,5},{8,10},{9,11},{10,... | collective-permute-start | bytes 49160 | tf_op jit(solution)/shard_map/ppermute | solution.py:19
  72.9 4.7 %collective-permute-start.16 = (f32[16,256]{1,0:T(8,128)S(1)}, f32[16,256]{1,0:T(8,128)S(1)}, u32[]{:S(2)}, u32[]{:S(2)}) collective-permute-start(f32[16,256]{1,0:T(8,128)S(1)} %concatenate.70), channel_id=1, source_target_pairs={{0,4},{1,5},{2,6},{3,7},{4,0},{5,1},{6,2},{7,3},{8,12},{9,13},{10,... | collective-permute-start | bytes 49160 | tf_op jit(solution)/shard_map/ppermute | solution.py:19
  79.3 11.7 %collective-permute-start.17 = (bf16[96,1280]{1,0:T(8,128)(2,1)S(1)}, bf16[96,1280]{1,0:T(8,128)(2,1)S(1)}, u32[]{:S(2)}, u32[]{:S(2)}) collective-permute-start(bf16[96,1280]{1,0:T(8,128)(2,1)S(1)} %grad.2), channel_id=1, source_target_pairs={{0,8},{8,0},{16,24},{24,16},{1,9},{9,1},{17,25},{25,17},{2,10},{10... | collective-permute-start | bytes 737288 | tf_op jit(solution)/shard_map/ppermute | solution.py:19
  79.5 11.6 %collective-permute-start.18 = (bf16[96,1280]{1,0:T(8,128)(2,1)S(1)}, bf16[96,1280]{1,0:T(8,128)(2,1)S(1)}, u32[]{:S(2)}, u32[]{:S(2)}) collective-permute-start(bf16[96,1280]{1,0:T(8,128)(2,1)S(1)} %grad.2), channel_id=1, source_target_pairs={{0,16},{8,24},{16,0},{24,8},{1,17},{9,25},{17,1},{25,9},{2,18},{10... | collective-permute-start | bytes 737288 | tf_op jit(solution)/shard_map/ppermute | solution.py:19
  81.0 10.3 %collective-permute-start.19 = (bf16[96,1280]{1,0:T(8,128)(2,1)S(1)}, bf16[96,1280]{1,0:T(8,128)(2,1)S(1)}, u32[]{:S(2)}, u32[]{:S(2)}) collective-permute-start(bf16[96,1280]{1,0:T(8,128)(2,1)S(1)} %grad.2), channel_id=1, source_target_pairs={{0,24},{8,16},{16,8},{24,0},{1,25},{9,17},{17,9},{25,1},{2,26},{10... | collective-permute-start | bytes 737288 | tf_op jit(solution)/shard_map/ppermute | solution.py:19
  84.4 2.5 %copy-start = (bf16[2048,1280]{1,0:T(8,128)(2,1)S(1)}, bf16[2048,1280]{1,0:T(8,128)(2,1)}, u32[]{:S(2)}) copy-start(bf16[2048,1280]{1,0:T(8,128)(2,1)} %in_ref) | copy-start | bytes 15728644
  93.2 5.2 %collective-permute-start.20 = (bf16[4,256,384]{2,1,0:T(8,128)(2,1)S(1)}, bf16[4,256,384]{2,1,0:T(8,128)(2,1)S(1)}, u32[]{:S(2)}, u32[]{:S(2)}) collective-permute-start(bf16[4,256,384]{2,1,0:T(8,128)(2,1)S(1)} %convolution_convert_fusion.2), channel_id=1, source_target_pairs={{0,1},{1,0},{2,3},{3,2},{4,5},{5,4},{6,7},{7,6},{8,9},{9,8},{10,11... | collective-permute-start | bytes 2359304 | tf_op jit(solution)/shard_map/ppermute | solution.py:19
  93.3 8.8 %collective-permute-start.21 = (bf16[96,1280]{1,0:T(8,128)(2,1)S(1)}, bf16[96,1280]{1,0:T(8,128)(2,1)S(1)}, u32[]{:S(2)}, u32[]{:S(2)}) collective-permute-start(bf16[96,1280]{1,0:T(8,128)(2,1)S(1)} %grad.3), channel_id=1, source_target_pairs={{0,8},{8,0},{16,24},{24,16},{1,9},{9,1},{17,25},{25,17},{2,10},{10... | collective-permute-start | bytes 737288 | tf_op jit(solution)/shard_map/ppermute | solution.py:19
  94.1 12.4 %collective-permute-start.24 = (bf16[96,1280]{1,0:T(8,128)(2,1)S(1)}, bf16[96,1280]{1,0:T(8,128)(2,1)S(1)}, u32[]{:S(2)}, u32[]{:S(2)}) collective-permute-start(bf16[96,1280]{1,0:T(8,128)(2,1)S(1)} %grad.3), channel_id=1, source_target_pairs={{0,16},{8,24},{16,0},{24,8},{1,17},{9,25},{17,1},{25,9},{2,18},{10... | collective-permute-start | bytes 737288 | tf_op jit(solution)/shard_map/ppermute | solution.py:19
  95.7 11.9 %collective-permute-start.25 = (bf16[96,1280]{1,0:T(8,128)(2,1)S(1)}, bf16[96,1280]{1,0:T(8,128)(2,1)S(1)}, u32[]{:S(2)}, u32[]{:S(2)}) collective-permute-start(bf16[96,1280]{1,0:T(8,128)(2,1)S(1)} %grad.3), channel_id=1, source_target_pairs={{0,24},{8,16},{16,8},{24,0},{1,25},{9,17},{17,9},{25,1},{2,26},{10... | collective-permute-start | bytes 737288 | tf_op jit(solution)/shard_map/ppermute | solution.py:19
  102.2 9.9 %collective-permute-start.22 = (bf16[2,128,384]{2,1,0:T(8,128)(2,1)S(1)}, bf16[2,128,384]{2,1,0:T(8,128)(2,1)S(1)}, u32[]{:S(2)}, u32[]{:S(2)}) collective-permute-start(bf16[2,128,384]{2,1,0:T(8,128)(2,1)S(1)} %pad_maximum_fusion.10), channel_id=1, source_target_pairs={{0,2},{1,3},{2,0},{3,1},{4,6},{5,7},{6,4},{7,5},{8,10},{9,11},{10,... | collective-permute-start | bytes 589832 | tf_op jit(solution)/shard_map/ppermute | solution.py:19
  102.6 11.0 %collective-permute-start.23 = (bf16[2,128,384]{2,1,0:T(8,128)(2,1)S(1)}, bf16[2,128,384]{2,1,0:T(8,128)(2,1)S(1)}, u32[]{:S(2)}, u32[]{:S(2)}) collective-permute-start(bf16[2,128,384]{2,1,0:T(8,128)(2,1)S(1)} %pad_maximum_fusion.11), channel_id=1, source_target_pairs={{0,4},{1,5},{2,6},{3,7},{4,0},{5,1},{6,2},{7,3},{8,12},{9,13},{10,... | collective-permute-start | bytes 589832 | tf_op jit(solution)/shard_map/ppermute | solution.py:19
  109.4 4.2 %collective-permute-start.26 = (bf16[4,256,384]{2,1,0:T(8,128)(2,1)S(1)}, bf16[4,256,384]{2,1,0:T(8,128)(2,1)S(1)}, u32[]{:S(2)}, u32[]{:S(2)}) collective-permute-start(bf16[4,256,384]{2,1,0:T(8,128)(2,1)S(1)} %convolution_convert_fusion.1), channel_id=1, source_target_pairs={{0,1},{1,0},{2,3},{3,2},{4,5},{5,4},{6,7},{7,6},{8,9},{9,8},{10,11... | collective-permute-start | bytes 2359304 | tf_op jit(solution)/shard_map/ppermute | solution.py:19
  113.9 15.0 %collective-permute-start.29 = (bf16[2,128,384]{2,1,0:T(8,128)(2,1)S(1)}, bf16[2,128,384]{2,1,0:T(8,128)(2,1)S(1)}, u32[]{:S(2)}, u32[]{:S(2)}) collective-permute-start(bf16[2,128,384]{2,1,0:T(8,128)(2,1)S(1)} %pad_maximum_fusion.12), channel_id=1, source_target_pairs={{0,2},{1,3},{2,0},{3,1},{4,6},{5,7},{6,4},{7,5},{8,10},{9,11},{10,... | collective-permute-start | bytes 589832 | tf_op jit(solution)/shard_map/ppermute | solution.py:19
  114.2 14.7 %collective-permute-start.30 = (bf16[2,128,384]{2,1,0:T(8,128)(2,1)S(1)}, bf16[2,128,384]{2,1,0:T(8,128)(2,1)S(1)}, u32[]{:S(2)}, u32[]{:S(2)}) collective-permute-start(bf16[2,128,384]{2,1,0:T(8,128)(2,1)S(1)} %pad_maximum_fusion.13), channel_id=1, source_target_pairs={{0,4},{1,5},{2,6},{3,7},{4,0},{5,1},{6,2},{7,3},{8,12},{9,13},{10,... | collective-permute-start | bytes 589832 | tf_op jit(solution)/shard_map/ppermute | solution.py:19
  117.0 11.9 %collective-permute-start.27 = (bf16[1,128,384]{2,1,0:T(8,128)(2,1)S(1)}, bf16[1,128,384]{2,1,0:T(8,128)(2,1)S(1)}, u32[]{:S(2)}, u32[]{:S(2)}) collective-permute-start(bf16[1,128,384]{2,1,0:T(8,128)(2,1)S(1)} %bitcast.241), channel_id=1, source_target_pairs={{0,4},{1,5},{2,6},{3,7},{4,0},{5,1},{6,2},{7,3},{8,12},{9,13},{10,... | collective-permute-start | bytes 294920 | tf_op jit(solution)/shard_map/ppermute | solution.py:19
  117.2 11.7 %collective-permute-start.28 = (bf16[1,128,384]{2,1,0:T(8,128)(2,1)S(1)}, bf16[1,128,384]{2,1,0:T(8,128)(2,1)S(1)}, u32[]{:S(2)}, u32[]{:S(2)}) collective-permute-start(bf16[1,128,384]{2,1,0:T(8,128)(2,1)S(1)} %bitcast.240), channel_id=1, source_target_pairs={{0,2},{1,3},{2,0},{3,1},{4,6},{5,7},{6,4},{7,5},{8,10},{9,11},{10,... | collective-permute-start | bytes 294920 | tf_op jit(solution)/shard_map/ppermute | solution.py:19
  119.2 1.4 %copy-start.3 = (bf16[384,2048]{1,0:T(8,128)(2,1)S(1)}, bf16[384,2048]{1,0:T(8,128)(2,1)}, u32[]{:S(2)}) copy-start(bf16[384,2048]{1,0:T(8,128)(2,1)} %copy-done.2) | copy-start | bytes 4718596
  129.0 5.8 %collective-permute-start.31 = (bf16[1,128,384]{2,1,0:T(8,128)(2,1)S(1)}, bf16[1,128,384]{2,1,0:T(8,128)(2,1)S(1)}, u32[]{:S(2)}, u32[]{:S(2)}) collective-permute-start(bf16[1,128,384]{2,1,0:T(8,128)(2,1)S(1)} %fusion.23), channel_id=1, source_target_pairs={{0,4},{1,5},{2,6},{3,7},{4,0},{5,1},{6,2},{7,3},{8,12},{9,13},{10,... | collective-permute-start | bytes 294920 | tf_op jit(solution)/shard_map/ppermute | solution.py:19
  129.1 6.3 %collective-permute-start.32 = (bf16[1,128,384]{2,1,0:T(8,128)(2,1)S(1)}, bf16[1,128,384]{2,1,0:T(8,128)(2,1)S(1)}, u32[]{:S(2)}, u32[]{:S(2)}) collective-permute-start(bf16[1,128,384]{2,1,0:T(8,128)(2,1)S(1)} %fusion.24), channel_id=1, source_target_pairs={{0,2},{1,3},{2,0},{3,1},{4,6},{5,7},{6,4},{7,5},{8,10},{9,11},{10,... | collective-permute-start | bytes 294920 | tf_op jit(solution)/shard_map/ppermute | solution.py:19

commit v9 on v8

--- a/solution.py
+++ b/solution.py
@@ -296,7 +296,7 @@
 
     arrived = [None, None]
     def exchange(grad):
-        return {r: swap(grad, "dp", r) for r in range(1, count_dp)}
+        return {r: swap(grad, "dp", r) for r in reversed(range(1, count_dp))}
 
     arrived[0] = exchange(grads[0])
     grads[1], head = lax.optimization_barrier((grads[1], head))

time: 137 us -> 137 us (level)
  no operation moved by 1% of the time
where the time goes in v9:
time: 137 us
  waiting for transfers between devices  62.7 us (46%)
  starting transfers between devices  33.9 us (25%)
  matrix products  16.7 us (12%)
  Pallas kernels  9.76 us (7%)
  local copies, waits for them, and re-layouts  8.35 us (6%)
  other arithmetic  3.9 us (3%)
  between operations  1.54 us (1%)
    ppermute x33, waiting for transfers between devices, swap(): return lax.ppermute(value, axis, [(k, k ^ mask) for k in range(count)])  62.7 us
    ppermute x33, starting transfers between devices, swap(): return lax.ppermute(value, axis, [(k, k ^ mask) for k in range(count)])  33.9 us
    unnamed x47, local copies, waits for them, and re-layouts  6.74 us
    dot_general x1, matrix products, shards(): lax.dot_general(jnp.concatenate(gathered, axis=0), jnp.concatenate([g.res...  6.17 us
    dot_general x4, matrix products, products(): lax.dot_general(blocks, grad, (((2,), (1,)), ((), ())), preferred_element...  6.16 us
    dot_general x2, matrix products, partial_logits(): partial = jnp.dot(gathered, head, preferred_element_type=jnp.float32)  4.4 us
    pallas_call x1, Pallas kernels, row_blocks(): pl.pallas_call(functools.partial(copy_kernel, rows), out_shape=[block] *...  4.18 us
    pallas_call x2, Pallas kernels, logit_grad(): pl.pallas_call(functools.partial(grad_kernel, heats, pieces), out_shape=j...  2.93 us
  transfers between devices with their start and end apart: 33, of which 21 were waited for; matrix products, arithmetic and copies ran while one was open for 13% of the time, Pallas kernels for 5%

profile of v9, /device:TPU:0, one launch (start us, length us, event | category | flops | bytes accessed | tf_op | source)
XLA Modules:
  0.0 136.9 jit_solution(9091944946314062654)
XLA Ops:
  0.7 1.3 copy.13
  2.0 4.1 %collective-permute-start.1 = (bf16[1,384,256]{2,1,0:T(8,128)(2,1)S(1)}, bf16[1,384,256]{2,1,0:T(8,128)(2,1)S(1)}, u32[]{:S(2)}, u32[]{:S(2)}) collective-permute-start(bf16[1,384,256]{2,1,0:T(8,128)(2,1)S(1)} %bitcast.223), channel_id=1, source_target_pairs={{0,4},{1,5},{2,6},{3,7},{4,0},{5,1},{6,2},{7,3},{8,12},{9,13},{10,... | collective-permute-start | bytes 589832 | tf_op jit(solution)/shard_map/ppermute | solution.py:19
  6.1 1.6 %collective-permute-start = (bf16[1,384,256]{2,1,0:T(8,128)(2,1)S(1)}, bf16[1,384,256]{2,1,0:T(8,128)(2,1)S(1)}, u32[]{:S(2)}, u32[]{:S(2)}) collective-permute-start(bf16[1,384,256]{2,1,0:T(8,128)(2,1)S(1)} %bitcast.227), channel_id=1, source_target_pairs={{0,2},{1,3},{2,0},{3,1},{4,6},{5,7},{6,4},{7,5},{8,10},{9,11},{10,... | collective-permute-start | bytes 589832 | tf_op jit(solution)/shard_map/ppermute | solution.py:19
  7.7 0.2 collective-permute-start.2
  7.9 0.6 fusion.44
  8.5 0.6 broadcast_divide_fusion
  9.2 1.3 stats.2
  10.6 5.9 %collective-permute-done = bf16[1,384,256]{2,1,0:T(8,128)(2,1)S(1)} collective-permute-done((bf16[1,384,256]{2,1,0:T(8,128)(2,1)S(1)}, bf16[1,384,256]{2,1,0:T(8,128)(2,1)S(1)}, u32[]{:S(2)}, u32[]{:S(2)}) %collective-permute-start) | collective-permute-done | bytes 196640 | tf_op jit(solution)/shard_map/ppermute | solution.py:19
  16.5 0.6 collective-permute-start.9
  17.1 2.6 %collective-permute-start.4 = (bf16[2,384,256]{2,1,0:T(8,128)(2,1)S(1)}, bf16[2,384,256]{2,1,0:T(8,128)(2,1)S(1)}, u32[]{:S(2)}, u32[]{:S(2)}) collective-permute-start(bf16[2,384,256]{2,1,0:T(8,128)(2,1)S(1)} %pad_maximum_fusion.6), channel_id=1, source_target_pairs={{0,4},{1,5},{2,6},{3,7},{4,0},{5,1},{6,2},{7,3},{8,12},{9,13},{10,... | collective-permute-start | bytes 1179656 | tf_op jit(solution)/shard_map/ppermute | solution.py:19
  19.8 0.6 collective-permute-start.3
  20.5 1.0 collective-permute-done.3
  21.5 13.9 %collective-permute-done.9 = bf16[2,384,256]{2,1,0:T(8,128)(2,1)S(1)} collective-permute-done((bf16[2,384,256]{2,1,0:T(8,128)(2,1)S(1)}, bf16[2,384,256]{2,1,0:T(8,128)(2,1)S(1)}, u32[]{:S(2)}, u32[]{:S(2)}) %collective-permute-start.9) | collective-permute-done | bytes 393248 | tf_op jit(solution)/shard_map/ppermute | solution.py:19
  35.4 1.6 %collective-permute-done.4 = bf16[2,384,256]{2,1,0:T(8,128)(2,1)S(1)} collective-permute-done((bf16[2,384,256]{2,1,0:T(8,128)(2,1)S(1)}, bf16[2,384,256]{2,1,0:T(8,128)(2,1)S(1)}, u32[]{:S(2)}, u32[]{:S(2)}) %collective-permute-start.4) | collective-permute-done | bytes 393248 | tf_op jit(solution)/shard_map/ppermute | solution.py:19
  37.3 1.5 %collective-permute-done.5 = bf16[2,384,256]{2,1,0:T(8,128)(2,1)S(1)} collective-permute-done((bf16[2,384,256]{2,1,0:T(8,128)(2,1)S(1)}, bf16[2,384,256]{2,1,0:T(8,128)(2,1)S(1)}, u32[]{:S(2)}, u32[]{:S(2)}) %collective-permute-start.5) | collective-permute-done | bytes 393248 | tf_op jit(solution)/shard_map/ppermute | solution.py:19
  39.2 2.2 %fusion.45 = f32[384,1280]{1,0:T(8,128)S(1)} fusion(bf16[384,2048]{1,0:T(8,128)(2,1)S(1)} %bitcast_dynamic-update-slice_fusion.8, bf16[2048,1280]{1,0:T(8,128)(2,1)S(1)} %bitcast.211), kind=kOutput, calls=%fused_computation.174 | convolution fusion | flops 2013265920 | bytes 8781824 | tf_op jit(solution)/shard_map/dot_general | solution.py:202
  41.4 1.6 %collective-permute-start.6 = (f16[2,96,1280]{2,1,0:T(8,128)(2,1)S(1)}, f16[2,96,1280]{2,1,0:T(8,128)(2,1)S(1)}, u32[]{:S(2)}, u32[]{:S(2)}) collective-permute-start(f16[2,96,1280]{2,1,0:T(8,128)(2,1)S(1)} %fusion.10), channel_id=1, source_target_pairs={{0,8},{8,0},{16,24},{24,16},{1,9},{9,1},{17,25},{25,17},{2,10},{10... | collective-permute-start | bytes 1474568 | tf_op jit(solution)/shard_map/ppermute | solution.py:19
  43.2 2.2 %fusion.46 = f32[384,1280]{1,0:T(8,128)S(1)} fusion(bf16[384,2048]{1,0:T(8,128)(2,1)S(1)} %bitcast_dynamic-update-slice_fusion, bf16[2048,1280]{1,0:T(8,128)(2,1)S(1)} %bitcast.211), kind=kOutput, calls=%fused_computation.175 | convolution fusion | flops 2013265920 | bytes 8781824 | tf_op jit(solution)/shard_map/dot_general | solution.py:202
  45.5 1.6 %collective-permute-start.12 = (f16[2,96,1280]{2,1,0:T(8,128)(2,1)S(1)}, f16[2,96,1280]{2,1,0:T(8,128)(2,1)S(1)}, u32[]{:S(2)}, u32[]{:S(2)}) collective-permute-start(f16[2,96,1280]{2,1,0:T(8,128)(2,1)S(1)} %fusion.9), channel_id=1, source_target_pairs={{0,16},{8,24},{16,0},{24,8},{1,17},{9,25},{17,1},{25,9},{2,18},{10... | collective-permute-start | bytes 1474568 | tf_op jit(solution)/shard_map/ppermute | solution.py:19
  47.1 7.7 %collective-permute-done.6 = f16[2,96,1280]{2,1,0:T(8,128)(2,1)S(1)} collective-permute-done((f16[2,96,1280]{2,1,0:T(8,128)(2,1)S(1)}, f16[2,96,1280]{2,1,0:T(8,128)(2,1)S(1)}, u32[]{:S(2)}, u32[]{:S(2)}) %collective-permute-start.6) | collective-permute-done | bytes 491552 | tf_op jit(solution)/shard_map/ppermute | solution.py:19
  54.9 1.6 %collective-permute-start.7 = (f16[96,1280]{1,0:T(8,128)(2,1)S(1)}, f16[96,1280]{1,0:T(8,128)(2,1)S(1)}, u32[]{:S(2)}, u32[]{:S(2)}) collective-permute-start(f16[96,1280]{1,0:T(8,128)(2,1)S(1)} %fusion.19), channel_id=1, source_target_pairs={{0,16},{8,24},{16,0},{24,8},{1,17},{9,25},{17,1},{25,9},{2,18},{10... | collective-permute-start | bytes 737288 | tf_op jit(solution)/shard_map/ppermute | solution.py:19
  56.5 3.1 %collective-permute-done.12 = f16[2,96,1280]{2,1,0:T(8,128)(2,1)S(1)} collective-permute-done((f16[2,96,1280]{2,1,0:T(8,128)(2,1)S(1)}, f16[2,96,1280]{2,1,0:T(8,128)(2,1)S(1)}, u32[]{:S(2)}, u32[]{:S(2)}) %collective-permute-start.12) | collective-permute-done | bytes 491552 | tf_op jit(solution)/shard_map/ppermute | solution.py:19
  59.9 3.9 %collective-permute-done.7 = f16[96,1280]{1,0:T(8,128)(2,1)S(1)} collective-permute-done((f16[96,1280]{1,0:T(8,128)(2,1)S(1)}, f16[96,1280]{1,0:T(8,128)(2,1)S(1)}, u32[]{:S(2)}, u32[]{:S(2)}) %collective-permute-start.7) | collective-permute-done | bytes 245792 | tf_op jit(solution)/shard_map/ppermute | solution.py:19
  63.9 2.2 %collective-permute-done.13 = f16[96,1280]{1,0:T(8,128)(2,1)S(1)} collective-permute-done((f16[96,1280]{1,0:T(8,128)(2,1)S(1)}, f16[96,1280]{1,0:T(8,128)(2,1)S(1)}, u32[]{:S(2)}, u32[]{:S(2)}) %collective-permute-start.13) | collective-permute-done | bytes 245792 | tf_op jit(solution)/shard_map/ppermute | solution.py:19
  66.1 1.4 %stats.3 = f32[8,256]{1,0:T(8,128)S(1)} custom-call(f32[5]{0:T(128)S(1)} %get-tuple-element.148.inverse_ref, f32[96,1280]{1,0:T(8,128)S(1)} %bitcast_add_fusion.3.refs_0_, f32[96,1280]{1,0:T(8,128)S(1)} %bitcast_add_fusion.2.refs_1_.refs_0_), custom_call_target="tpu_custom_call" | custom-call | flops 2457600 | bytes 491520 | tf_op jit(solution)/shard_map/stats/pallas_call | solution.py:70
  67.6 1.1 collective-permute-done.14
  68.9 0.3 collective-permute-start.15
  69.2 0.7 maximum_bitcast_fusion
  69.9 2.8 %collective-permute-done.15 = f32[16,256]{1,0:T(8,128)S(1)} collective-permute-done((f32[16,256]{1,0:T(8,128)S(1)}, f32[16,256]{1,0:T(8,128)S(1)}, u32[]{:S(2)}, u32[]{:S(2)}) %collective-permute-start.15) | collective-permute-done | bytes 16416 | tf_op jit(solution)/shard_map/ppermute | solution.py:19
  72.9 1.0 collective-permute-start.16
  74.0 3.6 %collective-permute-done.16 = f32[16,256]{1,0:T(8,128)S(1)} collective-permute-done((f32[16,256]{1,0:T(8,128)S(1)}, f32[16,256]{1,0:T(8,128)S(1)}, u32[]{:S(2)}, u32[]{:S(2)}) %collective-permute-start.16) | collective-permute-done | bytes 16416 | tf_op jit(solution)/shard_map/ppermute | solution.py:19
  77.9 1.5 %grad.2 = bf16[96,1280]{1,0:T(8,128)(2,1)S(1)} custom-call(f32[2,5]{1,0:T(2,128)S(1)} %pad_maximum_fusion.16.scalars_ref, bf16[192,1280]{1,0:T(8,128)(2,1)S(1)} %copy-done.1, f32[96,1280]{1,0:T(8,128)S(1)} %bitcast_add_fusion.3.refs_0_, f32[16,128]{1,0:T(8,128)S(1)} %get-tuple-element.135.refs_1_), custom_call_target="tpu_custom_call" | custom-call | flops 2949120 | bytes 983040 | tf_op jit(solution)/shard_map/grad/pallas_call | solution.py:119
  79.5 1.5 %collective-permute-start.18 = (bf16[96,1280]{1,0:T(8,128)(2,1)S(1)}, bf16[96,1280]{1,0:T(8,128)(2,1)S(1)}, u32[]{:S(2)}, u32[]{:S(2)}) collective-permute-start(bf16[96,1280]{1,0:T(8,128)(2,1)S(1)} %grad.2), channel_id=1, source_target_pairs={{0,16},{8,24},{16,0},{24,8},{1,17},{9,25},{17,1},{25,9},{2,18},{10... | collective-permute-start | bytes 737288 | tf_op jit(solution)/shard_map/ppermute | solution.py:19
  81.0 1.9 %collective-permute-start.19 = (bf16[96,1280]{1,0:T(8,128)(2,1)S(1)}, bf16[96,1280]{1,0:T(8,128)(2,1)S(1)}, u32[]{:S(2)}, u32[]{:S(2)}) collective-permute-start(bf16[96,1280]{1,0:T(8,128)(2,1)S(1)} %grad.2), channel_id=1, source_target_pairs={{0,24},{8,16},{16,8},{24,0},{1,25},{9,17},{17,9},{25,1},{2,26},{10... | collective-permute-start | bytes 737288 | tf_op jit(solution)/shard_map/ppermute | solution.py:19
  82.9 1.5 %grad.3 = bf16[96,1280]{1,0:T(8,128)(2,1)S(1)} custom-call(f32[2,5]{1,0:T(2,128)S(1)} %pad_maximum_fusion.16.scalars_ref, bf16[192,1280]{1,0:T(8,128)(2,1)S(1)} %copy-done.1, f32[96,1280]{1,0:T(8,128)S(1)} %bitcast_add_fusion.2.refs_1_.refs_0_, f32[16,128]{1,0:T(8,128)S(1)} %get-tuple-element.134.refs_1_), custom_call_target="tpu_custom_call" | custom-call | flops 2949120 | bytes 983040 | tf_op jit(solution)/shard_map/grad/pallas_call | solution.py:119
  84.4 2.5 %copy-done = bf16[2048,1280]{1,0:T(8,128)(2,1)S(1)} copy-done((bf16[2048,1280]{1,0:T(8,128)(2,1)S(1)}, bf16[2048,1280]{1,0:T(8,128)(2,1)}, u32[]{:S(2)}) %copy-start) | copy-done | bytes 5242904
  86.9 4.2 %row_blocks.1 = (bf16[4,256,1280]{2,1,0:T(8,128)(2,1)S(1)}, bf16[4,256,1280]{2,1,0:T(8,128)(2,1)S(1)}) custom-call(s32[2,4]{1,0:T(2,128)S(1)} %pad_add_fusion.order_ref, bf16[2048,1280]{1,0:T(8,128)(2,1)S(1)} %copy-done), custom_call_target="tpu_custom_call" | custom-call | bytes 10485760 | tf_op jit(solution)/shard_map/row_blocks/pallas_call | solution.py:164
  91.1 0.3 collective-permute-done.19
  91.7 1.5 %convolution_convert_fusion.2 = bf16[4,256,384]{2,1,0:T(8,128)(2,1)S(1)} fusion(bf16[4,256,1280]{2,1,0:T(8,128)(2,1)S(1)} %get-tuple-element.66, bf16[384,1280]{1,0:T(8,128)(2,1)S(1)} %pad_maximum_fusion.2), kind=kOutput, calls=%fused_computation.6 | convolution fusion | flops 1007026176 | bytes 4390912 | tf_op jit(solution)/shard_map/dot_general | solution.py:227
  93.3 0.9 collective-permute-start.21
  94.1 1.5 %collective-permute-start.24 = (bf16[96,1280]{1,0:T(8,128)(2,1)S(1)}, bf16[96,1280]{1,0:T(8,128)(2,1)S(1)}, u32[]{:S(2)}, u32[]{:S(2)}) collective-permute-start(bf16[96,1280]{1,0:T(8,128)(2,1)S(1)} %grad.3), channel_id=1, source_target_pairs={{0,16},{8,24},{16,0},{24,8},{1,17},{9,25},{17,1},{25,9},{2,18},{10... | collective-permute-start | bytes 737288 | tf_op jit(solution)/shard_map/ppermute | solution.py:19
  95.7 1.2 collective-permute-start.25
  96.8 1.5 %fusion.7 = f32[4,256,384]{2,1,0:T(8,128)S(1)} fusion(bf16[4,256,1280]{2,1,0:T(8,128)(2,1)S(1)} %get-tuple-element.59, bf16[384,1280]{1,0:T(8,128)(2,1)S(1)} %pad_maximum_fusion.2), kind=kOutput, calls=%fused_computation.16 | convolution fusion | flops 1006632960 | bytes 5177344 | tf_op jit(solution)/shard_map/dot_general | solution.py:227
  98.6 3.5 %collective-permute-done.21 = bf16[96,1280]{1,0:T(8,128)(2,1)S(1)} collective-permute-done((bf16[96,1280]{1,0:T(8,128)(2,1)S(1)}, bf16[96,1280]{1,0:T(8,128)(2,1)S(1)}, u32[]{:S(2)}, u32[]{:S(2)}) %collective-permute-start.21) | collective-permute-done | bytes 245792 | tf_op jit(solution)/shard_map/ppermute | solution.py:19
  102.2 0.4 collective-permute-start.22
  102.6 2.7 %collective-permute-start.23 = (bf16[2,128,384]{2,1,0:T(8,128)(2,1)S(1)}, bf16[2,128,384]{2,1,0:T(8,128)(2,1)S(1)}, u32[]{:S(2)}, u32[]{:S(2)}) collective-permute-start(bf16[2,128,384]{2,1,0:T(8,128)(2,1)S(1)} %pad_maximum_fusion.11), channel_id=1, source_target_pairs={{0,4},{1,5},{2,6},{3,7},{4,0},{5,1},{6,2},{7,3},{8,12},{9,13},{10,... | collective-permute-start | bytes 589832 | tf_op jit(solution)/shard_map/ppermute | solution.py:19
  105.3 1.2 collective-permute-done.24
  106.5 1.1 collective-permute-done.25
  107.9 1.5 %convolution_convert_fusion.1 = bf16[4,256,384]{2,1,0:T(8,128)(2,1)S(1)} fusion(bf16[4,256,1280]{2,1,0:T(8,128)(2,1)S(1)} %get-tuple-element.66, bf16[384,1280]{1,0:T(8,128)(2,1)S(1)} %pad_maximum_fusion.4), kind=kOutput, calls=%fused_computation.5 | convolution fusion | flops 1007026176 | bytes 4390912 | tf_op jit(solution)/shard_map/dot_general | solution.py:227
  109.5 1.5 %fusion.4 = f32[4,256,384]{2,1,0:T(8,128)S(1)} fusion(bf16[4,256,1280]{2,1,0:T(8,128)(2,1)S(1)} %get-tuple-element.59, bf16[384,1280]{1,0:T(8,128)(2,1)S(1)} %pad_maximum_fusion.4), kind=kOutput, calls=%fused_computation.13 | convolution fusion | flops 1006632960 | bytes 5177344 | tf_op jit(solution)/shard_map/dot_general | solution.py:227
  111.1 1.1 collective-permute-done.22
  112.1 1.4 %collective-permute-done.23 = bf16[2,128,384]{2,1,0:T(8,128)(2,1)S(1)} collective-permute-done((bf16[2,128,384]{2,1,0:T(8,128)(2,1)S(1)}, bf16[2,128,384]{2,1,0:T(8,128)(2,1)S(1)}, u32[]{:S(2)}, u32[]{:S(2)}) %collective-permute-start.23) | collective-permute-done | bytes 196640 | tf_op jit(solution)/shard_map/ppermute | solution.py:19
  113.9 0.3 collective-permute-start.29
  114.2 2.8 %collective-permute-start.30 = (bf16[2,128,384]{2,1,0:T(8,128)(2,1)S(1)}, bf16[2,128,384]{2,1,0:T(8,128)(2,1)S(1)}, u32[]{:S(2)}, u32[]{:S(2)}) collective-permute-start(bf16[2,128,384]{2,1,0:T(8,128)(2,1)S(1)} %pad_maximum_fusion.13), channel_id=1, source_target_pairs={{0,4},{1,5},{2,6},{3,7},{4,0},{5,1},{6,2},{7,3},{8,12},{9,13},{10,... | collective-permute-start | bytes 589832 | tf_op jit(solution)/shard_map/ppermute | solution.py:19
  117.0 0.2 collective-permute-start.27
  117.2 1.8 %collective-permute-start.28 = (bf16[1,128,384]{2,1,0:T(8,128)(2,1)S(1)}, bf16[1,128,384]{2,1,0:T(8,128)(2,1)S(1)}, u32[]{:S(2)}, u32[]{:S(2)}) collective-permute-start(bf16[1,128,384]{2,1,0:T(8,128)(2,1)S(1)} %bitcast.240), channel_id=1, source_target_pairs={{0,2},{1,3},{2,0},{3,1},{4,6},{5,7},{6,4},{7,5},{8,10},{9,11},{10,... | collective-permute-start | bytes 294920 | tf_op jit(solution)/shard_map/ppermute | solution.py:19
  119.3 1.3 copy-done.3
  120.6 6.2 %convolution_convert_fusion = bf16[2048,1280]{1,0:T(8,128)(2,1)} fusion(bf16[768,1280]{1,0:T(8,128)(2,1)S(1)} %bitcast.222, bf16[384,2048]{1,0:T(8,128)(2,1)S(1)} %bitcast_dynamic-update-slice_fusion, bf16[384,2048]{1,0:T(8,128)(2,1)S(1)} %copy-done.3), kind=kOutput, calls=%fused_computation | convolution fusion | flops 4035444736 | bytes 10354688 | tf_op jit(solution)/shard_map/dot_general | solution.py:318
  126.8 2.1 %collective-permute-done.27 = bf16[1,128,384]{2,1,0:T(8,128)(2,1)S(1)} collective-permute-done((bf16[1,128,384]{2,1,0:T(8,128)(2,1)S(1)}, bf16[1,128,384]{2,1,0:T(8,128)(2,1)S(1)}, u32[]{:S(2)}, u32[]{:S(2)}) %collective-permute-start.27) | collective-permute-done | bytes 98336 | tf_op jit(solution)/shard_map/ppermute | solution.py:19
  129.1 2.6 %collective-permute-start.32 = (bf16[1,128,384]{2,1,0:T(8,128)(2,1)S(1)}, bf16[1,128,384]{2,1,0:T(8,128)(2,1)S(1)}, u32[]{:S(2)}, u32[]{:S(2)}) collective-permute-start(bf16[1,128,384]{2,1,0:T(8,128)(2,1)S(1)} %fusion.24), channel_id=1, source_target_pairs={{0,2},{1,3},{2,0},{3,1},{4,6},{5,7},{6,4},{7,5},{8,10},{9,11},{10,... | collective-permute-start | bytes 294920 | tf_op jit(solution)/shard_map/ppermute | solution.py:19
  131.8 0.2 copy.15
  132.0 2.9 %collective-permute-done.31 = bf16[1,128,384]{2,1,0:T(8,128)(2,1)S(1)} collective-permute-done((bf16[1,128,384]{2,1,0:T(8,128)(2,1)S(1)}, bf16[1,128,384]{2,1,0:T(8,128)(2,1)S(1)}, u32[]{:S(2)}, u32[]{:S(2)}) %collective-permute-start.31) | collective-permute-done | bytes 98336 | tf_op jit(solution)/shard_map/ppermute | solution.py:19
  134.9 0.5 collective-permute-done.32
  135.7 1.1 copy.18
  (141 shorter events, 4.5 us)
Async XLA Ops:
  0.6 7.3 %copy-start.4 = (f32[2]{0:T(128)S(1)}, f32[2]{0:T(128)}, u32[]{:S(2)}) copy-start(f32[2]{0:T(128)} %param.11) | copy-start | bytes 28
  0.6 7.9 %copy-start.6 = (f32[4]{0:T(128)S(1)}, f32[4]{0:T(128)}, u32[]{:S(2)}) copy-start(f32[4]{0:T(128)} %param.10) | copy-start | bytes 52
  0.7 8.6 %copy-start.1 = (bf16[192,1280]{1,0:T(8,128)(2,1)S(1)}, bf16[192,1280]{1,0:T(8,128)(2,1)}, u32[]{:S(2)}) copy-start(bf16[192,1280]{1,0:T(8,128)(2,1)} %teacher_ref.3) | copy-start | bytes 1474564
  0.7 38.5 %slice-start = ((s8[5242880]{0:T(1024)(128)(4,1)}), s8[1048576]{0:T(1024)(128)(4,1)S(1)}, s32[]{:S(2)}) async-start(s8[5242880]{0:T(1024)(128)(4,1)} %bitcast.210), calls=%async_computation | async-start | bytes 2097152
  2.0 14.5 %collective-permute-start.1 = (bf16[1,384,256]{2,1,0:T(8,128)(2,1)S(1)}, bf16[1,384,256]{2,1,0:T(8,128)(2,1)S(1)}, u32[]{:S(2)}, u32[]{:S(2)}) collective-permute-start(bf16[1,384,256]{2,1,0:T(8,128)(2,1)S(1)} %bitcast.223), channel_id=1, source_target_pairs={{0,4},{1,5},{2,6},{3,7},{4,0},{5,1},{6,2},{7,3},{8,12},{9,13},{10,... | collective-permute-start | bytes 589832 | tf_op jit(solution)/shard_map/ppermute | solution.py:19
  6.1 14.3 %collective-permute-start.8 = (bf16[1,384,256]{2,1,0:T(8,128)(2,1)S(1)}, bf16[1,384,256]{2,1,0:T(8,128)(2,1)S(1)}, u32[]{:S(2)}, u32[]{:S(2)}) collective-permute-start(bf16[1,384,256]{2,1,0:T(8,128)(2,1)S(1)} %bitcast.224), channel_id=1, source_target_pairs={{0,1},{1,0},{2,3},{3,2},{4,5},{5,4},{6,7},{7,6},{8,9},{9,8},{10,11... | collective-permute-start | bytes 589832 | tf_op jit(solution)/shard_map/ppermute | solution.py:19
  6.1 10.4 %collective-permute-start = (bf16[1,384,256]{2,1,0:T(8,128)(2,1)S(1)}, bf16[1,384,256]{2,1,0:T(8,128)(2,1)S(1)}, u32[]{:S(2)}, u32[]{:S(2)}) collective-permute-start(bf16[1,384,256]{2,1,0:T(8,128)(2,1)S(1)} %bitcast.227), channel_id=1, source_target_pairs={{0,2},{1,3},{2,0},{3,1},{4,6},{5,7},{6,4},{7,5},{8,10},{9,11},{10,... | collective-permute-start | bytes 589832 | tf_op jit(solution)/shard_map/ppermute | solution.py:19
  7.7 12.1 %collective-permute-start.2 = (bf16[1,384,256]{2,1,0:T(8,128)(2,1)S(1)}, bf16[1,384,256]{2,1,0:T(8,128)(2,1)S(1)}, u32[]{:S(2)}, u32[]{:S(2)}) collective-permute-start(bf16[1,384,256]{2,1,0:T(8,128)(2,1)S(1)} %bitcast.228), channel_id=1, source_target_pairs={{0,1},{1,0},{2,3},{3,2},{4,5},{5,4},{6,7},{7,6},{8,9},{9,8},{10,11... | collective-permute-start | bytes 589832 | tf_op jit(solution)/shard_map/ppermute | solution.py:19
  16.5 18.9 %collective-permute-start.9 = (bf16[2,384,256]{2,1,0:T(8,128)(2,1)S(1)}, bf16[2,384,256]{2,1,0:T(8,128)(2,1)S(1)}, u32[]{:S(2)}, u32[]{:S(2)}) collective-permute-start(bf16[2,384,256]{2,1,0:T(8,128)(2,1)S(1)} %pad_maximum_fusion.7), channel_id=1, source_target_pairs={{0,2},{1,3},{2,0},{3,1},{4,6},{5,7},{6,4},{7,5},{8,10},{9,11},{10,... | collective-permute-start | bytes 1179656 | tf_op jit(solution)/shard_map/ppermute | solution.py:19
  17.1 19.9 %collective-permute-start.4 = (bf16[2,384,256]{2,1,0:T(8,128)(2,1)S(1)}, bf16[2,384,256]{2,1,0:T(8,128)(2,1)S(1)}, u32[]{:S(2)}, u32[]{:S(2)}) collective-permute-start(bf16[2,384,256]{2,1,0:T(8,128)(2,1)S(1)} %pad_maximum_fusion.6), channel_id=1, source_target_pairs={{0,4},{1,5},{2,6},{3,7},{4,0},{5,1},{6,2},{7,3},{8,12},{9,13},{10,... | collective-permute-start | bytes 1179656 | tf_op jit(solution)/shard_map/ppermute | solution.py:19
  19.8 17.4 %collective-permute-start.11 = (bf16[1,384,256]{2,1,0:T(8,128)(2,1)S(1)}, bf16[1,384,256]{2,1,0:T(8,128)(2,1)S(1)}, u32[]{:S(2)}, u32[]{:S(2)}) collective-permute-start(bf16[1,384,256]{2,1,0:T(8,128)(2,1)S(1)} %collective-permute-done.1), channel_id=1, source_target_pairs={{0,1},{1,0},{2,3},{3,2},{4,5},{5,4},{6,7},{7,6},{8,9},{9,8},{10,11... | collective-permute-start | bytes 589832 | tf_op jit(solution)/shard_map/ppermute | solution.py:19
  19.8 1.7 %collective-permute-start.3 = (bf16[1,384,256]{2,1,0:T(8,128)(2,1)S(1)}, bf16[1,384,256]{2,1,0:T(8,128)(2,1)S(1)}, u32[]{:S(2)}, u32[]{:S(2)}) collective-permute-start(bf16[1,384,256]{2,1,0:T(8,128)(2,1)S(1)} %collective-permute-done), channel_id=1, source_target_pairs={{0,1},{1,0},{2,3},{3,2},{4,5},{5,4},{6,7},{7,6},{8,9},{9,8},{10,11... | collective-permute-start | bytes 589832 | tf_op jit(solution)/shard_map/ppermute | solution.py:19
  20.4 18.7 %slice-start.1 = ((s8[5242880]{0:T(1024)(128)(4,1)}), s8[4194304]{0:T(1024)(128)(4,1)S(1)}, s32[]{:S(2)}) async-start(s8[5242880]{0:T(1024)(128)(4,1)} %bitcast.210), calls=%async_computation.1 | async-start | bytes 8388608
  35.4 1.7 %collective-permute-start.10 = (bf16[2,384,256]{2,1,0:T(8,128)(2,1)S(1)}, bf16[2,384,256]{2,1,0:T(8,128)(2,1)S(1)}, u32[]{:S(2)}, u32[]{:S(2)}) collective-permute-start(bf16[2,384,256]{2,1,0:T(8,128)(2,1)S(1)} %collective-permute-done.9), channel_id=1, source_target_pairs={{0,1},{1,0},{2,3},{3,2},{4,5},{5,4},{6,7},{7,6},{8,9},{9,8},{10,11... | collective-permute-start | bytes 1179656 | tf_op jit(solution)/shard_map/ppermute | solution.py:19
  37.1 1.7 %collective-permute-start.5 = (bf16[2,384,256]{2,1,0:T(8,128)(2,1)S(1)}, bf16[2,384,256]{2,1,0:T(8,128)(2,1)S(1)}, u32[]{:S(2)}, u32[]{:S(2)}) collective-permute-start(bf16[2,384,256]{2,1,0:T(8,128)(2,1)S(1)} %collective-permute-done.4), channel_id=1, source_target_pairs={{0,1},{1,0},{2,3},{3,2},{4,5},{5,4},{6,7},{7,6},{8,9},{9,8},{10,11... | collective-permute-start | bytes 1179656 | tf_op jit(solution)/shard_map/ppermute | solution.py:19
  39.1 2.2 %copy-start.2 = (bf16[384,2048]{1,0:T(8,128)(2,1)}, bf16[384,2048]{1,0:T(8,128)(2,1)S(1)}, u32[]{:S(2)}) copy-start(bf16[384,2048]{1,0:T(8,128)(2,1)S(1)} %bitcast_dynamic-update-slice_fusion.8) | copy-start | bytes 4718596
  41.4 13.3 %collective-permute-start.6 = (f16[2,96,1280]{2,1,0:T(8,128)(2,1)S(1)}, f16[2,96,1280]{2,1,0:T(8,128)(2,1)S(1)}, u32[]{:S(2)}, u32[]{:S(2)}) collective-permute-start(f16[2,96,1280]{2,1,0:T(8,128)(2,1)S(1)} %fusion.10), channel_id=1, source_target_pairs={{0,8},{8,0},{16,24},{24,16},{1,9},{9,1},{17,25},{25,17},{2,10},{10... | collective-permute-start | bytes 1474568 | tf_op jit(solution)/shard_map/ppermute | solution.py:19
  45.5 14.2 %collective-permute-start.12 = (f16[2,96,1280]{2,1,0:T(8,128)(2,1)S(1)}, f16[2,96,1280]{2,1,0:T(8,128)(2,1)S(1)}, u32[]{:S(2)}, u32[]{:S(2)}) collective-permute-start(f16[2,96,1280]{2,1,0:T(8,128)(2,1)S(1)} %fusion.9), channel_id=1, source_target_pairs={{0,16},{8,24},{16,0},{24,8},{1,17},{9,25},{17,1},{25,9},{2,18},{10... | collective-permute-start | bytes 1474568 | tf_op jit(solution)/shard_map/ppermute | solution.py:19
  54.9 8.9 %collective-permute-start.7 = (f16[96,1280]{1,0:T(8,128)(2,1)S(1)}, f16[96,1280]{1,0:T(8,128)(2,1)S(1)}, u32[]{:S(2)}, u32[]{:S(2)}) collective-permute-start(f16[96,1280]{1,0:T(8,128)(2,1)S(1)} %fusion.19), channel_id=1, source_target_pairs={{0,16},{8,24},{16,0},{24,8},{1,17},{9,25},{17,1},{25,9},{2,18},{10... | collective-permute-start | bytes 737288 | tf_op jit(solution)/shard_map/ppermute | solution.py:19
  59.8 6.3 %collective-permute-start.13 = (f16[96,1280]{1,0:T(8,128)(2,1)S(1)}, f16[96,1280]{1,0:T(8,128)(2,1)S(1)}, u32[]{:S(2)}, u32[]{:S(2)}) collective-permute-start(f16[96,1280]{1,0:T(8,128)(2,1)S(1)} %fusion.20), channel_id=1, source_target_pairs={{0,8},{8,0},{16,24},{24,16},{1,9},{9,1},{17,25},{25,17},{2,10},{10... | collective-permute-start | bytes 737288 | tf_op jit(solution)/shard_map/ppermute | solution.py:19
  63.8 3.7 %copy-start.5 = (s32[192]{0:T(256)S(1)}, s32[192]{0:T(256)}, u32[]{:S(2)}) copy-start(s32[192]{0:T(256)} %param.9) | copy-start | bytes 2308
  67.5 1.2 collective-permute-start.14
  68.9 3.8 %collective-permute-start.15 = (f32[16,256]{1,0:T(8,128)S(1)}, f32[16,256]{1,0:T(8,128)S(1)}, u32[]{:S(2)}, u32[]{:S(2)}) collective-permute-start(f32[16,256]{1,0:T(8,128)S(1)} %concatenate.69), channel_id=1, source_target_pairs={{0,2},{1,3},{2,0},{3,1},{4,6},{5,7},{6,4},{7,5},{8,10},{9,11},{10,... | collective-permute-start | bytes 49160 | tf_op jit(solution)/shard_map/ppermute | solution.py:19
  72.9 4.7 %collective-permute-start.16 = (f32[16,256]{1,0:T(8,128)S(1)}, f32[16,256]{1,0:T(8,128)S(1)}, u32[]{:S(2)}, u32[]{:S(2)}) collective-permute-start(f32[16,256]{1,0:T(8,128)S(1)} %concatenate.70), channel_id=1, source_target_pairs={{0,4},{1,5},{2,6},{3,7},{4,0},{5,1},{6,2},{7,3},{8,12},{9,13},{10,... | collective-permute-start | bytes 49160 | tf_op jit(solution)/shard_map/ppermute | solution.py:19
  79.3 11.7 %collective-permute-start.17 = (bf16[96,1280]{1,0:T(8,128)(2,1)S(1)}, bf16[96,1280]{1,0:T(8,128)(2,1)S(1)}, u32[]{:S(2)}, u32[]{:S(2)}) collective-permute-start(bf16[96,1280]{1,0:T(8,128)(2,1)S(1)} %grad.2), channel_id=1, source_target_pairs={{0,8},{8,0},{16,24},{24,16},{1,9},{9,1},{17,25},{25,17},{2,10},{10... | collective-permute-start | bytes 737288 | tf_op jit(solution)/shard_map/ppermute | solution.py:19
  79.5 11.6 %collective-permute-start.18 = (bf16[96,1280]{1,0:T(8,128)(2,1)S(1)}, bf16[96,1280]{1,0:T(8,128)(2,1)S(1)}, u32[]{:S(2)}, u32[]{:S(2)}) collective-permute-start(bf16[96,1280]{1,0:T(8,128)(2,1)S(1)} %grad.2), channel_id=1, source_target_pairs={{0,16},{8,24},{16,0},{24,8},{1,17},{9,25},{17,1},{25,9},{2,18},{10... | collective-permute-start | bytes 737288 | tf_op jit(solution)/shard_map/ppermute | solution.py:19
  81.0 10.3 %collective-permute-start.19 = (bf16[96,1280]{1,0:T(8,128)(2,1)S(1)}, bf16[96,1280]{1,0:T(8,128)(2,1)S(1)}, u32[]{:S(2)}, u32[]{:S(2)}) collective-permute-start(bf16[96,1280]{1,0:T(8,128)(2,1)S(1)} %grad.2), channel_id=1, source_target_pairs={{0,24},{8,16},{16,8},{24,0},{1,25},{9,17},{17,9},{25,1},{2,26},{10... | collective-permute-start | bytes 737288 | tf_op jit(solution)/shard_map/ppermute | solution.py:19
  84.4 2.5 %copy-start = (bf16[2048,1280]{1,0:T(8,128)(2,1)S(1)}, bf16[2048,1280]{1,0:T(8,128)(2,1)}, u32[]{:S(2)}) copy-start(bf16[2048,1280]{1,0:T(8,128)(2,1)} %in_ref) | copy-start | bytes 15728644
  93.2 5.2 %collective-permute-start.20 = (bf16[4,256,384]{2,1,0:T(8,128)(2,1)S(1)}, bf16[4,256,384]{2,1,0:T(8,128)(2,1)S(1)}, u32[]{:S(2)}, u32[]{:S(2)}) collective-permute-start(bf16[4,256,384]{2,1,0:T(8,128)(2,1)S(1)} %convolution_convert_fusion.2), channel_id=1, source_target_pairs={{0,1},{1,0},{2,3},{3,2},{4,5},{5,4},{6,7},{7,6},{8,9},{9,8},{10,11... | collective-permute-start | bytes 2359304 | tf_op jit(solution)/shard_map/ppermute | solution.py:19
  93.3 8.8 %collective-permute-start.21 = (bf16[96,1280]{1,0:T(8,128)(2,1)S(1)}, bf16[96,1280]{1,0:T(8,128)(2,1)S(1)}, u32[]{:S(2)}, u32[]{:S(2)}) collective-permute-start(bf16[96,1280]{1,0:T(8,128)(2,1)S(1)} %grad.3), channel_id=1, source_target_pairs={{0,8},{8,0},{16,24},{24,16},{1,9},{9,1},{17,25},{25,17},{2,10},{10... | collective-permute-start | bytes 737288 | tf_op jit(solution)/shard_map/ppermute | solution.py:19
  94.1 12.4 %collective-permute-start.24 = (bf16[96,1280]{1,0:T(8,128)(2,1)S(1)}, bf16[96,1280]{1,0:T(8,128)(2,1)S(1)}, u32[]{:S(2)}, u32[]{:S(2)}) collective-permute-start(bf16[96,1280]{1,0:T(8,128)(2,1)S(1)} %grad.3), channel_id=1, source_target_pairs={{0,16},{8,24},{16,0},{24,8},{1,17},{9,25},{17,1},{25,9},{2,18},{10... | collective-permute-start | bytes 737288 | tf_op jit(solution)/shard_map/ppermute | solution.py:19
  95.7 11.9 %collective-permute-start.25 = (bf16[96,1280]{1,0:T(8,128)(2,1)S(1)}, bf16[96,1280]{1,0:T(8,128)(2,1)S(1)}, u32[]{:S(2)}, u32[]{:S(2)}) collective-permute-start(bf16[96,1280]{1,0:T(8,128)(2,1)S(1)} %grad.3), channel_id=1, source_target_pairs={{0,24},{8,16},{16,8},{24,0},{1,25},{9,17},{17,9},{25,1},{2,26},{10... | collective-permute-start | bytes 737288 | tf_op jit(solution)/shard_map/ppermute | solution.py:19
  102.2 9.9 %collective-permute-start.22 = (bf16[2,128,384]{2,1,0:T(8,128)(2,1)S(1)}, bf16[2,128,384]{2,1,0:T(8,128)(2,1)S(1)}, u32[]{:S(2)}, u32[]{:S(2)}) collective-permute-start(bf16[2,128,384]{2,1,0:T(8,128)(2,1)S(1)} %pad_maximum_fusion.10), channel_id=1, source_target_pairs={{0,2},{1,3},{2,0},{3,1},{4,6},{5,7},{6,4},{7,5},{8,10},{9,11},{10,... | collective-permute-start | bytes 589832 | tf_op jit(solution)/shard_map/ppermute | solution.py:19
  102.6 11.0 %collective-permute-start.23 = (bf16[2,128,384]{2,1,0:T(8,128)(2,1)S(1)}, bf16[2,128,384]{2,1,0:T(8,128)(2,1)S(1)}, u32[]{:S(2)}, u32[]{:S(2)}) collective-permute-start(bf16[2,128,384]{2,1,0:T(8,128)(2,1)S(1)} %pad_maximum_fusion.11), channel_id=1, source_target_pairs={{0,4},{1,5},{2,6},{3,7},{4,0},{5,1},{6,2},{7,3},{8,12},{9,13},{10,... | collective-permute-start | bytes 589832 | tf_op jit(solution)/shard_map/ppermute | solution.py:19
  109.4 4.2 %collective-permute-start.26 = (bf16[4,256,384]{2,1,0:T(8,128)(2,1)S(1)}, bf16[4,256,384]{2,1,0:T(8,128)(2,1)S(1)}, u32[]{:S(2)}, u32[]{:S(2)}) collective-permute-start(bf16[4,256,384]{2,1,0:T(8,128)(2,1)S(1)} %convolution_convert_fusion.1), channel_id=1, source_target_pairs={{0,1},{1,0},{2,3},{3,2},{4,5},{5,4},{6,7},{7,6},{8,9},{9,8},{10,11... | collective-permute-start | bytes 2359304 | tf_op jit(solution)/shard_map/ppermute | solution.py:19
  113.9 15.0 %collective-permute-start.29 = (bf16[2,128,384]{2,1,0:T(8,128)(2,1)S(1)}, bf16[2,128,384]{2,1,0:T(8,128)(2,1)S(1)}, u32[]{:S(2)}, u32[]{:S(2)}) collective-permute-start(bf16[2,128,384]{2,1,0:T(8,128)(2,1)S(1)} %pad_maximum_fusion.12), channel_id=1, source_target_pairs={{0,2},{1,3},{2,0},{3,1},{4,6},{5,7},{6,4},{7,5},{8,10},{9,11},{10,... | collective-permute-start | bytes 589832 | tf_op jit(solution)/shard_map/ppermute | solution.py:19
  114.2 14.7 %collective-permute-start.30 = (bf16[2,128,384]{2,1,0:T(8,128)(2,1)S(1)}, bf16[2,128,384]{2,1,0:T(8,128)(2,1)S(1)}, u32[]{:S(2)}, u32[]{:S(2)}) collective-permute-start(bf16[2,128,384]{2,1,0:T(8,128)(2,1)S(1)} %pad_maximum_fusion.13), channel_id=1, source_target_pairs={{0,4},{1,5},{2,6},{3,7},{4,0},{5,1},{6,2},{7,3},{8,12},{9,13},{10,... | collective-permute-start | bytes 589832 | tf_op jit(solution)/shard_map/ppermute | solution.py:19
  117.0 11.9 %collective-permute-start.27 = (bf16[1,128,384]{2,1,0:T(8,128)(2,1)S(1)}, bf16[1,128,384]{2,1,0:T(8,128)(2,1)S(1)}, u32[]{:S(2)}, u32[]{:S(2)}) collective-permute-start(bf16[1,128,384]{2,1,0:T(8,128)(2,1)S(1)} %bitcast.241), channel_id=1, source_target_pairs={{0,4},{1,5},{2,6},{3,7},{4,0},{5,1},{6,2},{7,3},{8,12},{9,13},{10,... | collective-permute-start | bytes 294920 | tf_op jit(solution)/shard_map/ppermute | solution.py:19
  117.2 11.7 %collective-permute-start.28 = (bf16[1,128,384]{2,1,0:T(8,128)(2,1)S(1)}, bf16[1,128,384]{2,1,0:T(8,128)(2,1)S(1)}, u32[]{:S(2)}, u32[]{:S(2)}) collective-permute-start(bf16[1,128,384]{2,1,0:T(8,128)(2,1)S(1)} %bitcast.240), channel_id=1, source_target_pairs={{0,2},{1,3},{2,0},{3,1},{4,6},{5,7},{6,4},{7,5},{8,10},{9,11},{10,... | collective-permute-start | bytes 294920 | tf_op jit(solution)/shard_map/ppermute | solution.py:19
  119.2 1.4 %copy-start.3 = (bf16[384,2048]{1,0:T(8,128)(2,1)S(1)}, bf16[384,2048]{1,0:T(8,128)(2,1)}, u32[]{:S(2)}) copy-start(bf16[384,2048]{1,0:T(8,128)(2,1)} %copy-done.2) | copy-start | bytes 4718596
  129.0 5.8 %collective-permute-start.31 = (bf16[1,128,384]{2,1,0:T(8,128)(2,1)S(1)}, bf16[1,128,384]{2,1,0:T(8,128)(2,1)S(1)}, u32[]{:S(2)}, u32[]{:S(2)}) collective-permute-start(bf16[1,128,384]{2,1,0:T(8,128)(2,1)S(1)} %fusion.23), channel_id=1, source_target_pairs={{0,4},{1,5},{2,6},{3,7},{4,0},{5,1},{6,2},{7,3},{8,12},{9,13},{10,... | collective-permute-start | bytes 294920 | tf_op jit(solution)/shard_map/ppermute | solution.py:19
  129.1 6.3 %collective-permute-start.32 = (bf16[1,128,384]{2,1,0:T(8,128)(2,1)S(1)}, bf16[1,128,384]{2,1,0:T(8,128)(2,1)S(1)}, u32[]{:S(2)}, u32[]{:S(2)}) collective-permute-start(bf16[1,128,384]{2,1,0:T(8,128)(2,1)S(1)} %fusion.24), channel_id=1, source_target_pairs={{0,2},{1,3},{2,0},{3,1},{4,6},{5,7},{6,4},{7,5},{8,10},{9,11},{10,... | collective-permute-start | bytes 294920 | tf_op jit(solution)/shard_map/ppermute | solution.py:19
